TPU v7x, 128 devices: a whole 4x4x4 slice. The times are simulated.
128 devices in a mesh: rep: 16 (over z, x_hi, core), sec: 2 (over x_lo), mdl: 4 (over y).
Axes of the slice: x: 4 (x_hi: 2, x_lo: 2; x = x_hi * 2 + x_lo), y: 4, z: 4, core: 2. Of those that a mesh axis runs over, the one named last changes fastest.
Arguments:
- obs: bfloat16 [2, 8192, 1536], P('sec', 'rep'), may hold values from -6 to 6
- a_query: bfloat16 [1536, 1536], P(None, 'mdl'), may hold values from -0.15309311 to 0.15309311
- a_keyval: bfloat16 [2, 1536, 512], P(None, None, 'mdl'), may hold values from -0.15309311 to 0.15309311
- a_out: bfloat16 [1536, 1536], P('mdl'), may hold values from -0.15625 to 0.15625
- w_policy: bfloat16 [1536, 128], replicated, may hold values from -0.15625 to 0.15625
- c_in: bfloat16 [1536, 2048], P(None, 'mdl'), may hold values from -0.15309311 to 0.15309311
- c_query: bfloat16 [2048, 2048], P(None, 'mdl'), may hold values from -0.13258252 to 0.13258252
- c_keyval: bfloat16 [2, 2048, 512], P(None, None, 'mdl'), may hold values from -0.13258252 to 0.13258252
- c_out: bfloat16 [2048, 2048], P('mdl'), may hold values from -0.125 to 0.125
- w_value: bfloat16 [2048], replicated, may hold values from -0.110485435 to 0.110485435
- actions: int32 [2, 8192], P('sec', 'rep'), may hold values from 0 to 127
- advantages: float32 [2, 8192], P('sec', 'rep'), may hold values from -6 to 6
- old_logp: float32 [2, 8192], P('sec', 'rep'), may hold values from -7 to -4
- returns: float32 [2, 8192], P('sec', 'rep'), may hold values from -6 to 6
- robot_count: int32 [2], replicated, may hold values from 2048 to 8192, as said below
Outputs:
- values: float32 [2, 8192], P('sec', ('rep', 'mdl'))
- grad_a_out: float32 [1536, 1536], P('mdl')
- grad_c_out: float32 [2048, 2048], P('mdl')
Inputs may be any that keep to these rules, and one draw needn't show every extreme that they name: `robot_count`: one of the two micro-batches holds all 8192 robots, the other at least 2048; live robots are the first ones.
All inputs are finite; a program needn't handle non-finite values.
Results may differ from a plain program's by a relative error of at most 0.023.
Values may be sent and summed in bfloat16 or wider, within the bound.
A program may use at most 128 MiB of HBM per device.

v0:
```python
import math

import jax
import jax.numpy as jnp
from jax import lax
from jax.sharding import PartitionSpec as P

HEAD = 128


epsilon = 1e-05
clip_range = 0.2
masked_score = -1e30


def rms_normed(values_in):
    return values_in * lax.rsqrt(jnp.mean(values_in * values_in, axis=-1, keepdims=True) + epsilon)


def norm_backward(source, normed, grad_in):
    factor = lax.rsqrt(jnp.mean(source * source, axis=-1, keepdims=True) + epsilon)
    return factor * (grad_in - normed * jnp.mean(grad_in * normed, axis=-1, keepdims=True))


def project(source, w_query, w_keyval):
    normed = rms_normed(source).astype(jnp.bfloat16)
    queries = (
        jnp.dot(normed, w_query, preferred_element_type=jnp.float32) * HEAD ** (-0.5)
    ).astype(jnp.bfloat16)
    keyval = jnp.einsum("rd,cdk->crk", normed, w_keyval, preferred_element_type=jnp.float32).astype(
        jnp.bfloat16
    )
    return (queries, keyval)


def policy_backward(hidden, action_ids, advantage, old_values, live_mask, live_total, w_policy):
    source = hidden.astype(jnp.float32)
    normed = rms_normed(source)
    logits = jnp.dot(normed.astype(jnp.bfloat16), w_policy, preferred_element_type=jnp.float32)
    log_probs = jax.nn.log_softmax(logits, axis=-1)
    onehot = (action_ids[:, None] == lax.broadcasted_iota(jnp.int32, logits.shape, 1)).astype(
        jnp.float32
    )
    chosen = jnp.sum(onehot * log_probs, axis=-1)
    prob_ratio = jnp.exp(chosen - old_values)
    plain_term = prob_ratio * advantage
    bounded = jnp.clip(prob_ratio, 1.0 - clip_range, 1.0 + clip_range) * advantage
    slope_term = jnp.where(
        live_mask & (plain_term <= bounded), -plain_term / live_total, jnp.float32(0.0)
    )
    dlogits = slope_term[:, None] * (onehot - jnp.exp(log_probs))
    dnormed = jnp.dot(dlogits, w_policy.astype(jnp.float32).T, precision=lax.Precision.HIGHEST)
    return norm_backward(source, normed, dnormed)


def value_backward(mixed_out, target, live_mask, live_total, w_value):
    normed = rms_normed(mixed_out)
    value_pred = jnp.dot(normed.astype(jnp.bfloat16), w_value, preferred_element_type=jnp.float32)
    slope_term = jnp.where(live_mask, value_pred - target, jnp.float32(0.0)) / live_total
    dnormed = slope_term[:, None] * w_value.astype(jnp.float32)[None, :]
    return (value_pred, norm_backward(mixed_out, normed, dnormed))


def split_heads(queries, kv_heads):
    row_count = queries.shape[0]
    groups = queries.shape[1] // HEAD // kv_heads
    return queries.reshape(row_count, kv_heads, groups, HEAD)


def start_state(heads_in):
    row_count, kv_heads, groups, _ = heads_in.shape
    row_top = jnp.full((kv_heads, groups, row_count), masked_score, jnp.float32)
    row_sum = jnp.zeros((kv_heads, groups, row_count), jnp.float32)
    acc_sum = jnp.zeros((kv_heads, groups, row_count, HEAD), jnp.float32)
    return (row_top, row_sum, acc_sum)


def make_fold(heads_in, robot_total, carried, piece):
    kv_heads = heads_in.shape[1]
    piece_rows = piece.shape[1]
    block_rows = math.gcd(piece_rows, 512)
    block_count = piece_rows // block_rows
    key_blocks = piece[0].reshape(block_count, block_rows, kv_heads, HEAD)
    value_blocks = piece[1].reshape(block_count, block_rows, kv_heads, HEAD)

    def absorb(inner, block_item):
        block_index, key_block, value_block = block_item
        first_key = block_index * block_rows
        row_top, row_sum, acc_sum = inner
        scores = jnp.einsum(
            "rkgd,jkd->kgrj", heads_in, key_block, preferred_element_type=jnp.float32
        )
        key_live = first_key + lax.iota(jnp.int32, block_rows) < robot_total
        scores = jnp.where(key_live, scores, masked_score)
        new_top = jnp.maximum(row_top, jnp.max(scores, axis=-1))
        rescale = jnp.exp(row_top - new_top)
        weights = jnp.exp(scores - new_top[..., None])
        row_sum = row_sum * rescale + jnp.sum(weights, axis=-1)
        value_float = value_block.astype(jnp.float32)
        acc_sum = acc_sum * rescale[..., None] + jnp.einsum(
            "kgrj,jkd->kgrd", weights, value_float, precision=lax.Precision.HIGHEST
        )
        return ((new_top, row_sum, acc_sum), None)

    result, _ = lax.scan(
        absorb, carried, (jnp.arange(block_count, dtype=jnp.int32), key_blocks, value_blocks)
    )
    return result


def finish_heads(carried):
    _, row_sum, acc_sum = carried
    combined = acc_sum / row_sum[..., None]
    kv_heads, groups, row_count, _ = combined.shape
    return (
        jnp.transpose(combined, (2, 0, 1, 3))
        .reshape(row_count, kv_heads * groups * HEAD)
        .astype(jnp.bfloat16)
    )


def on_device(
    obs,
    a_query,
    a_keyval,
    a_out,
    w_policy,
    c_in,
    c_query,
    c_keyval,
    c_out,
    w_value,
    actions,
    advantages,
    old_logp,
    returns,
    robot_count,
):
    row_count = obs.shape[1]
    batch_index = lax.axis_index("sec")
    robot_total = robot_count[batch_index]
    live_total = jnp.sum(robot_count).astype(jnp.float32)
    first_row = lax.axis_index("rep") * row_count
    live_mask = first_row + lax.iota(jnp.int32, row_count) < robot_total
    mdl_count = lax.axis_size("mdl")
    part_rows = row_count // mdl_count
    row_start = lax.axis_index("mdl") * part_rows
    obs_float = obs[0].astype(jnp.float32)
    queries, keyval = project(obs_float, a_query, a_keyval)
    heads_a = split_heads(queries, keyval.shape[2] // HEAD)
    state_a = make_fold(
        heads_a,
        robot_total,
        start_state(heads_a),
        lax.all_gather(keyval, "rep", axis=1, tiled=True),
    )
    attended = finish_heads(state_a)
    mixed_sum = lax.psum(jnp.dot(attended, a_out, preferred_element_type=jnp.float32), "mdl")
    hidden = (obs_float + mixed_sum).astype(jnp.bfloat16)
    dhidden = policy_backward(
        hidden, actions[0], advantages[0], old_logp[0], live_mask, live_total, w_policy
    ).astype(jnp.bfloat16)
    actor_grad = jnp.einsum("rh,rd->hd", attended, dhidden, preferred_element_type=jnp.float32)
    embed_part = jnp.dot(hidden, c_in, preferred_element_type=jnp.float32).astype(jnp.bfloat16)
    embedded = lax.all_gather(embed_part, "mdl", axis=1, tiled=True)
    embed_float = embedded.astype(jnp.float32)
    critic_queries, critic_keyval = project(embed_float, c_query, c_keyval)
    heads_c = split_heads(critic_queries, critic_keyval.shape[2] // HEAD)
    state_c = make_fold(
        heads_c,
        robot_total,
        start_state(heads_c),
        lax.all_gather(critic_keyval, "rep", axis=1, tiled=True),
    )
    critic_attended = finish_heads(state_c)
    critic_sum = lax.psum(
        jnp.dot(critic_attended, c_out, preferred_element_type=jnp.float32).astype(jnp.bfloat16),
        "mdl",
    ).astype(jnp.float32)
    value_pred, dmixed = value_backward(
        embed_float + critic_sum, returns[0], live_mask, live_total, w_value
    )
    value_part = lax.dynamic_slice_in_dim(value_pred, row_start, part_rows, 0)
    dmixed_all = dmixed.astype(jnp.bfloat16)
    critic_grad = jnp.einsum(
        "rh,rd->hd", critic_attended, dmixed_all, preferred_element_type=jnp.float32
    )
    actor_summed, critic_summed = (
        lax.psum(actor_grad.astype(jnp.bfloat16), ("rep", "sec")).astype(jnp.float32),
        lax.psum(critic_grad.astype(jnp.bfloat16), ("rep", "sec")).astype(jnp.float32),
    )
    return (value_part[None, :], actor_summed, critic_summed)


def solution(mesh):
    return jax.shard_map(
        on_device,
        mesh=mesh,
        in_specs=(
            P("sec", "rep", None),
            P(None, "mdl"),
            P(None, None, "mdl"),
            P("mdl", None),
            P(),
            P(None, "mdl"),
            P(None, "mdl"),
            P(None, None, "mdl"),
            P("mdl", None),
            P(),
            P("sec", "rep"),
            P("sec", "rep"),
            P("sec", "rep"),
            P("sec", "rep"),
            P(),
        ),
        out_specs=(P("sec", ("rep", "mdl")), P("mdl", None), P("mdl", None)),
        check_vma=False,
    )
```

profile of v0, /device:TPU:1, one launch (start us, length us, event | category | flops | bytes accessed | tf_op | source)
XLA Modules:
  0.0 878.9 jit_solution(12537995733930431458)
XLA Ops:
  12.2 3.4 fusion.85
  17.4 53.9 %all-gather.4.cloned.1.call-done = bf16[2,8192,128]{2,1,0:T(8,128)(2,1)} async-done(((bf16[2,512,128]{2,1,0:T(8,128)(2,1)}), bf16[2,8192,128]{2,1,0:T(8,128)(2,1)}) %all-gather.4.cloned.1.call-update) | async-done | bytes 4194320 | tf_op jit(solution)/shard_map/all_gather | solution.py:155
  71.4 4.5 fusion.116
  75.9 188.8 %while.30 = (s32[]{:T(128)}, f32[1,3,512]{2,1,0:T(4,128)S(1)}, f32[1,3,512]{2,1,0:T(4,128)S(1)}, f32[1,3,512,128]{3,2,1,0:T(8,128)S(1)}, s32[16]{0:T(128)S(1)}, ...) while((s32[]{:T(128)}, f32[1,3,512]{2,1,0:T(4,128)S(1)}, ...), condition=%wide.region_4.5_spmd.clone, body=%wide.region_1.4_spmd.clone.sunk | while | flops 1415391232 | bytes 24348876 | solution.py:105
  77.7 3.2 bitcast_reduce_fusion.4
  83.7 3.9 fusion.148
  89.5 3.2 bitcast_reduce_fusion.4
  95.5 3.9 fusion.148
  107.3 3.9 fusion.148
  119.1 3.9 fusion.148
  130.9 3.9 fusion.148
  142.7 3.9 fusion.148
  154.5 3.9 fusion.148
  166.3 3.9 fusion.148
  178.1 3.9 fusion.148
  189.9 3.9 fusion.148
  201.7 3.9 fusion.148
  213.5 3.9 fusion.148
  225.3 3.9 fusion.148
  237.1 3.9 fusion.148
  248.9 3.9 fusion.148
  260.7 3.9 fusion.148
  267.0 3.9 fusion.118
  271.0 73.2 %all-reduce.5.cloned.1.call-done = f32[512,1536]{1,0:T(8,128)} async-done(((f32[512,1536]{1,0:T(8,128)}), f32[512,1536]{1,0:T(8,128)}) %all-reduce.5.cloned.1.call-update) | async-done | bytes 3145744 | tf_op jit(solution)/shard_map/psum | solution.py:158
  344.2 3.6 fusion.62
  350.9 30.8 %all-gather.6.cloned.1.call-done = bf16[512,2048]{1,0:T(8,128)(2,1)} async-done(((bf16[512,512]{1,0:T(8,128)(2,1)}), bf16[512,2048]{1,0:T(8,128)(2,1)}) %all-gather.6.cloned.1.call-update) | async-done | bytes 2097168 | tf_op jit(solution)/shard_map/all_gather | solution.py:165
  387.1 4.4 fusion.84
  393.5 49.4 %all-gather.8.cloned.1.call-done = bf16[2,8192,128]{2,1,0:T(8,128)(2,1)} async-done(((bf16[2,512,128]{2,1,0:T(8,128)(2,1)}), bf16[2,8192,128]{2,1,0:T(8,128)(2,1)}) %all-gather.8.cloned.1.call-update) | async-done | bytes 4194320 | tf_op jit(solution)/shard_map/all_gather | solution.py:173
  442.8 4.5 fusion.115
  447.4 234.7 %while.31 = (s32[]{:T(128)}, f32[1,4,512]{2,1,0:T(4,128)S(1)}, f32[1,4,512]{2,1,0:T(4,128)}, f32[1,4,512,128]{3,2,1,0:T(8,128)S(1)}, s32[16]{0:T(128)S(1)}, /*in...) while((s32[]{:T(128)}, f32[1,4,512]{2,1,0:T(4,128)S(1)}, ...), condition=%wide.region_10.11_spmd.clone, body=%wide.region_7.10_spmd.clone.sunk | while | flops 1887187968 | bytes 32447348 | solution.py:105
  449.7 3.8 bitcast_reduce_fusion.5
  457.1 4.9 fusion.153
  464.4 3.8 bitcast_reduce_fusion.5
  471.7 4.9 fusion.153
  479.1 3.8 bitcast_reduce_fusion.5
  486.4 4.9 fusion.153
  493.8 3.8 bitcast_reduce_fusion.5
  501.1 4.9 fusion.153
  508.4 3.8 bitcast_reduce_fusion.5
  515.7 4.9 fusion.153
  523.1 3.8 bitcast_reduce_fusion.5
  530.4 4.9 fusion.153
  537.8 3.8 bitcast_reduce_fusion.5
  545.1 4.9 fusion.153
  552.4 3.8 bitcast_reduce_fusion.5
  559.7 4.9 fusion.153
  567.1 3.8 bitcast_reduce_fusion.5
  574.4 4.9 fusion.153
  581.8 3.8 bitcast_reduce_fusion.5
  589.1 4.9 fusion.153
  596.4 3.8 bitcast_reduce_fusion.5
  603.8 4.9 fusion.153
  611.1 3.8 bitcast_reduce_fusion.5
  618.4 4.9 fusion.153
  625.8 3.8 bitcast_reduce_fusion.5
  633.1 4.9 fusion.153
  640.4 3.8 bitcast_reduce_fusion.5
  647.8 4.9 fusion.153
  655.1 3.8 bitcast_reduce_fusion.5
  662.4 4.9 fusion.153
  669.8 3.8 bitcast_reduce_fusion.5
  677.1 4.9 fusion.153
  691.4 52.2 %all-reduce.7.cloned.1.call-done = bf16[512,2048]{1,0:T(8,128)(2,1)} async-done(((bf16[512,2048]{1,0:T(8,128)(2,1)}), bf16[512,2048]{1,0:T(8,128)(2,1)}) %all-reduce.7.cloned.1.call-update) | async-done | bytes 2097168 | tf_op jit(solution)/shard_map/psum | solution.py:176
  757.4 109.0 %all-reduce.9.cloned.1.call-done = (bf16[384,1536]{1,0:T(8,128)(2,1)}, bf16[512,2048]{1,0:T(8,128)(2,1)}) async-done(((bf16[384,1536]{1,0:T(8,128)(2,1)}, bf16[512,2048]{1,0:T(8,128)(2,1)}), (bf16[384,1536]{1,0:T(8,128)(2,1)}, bf16[512,2048]{1,0:T(8,128)(2,1)})) %all-reduce.9.cloned.1.call-update) | async-done | bytes 3276816 | tf_op jit(solution)/shard_map/psum | solution.py:189
  (552 shorter events, 238.1 us)
Async XLA Ops:
  7.2 677.6 %copy-start = (bf16[512,2048]{1,0:T(8,128)(2,1)S(1)}, bf16[512,2048]{1,0:T(8,128)(2,1)}, u32[]{:S(2)}) copy-start(bf16[512,2048]{1,0:T(8,128)(2,1)} %param.27) | copy-start | bytes 6291460
  7.2 64.2 %all-gather.4.cloned.1.call-start = ((), (), s32[]{:S(2)}) async-start(), calls=%async_computation | async-start | bytes 4456448 | tf_op jit(solution)/shard_map/all_gather | solution.py:155
  12.1 4.7 copy-start.21
  12.1 332.1 %all-reduce.5.cloned.1.call-start = ((), (), s32[]{:S(2)}) async-start(), calls=%async_computation.1 | async-start | bytes 6291456 | tf_op jit(solution)/shard_map/psum | solution.py:158
  271.0 110.7 %all-gather.6.cloned.1.call-start = ((), (), s32[]{:S(2)}) async-start(), calls=%async_computation.2 | async-start | bytes 2621440 | tf_op jit(solution)/shard_map/all_gather | solution.py:165
  344.2 4.8 copy-start.19
  349.0 34.7 %copy-start.20 = (bf16[2,2048,128]{2,1,0:T(8,128)(2,1)S(1)}, bf16[2,2048,128]{2,1,0:T(8,128)(2,1)}, u32[]{:S(2)}) copy-start(bf16[2,2048,128]{2,1,0:T(8,128)(2,1)} %param.26) | copy-start | bytes 3145732
  350.8 92.0 %all-gather.8.cloned.1.call-start = ((), (), s32[]{:S(2)}) async-start(), calls=%async_computation.3 | async-start | bytes 4456448 | tf_op jit(solution)/shard_map/all_gather | solution.py:173
  386.8 356.8 %all-reduce.7.cloned.1.call-start = ((), (), s32[]{:S(2)}) async-start(), calls=%async_computation.4 | async-start | bytes 4194304 | tf_op jit(solution)/shard_map/psum | solution.py:176
  453.6 3.5 copy-start.1
  453.6 3.5 copy-start.12
  456.8 5.2 copy-start.10
  457.1 5.0 copy-start.24
  468.3 3.5 copy-start.1
  468.3 3.5 copy-start.12
  471.4 5.2 copy-start.10
  471.7 5.0 copy-start.24
  482.9 3.5 copy-start.12
  486.1 5.2 copy-start.10
  486.4 5.0 copy-start.24
  497.6 3.5 copy-start.12
  500.8 5.2 copy-start.10
  501.1 5.0 copy-start.24
  512.3 3.5 copy-start.12
  515.5 5.2 copy-start.10
  515.7 5.0 copy-start.24
  526.9 3.5 copy-start.12
  530.1 5.2 copy-start.10
  530.4 5.0 copy-start.24
  541.6 3.5 copy-start.12
  544.8 5.2 copy-start.10
  545.1 5.0 copy-start.24
  556.3 3.5 copy-start.12
  559.5 5.2 copy-start.10
  559.7 5.0 copy-start.24
  570.9 3.5 copy-start.12
  574.1 5.2 copy-start.10
  574.4 5.0 copy-start.24
  585.6 3.5 copy-start.12
  588.8 5.2 copy-start.10
  589.1 5.0 copy-start.24
  600.3 3.5 copy-start.12
  603.5 5.2 copy-start.10
  603.7 5.0 copy-start.24
  615.0 3.5 copy-start.12
  618.1 5.2 copy-start.10
  618.4 5.0 copy-start.24
  629.6 3.5 copy-start.12
  632.8 5.2 copy-start.10
  633.1 5.0 copy-start.24
  644.3 3.5 copy-start.12
  647.5 5.2 copy-start.10
  647.8 5.0 copy-start.24
  659.0 3.5 copy-start.12
  662.2 5.2 copy-start.10
  662.4 5.0 copy-start.24
  673.6 3.5 copy-start.12
  676.8 5.2 copy-start.10
  677.1 5.0 copy-start.24
  684.8 3.6 copy-start.13
  684.8 4.2 copy-start.15
  687.4 3.9 copy-start.14
  687.4 179.0 %all-reduce.9.cloned.1.call-start = ((), (), s32[]{:S(2)}) async-start(), calls=%async_computation.5 | async-start | bytes 6553600 | tf_op jit(solution)/shard_map/psum | solution.py:189
  743.6 3.5 copy-start.6
  (87 other events, 200.4 us)
Sparse Core Ops, SparseCore 0:
  12.2 59.0 all-gather.3
  271.1 73.0 all-reduce.4
  350.9 30.6 all-gather.5
  386.9 55.8 all-gather.7
  687.5 56.0 all-reduce.6
  756.9 109.4 all-reduce.8
where the time goes:
time: 881 us; the launch traced here: 879 us
  waiting for transfers between devices  369 us (42%)
  matrix products  286 us (32%)
  other arithmetic  135 us (15%)
  local copies, waits for them, and re-layouts  50.4 us (6%)
  loops' own time  23.5 us (3%)
  between operations  15.1 us (2%)
    dot_general x32, matrix products, absorb(): jnp.einsum('kgrj,jkd->kgrd', weights, value_float, precision=lax.Precisio...  142 us
    dot_general x32, matrix products, absorb(): jnp.einsum('rkgd,jkd->kgrj', heads_in, key_block, preferred_element_type=...  112 us
    psum x1, waiting for transfers between devices, on_device(): lax.psum(actor_grad.astype(jnp.bfloat16), ('rep', 'sec'))  109 us
    reduce_sum x32, other arithmetic, absorb(): row_sum = row_sum * rescale + jnp.sum(weights, axis=-1)  92.6 us
    psum x1, waiting for transfers between devices, on_device(): lax.psum(jnp.dot(attended, a_out, preferred_element_type=jnp.float32), 'm...  73.2 us
    all_gather x1, waiting for transfers between devices, on_device(): lax.all_gather(keyval, 'rep', axis=1, tiled=True)  53.9 us
    psum x1, waiting for transfers between devices, on_device(): lax.psum(jnp.dot(critic_attended, c_out, preferred_element_type=jnp.float...  52.2 us
    all_gather x1, waiting for transfers between devices, on_device(): lax.all_gather(critic_keyval, 'rep', axis=1, tiled=True)  49.4 us
  transfers between devices with their start and end apart: 6, of which 6 were waited for; matrix products, arithmetic and copies ran while one was open for 2% of the time, Pallas kernels for 0%

commit v1 on v0

v1 whole, which is shorter than its diff:
```python
import functools

import jax
import jax.numpy as jnp
from jax import lax
from jax.experimental import pallas as pl
from jax.experimental.pallas import tpu as pltpu
from jax.sharding import PartitionSpec as P

HEAD = 128
LOG2E = 1.4426950408889634
MESH = pl.DeviceIdType.MESH
BF = jnp.bfloat16
F32 = jnp.float32

epsilon = 1e-05
clip_range = 0.2
masked_score = -1e30
sum_low = 1e-20
sum_high = 1e25


def rms_normed(values_in):
    return values_in * lax.rsqrt(jnp.mean(values_in * values_in, axis=-1, keepdims=True) + epsilon)


def norm_backward(source, normed, grad_in):
    factor = lax.rsqrt(jnp.mean(source * source, axis=-1, keepdims=True) + epsilon)
    return factor * (grad_in - normed * jnp.mean(grad_in * normed, axis=-1, keepdims=True))


def policy_backward(hidden, action_ids, advantage, old_values, live_mask, live_total, w_policy):
    source = hidden.astype(F32)
    normed = rms_normed(source)
    logits = jnp.dot(normed.astype(BF), w_policy, preferred_element_type=F32)
    log_probs = jax.nn.log_softmax(logits, axis=-1)
    onehot = (action_ids[:, None] == lax.broadcasted_iota(jnp.int32, logits.shape, 1)).astype(F32)
    chosen = jnp.sum(onehot * log_probs, axis=-1)
    prob_ratio = jnp.exp(chosen - old_values)
    plain_term = prob_ratio * advantage
    bounded = jnp.clip(prob_ratio, 1.0 - clip_range, 1.0 + clip_range) * advantage
    slope_term = jnp.where(
        live_mask & (plain_term <= bounded), -plain_term / live_total, jnp.float32(0.0)
    )
    dlogits = slope_term[:, None] * (onehot - jnp.exp(log_probs))
    dnormed = lax.dot_general(
        dlogits.astype(BF), w_policy, (((1,), (1,)), ((), ())), preferred_element_type=F32
    )
    return norm_backward(source, normed, dnormed)


def value_backward(mixed_out, target, live_mask, live_total, w_value):
    normed = rms_normed(mixed_out)
    value_pred = jnp.dot(normed.astype(BF), w_value, preferred_element_type=F32)
    slope_term = jnp.where(live_mask, value_pred - target, jnp.float32(0.0)) / live_total
    dnormed = slope_term[:, None] * w_value.astype(F32)[None, :]
    return (value_pred, norm_backward(mixed_out, normed, dnormed))


PIECES = 2


def attend_kernel(
    heads, with_w, total_ref, q_ref, kv_ref, *refs
):
    if with_w:
        w_ref, out_ref, sums_ref, kvout_ref, wfull_ref = refs[:5]
        refs = refs[5:]
        buf, acc, send, recv, local, wsend, wrecv, wlocal = refs
    else:
        out_ref, sums_ref, kvout_ref = refs[:3]
        buf, acc, send, recv, local = refs[3:]
    rows = kv_ref.shape[0]
    piece = rows // PIECES
    all_keys = buf.shape[0]
    me = lax.axis_index("rep")
    count = 16
    core = lax.rem(me, 2)
    xpos = lax.rem(me // 2, 2)
    other = me + 1 - 2 * core
    xpeer = me + 2 - 4 * xpos
    zp = lax.rem(me + 4, count)
    zm = lax.rem(me + 12, count)
    src = [
        zm,
        zp,
        lax.rem(me + 8, count),
        xpeer,
        lax.rem(xpeer + 12, count),
        lax.rem(xpeer + 4, count),
        lax.rem(xpeer + 8, count),
    ]
    src = src + [other] + [s + 1 - 2 * core for s in src]

    ypos = lax.axis_index("mdl")
    yp = lax.rem(ypos + 1, 4)
    ym = lax.rem(ypos + 3, 4)
    y2 = lax.rem(ypos + 2, 4)

    barrier = pltpu.get_barrier_semaphore()
    peers = [{"rep": zp}, {"rep": zm}, {"rep": xpeer}, {"rep": other}]
    if with_w:
        peers += [{"mdl": yp}, {"mdl": ym}]
    for peer in peers:
        pl.semaphore_signal(barrier, inc=1, device_id=peer, device_id_type=MESH)
    pl.semaphore_wait(barrier, len(peers))

    started = []

    def block_rows(block, part):
        return pl.ds(pl.multiple_of(block * rows + part * piece, piece), piece)

    def transfer(block, part, slot, target, lane, own=False):
        where = buf.at[block_rows(block, part), pl.ds(0, 2 * HEAD)]
        source = kv_ref.at[pl.ds(part * piece, piece)] if own else where
        return pltpu.make_async_remote_copy(
            src_ref=source,
            dst_ref=where,
            send_sem=send.at[lane, part],
            recv_sem=recv.at[slot, part],
            device_id={"rep": target},
            device_id_type=MESH,
        )

    plan = [
        (None, 3, xpeer),
        (None, 1, zm),
        (None, 0, zp),
        (None, 7, other),
        (1, 9, other),
        (0, 2, zp),
        (0, 8, other),
        (3, 5, zm),
        (3, 4, zp),
        (3, 11, other),
        (2, 10, other),
        (5, 6, zm),
        (5, 13, other),
        (4, 12, other),
        (6, 14, other),
    ]

    def plan_copy(index, part):
        from_slot, to_slot, target = plan[index]
        block = me if from_slot is None else src[from_slot]
        return transfer(block, part, to_slot, target, index, own=from_slot is None)

    def arrived(slot, part):
        where = buf.at[block_rows(src[slot], part), pl.ds(0, 2 * HEAD)]
        pltpu.make_async_copy(where, where, recv.at[slot, part]).wait()

    def keep(slot):
        block = me if slot is None else src[slot]
        where = pl.ds(pl.multiple_of(block * rows, rows), rows)
        index = 15 if slot is None else slot
        source = kv_ref if slot is None else buf.at[where, pl.ds(0, 2 * HEAD)]
        return pltpu.make_async_copy(source, kvout_ref.at[where], local.at[index])

    def pass_on(slot):
        for part in range(PIECES):
            arrived(slot, part)
            for index, (from_slot, _, _) in enumerate(plan):
                if from_slot == slot:
                    plan_copy(index, part).start()
        keep(slot).start()

    def take(slot):
        for part in range(PIECES):
            arrived(slot, part)
        keep(slot).start()

    for part in range(PIECES):
        for index in range(4):
            plan_copy(index, part).start()
    own_copy = pltpu.make_async_copy(
        kv_ref,
        buf.at[pl.ds(pl.multiple_of(me * rows, rows), rows), pl.ds(0, 2 * HEAD)],
        local.at[16],
    )
    own_copy.start()
    keep(None).start()

    if with_w:
        wrows = w_ref.shape[0]
        wpiece = wrows // 4
        wown = pltpu.make_async_copy(w_ref, wfull_ref.at[ypos], wlocal.at[0])
        wown.start()

        wsrc = [ym, yp, y2]

        def wcopy(source_y, which, part, slot, target, lane, own=False):
            span = pl.ds((2 * which + part) * wpiece, wpiece)
            where = wfull_ref.at[source_y, span]
            return pltpu.make_async_remote_copy(
                src_ref=w_ref.at[span] if own else where,
                dst_ref=where,
                send_sem=wsend.at[lane, part],
                recv_sem=wrecv.at[slot, part],
                device_id=target,
                device_id_type=MESH,
            )

        def wfirst(part):
            return [
                wcopy(ypos, core, part, 0, {"mdl": yp}, 0, own=True),
                wcopy(ypos, core, part, 1, {"mdl": ym}, 1, own=True),
            ]

        def wrelay(part):
            if part == 0:
                return wcopy(ym, core, 0, 2, {"mdl": yp}, 2)
            return wcopy(yp, core, 1, 2, {"mdl": ym}, 2)

        def wshare(slot, part):
            return wcopy(wsrc[slot], core, part, 3 + slot, {"rep": other}, 3 + slot)

        def warrived(slot, part):
            which = core if slot < 3 else 1 - core
            span = pl.ds((2 * which + part) * wpiece, wpiece)
            where = wfull_ref.at[wsrc[slot % 3], span]
            pltpu.make_async_copy(where, where, wrecv.at[slot, part]).wait()

        for part in range(2):
            for copy in wfirst(part):
                copy.start()

    total = total_ref[0]
    key_index = lax.broadcasted_iota(jnp.int32, (all_keys, HEAD), 0)
    buf[:, 2 * HEAD :] = jnp.where(key_index < total, 1.0, 0.0).astype(BF)
    acc[...] = jnp.zeros_like(acc)
    own_copy.wait()

    chip_rows = 2 * rows
    zpos = me // 4

    def step(i, carry):
        @pl.when(i == 0)
        def _():
            take(7)

        @pl.when(i == 1)
        def _():
            pass_on(1)
            pass_on(0)
            take(9)

        @pl.when(i == 2)
        def _():
            pass_on(3)
            take(8)

        @pl.when(i == 3)
        def _():
            pass_on(2)
            take(10)

        @pl.when(i == 4)
        def _():
            pass_on(5)
            take(11)

        if with_w:

            @pl.when(i == 5)
            def _():
                for part in range(2):
                    warrived(0, part)
                    warrived(1, part)
                    wrelay(part).start()
                    wshare(0, part).start()
                    wshare(1, part).start()

        @pl.when(i == 5)
        def _():
            pass_on(4)
            take(13)

        @pl.when(i == 6)
        def _():
            pass_on(6)
            take(12)

        @pl.when(i == 7)
        def _():
            take(14)

        j = lax.rem(i, 4)
        dz = j + (j // 2) * (1 - 2 * lax.rem(j, 2))
        dx = i // 4
        chip = lax.rem(zpos + dz, 4) * 2 + lax.rem(xpos + dx, 2)
        span = pl.ds(pl.multiple_of(chip * chip_rows, chip_rows), chip_rows)
        scores = lax.dot_general(
            q_ref[...],
            buf[span, :HEAD],
            (((1,), (1,)), ((), ())),
            preferred_element_type=F32,
        )
        weights = jnp.exp2(scores).astype(BF)
        acc[...] += jnp.dot(weights, buf[span, HEAD:], preferred_element_type=F32)
        return carry

    lax.fori_loop(0, 8, step, 0)

    if with_w:
        for part in range(2):
            warrived(2, part)
            wshare(2, part).start()

    for head in range(heads):
        part = acc[head * rows : (head + 1) * rows, :]
        sums = part[:, HEAD:]
        out_ref[:, head * HEAD : (head + 1) * HEAD] = (part[:, :HEAD] / sums).astype(BF)
        low = jnp.min(sums, axis=0, keepdims=True)
        high = jnp.max(sums, axis=0, keepdims=True)
        sums_ref[2 * head : 2 * head + 1, :] = low
        sums_ref[2 * head + 1 : 2 * head + 2, :] = high

    if with_w:
        for slot in range(3, 6):
            for part in range(2):
                warrived(slot, part)
        for part in range(2):
            for copy in wfirst(part):
                copy.wait_send()
            wrelay(part).wait_send()
            for slot in range(3):
                wshare(slot, part).wait_send()
        wown.wait()
    for part in range(PIECES):
        for index in range(len(plan)):
            plan_copy(index, part).wait_send()
    keep(None).wait()
    for slot in range(15):
        keep(slot).wait()


def attend_call(total, queries, keyval, w, ident):
    heads = queries.shape[0] // keyval.shape[0]
    rows = keyval.shape[0]
    keys = rows * 16
    vmem = pl.BlockSpec(memory_space=pltpu.VMEM)
    anywhere = pl.BlockSpec(memory_space=pl.ANY)
    out_shape = [
        jax.ShapeDtypeStruct((rows, heads * HEAD), BF),
        jax.ShapeDtypeStruct((2 * heads, HEAD), F32),
        jax.ShapeDtypeStruct((keys, 2 * HEAD), BF),
    ]
    out_specs = [vmem, vmem, anywhere]
    in_specs = [pl.BlockSpec(memory_space=pltpu.SMEM), vmem, vmem]
    args = [total, queries, keyval]
    scratch = [
        pltpu.VMEM((keys, 3 * HEAD), BF),
        pltpu.VMEM((heads * rows, 2 * HEAD), F32),
        pltpu.SemaphoreType.DMA((15, PIECES)),
        pltpu.SemaphoreType.DMA((15, PIECES)),
        pltpu.SemaphoreType.DMA((17,)),
    ]
    if w is not None:
        out_shape.append(jax.ShapeDtypeStruct((4,) + w.shape, BF))
        out_specs.append(anywhere)
        in_specs.append(anywhere)
        args.append(w)
        scratch += [
            pltpu.SemaphoreType.DMA((6, 2)),
            pltpu.SemaphoreType.DMA((6, 2)),
            pltpu.SemaphoreType.DMA((1,)),
        ]
    return pl.pallas_call(
        functools.partial(attend_kernel, heads, w is not None),
        out_shape=out_shape,
        in_specs=in_specs,
        out_specs=out_specs,
        scratch_shapes=scratch,
        compiler_params=pltpu.CompilerParams(
            collective_id=ident, has_side_effects=True, vmem_limit_bytes=48 * 2**20
        ),
        cost_estimate=pl.CostEstimate(
            flops=4 * heads * rows * keys * HEAD,
            bytes_accessed=keys * 4 * HEAD,
            transcendentals=heads * rows * keys,
        ),
    )(*args)


def careful_kernel(total_ref, q_ref, kv_ref, out_ref, top, acc, total_sum):
    step = pl.program_id(0)
    block = kv_ref.shape[0]

    @pl.when(step == 0)
    def _():
        top[...] = jnp.full_like(top, masked_score)
        acc[...] = jnp.zeros_like(acc)
        total_sum[...] = jnp.zeros_like(total_sum)

    scores = lax.dot_general(
        q_ref[...], kv_ref[:, :HEAD], (((1,), (1,)), ((), ())), preferred_element_type=F32
    )
    key_index = step * block + lax.broadcasted_iota(jnp.int32, scores.shape, 1)
    live = key_index < total_ref[0]
    scores = jnp.where(live, scores, masked_score)
    old = top[...]
    new = jnp.maximum(old, jnp.max(scores, axis=1, keepdims=True))
    top[...] = new
    rescale = jnp.exp2(old - new)
    weights = jnp.where(live, jnp.exp2(scores - new[:, :1]), 0.0)
    total_sum[...] = total_sum[...] * rescale + jnp.sum(weights, axis=1, keepdims=True)
    acc[...] = acc[...] * rescale + jnp.dot(
        weights.astype(BF), kv_ref[:, HEAD:], preferred_element_type=F32
    )

    @pl.when(step == pl.num_programs(0) - 1)
    def _():
        rows, width = out_ref.shape
        for head in range(width // HEAD):
            span = slice(head * rows, (head + 1) * rows)
            out_ref[:, head * HEAD : (head + 1) * HEAD] = (acc[span, :] / total_sum[span, :]).astype(
                BF
            )


def careful_call(total, queries, kv_full, rows):
    heads = queries.shape[0] // rows
    block = 512
    return pl.pallas_call(
        careful_kernel,
        out_shape=jax.ShapeDtypeStruct((rows, heads * HEAD), BF),
        grid=(kv_full.shape[0] // block,),
        in_specs=[
            pl.BlockSpec(memory_space=pltpu.SMEM),
            pl.BlockSpec(queries.shape, lambda i: (0, 0)),
            pl.BlockSpec((block, 2 * HEAD), lambda i: (i, 0)),
        ],
        out_specs=pl.BlockSpec((rows, heads * HEAD), lambda i: (0, 0)),
        scratch_shapes=[pltpu.VMEM((heads * rows, HEAD), F32)] * 3,
        compiler_params=pltpu.CompilerParams(vmem_limit_bytes=48 * 2**20),
    )(total, queries, kv_full)


def attend(total, queries, keyval, w, ident):
    results = attend_call(total, queries, keyval, w, ident)
    plain, sums, kv_full = results[:3]
    safe = jnp.all((sums > sum_low) & (sums < sum_high))
    attended = lax.cond(
        safe,
        lambda: plain,
        lambda: careful_call(total, queries, kv_full, keyval.shape[0]),
    )
    return attended if w is None else (attended, results[3])


def gather_kernel(x_ref, out_ref, send, recv, local):
    rows, width = x_ref.shape
    half = rows // 2
    ypos = lax.axis_index("mdl")
    yp = lax.rem(ypos + 1, 4)
    ym = lax.rem(ypos + 3, 4)
    y2 = lax.rem(ypos + 2, 4)
    barrier = pltpu.get_barrier_semaphore()
    for peer in (yp, ym):
        pl.semaphore_signal(barrier, inc=1, device_id={"mdl": peer}, device_id_type=MESH)
    pl.semaphore_wait(barrier, 2)

    def place(source_y, part):
        return out_ref.at[
            pl.ds(part * half, half), pl.ds(pl.multiple_of(source_y * width, HEAD), width)
        ]

    def copy(source_y, part, slot, target, lane, own=False):
        where = place(source_y, part)
        return pltpu.make_async_remote_copy(
            src_ref=x_ref.at[pl.ds(part * half, half)] if own else where,
            dst_ref=where,
            send_sem=send.at[lane, part],
            recv_sem=recv.at[slot, part],
            device_id={"mdl": target},
            device_id_type=MESH,
        )

    def arrived(slot, source_y, part):
        where = place(source_y, part)
        pltpu.make_async_copy(where, where, recv.at[slot, part]).wait()

    first = [
        copy(ypos, 0, 0, yp, 0, own=True),
        copy(ypos, 1, 1, ym, 1, own=True),
        copy(ypos, 1, 0, yp, 0, own=True),
        copy(ypos, 0, 1, ym, 1, own=True),
    ]
    for item in first:
        item.start()
    mine = pltpu.make_async_copy(
        x_ref, out_ref.at[:, pl.ds(pl.multiple_of(ypos * width, HEAD), width)], local.at[0]
    )
    mine.start()
    arrived(0, ym, 0)
    up = copy(ym, 0, 2, yp, 2)
    up.start()
    arrived(1, yp, 1)
    down = copy(yp, 1, 2, ym, 2)
    down.start()
    arrived(0, ym, 1)
    arrived(1, yp, 0)
    arrived(2, y2, 0)
    arrived(2, y2, 1)
    for item in first:
        item.wait_send()
    up.wait_send()
    down.wait_send()
    mine.wait()


def gather_columns(x, ident):
    vmem = pl.BlockSpec(memory_space=pltpu.VMEM)
    return pl.pallas_call(
        gather_kernel,
        out_shape=jax.ShapeDtypeStruct((x.shape[0], 4 * x.shape[1]), x.dtype),
        in_specs=[vmem],
        out_specs=vmem,
        scratch_shapes=[
            pltpu.SemaphoreType.DMA((3, 2)),
            pltpu.SemaphoreType.DMA((3, 2)),
            pltpu.SemaphoreType.DMA((1,)),
        ],
        compiler_params=pltpu.CompilerParams(
            collective_id=ident, has_side_effects=True, vmem_limit_bytes=48 * 2**20
        ),
    )(x)


def project(source, w_query, w_keyval, live_mask):
    rows = source.shape[0]
    normed = rms_normed(source).astype(BF)
    queries = (
        jnp.dot(normed, w_query, preferred_element_type=F32) * (HEAD ** (-0.5) * LOG2E)
    ).astype(BF)
    heads = queries.shape[1] // HEAD
    stacked = jnp.transpose(queries.reshape(rows, heads, HEAD), (1, 0, 2)).reshape(
        heads * rows, HEAD
    )
    keyval = [jnp.dot(normed, w_keyval[part], preferred_element_type=F32) for part in range(2)]
    joined = jnp.where(live_mask[:, None], jnp.concatenate(keyval, axis=1), 0.0).astype(BF)
    return (stacked, joined)


def on_device(
    obs,
    a_query,
    a_keyval,
    a_out,
    w_policy,
    c_in,
    c_query,
    c_keyval,
    c_out,
    w_value,
    actions,
    advantages,
    old_logp,
    returns,
    robot_count,
):
    row_count = obs.shape[1]
    batch_index = lax.axis_index("sec")
    robot_total = robot_count[batch_index]
    total = robot_total.reshape(1)
    live_total = jnp.sum(robot_count).astype(F32)
    first_row = lax.axis_index("rep") * row_count
    live_mask = first_row + lax.iota(jnp.int32, row_count) < robot_total
    mdl_count = lax.axis_size("mdl")
    part_rows = row_count // mdl_count
    row_start = lax.axis_index("mdl") * part_rows
    obs_float = obs[0].astype(F32)

    queries, keyval = project(obs_float, a_query, a_keyval, live_mask)
    attended, a_out_full = attend(total, queries, keyval, a_out, 1)
    attended_full = gather_columns(attended, 3)
    hidden = (
        obs_float
        + jnp.dot(
            attended_full,
            a_out_full.reshape(4 * a_out.shape[0], a_out.shape[1]),
            preferred_element_type=F32,
        )
    ).astype(BF)
    embed_part = jnp.dot(hidden, c_in, preferred_element_type=F32).astype(BF)
    embedded = gather_columns(embed_part, 4)
    dhidden = policy_backward(
        hidden, actions[0], advantages[0], old_logp[0], live_mask, live_total, w_policy
    ).astype(BF)
    actor_grad = lax.dot_general(
        attended, dhidden, (((0,), (0,)), ((), ())), preferred_element_type=F32
    ).astype(BF)
    embed_float = embedded.astype(F32)
    critic_queries, critic_keyval = project(embed_float, c_query, c_keyval, live_mask)
    critic_attended = attend(total, critic_queries, critic_keyval, None, 2)
    critic_sum = lax.psum(
        jnp.dot(critic_attended, c_out, preferred_element_type=F32).astype(BF),
        "mdl",
    ).astype(F32)
    value_pred, dmixed = value_backward(
        embed_float + critic_sum, returns[0], live_mask, live_total, w_value
    )
    value_part = lax.dynamic_slice_in_dim(value_pred, row_start, part_rows, 0)
    critic_grad = lax.dot_general(
        critic_attended, dmixed.astype(BF), (((0,), (0,)), ((), ())), preferred_element_type=F32
    )
    actor_summed = lax.psum(actor_grad, ("rep", "sec")).astype(F32)
    critic_summed = lax.psum(critic_grad.astype(BF), ("rep", "sec")).astype(F32)
    return (value_part[None, :], actor_summed, critic_summed)


def solution(mesh):
    return jax.shard_map(
        on_device,
        mesh=mesh,
        in_specs=(
            P("sec", "rep", None),
            P(None, "mdl"),
            P(None, None, "mdl"),
            P("mdl", None),
            P(),
            P(None, "mdl"),
            P(None, "mdl"),
            P(None, None, "mdl"),
            P("mdl", None),
            P(),
            P("sec", "rep"),
            P("sec", "rep"),
            P("sec", "rep"),
            P("sec", "rep"),
            P(),
        ),
        out_specs=(P("sec", ("rep", "mdl")), P("mdl", None), P("mdl", None)),
        check_vma=False,
    )
```

time: 881 us -> 459 us (0.52)
  matrix products: 286 us -> 27.2 us
  Pallas kernels: 0 us -> 225 us
  waiting for transfers between devices: 369 us -> 164 us
  other arithmetic: 135 us -> 16.2 us
  local copies, waits for them, and re-layouts: 50.4 us -> 8.57 us
  loops' own time: 23.5 us -> 0.25 us
    dot_general x76 -> x14, matrix products: 286 us -> 27.2 us  [the longest x1 5.68 us: on_device(): jnp.dot(attended_full, a_out_full.reshape(4 * a_out.shape[0], a_out.shape...]
    pallas_call x0 -> x6, Pallas kernels: none -> 225 us  [the longest x2 114 us: careful_call(): pl.pallas_call(careful_kernel, out_shape=jax.ShapeDtypeStruct((rows, head...]
    all_gather x3 -> x0, waiting for transfers between devices: 134 us -> none  [the longest x1 53.9 us: on_device(): lax.all_gather(keyval, 'rep', axis=1, tiled=True)]
    reduce_sum x34 -> x1, other arithmetic: 96.8 us -> 0.64 us  [on_device(): live_total = jnp.sum(robot_count).astype(F32)]
    psum x3 -> x2, waiting for transfers between devices: 234 us -> 164 us  [the longest x1 109 us: on_device(): actor_summed = lax.psum(actor_grad, ('rep', 'sec')).astype(F32)]
    another operation x2, loops' own time: 23.5 us -> 0.25 us  [attend(): lax.cond(safe, lambda: plain, lambda: careful_call(total, queries, kv_ful...]
    lt x32 -> x1, other arithmetic: 19.9 us -> 0.65 us  [on_device(): live_mask = first_row + lax.iota(jnp.int32, row_count) < robot_total]
    dynamic_slice x32 -> x0, local copies, waits for them, and re-layouts: 18.8 us -> none  [make_fold(): lax.scan(absorb, carried, (jnp.arange(block_count, dtype=jnp.int32), key_...]
  transfers between devices with their start and end apart: 6 -> 2, of which waited for: 6 -> 2; matrix products, arithmetic and copies ran while one was open for 2% -> 1% of each run, Pallas kernels for 0% -> 0%
where the time goes in v1:
time: 459 us; the launch traced here: 458 us
  Pallas kernels  225 us (49%)
  waiting for transfers between devices  164 us (36%)
  matrix products  27.2 us (6%)
  between operations  16.3 us (4%)
  other arithmetic  16.2 us (4%)
  local copies, waits for them, and re-layouts  8.57 us (2%)
    pallas_call x2, Pallas kernels, careful_call(): pl.pallas_call(careful_kernel, out_shape=jax.ShapeDtypeStruct((rows, head...  114 us
    psum x1, waiting for transfers between devices, on_device(): actor_summed = lax.psum(actor_grad, ('rep', 'sec')).astype(F32)  109 us
    pallas_call x2, Pallas kernels, attend_call(): pl.pallas_call(functools.partial(attend_kernel, heads, w is not None), ou...  75.5 us
    psum x1, waiting for transfers between devices, on_device(): lax.psum(jnp.dot(critic_attended, c_out, preferred_element_type=F32).asty...  55.2 us
    pallas_call x2, Pallas kernels, gather_columns(): pl.pallas_call(gather_kernel, out_shape=jax.ShapeDtypeStruct((x.shape[0],...  36.1 us
  transfers between devices with their start and end apart: 2, of which 2 were waited for; matrix products, arithmetic and copies ran while one was open for 1% of the time, Pallas kernels for 0%

profile of v1, /device:TPU:1, one launch (start us, length us, event | category | flops | bytes accessed | tf_op | source)
XLA Modules:
  0.0 458.2 jit_solution(4370659034407973557)
XLA Ops:
  7.2 0.0 copy-start
  7.2 0.0 all-reduce.4.cloned.1.call-start
  7.2 0.0 copy-start.6
  7.2 0.0 copy-start.20
  7.3 1.9 fusion.18
  9.2 2.1 fusion.47
  11.3 0.6 fusion.49
  12.0 0.0 copy-start.21
  12.0 0.0 copy-start.3
  12.0 3.5 fusion.44
  15.5 1.9 copy.18
  17.4 0.6 dynamic_slice.6.total_ref
  18.0 0.7 add_compare_fusion
  18.6 0.1 fusion.51.kv_ref
  18.8 40.9 %shard_map.166 = (bf16[512,384]{1,0:T(8,128)(2,1)}, f32[6,128]{1,0:T(8,128)S(1)}, bf16[8192,256]{1,0:T(8,128)(2,1)}, bf16[4,384,1536]{2,1,0:T(8,128)(2,1)S(1)}) custom-call(s32[1]{0:T(128)} %dynamic_slice.6.total_ref, bf16[1536,128]{1,0:T(8,128)(2,1)} %bitcast.68, bf16[512,256]{1,0:T(8,128)(2,1)S(1)} %fusion.51.kv_ref, bf16[384,1536]{1,0:T(8,128)(2,1)S(1)} %copy-done.3), custom_call_target="tpu_custom_call" | custom-call | flops 6442450944 | bytes 4194304 | tf_op jit(solution)/shard_map/pallas_call | solution.py:368
  59.7 2.1 copy-done.4
  61.9 0.6 and_reduce_fusion.1
  63.1 49.5 %conditional.2 = (bf16[512,384]{1,0:T(8,128)(2,1)}) conditional(s32[]{:T(128)} %convert_element_type.102, (s32[1]{0:T(128)}, bf16[1536,128]{1,0:T(8,128)(2,1)}, bf16[8192,256]{1,0:T(8,128)(2,1)}) %tuple.37, bf16[512,384]{1,0:T(8,128)(2,1)} %get-tuple-element.38), branch_computations={%region_2.3_spmd, %region_3.4_spmd} | conditional | bytes 8 | solution.py:443
  63.2 49.5 %branch_0_fun.2 = bf16[512,384]{1,0:T(8,128)(2,1)} custom-call(s32[1]{0:T(128)} %get-tuple-element.20.total_ref, bf16[1536,128]{1,0:T(8,128)(2,1)} %get-tuple-element.21.q_ref, bf16[8192,256]{1,0:T(8,128)(2,1)} %get-tuple-element.22.kv_ref), custom_call_target="tpu_custom_call" | custom-call | tf_op jit(solution)/shard_map/cond/branch_0_fun/pallas_call | solution.py:424
  112.7 16.9 %shard_map.167 = bf16[512,1536]{1,0:T(8,128)(2,1)S(1)} custom-call(bf16[512,384]{1,0:T(8,128)(2,1)} %get-tuple-element.55.x_ref), custom_call_target="tpu_custom_call" | custom-call | tf_op jit(solution)/shard_map/pallas_call | solution.py:514
  129.5 0.0 copy-start.18
  129.5 5.7 %fusion.17 = (f32[512]{0:T(512)S(1)}, bf16[512,1536]{1,0:T(8,128)(2,1)S(1)}) fusion(bf16[512,1536]{1,0:T(8,128)(2,1)S(1)} %shard_map.167, bf16[1536,1536]{1,0:T(8,128)(2,1)} %bitcast.65, bf16[1,512,1536]{2,1,0:T(8,128)(2,1)} %param.19), kind=kOutput, calls=%fused_computation.27 | convolution fusion | flops 2420637184 | bytes 9439232 | tf_op jit(solution)/shard_map/dot_general | solution.py:579
  135.2 1.2 copy-done.7
  136.4 1.0 convolution_convert_fusion.3.x_ref
  137.4 0.0 copy-start.19
  137.4 19.2 %shard_map.168 = bf16[512,2048]{1,0:T(8,128)(2,1)S(1)} custom-call(bf16[512,512]{1,0:T(8,128)(2,1)S(1)} %convolution_convert_fusion.3.x_ref), custom_call_target="tpu_custom_call" | custom-call | tf_op jit(solution)/shard_map/pallas_call | solution.py:514
  156.7 0.0 copy-start.1
  156.7 0.5 fusion.3
  157.2 0.8 fusion.55
  158.0 0.0 copy-start.17
  158.0 0.8 fusion.53
  158.7 0.8 copy-done.17
  159.5 1.4 fusion.40
  160.9 0.3 copy.21
  161.2 0.1 fusion.52.kv_ref
  161.4 34.5 %shard_map.169 = (bf16[512,512]{1,0:T(8,128)(2,1)S(1)}, f32[8,128]{1,0:T(8,128)S(1)}, bf16[8192,256]{1,0:T(8,128)(2,1)}) custom-call(s32[1]{0:T(128)} %dynamic_slice.6.total_ref, bf16[2048,128]{1,0:T(8,128)(2,1)S(1)} %bitcast.66, bf16[512,256]{1,0:T(8,128)(2,1)S(1)} %fusion.52.kv_ref), custom_call_target="tpu_custom_call" | custom-call | flops 8589934592 | bytes 4194304 | tf_op jit(solution)/shard_map/pallas_call | solution.py:368
  195.9 0.6 and_reduce_fusion
  197.2 64.4 %conditional.3 = (bf16[512,512]{1,0:T(8,128)(2,1)S(1)}) conditional(s32[]{:T(128)} %convert_element_type.109, (s32[1]{0:T(128)}, bf16[2048,128]{1,0:T(8,128)(2,1)S(1)}, bf16[8192,256]{1,0:T(8,128)(2,1)}) %tuple.36, bf16[512,512]{1,0:T(8,128)(2,1)S(1)} %get-tuple-element.42), branch_computations={%region_6.7_spmd, %region_7.8_spmd} | conditional | bytes 8 | solution.py:443
  197.4 64.2 %branch_0_fun.3 = bf16[512,512]{1,0:T(8,128)(2,1)S(1)} custom-call(s32[1]{0:T(128)} %get-tuple-element.23.total_ref, bf16[2048,128]{1,0:T(8,128)(2,1)S(1)} %get-tuple-element.24.q_ref, bf16[8192,256]{1,0:T(8,128)(2,1)} %get-tuple-element.25.kv_ref), custom_call_target="tpu_custom_call" | custom-call | tf_op jit(solution)/shard_map/cond/branch_0_fun/pallas_call | solution.py:424
  261.6 2.6 convolution_convert_fusion.1
  264.2 0.0 all-reduce.4.cloned.1.call-update
  264.2 0.0 all-reduce.6.cloned.1.call-start
  264.3 0.6 reduce_sum.96
  265.0 0.3 copy-done.10
  265.2 2.2 fusion.72
  267.4 0.1 exponential_reduce_fusion
  268.1 0.1 select_reduce_fusion
  268.2 55.2 %all-reduce.4.cloned.1.call-done = bf16[512,2048]{1,0:T(8,128)(2,1)} async-done(((bf16[512,2048]{1,0:T(8,128)(2,1)}), bf16[512,2048]{1,0:T(8,128)(2,1)}) %all-reduce.4.cloned.1.call-update) | async-done | bytes 2097168 | tf_op jit(solution)/shard_map/psum | solution.py:596
  323.3 3.1 multiply_reduce_fusion
  326.5 0.3 copy-done.5
  326.8 0.8 fusion.22
  327.7 0.0 copy-done.16
  327.7 0.7 select_divide_fusion
  328.4 1.1 fusion
  329.4 0.3 copy-done.8
  329.8 0.9 fusion.13
  330.6 0.1 copy-done.11
  330.8 2.1 convolution_convert_fusion.2
  332.8 3.0 convolution_convert_fusion
  335.8 0.0 all-reduce.6.cloned.1.call-update
  335.8 0.6 dynamic-slice_bitcast_fusion
  336.4 109.0 %all-reduce.6.cloned.1.call-done = (bf16[384,1536]{1,0:T(8,128)(2,1)}, bf16[512,2048]{1,0:T(8,128)(2,1)}) async-done(((bf16[384,1536]{1,0:T(8,128)(2,1)}, bf16[512,2048]{1,0:T(8,128)(2,1)}), (bf16[384,1536]{1,0:T(8,128)(2,1)}, bf16[512,2048]{1,0:T(8,128)(2,1)})) %all-reduce.6.cloned.1.call-update) | async-done | bytes 3276816 | tf_op jit(solution)/shard_map/psum | solution.py:607
  445.4 4.2 convert_element_type.124
  449.7 1.7 convert_element_type.120
  (36 shorter events, 0.1 us)
Async XLA Ops:
  7.2 254.4 %copy-start = (bf16[512,2048]{1,0:T(8,128)(2,1)S(1)}, bf16[512,2048]{1,0:T(8,128)(2,1)}, u32[]{:S(2)}) copy-start(bf16[512,2048]{1,0:T(8,128)(2,1)} %param.27) | copy-start | bytes 6291460
  7.2 316.2 %all-reduce.4.cloned.1.call-start = ((), (), s32[]{:S(2)}) async-start(), calls=%async_computation | async-start | bytes 4194304 | tf_op jit(solution)/shard_map/psum | solution.py:596
  7.2 4.1 copy-start.6
  7.2 4.1 copy-start.20
  12.0 5.4 %copy-start.21 = (s32[2]{0:T(128)S(1)}, s32[2]{0:T(128)}, u32[]{:S(2)}) copy-start(s32[2]{0:T(128)} %param.33) | copy-start | bytes 28
  12.0 6.8 %copy-start.3 = (bf16[384,1536]{1,0:T(8,128)(2,1)S(1)}, bf16[384,1536]{1,0:T(8,128)(2,1)}, u32[]{:S(2)}) copy-start(bf16[384,1536]{1,0:T(8,128)(2,1)} %refs_0_.1) | copy-start | bytes 3538948
  59.7 2.1 copy-start.4
  129.5 6.9 %copy-start.18 = (bf16[1536,512]{1,0:T(8,128)(2,1)S(1)}, bf16[1536,512]{1,0:T(8,128)(2,1)}, u32[]{:S(2)}) copy-start(bf16[1536,512]{1,0:T(8,128)(2,1)} %param.24) | copy-start | bytes 4718596
  135.2 1.2 copy-start.7
  137.4 19.8 %copy-start.19 = (bf16[2,2048,128]{2,1,0:T(8,128)(2,1)S(1)}, bf16[2,2048,128]{2,1,0:T(8,128)(2,1)}, u32[]{:S(2)}) copy-start(bf16[2,2048,128]{2,1,0:T(8,128)(2,1)} %param.26) | copy-start | bytes 3145732
  156.7 2.1 copy-start.1
  158.0 1.6 copy-start.17
  264.2 0.7 copy-start.12
  264.2 1.0 copy-start.10
  264.2 3.9 copy-start.13
  264.2 181.2 %all-reduce.6.cloned.1.call-start = ((), (), s32[]{:S(2)}) async-start(), calls=%async_computation.1 | async-start | bytes 6553600 | tf_op jit(solution)/shard_map/psum | solution.py:607
  323.3 3.1 copy-start.2
  323.3 3.5 copy-start.5
  326.8 0.8 copy-start.14
  326.8 0.8 copy-start.15
  326.8 0.9 copy-start.16
  328.4 1.4 copy-start.8
  329.8 1.0 copy-start.11
  445.4 4.2 copy-start.9
Sparse Core Ops, SparseCore 0:
  264.3 58.9 all-reduce.3
  335.9 109.4 all-reduce.5

commit v2 on v1

--- a/solution.py
+++ b/solution.py
@@ -104,8 +104,6 @@
     for peer in peers:
         pl.semaphore_signal(barrier, inc=1, device_id=peer, device_id_type=MESH)
     pl.semaphore_wait(barrier, len(peers))
-
-    started = []
 
     def block_rows(block, part):
         return pl.ds(pl.multiple_of(block * rows + part * piece, piece), piece)
@@ -522,9 +520,202 @@
             pltpu.SemaphoreType.DMA((1,)),
         ],
         compiler_params=pltpu.CompilerParams(
-            collective_id=ident, has_side_effects=True, vmem_limit_bytes=48 * 2**20
+            collective_id=ident, has_side_effects=True, vmem_limit_bytes=8 * 2**20
         ),
     )(x)
+
+
+def reduce_kernel(att_ref, d_ref, out_ref, theirs, mine, got, part_in, part_sum, sub_in, send, recv, csend, crecv):
+    half = theirs.shape[0]
+    block = half // 2
+    width = out_ref.shape[1] // 4
+    sub = block // 4
+    me = lax.axis_index("rep")
+    xlow = lax.axis_index("sec")
+    core = lax.rem(me, 2)
+    other = me + 1 - 2 * core
+    zpos = me // 4
+    xpos = lax.rem(me // 2, 2) * 2 + xlow
+
+    def at_x(k):
+        there = lax.rem(xpos + k, 4)
+        return {"rep": zpos * 4 + (there // 2) * 2 + core, "sec": lax.rem(there, 2)}
+
+    def at_z(k):
+        return {"rep": lax.rem(me + 4 * k, 16)}
+
+    near = [at_x, at_z]
+    first = [xpos, zpos]
+    second = [zpos, xpos]
+
+    barrier = pltpu.get_barrier_semaphore()
+    for k in range(1, 4):
+        pl.semaphore_signal(barrier, inc=1, device_id=at_x(k), device_id_type=MESH)
+        pl.semaphore_signal(barrier, inc=1, device_id=at_z(k), device_id_type=MESH)
+    pl.semaphore_signal(barrier, inc=1, device_id={"rep": other}, device_id_type=MESH)
+
+    def grad_rows(which):
+        span = pl.ds(pl.multiple_of(which * half, half), half)
+        return lax.dot_general(
+            att_ref[:, span], d_ref[...], (((0,), (0,)), ((), ())), preferred_element_type=F32
+        )
+
+    theirs[...] = grad_rows(1 - core).astype(BF)
+    pl.semaphore_wait(barrier, 7)
+    swap = pltpu.make_async_remote_copy(
+        src_ref=theirs,
+        dst_ref=got,
+        send_sem=csend.at[0],
+        recv_sem=crecv.at[0],
+        device_id={"rep": other},
+        device_id_type=MESH,
+    )
+    swap.start()
+    own = grad_rows(core)
+    swap.wait_recv()
+    mine[...] = (own + got[...].astype(F32)).astype(BF)
+
+    def columns(index):
+        return pl.ds(pl.multiple_of(index * width, width), width)
+
+    def scatter_one(part, k):
+        return pltpu.make_async_remote_copy(
+            src_ref=mine.at[pl.ds(part * block, block), columns(lax.rem(first[part] + k, 4))],
+            dst_ref=part_in.at[part, k - 1],
+            send_sem=send.at[0, part, k - 1],
+            recv_sem=recv.at[0, part, k - 1],
+            device_id=near[part](k),
+            device_id_type=MESH,
+        )
+
+    def sub_rows(index):
+        return pl.ds(pl.multiple_of(index * sub, sub), sub)
+
+    def scatter_two(part, k):
+        return pltpu.make_async_remote_copy(
+            src_ref=part_sum.at[part, sub_rows(lax.rem(second[part] + k, 4))],
+            dst_ref=sub_in.at[part, k - 1],
+            send_sem=send.at[1, part, k - 1],
+            recv_sem=recv.at[1, part, k - 1],
+            device_id=near[1 - part](k),
+            device_id_type=MESH,
+        )
+
+    def out_rows(which, part, offset, size):
+        return pl.ds(pl.multiple_of(which * half + part * block + offset, size), size)
+
+    def gather_two(part, k):
+        where = out_ref.at[
+            out_rows(core, part, second[part] * sub, sub), columns(first[part])
+        ]
+        return pltpu.make_async_remote_copy(
+            src_ref=where,
+            dst_ref=where,
+            send_sem=send.at[2, part, k - 1],
+            recv_sem=recv.at[2, part, k - 1],
+            device_id=near[1 - part](k),
+            device_id_type=MESH,
+        )
+
+    def gather_one(part, k):
+        where = out_ref.at[out_rows(core, part, 0, block), columns(first[part])]
+        return pltpu.make_async_remote_copy(
+            src_ref=where,
+            dst_ref=where,
+            send_sem=send.at[3, part, k - 1],
+            recv_sem=recv.at[3, part, k - 1],
+            device_id=near[part](k),
+            device_id_type=MESH,
+        )
+
+    def share(part, k, which):
+        where = out_ref.at[
+            out_rows(which, part, 0, block), columns(lax.rem(first[part] + 4 - k, 4))
+        ]
+        index = 1 + part * 4 + k
+        return pltpu.make_async_remote_copy(
+            src_ref=where,
+            dst_ref=where,
+            send_sem=csend.at[index],
+            recv_sem=crecv.at[index],
+            device_id={"rep": other},
+            device_id_type=MESH,
+        )
+
+    parts = range(2)
+    hops = (2, 1, 3)
+    for k in hops:
+        for part in parts:
+            scatter_one(part, k).start()
+    for part in parts:
+        total = mine[pl.ds(part * block, block), columns(first[part])].astype(F32)
+        for k in (1, 3, 2):
+            scatter_one(part, k).wait_recv()
+            total += part_in[part, k - 1].astype(F32)
+        part_sum[part] = total.astype(BF)
+        for k in hops:
+            scatter_two(part, k).start()
+    for part in parts:
+        total = part_sum[part, sub_rows(second[part])].astype(F32)
+        for k in (1, 3, 2):
+            scatter_two(part, k).wait_recv()
+            total += sub_in[part, k - 1].astype(F32)
+        out_ref[out_rows(core, part, second[part] * sub, sub), columns(first[part])] = total.astype(
+            BF
+        )
+        for k in hops:
+            gather_two(part, k).start()
+    for part in parts:
+        for k in range(1, 4):
+            gather_two(part, k).wait_recv()
+        for k in hops:
+            gather_one(part, k).start()
+        share(part, 0, core).start()
+    for k in (1, 3, 2):
+        for part in parts:
+            gather_one(part, k).wait_recv()
+            share(part, k, core).start()
+    for part in parts:
+        for k in range(4):
+            share(part, k, 1 - core).wait_recv()
+    swap.wait_send()
+    for part in parts:
+        for k in range(1, 4):
+            scatter_one(part, k).wait_send()
+            scatter_two(part, k).wait_send()
+            gather_two(part, k).wait_send()
+            gather_one(part, k).wait_send()
+        for k in range(4):
+            share(part, k, core).wait_send()
+
+
+def reduced_grad(attended, grad_in, ident):
+    heads_width = attended.shape[1]
+    columns = grad_in.shape[1]
+    half = heads_width // 2
+    block = half // 2
+    vmem = pl.BlockSpec(memory_space=pltpu.VMEM)
+    return pl.pallas_call(
+        reduce_kernel,
+        out_shape=jax.ShapeDtypeStruct((heads_width, columns), BF),
+        in_specs=[vmem, vmem],
+        out_specs=vmem,
+        scratch_shapes=[
+            pltpu.VMEM((half, columns), BF),
+            pltpu.VMEM((half, columns), BF),
+            pltpu.VMEM((half, columns), BF),
+            pltpu.VMEM((2, 3, block, columns // 4), BF),
+            pltpu.VMEM((2, block, columns // 4), BF),
+            pltpu.VMEM((2, 3, block // 4, columns // 4), BF),
+            pltpu.SemaphoreType.DMA((4, 2, 3)),
+            pltpu.SemaphoreType.DMA((4, 2, 3)),
+            pltpu.SemaphoreType.DMA((9,)),
+            pltpu.SemaphoreType.DMA((9,)),
+        ],
+        compiler_params=pltpu.CompilerParams(
+            collective_id=ident, has_side_effects=True, vmem_limit_bytes=24 * 2**20
+        ),
+    )(attended, grad_in)
 
 
 def project(source, w_query, w_keyval, live_mask):
@@ -592,20 +783,19 @@
     ).astype(BF)
     embed_float = embedded.astype(F32)
     critic_queries, critic_keyval = project(embed_float, c_query, c_keyval, live_mask)
-    critic_attended = attend(total, critic_queries, critic_keyval, None, 2)
-    critic_sum = lax.psum(
-        jnp.dot(critic_attended, c_out, preferred_element_type=F32).astype(BF),
-        "mdl",
-    ).astype(F32)
+    critic_attended, c_out_full = attend(total, critic_queries, critic_keyval, c_out, 2)
+    critic_full = gather_columns(critic_attended, 5)
+    critic_sum = jnp.dot(
+        critic_full,
+        c_out_full.reshape(4 * c_out.shape[0], c_out.shape[1]),
+        preferred_element_type=F32,
+    )
     value_pred, dmixed = value_backward(
         embed_float + critic_sum, returns[0], live_mask, live_total, w_value
     )
     value_part = lax.dynamic_slice_in_dim(value_pred, row_start, part_rows, 0)
-    critic_grad = lax.dot_general(
-        critic_attended, dmixed.astype(BF), (((0,), (0,)), ((), ())), preferred_element_type=F32
-    )
+    critic_summed = reduced_grad(critic_attended, dmixed.astype(BF), 6).astype(F32)
     actor_summed = lax.psum(actor_grad, ("rep", "sec")).astype(F32)
-    critic_summed = lax.psum(critic_grad.astype(BF), ("rep", "sec")).astype(F32)
     return (value_part[None, :], actor_summed, critic_summed)
 
 

time: 459 us -> 430 us (0.937)
  waiting for transfers between devices: 164 us -> 66.4 us
  Pallas kernels: 225 us -> 288 us
  matrix products: 27.2 us -> 35.4 us
    psum x1 -> x0, waiting for transfers between devices: 55.2 us -> none  [on_device(): lax.psum(jnp.dot(critic_attended, c_out, preferred_element_type=F32).asty...]
    psum x1, waiting for transfers between devices: 109 us -> 66.4 us  [on_device(): actor_summed = lax.psum(actor_grad, ('rep', 'sec')).astype(F32)]
    pallas_call x0 -> x1, Pallas kernels: none -> 33.1 us  [reduced_grad(): pl.pallas_call(reduce_kernel, out_shape=jax.ShapeDtypeStruct((heads_width...]
    pallas_call x2 -> x3, Pallas kernels: 36.1 us -> 56.5 us  [gather_columns(): pl.pallas_call(gather_kernel, out_shape=jax.ShapeDtypeStruct((x.shape[0],...]
    pallas_call x2, Pallas kernels: 75.5 us -> 84.6 us  [attend_call(): pl.pallas_call(functools.partial(attend_kernel, heads, w is not None), ou...]
    dot_general x2 -> x1, matrix products: 5.56 us -> 10 us  [on_device(): jnp.dot(critic_full, c_out_full.reshape(4 * c_out.shape[0], c_out.shape[1...]
  transfers between devices with their start and end apart: 2 -> 1, of which waited for: 2 -> 1; matrix products, arithmetic and copies ran while one was open for 1% -> 2% of each run, Pallas kernels for 0% -> 8%
where the time goes in v2:
time: 430 us
  Pallas kernels  288 us (67%)
  waiting for transfers between devices  66.4 us (15%)
  matrix products  35.4 us (8%)
  between operations  16.4 us (4%)
  other arithmetic  15.5 us (4%)
  local copies, waits for them, and re-layouts  7.58 us (2%)
    pallas_call x2, Pallas kernels, careful_call(): pl.pallas_call(careful_kernel, out_shape=jax.ShapeDtypeStruct((rows, head...  114 us
    pallas_call x2, Pallas kernels, attend_call(): pl.pallas_call(functools.partial(attend_kernel, heads, w is not None), ou...  84.6 us
    psum x1, waiting for transfers between devices, on_device(): actor_summed = lax.psum(actor_grad, ('rep', 'sec')).astype(F32)  66.4 us
    pallas_call x3, Pallas kernels, gather_columns(): pl.pallas_call(gather_kernel, out_shape=jax.ShapeDtypeStruct((x.shape[0],...  56.5 us
    pallas_call x1, Pallas kernels, reduced_grad(): pl.pallas_call(reduce_kernel, out_shape=jax.ShapeDtypeStruct((heads_width...  33.1 us
    dot_general x1, matrix products, on_device(): jnp.dot(critic_full, c_out_full.reshape(4 * c_out.shape[0], c_out.shape[1...  10 us
  transfers between devices with their start and end apart: 1, of which 1 were waited for; matrix products, arithmetic and copies ran while one was open for 2% of the time, Pallas kernels for 8%

profile of v2, /device:TPU:1, one launch (start us, length us, event | category | flops | bytes accessed | tf_op | source)
XLA Modules:
  0.0 429.5 jit_solution(4616116167004647578)
XLA Ops:
  7.2 0.0 copy-start
  7.2 0.0 copy-start.18
  7.2 0.0 all-reduce.2.cloned.1.call-start
  7.2 0.0 copy-start.6
  7.3 1.9 fusion.16
  9.2 2.1 fusion.39
  11.3 0.6 fusion.41
  12.0 0.0 copy-start.19
  12.0 0.0 copy-start.3
  12.0 3.5 fusion.36
  15.5 1.9 copy.18
  17.4 0.6 dynamic_slice.6.total_ref
  18.0 0.7 add_compare_fusion
  18.6 0.1 fusion.43.kv_ref
  18.8 40.9 %shard_map.166 = (bf16[512,384]{1,0:T(8,128)(2,1)}, f32[6,128]{1,0:T(8,128)S(1)}, bf16[8192,256]{1,0:T(8,128)(2,1)}, bf16[4,384,1536]{2,1,0:T(8,128)(2,1)S(1)}) custom-call(s32[1]{0:T(128)} %dynamic_slice.6.total_ref, bf16[1536,128]{1,0:T(8,128)(2,1)} %bitcast.68, bf16[512,256]{1,0:T(8,128)(2,1)S(1)} %fusion.43.kv_ref, bf16[384,1536]{1,0:T(8,128)(2,1)S(1)} %copy-done.3), custom_call_target="tpu_custom_call" | custom-call | flops 6442450944 | bytes 4194304 | tf_op jit(solution)/shard_map/pallas_call | solution.py:366
  59.7 2.1 copy-done.4
  61.8 0.6 and_reduce_fusion.1
  63.1 49.5 %conditional.2 = (bf16[512,384]{1,0:T(8,128)(2,1)}) conditional(s32[]{:T(128)} %convert_element_type.93, (s32[1]{0:T(128)}, bf16[1536,128]{1,0:T(8,128)(2,1)}, bf16[8192,256]{1,0:T(8,128)(2,1)}) %tuple.35, bf16[512,384]{1,0:T(8,128)(2,1)} %get-tuple-element.39), branch_computations={%region_2.3_spmd, %region_3.4_spmd} | conditional | bytes 8 | solution.py:441
  63.1 49.5 %branch_0_fun.2 = bf16[512,384]{1,0:T(8,128)(2,1)} custom-call(s32[1]{0:T(128)} %get-tuple-element.20.total_ref, bf16[1536,128]{1,0:T(8,128)(2,1)} %get-tuple-element.21.q_ref, bf16[8192,256]{1,0:T(8,128)(2,1)} %get-tuple-element.22.kv_ref), custom_call_target="tpu_custom_call" | custom-call | tf_op jit(solution)/shard_map/cond/branch_0_fun/pallas_call | solution.py:422
  112.6 16.9 %shard_map.167 = bf16[512,1536]{1,0:T(8,128)(2,1)S(1)} custom-call(bf16[512,384]{1,0:T(8,128)(2,1)} %get-tuple-element.55.x_ref), custom_call_target="tpu_custom_call" | custom-call | tf_op jit(solution)/shard_map/pallas_call | solution.py:512
  129.4 0.0 copy-start.16
  129.4 5.7 %fusion.15 = (f32[512]{0:T(512)S(1)}, bf16[512,1536]{1,0:T(8,128)(2,1)S(1)}) fusion(bf16[512,1536]{1,0:T(8,128)(2,1)S(1)} %shard_map.167, bf16[1536,1536]{1,0:T(8,128)(2,1)} %bitcast.65, bf16[1,512,1536]{2,1,0:T(8,128)(2,1)} %param.19), kind=kOutput, calls=%fused_computation.26 | convolution fusion | flops 2420637184 | bytes 9439232 | tf_op jit(solution)/shard_map/dot_general | solution.py:770
  135.2 1.0 convolution_convert_fusion.1.x_ref
  136.2 0.0 copy-start.17
  136.2 19.2 %shard_map.168 = bf16[512,2048]{1,0:T(8,128)(2,1)S(1)} custom-call(bf16[512,512]{1,0:T(8,128)(2,1)S(1)} %convolution_convert_fusion.1.x_ref), custom_call_target="tpu_custom_call" | custom-call | tf_op jit(solution)/shard_map/pallas_call | solution.py:512
  155.5 0.0 copy-start.1
  155.5 0.5 fusion.3
  156.0 0.0 copy-start.11
  156.0 0.8 fusion.45
  156.8 0.0 copy-done.1
  156.8 0.8 fusion.47
  157.5 0.7 reduce_sum.96
  158.2 3.0 fusion.32
  161.2 0.3 copy.21
  161.5 0.1 fusion.44.kv_ref
  161.6 0.0 copy-start.2
  161.6 1.6 copy-done.2
  163.2 43.7 %shard_map.169 = (bf16[512,512]{1,0:T(8,128)(2,1)S(1)}, f32[8,128]{1,0:T(8,128)S(1)}, bf16[8192,256]{1,0:T(8,128)(2,1)}, bf16[4,512,2048]{2,1,0:T(8,128)(2,1)}) custom-call(s32[1]{0:T(128)} %dynamic_slice.6.total_ref, bf16[2048,128]{1,0:T(8,128)(2,1)S(1)} %bitcast.66, bf16[512,256]{1,0:T(8,128)(2,1)S(1)} %fusion.44.kv_ref, bf16[512,2048]{1,0:T(8,128)(2,1)S(1)} %copy-done.2), custom_call_target="tpu_custom_call" | custom-call | flops 8589934592 | bytes 4194304 | tf_op jit(solution)/shard_map/pallas_call | solution.py:366
  207.0 0.6 and_reduce_fusion
  208.3 64.4 %conditional.3 = (bf16[512,512]{1,0:T(8,128)(2,1)S(1)}) conditional(s32[]{:T(128)} %convert_element_type.100, (s32[1]{0:T(128)}, bf16[2048,128]{1,0:T(8,128)(2,1)S(1)}, bf16[8192,256]{1,0:T(8,128)(2,1)}) %tuple.34, bf16[512,512]{1,0:T(8,128)(2,1)S(1)} %get-tuple-element.43), branch_computations={%region_6.7_spmd, %region_7.8_spmd} | conditional | bytes 8 | solution.py:441
  208.5 64.2 %branch_0_fun.3 = bf16[512,512]{1,0:T(8,128)(2,1)S(1)} custom-call(s32[1]{0:T(128)} %get-tuple-element.23.total_ref, bf16[2048,128]{1,0:T(8,128)(2,1)S(1)} %get-tuple-element.24.q_ref, bf16[8192,256]{1,0:T(8,128)(2,1)} %get-tuple-element.25.kv_ref), custom_call_target="tpu_custom_call" | custom-call | tf_op jit(solution)/shard_map/cond/branch_0_fun/pallas_call | solution.py:422
  272.7 20.4 %shard_map.170 = bf16[512,2048]{1,0:T(8,128)(2,1)S(1)} custom-call(bf16[512,512]{1,0:T(8,128)(2,1)S(1)} %get-tuple-element.56.x_ref.att_ref), custom_call_target="tpu_custom_call" | custom-call | tf_op jit(solution)/shard_map/pallas_call | solution.py:512
  293.1 0.0 copy-start.9
  293.2 0.0 copy-start.12
  293.2 10.0 %multiply_reduce_fusion = (f32[512]{0:T(512)S(1)}, f32[512,2048]{1,0:T(8,128)}) fusion(bf16[512,2048]{1,0:T(8,128)(2,1)S(1)} %shard_map.170, bf16[2048,2048]{1,0:T(8,128)(2,1)} %bitcast.79, bf16[512,2048]{1,0:T(8,128)(2,1)} %copy-done.1), kind=kOutput, calls=%fused_computation.10 | convolution fusion | flops 4299161088 | bytes 16779264 | tf_op jit(solution)/shard_map/dot_general | solution.py:788
  303.8 0.0 copy-start.13
  303.9 0.0 copy-start.14
  303.9 0.0 copy-start.15
  303.9 2.3 fusion.64
  306.2 0.1 exponential_reduce_fusion
  306.3 0.1 select_reduce_fusion
  306.3 2.9 fusion.20
  309.2 0.7 select_divide_fusion
  310.0 0.8 fusion.11
  310.8 2.0 convolution_convert_fusion
  312.8 0.0 all-reduce.2.cloned.1.call-update
  312.9 3.0 fusion
  315.9 0.4 copy-done.5
  316.3 0.8 fusion.2.d_ref
  317.1 33.1 %shard_map.171 = bf16[512,2048]{1,0:T(8,128)(2,1)S(1)} custom-call(bf16[512,512]{1,0:T(8,128)(2,1)S(1)} %get-tuple-element.56.x_ref.att_ref, bf16[512,2048]{1,0:T(8,128)(2,1)S(1)} %fusion.2.d_ref), custom_call_target="tpu_custom_call" | custom-call | tf_op jit(solution)/shard_map/pallas_call | solution.py:698
  350.2 2.5 convert_element_type.112
  352.7 0.6 dynamic-slice_bitcast_fusion
  353.3 66.4 %all-reduce.2.cloned.1.call-done = bf16[384,1536]{1,0:T(8,128)(2,1)} async-done(((bf16[384,1536]{1,0:T(8,128)(2,1)}), bf16[384,1536]{1,0:T(8,128)(2,1)}) %all-reduce.2.cloned.1.call-update) | async-done | bytes 1179664 | tf_op jit(solution)/shard_map/psum | solution.py:798
  419.7 3.0 convert_element_type.109
  (30 shorter events, 0.1 us)
Async XLA Ops:
  7.2 151.1 %copy-start = (bf16[2048,512]{1,0:T(8,128)(2,1)S(1)}, bf16[2048,512]{1,0:T(8,128)(2,1)}, u32[]{:S(2)}) copy-start(bf16[2048,512]{1,0:T(8,128)(2,1)} %param.25) | copy-start | bytes 6291460
  7.2 4.1 copy-start.18
  7.2 412.5 %all-reduce.2.cloned.1.call-start = ((), (), s32[]{:S(2)}) async-start(), calls=%async_computation | async-start | bytes 2359296 | tf_op jit(solution)/shard_map/psum | solution.py:798
  7.2 4.1 copy-start.6
  12.0 5.4 %copy-start.19 = (s32[2]{0:T(128)S(1)}, s32[2]{0:T(128)}, u32[]{:S(2)}) copy-start(s32[2]{0:T(128)} %param.33) | copy-start | bytes 28
  12.0 6.8 %copy-start.3 = (bf16[384,1536]{1,0:T(8,128)(2,1)S(1)}, bf16[384,1536]{1,0:T(8,128)(2,1)}, u32[]{:S(2)}) copy-start(bf16[384,1536]{1,0:T(8,128)(2,1)} %refs_0_.2) | copy-start | bytes 3538948
  59.7 2.1 copy-start.4
  129.4 5.8 %copy-start.16 = (bf16[1536,512]{1,0:T(8,128)(2,1)S(1)}, bf16[1536,512]{1,0:T(8,128)(2,1)}, u32[]{:S(2)}) copy-start(bf16[1536,512]{1,0:T(8,128)(2,1)} %param.24) | copy-start | bytes 4718596
  135.2 20.3 %copy-start.7 = (bf16[512,1536]{1,0:T(8,128)(2,1)}, bf16[512,1536]{1,0:T(8,128)(2,1)S(1)}, u32[]{:S(2)}) copy-start(bf16[512,1536]{1,0:T(8,128)(2,1)S(1)} %get-tuple-element.50) | copy-start | bytes 4718596
  136.2 19.8 %copy-start.17 = (bf16[2,2048,128]{2,1,0:T(8,128)(2,1)S(1)}, bf16[2,2048,128]{2,1,0:T(8,128)(2,1)}, u32[]{:S(2)}) copy-start(bf16[2,2048,128]{2,1,0:T(8,128)(2,1)} %param.26) | copy-start | bytes 3145732
  155.5 1.3 copy-start.1
  156.0 2.2 copy-start.11
  161.6 1.6 copy-start.2
  293.1 10.7 %copy-start.9 = (bf16[1536,128]{1,0:T(8,128)(2,1)S(1)}, bf16[1536,128]{1,0:T(8,128)(2,1)}, u32[]{:S(2)}) copy-start(bf16[1536,128]{1,0:T(8,128)(2,1)} %param.23) | copy-start | bytes 1179652
  293.2 13.1 %copy-start.12 = (s32[1,512]{1,0:T(1,128)S(1)}, s32[1,512]{1,0:T(1,128)}, u32[]{:S(2)}) copy-start(s32[1,512]{1,0:T(1,128)} %param.29) | copy-start | bytes 6148
  303.8 5.4 %copy-start.13 = (f32[1,512]{1,0:T(1,128)S(1)}, f32[1,512]{1,0:T(1,128)}, u32[]{:S(2)}) copy-start(f32[1,512]{1,0:T(1,128)} %param.32) | copy-start | bytes 6148
  303.9 5.4 %copy-start.14 = (f32[1,512]{1,0:T(1,128)S(1)}, f32[1,512]{1,0:T(1,128)}, u32[]{:S(2)}) copy-start(f32[1,512]{1,0:T(1,128)} %param.30) | copy-start | bytes 6148
  303.9 5.4 %copy-start.15 = (f32[1,512]{1,0:T(1,128)S(1)}, f32[1,512]{1,0:T(1,128)}, u32[]{:S(2)}) copy-start(f32[1,512]{1,0:T(1,128)} %param.31) | copy-start | bytes 6148
  303.9 6.1 %copy-start.8 = (bf16[512,1536]{1,0:T(8,128)(2,1)S(1)}, bf16[512,1536]{1,0:T(8,128)(2,1)}, u32[]{:S(2)}) copy-start(bf16[512,1536]{1,0:T(8,128)(2,1)} %copy-done.7) | copy-start | bytes 4718596
  309.2 1.6 copy-start.10
  312.9 3.5 copy-start.5
Sparse Core Ops, SparseCore 0:
  313.0 106.7 all-reduce.1

commit v3 on v1

--- a/solution.py
+++ b/solution.py
@@ -104,8 +104,6 @@
     for peer in peers:
         pl.semaphore_signal(barrier, inc=1, device_id=peer, device_id_type=MESH)
     pl.semaphore_wait(barrier, len(peers))
-
-    started = []
 
     def block_rows(block, part):
         return pl.ds(pl.multiple_of(block * rows + part * piece, piece), piece)
@@ -448,64 +446,85 @@
     return attended if w is None else (attended, results[3])
 
 
+class YGather:
+    def __init__(self, own_half, place, send, recv):
+        self.ypos = lax.axis_index("mdl")
+        self.yp = lax.rem(self.ypos + 1, 4)
+        self.ym = lax.rem(self.ypos + 3, 4)
+        self.y2 = lax.rem(self.ypos + 2, 4)
+        self.own_half, self.place, self.send, self.recv = own_half, place, send, recv
+
+    def greet(self, barrier):
+        for peer in (self.yp, self.ym):
+            pl.semaphore_signal(barrier, inc=1, device_id={"mdl": peer}, device_id_type=MESH)
+        return 2
+
+    def copy(self, source_y, part, slot, target, lane, own=False):
+        return pltpu.make_async_remote_copy(
+            src_ref=self.own_half(part) if own else self.place(source_y, part, lane - 2),
+            dst_ref=self.place(source_y, part, slot),
+            send_sem=self.send.at[lane, part],
+            recv_sem=self.recv.at[slot, part],
+            device_id={"mdl": target},
+            device_id_type=MESH,
+        )
+
+    def first(self):
+        return [
+            self.copy(self.ypos, 0, 0, self.yp, 0, own=True),
+            self.copy(self.ypos, 1, 1, self.ym, 1, own=True),
+            self.copy(self.ypos, 1, 0, self.yp, 0, own=True),
+            self.copy(self.ypos, 0, 1, self.ym, 1, own=True),
+        ]
+
+    def start(self):
+        for item in self.first():
+            item.start()
+
+    def arrived(self, slot, part):
+        where = self.place((self.ym, self.yp, self.y2)[slot], part, slot)
+        pltpu.make_async_copy(where, where, self.recv.at[slot, part]).wait()
+
+    def relay(self, part):
+        if part == 0:
+            return self.copy(self.ym, 0, 2, self.yp, 2)
+        return self.copy(self.yp, 1, 2, self.ym, 3)
+
+    def pass_on(self, part):
+        self.arrived(part, part)
+        self.relay(part).start()
+
+    def wait_sent(self):
+        for item in self.first():
+            item.wait_send()
+        for part in range(2):
+            self.relay(part).wait_send()
+
+
 def gather_kernel(x_ref, out_ref, send, recv, local):
     rows, width = x_ref.shape
     half = rows // 2
-    ypos = lax.axis_index("mdl")
-    yp = lax.rem(ypos + 1, 4)
-    ym = lax.rem(ypos + 3, 4)
-    y2 = lax.rem(ypos + 2, 4)
-    barrier = pltpu.get_barrier_semaphore()
-    for peer in (yp, ym):
-        pl.semaphore_signal(barrier, inc=1, device_id={"mdl": peer}, device_id_type=MESH)
-    pl.semaphore_wait(barrier, 2)
-
-    def place(source_y, part):
+
+    def place(source_y, part, slot):
         return out_ref.at[
             pl.ds(part * half, half), pl.ds(pl.multiple_of(source_y * width, HEAD), width)
         ]
 
-    def copy(source_y, part, slot, target, lane, own=False):
-        where = place(source_y, part)
-        return pltpu.make_async_remote_copy(
-            src_ref=x_ref.at[pl.ds(part * half, half)] if own else where,
-            dst_ref=where,
-            send_sem=send.at[lane, part],
-            recv_sem=recv.at[slot, part],
-            device_id={"mdl": target},
-            device_id_type=MESH,
-        )
-
-    def arrived(slot, source_y, part):
-        where = place(source_y, part)
-        pltpu.make_async_copy(where, where, recv.at[slot, part]).wait()
-
-    first = [
-        copy(ypos, 0, 0, yp, 0, own=True),
-        copy(ypos, 1, 1, ym, 1, own=True),
-        copy(ypos, 1, 0, yp, 0, own=True),
-        copy(ypos, 0, 1, ym, 1, own=True),
-    ]
-    for item in first:
-        item.start()
+    ring = YGather(lambda part: x_ref.at[pl.ds(part * half, half)], place, send, recv)
+    barrier = pltpu.get_barrier_semaphore()
+    pl.semaphore_wait(barrier, ring.greet(barrier))
+    ring.start()
     mine = pltpu.make_async_copy(
-        x_ref, out_ref.at[:, pl.ds(pl.multiple_of(ypos * width, HEAD), width)], local.at[0]
+        x_ref, out_ref.at[:, pl.ds(pl.multiple_of(ring.ypos * width, HEAD), width)], local.at[0]
     )
     mine.start()
-    arrived(0, ym, 0)
-    up = copy(ym, 0, 2, yp, 2)
-    up.start()
-    arrived(1, yp, 1)
-    down = copy(yp, 1, 2, ym, 2)
-    down.start()
-    arrived(0, ym, 1)
-    arrived(1, yp, 0)
-    arrived(2, y2, 0)
-    arrived(2, y2, 1)
-    for item in first:
-        item.wait_send()
-    up.wait_send()
-    down.wait_send()
+    ring.pass_on(0)
+    ring.pass_on(1)
+    ring.arrived(0, 1)
+    ring.arrived(1, 0)
+    ring.arrived(2, 0)
+    ring.arrived(2, 1)
+    ring.wait_sent()
     mine.wait()
 
 
@@ -517,14 +536,371 @@
         in_specs=[vmem],
         out_specs=vmem,
         scratch_shapes=[
-            pltpu.SemaphoreType.DMA((3, 2)),
+            pltpu.SemaphoreType.DMA((4, 2)),
             pltpu.SemaphoreType.DMA((3, 2)),
             pltpu.SemaphoreType.DMA((1,)),
         ],
         compiler_params=pltpu.CompilerParams(
+            collective_id=ident, has_side_effects=True, vmem_limit_bytes=8 * 2**20
+        ),
+    )(x)
+
+
+class Geometry:
+    def __init__(self, rows, columns, by_rows):
+        self.by_rows = by_rows
+        self.rows, self.columns = rows, columns
+        if by_rows:
+            self.half = (rows // 2, columns)
+            self.quarter_shape = [(rows // 4, columns // 4)] * 2
+            self.sub_shape = [(rows // 16, columns // 4)] * 2
+        else:
+            third = columns // 6
+            self.half = (rows, columns // 2)
+            self.quarter_shape = [(rows // 4, 2 * third), (rows // 4, third)]
+            self.sub_shape = [(rows // 4, third // 2), (rows // 8, third // 2)]
+
+    def whole(self, core):
+        if self.by_rows:
+            return (core * self.half[0], 0)
+        return (0, core * self.half[1])
+
+    def quarter(self, part, index):
+        rows, columns = self.quarter_shape[part]
+        if self.by_rows:
+            return (part * rows, index * columns)
+        return (index * rows, part * self.quarter_shape[0][1])
+
+    def sub(self, part, index):
+        rows, columns = self.sub_shape[part]
+        if self.by_rows:
+            return (index * rows, 0)
+        if part == 0:
+            return (0, index * columns)
+        return ((index // 2) * rows, lax.rem(index, 2) * columns)
+
+    def scratch(self):
+        vmem = pltpu.VMEM
+        shapes = [vmem(self.half, BF)] * 3
+        for part in range(2):
+            shapes.append(vmem((3,) + self.quarter_shape[part], BF))
+            shapes.append(vmem(self.quarter_shape[part], BF))
+            shapes.append(vmem((3,) + self.sub_shape[part], BF))
+        dma = pltpu.SemaphoreType.DMA
+        return shapes + [dma((4, 2, 3)), dma((4, 2, 3)), dma((9,)), dma((9,))]
+
+
+def box(start, shape):
+    row, column = start
+    return (
+        pl.ds(row if isinstance(row, int) else pl.multiple_of(row, 16), shape[0]),
+        pl.ds(column if isinstance(column, int) else pl.multiple_of(column, HEAD), shape[1]),
+    )
+
+
+def plus(left, right):
+    return (left[0] + right[0], left[1] + right[1])
+
+
+class Reduce:
+    hops = (2, 1, 3)
+
+    def __init__(self, shape, att_ref, d_ref, out_ref, scratch):
+        self.g = shape
+        self.att, self.d, self.out = att_ref, d_ref, out_ref
+        self.theirs, self.mine, self.got = scratch[:3]
+        self.part_in = [scratch[3], scratch[6]]
+        self.part_sum = [scratch[4], scratch[7]]
+        self.sub_in = [scratch[5], scratch[8]]
+        self.send, self.recv, self.csend, self.crecv = scratch[9:13]
+        me = lax.axis_index("rep")
+        self.me = me
+        self.core = lax.rem(me, 2)
+        self.other = me + 1 - 2 * self.core
+        self.zpos = me // 4
+        self.xpos = lax.rem(me // 2, 2) * 2 + lax.axis_index("sec")
+        self.first = [self.xpos, self.zpos]
+        self.second = [self.zpos, self.xpos]
+        self.near = [self.at_x, self.at_z]
+
+    def at_x(self, k):
+        there = lax.rem(self.xpos + k, 4)
+        return {"rep": self.zpos * 4 + (there // 2) * 2 + self.core, "sec": lax.rem(there, 2)}
+
+    def at_z(self, k):
+        return {"rep": lax.rem(self.me + 4 * k, 16)}
+
+    def greet(self, barrier):
+        for k in range(1, 4):
+            pl.semaphore_signal(barrier, inc=1, device_id=self.at_x(k), device_id_type=MESH)
+            pl.semaphore_signal(barrier, inc=1, device_id=self.at_z(k), device_id_type=MESH)
+        pl.semaphore_signal(barrier, inc=1, device_id={"rep": self.other}, device_id_type=MESH)
+        return 7
+
+    def grad(self, which):
+        left, right = self.att, self.d
+        if self.g.by_rows:
+            size = self.g.half[0]
+            left = left[:, pl.ds(pl.multiple_of(which * size, size), size)]
+            right = right[...]
+        else:
+            size = self.g.half[1]
+            left = left[...]
+            right = right[:, pl.ds(pl.multiple_of(which * size, HEAD), size)]
+        return lax.dot_general(left, right, (((0,), (0,)), ((), ())), preferred_element_type=F32)
+
+    def copy(self, source, target, send, recv, device):
+        return pltpu.make_async_remote_copy(
+            src_ref=source,
+            dst_ref=target,
+            send_sem=send,
+            recv_sem=recv,
+            device_id=device,
+            device_id_type=MESH,
+        )
+
+    def swap(self):
+        return self.copy(
+            self.theirs, self.got, self.csend.at[0], self.crecv.at[0], {"rep": self.other}
+        )
+
+    def stage(self, level, part, k, source, target, device):
+        return self.copy(
+            source,
+            target,
+            self.send.at[level, part, k - 1],
+            self.recv.at[level, part, k - 1],
+            device,
+        )
+
+    def scatter_one(self, part, k):
+        start = self.g.quarter(part, lax.rem(self.first[part] + k, 4))
+        return self.stage(
+            0,
+            part,
+            k,
+            self.mine.at[box(start, self.g.quarter_shape[part])],
+            self.part_in[part].at[k - 1],
+            self.near[part](k),
+        )
+
+    def scatter_two(self, part, k):
+        start = self.g.sub(part, lax.rem(self.second[part] + k, 4))
+        return self.stage(
+            1,
+            part,
+            k,
+            self.part_sum[part].at[box(start, self.g.sub_shape[part])],
+            self.sub_in[part].at[k - 1],
+            self.near[1 - part](k),
+        )
+
+    def my_sub(self, part):
+        start = plus(
+            self.g.whole(self.core),
+            plus(self.g.quarter(part, self.first[part]), self.g.sub(part, self.second[part])),
+        )
+        return box(start, self.g.sub_shape[part])
+
+    def out_quarter(self, core, part, index):
+        start = plus(self.g.whole(core), self.g.quarter(part, index))
+        return self.out.at[box(start, self.g.quarter_shape[part])]
+
+    def gather_two(self, part, k):
+        where = self.out.at[self.my_sub(part)]
+        return self.stage(2, part, k, where, where, self.near[1 - part](k))
+
+    def gather_one(self, part, k):
+        where = self.out_quarter(self.core, part, self.first[part])
+        return self.stage(3, part, k, where, where, self.near[part](k))
+
+    def share(self, part, k, core):
+        where = self.out_quarter(core, part, lax.rem(self.first[part] + 4 - k, 4))
+        index = 1 + part * 4 + k
+        return self.copy(
+            where, where, self.csend.at[index], self.crecv.at[index], {"rep": self.other}
+        )
+
+    def begin(self):
+        self.theirs[...] = self.grad(1 - self.core).astype(BF)
+
+    def swap_and_scatter(self):
+        self.swap().start()
+        own = self.grad(self.core)
+        self.swap().wait_recv()
+        self.mine[...] = (own + self.got[...].astype(F32)).astype(BF)
+        for k in self.hops:
+            for part in range(2):
+                self.scatter_one(part, k).start()
+
+    def second_scatter(self):
+        for part in range(2):
+            start = self.g.quarter(part, self.first[part])
+            total = self.mine[box(start, self.g.quarter_shape[part])].astype(F32)
+            for k in (1, 3, 2):
+                self.scatter_one(part, k).wait_recv()
+                total += self.part_in[part][k - 1].astype(F32)
+            self.part_sum[part][...] = total.astype(BF)
+            for k in self.hops:
+                self.scatter_two(part, k).start()
+
+    def first_gather(self):
+        for part in range(2):
+            start = self.g.sub(part, self.second[part])
+            total = self.part_sum[part][box(start, self.g.sub_shape[part])].astype(F32)
+            for k in (1, 3, 2):
+                self.scatter_two(part, k).wait_recv()
+                total += self.sub_in[part][k - 1].astype(F32)
+            self.out[self.my_sub(part)] = total.astype(BF)
+            for k in self.hops:
+                self.gather_two(part, k).start()
+
+    def second_gather(self):
+        for part in range(2):
+            for k in range(1, 4):
+                self.gather_two(part, k).wait_recv()
+            for k in self.hops:
+                self.gather_one(part, k).start()
+            self.share(part, 0, self.core).start()
+
+    def last_shares(self):
+        for k in (1, 3, 2):
+            for part in range(2):
+                self.gather_one(part, k).wait_recv()
+                self.share(part, k, self.core).start()
+
+    def finish(self):
+        for part in range(2):
+            for k in range(4):
+                self.share(part, k, 1 - self.core).wait_recv()
+        self.swap().wait_send()
+        for part in range(2):
+            for k in range(1, 4):
+                self.scatter_one(part, k).wait_send()
+                self.scatter_two(part, k).wait_send()
+                self.gather_two(part, k).wait_send()
+                self.gather_one(part, k).wait_send()
+            for k in range(4):
+                self.share(part, k, self.core).wait_send()
+
+
+def reduce_kernel(shape, att_ref, d_ref, out_ref, *scratch):
+    work = Reduce(shape, att_ref, d_ref, out_ref, scratch)
+    barrier = pltpu.get_barrier_semaphore()
+    expected = work.greet(barrier)
+    work.begin()
+    pl.semaphore_wait(barrier, expected)
+    work.swap_and_scatter()
+    work.second_scatter()
+    work.first_gather()
+    work.second_gather()
+    work.last_shares()
+    work.finish()
+
+
+def reduced_grad(attended, grad_in, ident):
+    shape = Geometry(attended.shape[1], grad_in.shape[1], True)
+    vmem = pl.BlockSpec(memory_space=pltpu.VMEM)
+    return pl.pallas_call(
+        functools.partial(reduce_kernel, shape),
+        out_shape=jax.ShapeDtypeStruct((shape.rows, shape.columns), BF),
+        in_specs=[vmem, vmem],
+        out_specs=vmem,
+        scratch_shapes=shape.scratch(),
+        compiler_params=pltpu.CompilerParams(
+            collective_id=ident, has_side_effects=True, vmem_limit_bytes=24 * 2**20
+        ),
+    )(attended, grad_in)
+
+
+def output_kernel(shape, x_ref, w_ref, base_ref, *refs):
+    if shape is None:
+        out_ref, acc, blocks, send, recv = refs
+        work = None
+    else:
+        att_ref, d_ref, out_ref, grad_ref, acc, blocks, send, recv = refs[:8]
+        work = Reduce(shape, att_ref, d_ref, grad_ref, refs[8:])
+    rows = x_ref.shape[0]
+    half = rows // 2
+    ring = YGather(
+        lambda part: x_ref.at[pl.ds(part * half, half)],
+        lambda source_y, part, slot: blocks.at[slot, pl.ds(part * half, half)],
+        send,
+        recv,
+    )
+    barrier = pltpu.get_barrier_semaphore()
+    expected = ring.greet(barrier)
+    if work is not None:
+        expected += work.greet(barrier)
+    pl.semaphore_wait(barrier, expected)
+    ring.start()
+    if work is not None:
+        work.begin()
+        work.swap_and_scatter()
+    acc[...] = base_ref[...].astype(F32) + jnp.dot(
+        x_ref[...], w_ref[ring.ypos], preferred_element_type=F32
+    )
+
+    def add(slot, part):
+        source_y = (ring.ym, ring.yp, ring.y2)[slot]
+        span = pl.ds(part * half, half)
+        acc[span, :] += jnp.dot(
+            blocks[slot, span, :], w_ref[source_y], preferred_element_type=F32
+        )
+
+    ring.pass_on(0)
+    ring.pass_on(1)
+    add(0, 0)
+    add(1, 1)
+    if work is not None:
+        work.second_scatter()
+    ring.arrived(0, 1)
+    add(0, 1)
+    if work is not None:
+        work.first_gather()
+    ring.arrived(1, 0)
+    add(1, 0)
+    if work is not None:
+        work.second_gather()
+    ring.arrived(2, 0)
+    add(2, 0)
+    ring.arrived(2, 1)
+    add(2, 1)
+    out_ref[...] = acc[...].astype(out_ref.dtype)
+    if work is not None:
+        work.last_shares()
+        work.finish()
+    ring.wait_sent()
+
+
+def output_call(x, w_full, base, out_type, grads, ident):
+    rows, width = x.shape
+    columns = w_full.shape[2]
+    vmem = pl.BlockSpec(memory_space=pltpu.VMEM)
+    args = [x, w_full, base]
+    out_shape = [jax.ShapeDtypeStruct((rows, columns), out_type)]
+    scratch = [
+        pltpu.VMEM((rows, columns), F32),
+        pltpu.VMEM((3, rows, width), BF),
+        pltpu.SemaphoreType.DMA((4, 2)),
+        pltpu.SemaphoreType.DMA((3, 2)),
+    ]
+    shape = None
+    if grads is not None:
+        shape = Geometry(grads[0].shape[1], grads[1].shape[1], False)
+        args += list(grads)
+        out_shape.append(jax.ShapeDtypeStruct((shape.rows, shape.columns), BF))
+        scratch += shape.scratch()
+    return pl.pallas_call(
+        functools.partial(output_kernel, shape),
+        out_shape=out_shape,
+        in_specs=[vmem] * len(args),
+        out_specs=[vmem] * len(out_shape),
+        scratch_shapes=scratch,
+        compiler_params=pltpu.CompilerParams(
             collective_id=ident, has_side_effects=True, vmem_limit_bytes=48 * 2**20
         ),
-    )(x)
+    )(*args)
 
 
 def project(source, w_query, w_keyval, live_mask):
@@ -573,40 +949,22 @@
 
     queries, keyval = project(obs_float, a_query, a_keyval, live_mask)
     attended, a_out_full = attend(total, queries, keyval, a_out, 1)
-    attended_full = gather_columns(attended, 3)
-    hidden = (
-        obs_float
-        + jnp.dot(
-            attended_full,
-            a_out_full.reshape(4 * a_out.shape[0], a_out.shape[1]),
-            preferred_element_type=F32,
-        )
-    ).astype(BF)
+    (hidden,) = output_call(attended, a_out_full, obs[0], BF, None, 3)
     embed_part = jnp.dot(hidden, c_in, preferred_element_type=F32).astype(BF)
     embedded = gather_columns(embed_part, 4)
     dhidden = policy_backward(
         hidden, actions[0], advantages[0], old_logp[0], live_mask, live_total, w_policy
     ).astype(BF)
-    actor_grad = lax.dot_general(
-        attended, dhidden, (((0,), (0,)), ((), ())), preferred_element_type=F32
-    ).astype(BF)
     embed_float = embedded.astype(F32)
     critic_queries, critic_keyval = project(embed_float, c_query, c_keyval, live_mask)
-    critic_attended = attend(total, critic_queries, critic_keyval, None, 2)
-    critic_sum = lax.psum(
-        jnp.dot(critic_attended, c_out, preferred_element_type=F32).astype(BF),
-        "mdl",
-    ).astype(F32)
-    value_pred, dmixed = value_backward(
-        embed_float + critic_sum, returns[0], live_mask, live_total, w_value
-    )
+    critic_attended, c_out_full = attend(total, critic_queries, critic_keyval, c_out, 2)
+    mixed, actor_summed = output_call(
+        critic_attended, c_out_full, embedded, F32, (attended, dhidden), 5
+    )
+    value_pred, dmixed = value_backward(mixed, returns[0], live_mask, live_total, w_value)
     value_part = lax.dynamic_slice_in_dim(value_pred, row_start, part_rows, 0)
-    critic_grad = lax.dot_general(
-        critic_attended, dmixed.astype(BF), (((0,), (0,)), ((), ())), preferred_element_type=F32
-    )
-    actor_summed = lax.psum(actor_grad, ("rep", "sec")).astype(F32)
-    critic_summed = lax.psum(critic_grad.astype(BF), ("rep", "sec")).astype(F32)
-    return (value_part[None, :], actor_summed, critic_summed)
+    critic_summed = reduced_grad(critic_attended, dmixed.astype(BF), 6).astype(F32)
+    return (value_part[None, :], actor_summed.astype(F32), critic_summed)
 
 
 def solution(mesh):

time: 459 us -> 355 us (0.77); the launches traced: 458 us -> 348 us
  waiting for transfers between devices: 164 us -> 0 us
  Pallas kernels: 225 us -> 301 us
  matrix products: 27.2 us -> 12.1 us
  between operations: 16.3 us -> 3.22 us
  local copies, waits for them, and re-layouts: 8.57 us -> 13.8 us
    psum x2 -> x0, waiting for transfers between devices: 164 us -> none  [the longest x1 109 us: on_device(): actor_summed = lax.psum(actor_grad, ('rep', 'sec')).astype(F32)]
    pallas_call x0 -> x3, Pallas kernels: none -> 83.9 us  [the longest x2 53.3 us: output_call(): pl.pallas_call(functools.partial(output_kernel, shape), out_shape=out_sha...]
    pallas_call x2 -> x1, Pallas kernels: 36.1 us -> 19.3 us  [gather_columns(): pl.pallas_call(gather_kernel, out_shape=jax.ShapeDtypeStruct((x.shape[0],...]
    dot_general x4 -> x0, matrix products: 13.3 us -> none  [the longest x1 5.68 us: on_device(): jnp.dot(attended_full, a_out_full.reshape(4 * a_out.shape[0], a_out.shape...]
    pallas_call x2, Pallas kernels: 75.5 us -> 84.1 us  [attend_call(): pl.pallas_call(functools.partial(attend_kernel, heads, w is not None), ou...]
    unnamed x45 -> x47, local copies, waits for them, and re-layouts: 5.21 us -> 9.62 us
  transfers between devices with their start and end apart: 2 -> 0, of which waited for: 2 -> 0; matrix products, arithmetic and copies ran while one was open for 1% -> 0% of each run, Pallas kernels for 0% -> 0%
where the time goes in v3:
time: 355 us; the launch traced here: 348 us
  Pallas kernels  301 us (85%)
  other arithmetic  17.5 us (5%)
  local copies, waits for them, and re-layouts  13.8 us (4%)
  matrix products  12.1 us (3%)
    pallas_call x2, Pallas kernels, careful_call(): pl.pallas_call(careful_kernel, out_shape=jax.ShapeDtypeStruct((rows, head...  114 us
    pallas_call x2, Pallas kernels, attend_call(): pl.pallas_call(functools.partial(attend_kernel, heads, w is not None), ou...  84.1 us
    pallas_call x2, Pallas kernels, output_call(): pl.pallas_call(functools.partial(output_kernel, shape), out_shape=out_sha...  53.3 us
    pallas_call x1, Pallas kernels, reduced_grad(): pl.pallas_call(functools.partial(reduce_kernel, shape), out_shape=jax.Sha...  30.6 us
    pallas_call x1, Pallas kernels, gather_columns(): pl.pallas_call(gather_kernel, out_shape=jax.ShapeDtypeStruct((x.shape[0],...  19.3 us
    unnamed x47, local copies, waits for them, and re-layouts  9.62 us

profile of v3, /device:TPU:1, one launch (start us, length us, event | category | flops | bytes accessed | tf_op | source)
XLA Modules:
  0.0 348.2 jit_solution(15437060544955869837)
XLA Ops:
  0.6 0.0 copy-start
  0.6 0.0 copy-start.21
  0.7 1.4 dynamic_slice.6.total_ref
  2.1 0.8 add_compare_fusion
  2.8 1.8 fusion.8
  4.7 2.2 fusion.31
  6.9 0.6 fusion.33
  7.5 0.0 copy-start.10
  7.5 0.1 fusion.35.kv_ref
  7.7 1.7 fusion.28
  9.4 1.9 copy.18
  11.3 40.9 %shard_map.166 = (bf16[512,384]{1,0:T(8,128)(2,1)}, f32[6,128]{1,0:T(8,128)S(1)}, bf16[8192,256]{1,0:T(8,128)(2,1)}, bf16[4,384,1536]{2,1,0:T(8,128)(2,1)S(1)}) custom-call(s32[1]{0:T(128)} %dynamic_slice.6.total_ref, bf16[1536,128]{1,0:T(8,128)(2,1)} %bitcast.48, bf16[512,256]{1,0:T(8,128)(2,1)S(1)} %fusion.35.kv_ref, bf16[384,1536]{1,0:T(8,128)(2,1)S(1)} %copy-done.10), custom_call_target="tpu_custom_call" | custom-call | flops 6442450944 | bytes 4194304 | tf_op jit(solution)/shard_map/pallas_call | solution.py:366
  52.2 2.1 copy-done.8
  54.3 0.6 and_reduce_fusion.1
  55.6 49.9 %conditional.2 = (bf16[512,384]{1,0:T(8,128)(2,1)}) conditional(s32[]{:T(128)} %convert_element_type.83, (s32[1]{0:T(128)}, bf16[1536,128]{1,0:T(8,128)(2,1)}, bf16[8192,256]{1,0:T(8,128)(2,1)}) %tuple.30, bf16[512,384]{1,0:T(8,128)(2,1)} %get-tuple-element.41), branch_computations={%region_2.3_spmd, %region_3.4_spmd} | conditional | bytes 8 | solution.py:441
  55.6 49.5 %branch_0_fun.2 = bf16[512,384]{1,0:T(8,128)(2,1)} custom-call(s32[1]{0:T(128)} %get-tuple-element.20.total_ref, bf16[1536,128]{1,0:T(8,128)(2,1)} %get-tuple-element.21.q_ref, bf16[8192,256]{1,0:T(8,128)(2,1)} %get-tuple-element.22.kv_ref), custom_call_target="tpu_custom_call" | custom-call | tf_op jit(solution)/shard_map/cond/branch_0_fun/pallas_call | solution.py:422
  105.6 0.0 copy-start.7
  105.6 1.4 copy-done.7
  107.0 19.6 %shard_map.167 = bf16[512,1536]{1,0:T(8,128)(2,1)S(1)} custom-call(bf16[512,384]{1,0:T(8,128)(2,1)} %get-tuple-element.53.x_ref.refs_0_, bf16[4,384,1536]{2,1,0:T(8,128)(2,1)} %copy-done.8, bf16[512,1536]{1,0:T(8,128)(2,1)S(1)} %bitcast.45), custom_call_target="tpu_custom_call" | custom-call | tf_op jit(solution)/shard_map/pallas_call | solution.py:894
  126.6 0.0 copy-start.1
  126.6 0.0 copy-start.14
  126.6 0.0 copy-start.22
  126.6 0.0 copy-start.15
  126.6 0.0 copy-start.16
  126.6 0.4 fusion.14
  127.0 0.7 copy-done.1
  127.7 0.7 fusion.57
  128.5 0.1 exponential_reduce_fusion
  128.5 0.1 select_reduce_fusion
  128.6 0.6 reduce_sum.95
  129.9 0.0 copy-start.2
  129.9 0.8 divide_select_fusion
  130.7 2.2 fusion.10
  132.9 0.0 copy-start.18
  132.9 1.8 fusion.13.refs_1_
  134.7 1.0 convolution_convert_fusion.x_ref
  135.7 19.3 %shard_map.168.base_ref = bf16[512,2048]{1,0:T(8,128)(2,1)S(1)} custom-call(bf16[512,512]{1,0:T(8,128)(2,1)S(1)} %convolution_convert_fusion.x_ref), custom_call_target="tpu_custom_call" | custom-call | tf_op jit(solution)/shard_map/pallas_call | solution.py:533
  155.0 0.0 copy-start.3
  155.0 0.5 fusion
  155.5 0.8 fusion.39
  156.3 0.8 fusion.37
  157.0 0.1 fusion.36.kv_ref
  157.2 1.4 fusion.24
  158.6 0.3 copy.21
  158.9 0.0 copy-start.9
  158.9 1.6 copy-done.9
  160.5 43.2 %shard_map.169 = (bf16[512,512]{1,0:T(8,128)(2,1)S(1)}, f32[8,128]{1,0:T(8,128)S(1)}, bf16[8192,256]{1,0:T(8,128)(2,1)}, bf16[4,512,2048]{2,1,0:T(8,128)(2,1)}) custom-call(s32[1]{0:T(128)} %dynamic_slice.6.total_ref, bf16[2048,128]{1,0:T(8,128)(2,1)S(1)} %bitcast.46, bf16[512,256]{1,0:T(8,128)(2,1)S(1)} %fusion.36.kv_ref, bf16[512,2048]{1,0:T(8,128)(2,1)S(1)} %copy-done.9), custom_call_target="tpu_custom_call" | custom-call | flops 8589934592 | bytes 4194304 | tf_op jit(solution)/shard_map/pallas_call | solution.py:366
  203.7 0.7 and_reduce_fusion
  205.0 64.4 %conditional.3 = (bf16[512,512]{1,0:T(8,128)(2,1)S(1)}) conditional(s32[]{:T(128)} %convert_element_type.89, (s32[1]{0:T(128)}, bf16[2048,128]{1,0:T(8,128)(2,1)S(1)}, bf16[8192,256]{1,0:T(8,128)(2,1)}) %tuple.29, bf16[512,512]{1,0:T(8,128)(2,1)S(1)} %get-tuple-element.45), branch_computations={%region_6.7_spmd, %region_7.8_spmd} | conditional | bytes 8 | solution.py:441
  205.0 64.2 %branch_0_fun.3 = bf16[512,512]{1,0:T(8,128)(2,1)S(1)} custom-call(s32[1]{0:T(128)} %get-tuple-element.23.total_ref, bf16[2048,128]{1,0:T(8,128)(2,1)S(1)} %get-tuple-element.24.q_ref, bf16[8192,256]{1,0:T(8,128)(2,1)} %get-tuple-element.25.kv_ref), custom_call_target="tpu_custom_call" | custom-call | tf_op jit(solution)/shard_map/cond/branch_0_fun/pallas_call | solution.py:422
  269.4 1.6 copy-done.4
  271.0 1.4 copy-done.5
  272.4 33.7 %shard_map.170 = (f32[512,2048]{1,0:T(8,128)}, bf16[384,1536]{1,0:T(8,128)(2,1)S(1)}) custom-call(bf16[512,512]{1,0:T(8,128)(2,1)S(1)} %get-tuple-element.54.x_ref.att_ref, bf16[4,512,2048]{2,1,0:T(8,128)(2,1)} %get-tuple-element.46.w_ref, bf16[512,2048]{1,0:T(8,128)(2,1)S(1)} %copy-done.4, bf16[512,384]{1,0:T(8,128)(2,1)} %get-tuple-element.53.x_ref.refs_0_, ...), custom_call_target="tpu_custom_call" | custom-call | tf_op jit(solution)/shard_map/pallas_call | solution.py:894
  306.2 0.0 copy-start.13
  306.2 2.7 multiply_reduce_fusion
  308.9 0.7 copy-done.11
  309.6 0.7 fusion.15
  310.3 0.7 select_divide_fusion
  311.0 0.7 fusion.2
  311.7 0.8 fusion.4.d_ref
  312.6 30.6 %shard_map.171 = bf16[512,2048]{1,0:T(8,128)(2,1)S(1)} custom-call(bf16[512,512]{1,0:T(8,128)(2,1)S(1)} %get-tuple-element.54.x_ref.att_ref, bf16[512,2048]{1,0:T(8,128)(2,1)S(1)} %fusion.4.d_ref), custom_call_target="tpu_custom_call" | custom-call | tf_op jit(solution)/shard_map/pallas_call | solution.py:804
  343.2 2.5 convert_element_type.100
  345.7 1.7 convert_element_type.97
  347.4 0.6 dynamic-slice_bitcast_fusion
  (34 shorter events, 0.1 us)
Async XLA Ops:
  0.6 156.6 %copy-start = (bf16[2048,512]{1,0:T(8,128)(2,1)S(1)}, bf16[2048,512]{1,0:T(8,128)(2,1)}, u32[]{:S(2)}) copy-start(bf16[2048,512]{1,0:T(8,128)(2,1)} %param.25) | copy-start | bytes 6291460
  0.6 6.2 %copy-start.21 = (bf16[2,1536,128]{2,1,0:T(8,128)(2,1)S(1)}, bf16[2,1536,128]{2,1,0:T(8,128)(2,1)}, u32[]{:S(2)}) copy-start(bf16[2,1536,128]{2,1,0:T(8,128)(2,1)} %param.21) | copy-start | bytes 2359300
  2.1 4.8 %copy-start.6 = (bf16[1,512,1536]{2,1,0:T(8,128)(2,1)S(1)}, bf16[1,512,1536]{2,1,0:T(8,128)(2,1)}, u32[]{:S(2)}) copy-start(bf16[1,512,1536]{2,1,0:T(8,128)(2,1)} %param.19) | copy-start | bytes 4718596
  4.6 3.0 copy-start.19
  7.5 3.8 %copy-start.10 = (bf16[384,1536]{1,0:T(8,128)(2,1)S(1)}, bf16[384,1536]{1,0:T(8,128)(2,1)}, u32[]{:S(2)}) copy-start(bf16[384,1536]{1,0:T(8,128)(2,1)} %refs_0_.2) | copy-start | bytes 3538948
  52.2 2.1 copy-start.8
  105.6 1.4 copy-start.7
  107.0 20.7 %copy-start.12 = (bf16[1536,128]{1,0:T(8,128)(2,1)S(1)}, bf16[1536,128]{1,0:T(8,128)(2,1)}, u32[]{:S(2)}) copy-start(bf16[1536,128]{1,0:T(8,128)(2,1)} %param.23) | copy-start | bytes 1179652
  126.6 1.1 copy-start.1
  126.6 2.0 copy-start.14
  126.6 2.0 copy-start.22
  126.6 3.3 copy-start.15
  126.6 3.3 copy-start.16
  129.9 3.0 copy-start.2
  132.9 1.8 copy-start.18
  135.7 19.8 %copy-start.20 = (bf16[2,2048,128]{2,1,0:T(8,128)(2,1)S(1)}, bf16[2,2048,128]{2,1,0:T(8,128)(2,1)}, u32[]{:S(2)}) copy-start(bf16[2,2048,128]{2,1,0:T(8,128)(2,1)} %param.26) | copy-start | bytes 3145732
  155.0 2.2 copy-start.3
  158.9 1.6 copy-start.9
  269.4 1.6 copy-start.4
  271.0 1.4 copy-start.5
  306.2 2.7 copy-start.13
  306.2 3.5 copy-start.11
  308.9 1.5 copy-start.17

commit v4 on v3

--- a/solution.py
+++ b/solution.py
@@ -29,24 +29,26 @@
     return factor * (grad_in - normed * jnp.mean(grad_in * normed, axis=-1, keepdims=True))
 
 
-def policy_backward(hidden, action_ids, advantage, old_values, live_mask, live_total, w_policy):
+def policy_backward(hidden, side, w_policy):
     source = hidden.astype(F32)
-    normed = rms_normed(source)
+    factor = lax.rsqrt(jnp.mean(source * source, axis=-1, keepdims=True) + epsilon)
+    normed = source * factor
     logits = jnp.dot(normed.astype(BF), w_policy, preferred_element_type=F32)
-    log_probs = jax.nn.log_softmax(logits, axis=-1)
-    onehot = (action_ids[:, None] == lax.broadcasted_iota(jnp.int32, logits.shape, 1)).astype(F32)
-    chosen = jnp.sum(onehot * log_probs, axis=-1)
+    shifted = logits - jnp.max(logits, axis=-1, keepdims=True)
+    log_probs = shifted - jnp.log(jnp.sum(jnp.exp(shifted), axis=-1, keepdims=True))
+    action, advantage, old_values, scale = (side[:, k : k + 1] for k in range(4))
+    command = lax.broadcasted_iota(jnp.int32, logits.shape, 1).astype(F32)
+    onehot = (action == command).astype(F32)
+    chosen = jnp.sum(onehot * log_probs, axis=-1, keepdims=True)
     prob_ratio = jnp.exp(chosen - old_values)
     plain_term = prob_ratio * advantage
     bounded = jnp.clip(prob_ratio, 1.0 - clip_range, 1.0 + clip_range) * advantage
-    slope_term = jnp.where(
-        live_mask & (plain_term <= bounded), -plain_term / live_total, jnp.float32(0.0)
-    )
-    dlogits = slope_term[:, None] * (onehot - jnp.exp(log_probs))
+    slope_term = jnp.where((scale > 0.0) & (plain_term <= bounded), -plain_term * scale, 0.0)
+    dlogits = slope_term * (onehot - jnp.exp(log_probs))
     dnormed = lax.dot_general(
         dlogits.astype(BF), w_policy, (((1,), (1,)), ((), ())), preferred_element_type=F32
     )
-    return norm_backward(source, normed, dnormed)
+    return factor * (dnormed - normed * jnp.mean(dnormed * normed, axis=-1, keepdims=True))
 
 
 def value_backward(mixed_out, target, live_mask, live_total, w_value):
@@ -61,16 +63,10 @@
 
 
 def attend_kernel(
-    heads, with_w, total_ref, q_ref, kv_ref, *refs
+    heads, count_ref, x_ref, wq_ref, wkv_ref, w_ref, out_ref, sums_ref, kvout_ref, wfull_ref, *refs
 ):
-    if with_w:
-        w_ref, out_ref, sums_ref, kvout_ref, wfull_ref = refs[:5]
-        refs = refs[5:]
-        buf, acc, send, recv, local, wsend, wrecv, wlocal = refs
-    else:
-        out_ref, sums_ref, kvout_ref = refs[:3]
-        buf, acc, send, recv, local = refs[3:]
-    rows = kv_ref.shape[0]
+    buf, acc, q_ref, kv_ref, send, recv, local, wsend, wrecv, wlocal = refs
+    rows = x_ref.shape[0]
     piece = rows // PIECES
     all_keys = buf.shape[0]
     me = lax.axis_index("rep")
@@ -99,10 +95,16 @@
 
     barrier = pltpu.get_barrier_semaphore()
     peers = [{"rep": zp}, {"rep": zm}, {"rep": xpeer}, {"rep": other}]
-    if with_w:
-        peers += [{"mdl": yp}, {"mdl": ym}]
+    peers += [{"mdl": yp}, {"mdl": ym}]
     for peer in peers:
         pl.semaphore_signal(barrier, inc=1, device_id=peer, device_id_type=MESH)
+
+    total = count_ref[lax.axis_index("sec")]
+    normed = rms_normed(x_ref[...].astype(F32)).astype(BF)
+    live = me * rows + lax.broadcasted_iota(jnp.int32, (rows, HEAD), 0) < total
+    for part in range(2):
+        made = jnp.dot(normed, wkv_ref[part], preferred_element_type=F32)
+        kv_ref[:, part * HEAD : (part + 1) * HEAD] = jnp.where(live, made, 0.0).astype(BF)
     pl.semaphore_wait(barrier, len(peers))
 
     def block_rows(block, part):
@@ -178,51 +180,54 @@
     own_copy.start()
     keep(None).start()
 
-    if with_w:
-        wrows = w_ref.shape[0]
-        wpiece = wrows // 4
-        wown = pltpu.make_async_copy(w_ref, wfull_ref.at[ypos], wlocal.at[0])
-        wown.start()
-
-        wsrc = [ym, yp, y2]
-
-        def wcopy(source_y, which, part, slot, target, lane, own=False):
-            span = pl.ds((2 * which + part) * wpiece, wpiece)
-            where = wfull_ref.at[source_y, span]
-            return pltpu.make_async_remote_copy(
-                src_ref=w_ref.at[span] if own else where,
-                dst_ref=where,
-                send_sem=wsend.at[lane, part],
-                recv_sem=wrecv.at[slot, part],
-                device_id=target,
-                device_id_type=MESH,
-            )
-
-        def wfirst(part):
-            return [
-                wcopy(ypos, core, part, 0, {"mdl": yp}, 0, own=True),
-                wcopy(ypos, core, part, 1, {"mdl": ym}, 1, own=True),
-            ]
-
-        def wrelay(part):
-            if part == 0:
-                return wcopy(ym, core, 0, 2, {"mdl": yp}, 2)
-            return wcopy(yp, core, 1, 2, {"mdl": ym}, 2)
-
-        def wshare(slot, part):
-            return wcopy(wsrc[slot], core, part, 3 + slot, {"rep": other}, 3 + slot)
-
-        def warrived(slot, part):
-            which = core if slot < 3 else 1 - core
-            span = pl.ds((2 * which + part) * wpiece, wpiece)
-            where = wfull_ref.at[wsrc[slot % 3], span]
-            pltpu.make_async_copy(where, where, wrecv.at[slot, part]).wait()
-
-        for part in range(2):
-            for copy in wfirst(part):
-                copy.start()
-
-    total = total_ref[0]
+    wrows = w_ref.shape[0]
+    wpiece = wrows // 4
+    wown = pltpu.make_async_copy(w_ref, wfull_ref.at[ypos], wlocal.at[0])
+    wown.start()
+
+    wsrc = [ym, yp, y2]
+
+    def wcopy(source_y, which, part, slot, target, lane, own=False):
+        span = pl.ds((2 * which + part) * wpiece, wpiece)
+        where = wfull_ref.at[source_y, span]
+        return pltpu.make_async_remote_copy(
+            src_ref=w_ref.at[span] if own else where,
+            dst_ref=where,
+            send_sem=wsend.at[lane, part],
+            recv_sem=wrecv.at[slot, part],
+            device_id=target,
+            device_id_type=MESH,
+        )
+
+    def wfirst(part):
+        return [
+            wcopy(ypos, core, part, 0, {"mdl": yp}, 0, own=True),
+            wcopy(ypos, core, part, 1, {"mdl": ym}, 1, own=True),
+        ]
+
+    def wrelay(part):
+        if part == 0:
+            return wcopy(ym, core, 0, 2, {"mdl": yp}, 2)
+        return wcopy(yp, core, 1, 2, {"mdl": ym}, 2)
+
+    def wshare(slot, part):
+        return wcopy(wsrc[slot], core, part, 3 + slot, {"rep": other}, 3 + slot)
+
+    def warrived(slot, part):
+        which = core if slot < 3 else 1 - core
+        span = pl.ds((2 * which + part) * wpiece, wpiece)
+        where = wfull_ref.at[wsrc[slot % 3], span]
+        pltpu.make_async_copy(where, where, wrecv.at[slot, part]).wait()
+
+    for part in range(2):
+        for copy in wfirst(part):
+            copy.start()
+
+    queries = jnp.dot(normed, wq_ref[...], preferred_element_type=F32) * (HEAD ** (-0.5) * LOG2E)
+    for head in range(heads):
+        q_ref[head * rows : (head + 1) * rows, :] = queries[
+            :, head * HEAD : (head + 1) * HEAD
+        ].astype(BF)
     key_index = lax.broadcasted_iota(jnp.int32, (all_keys, HEAD), 0)
     buf[:, 2 * HEAD :] = jnp.where(key_index < total, 1.0, 0.0).astype(BF)
     acc[...] = jnp.zeros_like(acc)
@@ -257,16 +262,14 @@
             pass_on(5)
             take(11)
 
-        if with_w:
-
-            @pl.when(i == 5)
-            def _():
-                for part in range(2):
-                    warrived(0, part)
-                    warrived(1, part)
-                    wrelay(part).start()
-                    wshare(0, part).start()
-                    wshare(1, part).start()
+        @pl.when(i == 5)
+        def _():
+            for part in range(2):
+                warrived(0, part)
+                warrived(1, part)
+                wrelay(part).start()
+                wshare(0, part).start()
+                wshare(1, part).start()
 
         @pl.when(i == 5)
         def _():
@@ -299,10 +302,9 @@
 
     lax.fori_loop(0, 8, step, 0)
 
-    if with_w:
-        for part in range(2):
-            warrived(2, part)
-            wshare(2, part).start()
+    for part in range(2):
+        warrived(2, part)
+        wshare(2, part).start()
 
     for head in range(heads):
         part = acc[head * rows : (head + 1) * rows, :]
@@ -313,17 +315,16 @@
         sums_ref[2 * head : 2 * head + 1, :] = low
         sums_ref[2 * head + 1 : 2 * head + 2, :] = high
 
-    if with_w:
-        for slot in range(3, 6):
-            for part in range(2):
-                warrived(slot, part)
+    for slot in range(3, 6):
         for part in range(2):
-            for copy in wfirst(part):
-                copy.wait_send()
-            wrelay(part).wait_send()
-            for slot in range(3):
-                wshare(slot, part).wait_send()
-        wown.wait()
+            warrived(slot, part)
+    for part in range(2):
+        for copy in wfirst(part):
+            copy.wait_send()
+        wrelay(part).wait_send()
+        for slot in range(3):
+            wshare(slot, part).wait_send()
+    wown.wait()
     for part in range(PIECES):
         for index in range(len(plan)):
             plan_copy(index, part).wait_send()
@@ -332,52 +333,43 @@
         keep(slot).wait()
 
 
-def attend_call(total, queries, keyval, w, ident):
-    heads = queries.shape[0] // keyval.shape[0]
-    rows = keyval.shape[0]
+def attend_call(counts, source, w_query, w_keyval, w, ident):
+    heads = w_query.shape[1] // HEAD
+    rows = source.shape[0]
     keys = rows * 16
     vmem = pl.BlockSpec(memory_space=pltpu.VMEM)
-    anywhere = pl.BlockSpec(memory_space=pl.ANY)
-    out_shape = [
-        jax.ShapeDtypeStruct((rows, heads * HEAD), BF),
-        jax.ShapeDtypeStruct((2 * heads, HEAD), F32),
-        jax.ShapeDtypeStruct((keys, 2 * HEAD), BF),
-    ]
-    out_specs = [vmem, vmem, anywhere]
-    in_specs = [pl.BlockSpec(memory_space=pltpu.SMEM), vmem, vmem]
-    args = [total, queries, keyval]
-    scratch = [
-        pltpu.VMEM((keys, 3 * HEAD), BF),
-        pltpu.VMEM((heads * rows, 2 * HEAD), F32),
-        pltpu.SemaphoreType.DMA((15, PIECES)),
-        pltpu.SemaphoreType.DMA((15, PIECES)),
-        pltpu.SemaphoreType.DMA((17,)),
-    ]
-    if w is not None:
-        out_shape.append(jax.ShapeDtypeStruct((4,) + w.shape, BF))
-        out_specs.append(anywhere)
-        in_specs.append(anywhere)
-        args.append(w)
-        scratch += [
+    hbm = pl.BlockSpec(memory_space=pltpu.HBM)
+    return pl.pallas_call(
+        functools.partial(attend_kernel, heads),
+        out_shape=[
+            jax.ShapeDtypeStruct((rows, heads * HEAD), BF),
+            jax.ShapeDtypeStruct((2 * heads, HEAD), F32),
+            pltpu.HBM((keys, 2 * HEAD), BF),
+            pltpu.HBM((4,) + w.shape, BF),
+        ],
+        in_specs=[pl.BlockSpec(memory_space=pltpu.SMEM), vmem, vmem, vmem, hbm],
+        out_specs=[vmem, vmem, hbm, hbm],
+        scratch_shapes=[
+            pltpu.VMEM((keys, 3 * HEAD), BF),
+            pltpu.VMEM((heads * rows, 2 * HEAD), F32),
+            pltpu.VMEM((heads * rows, HEAD), BF),
+            pltpu.VMEM((rows, 2 * HEAD), BF),
+            pltpu.SemaphoreType.DMA((15, PIECES)),
+            pltpu.SemaphoreType.DMA((15, PIECES)),
+            pltpu.SemaphoreType.DMA((17,)),
             pltpu.SemaphoreType.DMA((6, 2)),
             pltpu.SemaphoreType.DMA((6, 2)),
             pltpu.SemaphoreType.DMA((1,)),
-        ]
-    return pl.pallas_call(
-        functools.partial(attend_kernel, heads, w is not None),
-        out_shape=out_shape,
-        in_specs=in_specs,
-        out_specs=out_specs,
-        scratch_shapes=scratch,
+        ],
         compiler_params=pltpu.CompilerParams(
-            collective_id=ident, has_side_effects=True, vmem_limit_bytes=48 * 2**20
+            collective_id=ident, has_side_effects=True, vmem_limit_bytes=40 * 2**20
         ),
         cost_estimate=pl.CostEstimate(
             flops=4 * heads * rows * keys * HEAD,
             bytes_accessed=keys * 4 * HEAD,
             transcendentals=heads * rows * keys,
         ),
-    )(*args)
+    )(counts, source, w_query, w_keyval, pltpu.with_memory_space_constraint(w, pltpu.HBM))
 
 
 def careful_kernel(total_ref, q_ref, kv_ref, out_ref, top, acc, total_sum):
@@ -418,7 +410,7 @@
 
 def careful_call(total, queries, kv_full, rows):
     heads = queries.shape[0] // rows
-    block = 512
+    block = 256
     return pl.pallas_call(
         careful_kernel,
         out_shape=jax.ShapeDtypeStruct((rows, heads * HEAD), BF),
@@ -430,20 +422,21 @@
         ],
         out_specs=pl.BlockSpec((rows, heads * HEAD), lambda i: (0, 0)),
         scratch_shapes=[pltpu.VMEM((heads * rows, HEAD), F32)] * 3,
-        compiler_params=pltpu.CompilerParams(vmem_limit_bytes=48 * 2**20),
+        compiler_params=pltpu.CompilerParams(vmem_limit_bytes=20 * 2**20),
     )(total, queries, kv_full)
 
 
-def attend(total, queries, keyval, w, ident):
-    results = attend_call(total, queries, keyval, w, ident)
-    plain, sums, kv_full = results[:3]
+def attend(counts, total, source, w_query, w_keyval, w, ident):
+    plain, sums, kv_full, w_full = attend_call(counts, source, w_query, w_keyval, w, ident)
     safe = jnp.all((sums > sum_low) & (sums < sum_high))
     attended = lax.cond(
         safe,
         lambda: plain,
-        lambda: careful_call(total, queries, kv_full, keyval.shape[0]),
-    )
-    return attended if w is None else (attended, results[3])
+        lambda: careful_call(
+            total, stacked_queries(source, w_query), kv_full, source.shape[0]
+        ),
+    )
+    return (attended, w_full)
 
 
 class YGather:
@@ -499,51 +492,6 @@
             item.wait_send()
         for part in range(2):
             self.relay(part).wait_send()
-
-
-def gather_kernel(x_ref, out_ref, send, recv, local):
-    rows, width = x_ref.shape
-    half = rows // 2
-
-    def place(source_y, part, slot):
-        return out_ref.at[
-            pl.ds(part * half, half), pl.ds(pl.multiple_of(source_y * width, HEAD), width)
-        ]
-
-    ring = YGather(lambda part: x_ref.at[pl.ds(part * half, half)], place, send, recv)
-    barrier = pltpu.get_barrier_semaphore()
-    pl.semaphore_wait(barrier, ring.greet(barrier))
-    ring.start()
-    mine = pltpu.make_async_copy(
-        x_ref, out_ref.at[:, pl.ds(pl.multiple_of(ring.ypos * width, HEAD), width)], local.at[0]
-    )
-    mine.start()
-    ring.pass_on(0)
-    ring.pass_on(1)
-    ring.arrived(0, 1)
-    ring.arrived(1, 0)
-    ring.arrived(2, 0)
-    ring.arrived(2, 1)
-    ring.wait_sent()
-    mine.wait()
-
-
-def gather_columns(x, ident):
-    vmem = pl.BlockSpec(memory_space=pltpu.VMEM)
-    return pl.pallas_call(
-        gather_kernel,
-        out_shape=jax.ShapeDtypeStruct((x.shape[0], 4 * x.shape[1]), x.dtype),
-        in_specs=[vmem],
-        out_specs=vmem,
-        scratch_shapes=[
-            pltpu.SemaphoreType.DMA((4, 2)),
-            pltpu.SemaphoreType.DMA((3, 2)),
-            pltpu.SemaphoreType.DMA((1,)),
-        ],
-        compiler_params=pltpu.CompilerParams(
-            collective_id=ident, has_side_effects=True, vmem_limit_bytes=8 * 2**20
-        ),
-    )(x)
 
 
 class Geometry:
@@ -579,15 +527,16 @@
             return (0, index * columns)
         return ((index // 2) * rows, lax.rem(index, 2) * columns)
 
-    def scratch(self):
+    def scatter_scratch(self):
         vmem = pltpu.VMEM
-        shapes = [vmem(self.half, BF)] * 3
-        for part in range(2):
-            shapes.append(vmem((3,) + self.quarter_shape[part], BF))
-            shapes.append(vmem(self.quarter_shape[part], BF))
-            shapes.append(vmem((3,) + self.sub_shape[part], BF))
+        return [vmem(self.half, BF)] * 3 + [vmem((3,) + q, BF) for q in self.quarter_shape]
+
+    def sub_scratch(self):
+        return [pltpu.VMEM((3,) + sub, BF) for sub in self.sub_shape]
+
+    def semaphores(self):
         dma = pltpu.SemaphoreType.DMA
-        return shapes + [dma((4, 2, 3)), dma((4, 2, 3)), dma((9,)), dma((9,))]
+        return [dma((4, 2, 3)), dma((4, 2, 3)), dma((9,)), dma((9,))]
 
 
 def box(start, shape):
@@ -605,14 +554,15 @@
 class Reduce:
     hops = (2, 1, 3)
 
-    def __init__(self, shape, att_ref, d_ref, out_ref, scratch):
+    def __init__(self, shape, att_ref, d_ref, out_ref, scatter, sums, sub_in, semaphores):
         self.g = shape
         self.att, self.d, self.out = att_ref, d_ref, out_ref
-        self.theirs, self.mine, self.got = scratch[:3]
-        self.part_in = [scratch[3], scratch[6]]
-        self.part_sum = [scratch[4], scratch[7]]
-        self.sub_in = [scratch[5], scratch[8]]
-        self.send, self.recv, self.csend, self.crecv = scratch[9:13]
+        if scatter is not None:
+            self.theirs, self.mine, self.got = scatter[:3]
+            self.part_in = scatter[3:5]
+        self.part_sum = sums
+        self.sub_in = sub_in
+        self.send, self.recv, self.csend, self.crecv = semaphores
         me = lax.axis_index("rep")
         self.me = me
         self.core = lax.rem(me, 2)
@@ -733,7 +683,7 @@
             for part in range(2):
                 self.scatter_one(part, k).start()
 
-    def second_scatter(self):
+    def first_sums(self):
         for part in range(2):
             start = self.g.quarter(part, self.first[part])
             total = self.mine[box(start, self.g.quarter_shape[part])].astype(F32)
@@ -741,7 +691,10 @@
                 self.scatter_one(part, k).wait_recv()
                 total += self.part_in[part][k - 1].astype(F32)
             self.part_sum[part][...] = total.astype(BF)
-            for k in self.hops:
+
+    def second_scatter(self):
+        for k in self.hops:
+            for part in range(2):
                 self.scatter_two(part, k).start()
 
     def first_gather(self):
@@ -769,14 +722,18 @@
                 self.gather_one(part, k).wait_recv()
                 self.share(part, k, self.core).start()
 
+    def finish_scatter(self):
+        self.swap().wait_send()
+        for part in range(2):
+            for k in range(1, 4):
+                self.scatter_one(part, k).wait_send()
+
     def finish(self):
         for part in range(2):
             for k in range(4):
                 self.share(part, k, 1 - self.core).wait_recv()
-        self.swap().wait_send()
         for part in range(2):
             for k in range(1, 4):
-                self.scatter_one(part, k).wait_send()
                 self.scatter_two(part, k).wait_send()
                 self.gather_two(part, k).wait_send()
                 self.gather_one(part, k).wait_send()
@@ -785,16 +742,20 @@
 
 
 def reduce_kernel(shape, att_ref, d_ref, out_ref, *scratch):
-    work = Reduce(shape, att_ref, d_ref, out_ref, scratch)
+    work = Reduce(
+        shape, att_ref, d_ref, out_ref, scratch[:5], scratch[5:7], scratch[7:9], scratch[9:13]
+    )
     barrier = pltpu.get_barrier_semaphore()
     expected = work.greet(barrier)
     work.begin()
     pl.semaphore_wait(barrier, expected)
     work.swap_and_scatter()
+    work.first_sums()
     work.second_scatter()
     work.first_gather()
     work.second_gather()
     work.last_shares()
+    work.finish_scatter()
     work.finish()
 
 
@@ -806,20 +767,87 @@
         out_shape=jax.ShapeDtypeStruct((shape.rows, shape.columns), BF),
         in_specs=[vmem, vmem],
         out_specs=vmem,
-        scratch_shapes=shape.scratch(),
+        scratch_shapes=shape.scatter_scratch()
+        + [pltpu.VMEM(q, BF) for q in shape.quarter_shape]
+        + shape.sub_scratch()
+        + shape.semaphores(),
         compiler_params=pltpu.CompilerParams(
             collective_id=ident, has_side_effects=True, vmem_limit_bytes=24 * 2**20
         ),
     )(attended, grad_in)
 
 
-def output_kernel(shape, x_ref, w_ref, base_ref, *refs):
+def policy_kernel(
+    shape, x_ref, cin_ref, wp_ref, side_ref, att_ref, out_ref, sum_a, sum_b, part_ref, d_ref, *refs
+):
+    scatter, semaphores, (send, recv, local) = refs[:5], refs[5:9], refs[9:]
+    work = Reduce(shape, att_ref, d_ref, None, scatter, (sum_a, sum_b), None, semaphores)
+    rows, width = part_ref.shape
+    half = rows // 2
+
+    def place(source_y, part, slot):
+        return out_ref.at[
+            pl.ds(part * half, half), pl.ds(pl.multiple_of(source_y * width, HEAD), width)
+        ]
+
+    ring = YGather(lambda part: part_ref.at[pl.ds(part * half, half)], place, send, recv)
+    barrier = pltpu.get_barrier_semaphore()
+    expected = ring.greet(barrier) + work.greet(barrier)
+    part_ref[...] = jnp.dot(x_ref[...], cin_ref[...], preferred_element_type=F32).astype(BF)
+    pl.semaphore_wait(barrier, expected)
+    ring.start()
+    mine = pltpu.make_async_copy(
+        part_ref, out_ref.at[:, pl.ds(pl.multiple_of(ring.ypos * width, HEAD), width)], local.at[0]
+    )
+    mine.start()
+    d_ref[...] = policy_backward(x_ref[...], side_ref[...], wp_ref[...]).astype(BF)
+    ring.pass_on(0)
+    ring.pass_on(1)
+    work.begin()
+    work.swap_and_scatter()
+    ring.arrived(0, 1)
+    ring.arrived(1, 0)
+    work.first_sums()
+    ring.arrived(2, 0)
+    ring.arrived(2, 1)
+    work.finish_scatter()
+    ring.wait_sent()
+    mine.wait()
+
+
+def policy_call(hidden, c_in, w_policy, side, attended, ident):
+    rows = hidden.shape[0]
+    width = c_in.shape[1]
+    shape = Geometry(attended.shape[1], hidden.shape[1], False)
+    vmem = pl.BlockSpec(memory_space=pltpu.VMEM)
+    return pl.pallas_call(
+        functools.partial(policy_kernel, shape),
+        out_shape=[jax.ShapeDtypeStruct((rows, 4 * width), BF)]
+        + [jax.ShapeDtypeStruct(q, BF) for q in shape.quarter_shape],
+        in_specs=[vmem] * 5,
+        out_specs=[vmem] * 3,
+        scratch_shapes=[pltpu.VMEM((rows, width), BF), pltpu.VMEM(hidden.shape, BF)]
+        + shape.scatter_scratch()
+        + shape.semaphores()
+        + [
+            pltpu.SemaphoreType.DMA((4, 2)),
+            pltpu.SemaphoreType.DMA((3, 2)),
+            pltpu.SemaphoreType.DMA((1,)),
+        ],
+        compiler_params=pltpu.CompilerParams(
+            collective_id=ident, has_side_effects=True, vmem_limit_bytes=32 * 2**20
+        ),
+    )(hidden, c_in, w_policy, side, attended)
+
+
+def output_kernel(shape, x_ref, w_hbm, base_ref, *refs):
+    *refs, w_ref, loaded = refs
     if shape is None:
         out_ref, acc, blocks, send, recv = refs
         work = None
     else:
-        att_ref, d_ref, out_ref, grad_ref, acc, blocks, send, recv = refs[:8]
-        work = Reduce(shape, att_ref, d_ref, grad_ref, refs[8:])
+        sum_a, sum_b, out_ref, grad_ref, acc, blocks, send, recv = refs[:8]
+        work = Reduce(shape, None, None, grad_ref, None, (sum_a, sum_b), refs[8:10], refs[10:14])
     rows = x_ref.shape[0]
     half = rows // 2
     ring = YGather(
@@ -828,6 +856,12 @@
         send,
         recv,
     )
+    loads = [
+        pltpu.make_async_copy(w_hbm.at[there], w_ref.at[there], loaded.at[k])
+        for k, there in enumerate((ring.ypos, ring.ym, ring.yp, ring.y2))
+    ]
+    for load in loads:
+        load.start()
     barrier = pltpu.get_barrier_semaphore()
     expected = ring.greet(barrier)
     if work is not None:
@@ -835,8 +869,9 @@
     pl.semaphore_wait(barrier, expected)
     ring.start()
     if work is not None:
-        work.begin()
-        work.swap_and_scatter()
+        work.second_scatter()
+    for load in loads:
+        load.wait()
     acc[...] = base_ref[...].astype(F32) + jnp.dot(
         x_ref[...], w_ref[ring.ypos], preferred_element_type=F32
     )
@@ -848,36 +883,35 @@
             blocks[slot, span, :], w_ref[source_y], preferred_element_type=F32
         )
 
+    if work is not None:
+        work.first_gather()
     ring.pass_on(0)
     ring.pass_on(1)
     add(0, 0)
     add(1, 1)
     if work is not None:
-        work.second_scatter()
+        work.second_gather()
     ring.arrived(0, 1)
     add(0, 1)
-    if work is not None:
-        work.first_gather()
     ring.arrived(1, 0)
     add(1, 0)
     if work is not None:
-        work.second_gather()
+        work.last_shares()
     ring.arrived(2, 0)
     add(2, 0)
     ring.arrived(2, 1)
     add(2, 1)
     out_ref[...] = acc[...].astype(out_ref.dtype)
     if work is not None:
-        work.last_shares()
         work.finish()
     ring.wait_sent()
 
 
-def output_call(x, w_full, base, out_type, grads, ident):
+def output_call(x, w_full, base, out_type, shape, sums, ident):
     rows, width = x.shape
     columns = w_full.shape[2]
     vmem = pl.BlockSpec(memory_space=pltpu.VMEM)
-    args = [x, w_full, base]
+    args = [x, pltpu.with_memory_space_constraint(w_full, pltpu.HBM), base]
     out_shape = [jax.ShapeDtypeStruct((rows, columns), out_type)]
     scratch = [
         pltpu.VMEM((rows, columns), F32),
@@ -885,37 +919,31 @@
         pltpu.SemaphoreType.DMA((4, 2)),
         pltpu.SemaphoreType.DMA((3, 2)),
     ]
-    shape = None
-    if grads is not None:
-        shape = Geometry(grads[0].shape[1], grads[1].shape[1], False)
-        args += list(grads)
+    if shape is not None:
+        args += list(sums)
         out_shape.append(jax.ShapeDtypeStruct((shape.rows, shape.columns), BF))
-        scratch += shape.scratch()
+        scratch += shape.sub_scratch() + shape.semaphores()
+    scratch += [pltpu.VMEM(w_full.shape, BF), pltpu.SemaphoreType.DMA((4,))]
     return pl.pallas_call(
         functools.partial(output_kernel, shape),
         out_shape=out_shape,
-        in_specs=[vmem] * len(args),
+        in_specs=[vmem, pl.BlockSpec(memory_space=pltpu.HBM)] + [vmem] * (len(args) - 2),
         out_specs=[vmem] * len(out_shape),
         scratch_shapes=scratch,
         compiler_params=pltpu.CompilerParams(
-            collective_id=ident, has_side_effects=True, vmem_limit_bytes=48 * 2**20
+            collective_id=ident, has_side_effects=True, vmem_limit_bytes=40 * 2**20
         ),
     )(*args)
 
 
-def project(source, w_query, w_keyval, live_mask):
+def stacked_queries(source, w_query):
     rows = source.shape[0]
-    normed = rms_normed(source).astype(BF)
+    normed = rms_normed(source.astype(F32)).astype(BF)
     queries = (
         jnp.dot(normed, w_query, preferred_element_type=F32) * (HEAD ** (-0.5) * LOG2E)
     ).astype(BF)
     heads = queries.shape[1] // HEAD
-    stacked = jnp.transpose(queries.reshape(rows, heads, HEAD), (1, 0, 2)).reshape(
-        heads * rows, HEAD
-    )
-    keyval = [jnp.dot(normed, w_keyval[part], preferred_element_type=F32) for part in range(2)]
-    joined = jnp.where(live_mask[:, None], jnp.concatenate(keyval, axis=1), 0.0).astype(BF)
-    return (stacked, joined)
+    return jnp.transpose(queries.reshape(rows, heads, HEAD), (1, 0, 2)).reshape(heads * rows, HEAD)
 
 
 def on_device(
@@ -945,22 +973,24 @@
     mdl_count = lax.axis_size("mdl")
     part_rows = row_count // mdl_count
     row_start = lax.axis_index("mdl") * part_rows
-    obs_float = obs[0].astype(F32)
-
-    queries, keyval = project(obs_float, a_query, a_keyval, live_mask)
-    attended, a_out_full = attend(total, queries, keyval, a_out, 1)
-    (hidden,) = output_call(attended, a_out_full, obs[0], BF, None, 3)
-    embed_part = jnp.dot(hidden, c_in, preferred_element_type=F32).astype(BF)
-    embedded = gather_columns(embed_part, 4)
-    dhidden = policy_backward(
-        hidden, actions[0], advantages[0], old_logp[0], live_mask, live_total, w_policy
-    ).astype(BF)
-    embed_float = embedded.astype(F32)
-    critic_queries, critic_keyval = project(embed_float, c_query, c_keyval, live_mask)
-    critic_attended, c_out_full = attend(total, critic_queries, critic_keyval, c_out, 2)
-    mixed, actor_summed = output_call(
-        critic_attended, c_out_full, embedded, F32, (attended, dhidden), 5
-    )
+    side = jnp.stack(
+        [
+            actions[0].astype(F32),
+            advantages[0],
+            old_logp[0],
+            jnp.where(live_mask, 1.0 / live_total, 0.0),
+        ],
+        axis=1,
+    )
+
+    attended, a_out_full = attend(robot_count, total, obs[0], a_query, a_keyval, a_out, 1)
+    (hidden,) = output_call(attended, a_out_full, obs[0], BF, None, None, 3)
+    embedded, *sums = policy_call(hidden, c_in, w_policy, side, attended, 4)
+    critic_attended, c_out_full = attend(
+        robot_count, total, embedded, c_query, c_keyval, c_out, 2
+    )
+    shape = Geometry(attended.shape[1], hidden.shape[1], False)
+    mixed, actor_summed = output_call(critic_attended, c_out_full, embedded, F32, shape, sums, 5)
     value_pred, dmixed = value_backward(mixed, returns[0], live_mask, live_total, w_value)
     value_part = lax.dynamic_slice_in_dim(value_pred, row_start, part_rows, 0)
     critic_summed = reduced_grad(critic_attended, dmixed.astype(BF), 6).astype(F32)

time: 355 us -> 473 us (1.33)
  Pallas kernels: 301 us -> 425 us
  loops' own time: 0.69 us -> 13.7 us
  matrix products: 12.1 us -> 4.59 us
  local copies, waits for them, and re-layouts: 13.8 us -> 7.03 us
  other arithmetic: 17.5 us -> 11.9 us
    pallas_call x2, Pallas kernels: 114 us -> 216 us  [careful_call(): pl.pallas_call(careful_kernel, out_shape=jax.ShapeDtypeStruct((rows, head...]
    pallas_call x3, Pallas kernels: 103 us -> 136 us  [the longest x2 112 us: attend_call(): pl.pallas_call(functools.partial(attend_kernel, heads), out_shape=[jax.Sh...]
    another operation x2, loops' own time: 0.69 us -> 13.7 us  [attend(): lax.cond(safe, lambda: plain, lambda: careful_call(total, stacked_queries...]
    pallas_call x2, Pallas kernels: 53.3 us -> 42 us  [output_call(): pl.pallas_call(functools.partial(output_kernel, shape), out_shape=out_sha...]
    dot_general x9 -> x2, matrix products: 11.4 us -> 3.88 us  [stacked_queries(): jnp.dot(normed, w_query, preferred_element_type=F32)]
    unnamed x47 -> x37, local copies, waits for them, and re-layouts: 9.62 us -> 4.57 us
where the time goes in v4:
time: 473 us; the launch traced here: 466 us
  Pallas kernels  425 us (90%)
  loops' own time  13.7 us (3%)
  other arithmetic  11.9 us (3%)
  local copies, waits for them, and re-layouts  7.03 us (1%)
    pallas_call x2, Pallas kernels, careful_call(): pl.pallas_call(careful_kernel, out_shape=jax.ShapeDtypeStruct((rows, head...  216 us
    pallas_call x2, Pallas kernels, attend_call(): pl.pallas_call(functools.partial(attend_kernel, heads), out_shape=[jax.Sh...  112 us
    pallas_call x2, Pallas kernels, output_call(): pl.pallas_call(functools.partial(output_kernel, shape), out_shape=out_sha...  42 us
    pallas_call x1, Pallas kernels, reduced_grad(): pl.pallas_call(functools.partial(reduce_kernel, shape), out_shape=jax.Sha...  31.7 us
    pallas_call x1, Pallas kernels, policy_call(): pl.pallas_call(functools.partial(policy_kernel, shape), out_shape=[jax.Sh...  23.8 us
    another operation x2, loops' own time, attend(): lax.cond(safe, lambda: plain, lambda: careful_call(total, stacked_queries...  13.7 us

profile of v4, /device:TPU:1, one launch (start us, length us, event | category | flops | bytes accessed | tf_op | source)
XLA Modules:
  0.0 465.9 jit_solution(14582463377507869929)
XLA Ops:
  0.6 1.2 dynamic_slice.6
  1.9 1.1 copy-done.3
  3.0 0.0 copy-start.4
  3.0 0.7 copy-done.4
  3.7 0.0 copy-start.8
  3.7 0.0 copy-start.17
  3.7 44.4 %shard_map.166 = (bf16[512,384]{1,0:T(8,128)(2,1)S(1)}, f32[6,128]{1,0:T(8,128)S(1)}, bf16[8192,256]{1,0:T(8,128)(2,1)}, bf16[4,384,1536]{2,1,0:T(8,128)(2,1)}) custom-call(s32[2]{0:T(128)S(1)} %copy-done.4, bf16[512,1536]{1,0:T(8,128)(2,1)} %bitcast.23, bf16[1536,384]{1,0:T(8,128)(2,1)} %wq_ref.2, bf16[2,1536,128]{2,1,0:T(8,128)(2,1)S(1)} %copy-done.3, ...), custom_call_target="tpu_custom_call" | custom-call | flops 6442450944 | bytes 4194304 | tf_op jit(solution)/shard_map/pallas_call | solution.py:342
  48.1 0.6 and_reduce_fusion.1
  49.4 0.0 copy-done.8
  49.4 0.0 copy-done.17
  49.4 107.1 %conditional.2 = (bf16[512,384]{1,0:T(8,128)(2,1)S(1)}) conditional(s32[]{:T(128)} %convert_element_type.55, (bf16[512,1536]{1,0:T(8,128)(2,1)S(1)}, bf16[1536,384]{1,0:T(8,128)(2,1)S(1)}, s32[1]{0:T(128)}, bf16[8192,256]{1,0:T(8,128)(2,1)}) %tuple.30, bf16[512,384]{1,0:T(8,128)(2,1)S(1)} %get-tuple-element.50), branch_computations={%region_1.0_spmd, %region_3.0_spmd} | conditional | flops 609092096 | bytes 5513224 | solution.py:432
  49.4 0.4 fusion
  49.8 0.9 fusion.8
  50.7 0.2 copy.25
  50.9 92.2 %branch_0_fun.2 = bf16[512,384]{1,0:T(8,128)(2,1)S(1)} custom-call(s32[1]{0:T(128)} %get-tuple-element.24.total_ref, bf16[1536,128]{1,0:T(8,128)(2,1)S(1)} %bitcast.22, bf16[8192,256]{1,0:T(8,128)(2,1)} %get-tuple-element.27.kv_ref), custom_call_target="tpu_custom_call" | custom-call | tf_op jit(solution)/shard_map/cond/branch_0_fun/pallas_call | solution.py:414
  156.5 0.0 copy-start.9
  156.5 0.7 copy-done.9
  157.3 0.0 copy-start.5
  157.3 0.0 copy-start.11
  157.3 0.0 copy-start.13
  157.3 0.0 copy-start.14
  157.3 0.0 copy-start
  157.3 18.7 %shard_map.167.x_ref = bf16[512,1536]{1,0:T(8,128)(2,1)S(1)} custom-call(bf16[512,384]{1,0:T(8,128)(2,1)} %copy-done.9, bf16[4,384,1536]{2,1,0:T(8,128)(2,1)} %get-tuple-element.51.w_hbm, bf16[512,1536]{1,0:T(8,128)(2,1)} %bitcast.24), custom_call_target="tpu_custom_call" | custom-call | tf_op jit(solution)/shard_map/pallas_call | solution.py:927
  176.0 0.0 copy-done.5
  176.0 0.6 reduce_sum.49
  177.3 0.7 compare_select_fusion
  178.0 0.0 copy-done.11
  178.0 0.0 copy-done.13
  178.0 0.0 copy-done.14
  178.0 0.1 copy.27.side_ref
  178.2 0.0 copy-done
  178.2 0.0 copy-start.1
  178.2 1.0 copy-done.1
  179.2 0.0 copy-start.2
  179.2 0.0 copy-start.15
  179.2 23.8 %shard_map.168 = (bf16[512,2048]{1,0:T(8,128)(2,1)S(1)}, bf16[96,512]{1,0:T(8,128)(2,1)S(1)}, bf16[96,256]{1,0:T(8,128)(2,1)S(1)}) custom-call(bf16[512,1536]{1,0:T(8,128)(2,1)S(1)} %shard_map.167.x_ref, bf16[1536,512]{1,0:T(8,128)(2,1)S(1)} %copy-done, bf16[1536,128]{1,0:T(8,128)(2,1)S(1)} %copy-done.1, f32[512,4]{1,0:T(8,128)S(1)} %copy.27.side_ref, ...), custom_call_target="tpu_custom_call" | custom-call | tf_op jit(solution)/shard_map/pallas_call | solution.py:823
  203.0 0.0 copy-start.7
  203.1 0.0 copy-done.2
  203.1 0.0 copy-done.15
  203.1 0.0 copy-start.6
  203.1 0.7 copy-done.6
  203.8 0.0 copy-start.16
  203.8 68.0 %shard_map.169 = (bf16[512,512]{1,0:T(8,128)(2,1)S(1)}, f32[8,128]{1,0:T(8,128)S(1)}, bf16[8192,256]{1,0:T(8,128)(2,1)}, bf16[4,512,2048]{2,1,0:T(8,128)(2,1)}) custom-call(s32[2]{0:T(128)S(1)} %copy-done.6, bf16[512,2048]{1,0:T(8,128)(2,1)S(1)} %get-tuple-element.52.x_ref.base_ref, bf16[2048,512]{1,0:T(8,128)(2,1)S(1)} %copy-done.15, ...), custom_call_target="tpu_custom_call" | custom-call | flops 8589934592 | bytes 4194304 | tf_op jit(solution)/shard_map/pallas_call | solution.py:342
  271.7 0.0 copy-done.7
  271.8 0.6 and_reduce_fusion
  273.0 0.0 copy-done.16
  273.0 129.0 %conditional.3 = (bf16[512,512]{1,0:T(8,128)(2,1)S(1)}) conditional(s32[]{:T(128)} %convert_element_type.59, (bf16[512,2048]{1,0:T(8,128)(2,1)}, bf16[2048,512]{1,0:T(8,128)(2,1)S(1)}, s32[1]{0:T(128)}, bf16[8192,256]{1,0:T(8,128)(2,1)}) %tuple.29, bf16[512,512]{1,0:T(8,128)(2,1)S(1)} %get-tuple-element.55), branch_computations={%region_6.8_spmd, %region_8.9_spmd} | conditional | flops 1080558080 | bytes 7872520 | solution.py:432
  273.1 2.1 fusion.11
  275.1 3.0 fusion.19
  278.1 0.3 copy.26
  278.4 123.4 %branch_0_fun.3 = bf16[512,512]{1,0:T(8,128)(2,1)S(1)} custom-call(s32[1]{0:T(128)} %get-tuple-element.28.total_ref, bf16[2048,128]{1,0:T(8,128)(2,1)S(1)} %bitcast.21, bf16[8192,256]{1,0:T(8,128)(2,1)} %get-tuple-element.31.kv_ref), custom_call_target="tpu_custom_call" | custom-call | tf_op jit(solution)/shard_map/cond/branch_0_fun/pallas_call | solution.py:414
  402.0 23.3 %shard_map.170 = (f32[512,2048]{1,0:T(8,128)S(1)}, bf16[384,1536]{1,0:T(8,128)(2,1)S(1)}) custom-call(bf16[512,512]{1,0:T(8,128)(2,1)S(1)} %get-tuple-element.62.x_ref.att_ref, bf16[4,512,2048]{2,1,0:T(8,128)(2,1)} %get-tuple-element.56.w_hbm, bf16[512,2048]{1,0:T(8,128)(2,1)} %copy-done.7, bf16[96,512]{1,0:T(8,128)(2,1)S(1)} %get-tuple-element.57.refs_0_, ...), custom_call_target="tpu_custom_call" | custom-call | tf_op jit(solution)/shard_map/pallas_call | solution.py:927
  425.4 0.0 copy-start.10
  425.4 0.3 multiply_reduce_fusion
  425.8 0.3 copy-done.10
  426.1 0.7 fusion.25
  426.8 0.0 copy-done.12
  426.8 0.7 select_divide_fusion
  427.5 0.7 fusion.22
  428.2 0.8 fusion.24.d_ref
  429.0 31.7 %shard_map.171 = bf16[512,2048]{1,0:T(8,128)(2,1)S(1)} custom-call(bf16[512,512]{1,0:T(8,128)(2,1)S(1)} %get-tuple-element.62.x_ref.att_ref, bf16[512,2048]{1,0:T(8,128)(2,1)S(1)} %fusion.24.d_ref), custom_call_target="tpu_custom_call" | custom-call | tf_op jit(solution)/shard_map/pallas_call | solution.py:765
  460.7 2.5 convert_element_type.64
  463.3 1.7 convert_element_type.61
  465.0 0.6 dynamic-slice_bitcast_fusion
  (10 shorter events, 0.1 us)
Async XLA Ops:
  1.9 1.1 copy-start.3
  3.0 0.7 copy-start.4
  3.7 45.7 %copy-start.8 = (bf16[1,512,1536]{2,1,0:T(8,128)(2,1)S(1)}, bf16[1,512,1536]{2,1,0:T(8,128)(2,1)}, u32[]{:S(2)}) copy-start(bf16[1,512,1536]{2,1,0:T(8,128)(2,1)} %param.19) | copy-start | bytes 4718596
  3.7 45.7 %copy-start.17 = (bf16[1536,384]{1,0:T(8,128)(2,1)S(1)}, bf16[1536,384]{1,0:T(8,128)(2,1)}, u32[]{:S(2)}) copy-start(bf16[1536,384]{1,0:T(8,128)(2,1)} %wq_ref.2) | copy-start | bytes 3538948
  156.5 0.7 copy-start.9
  157.3 18.7 %copy-start.5 = (s32[2]{0:T(128)S(1)}, s32[2]{0:T(128)}, u32[]{:S(2)}) copy-start(s32[2]{0:T(128)} %count_ref.3) | copy-start | bytes 28
  157.3 20.7 %copy-start.11 = (s32[1,512]{1,0:T(1,128)S(1)}, s32[1,512]{1,0:T(1,128)}, u32[]{:S(2)}) copy-start(s32[1,512]{1,0:T(1,128)} %param.29) | copy-start | bytes 6148
  157.3 20.7 %copy-start.13 = (f32[1,512]{1,0:T(1,128)S(1)}, f32[1,512]{1,0:T(1,128)}, u32[]{:S(2)}) copy-start(f32[1,512]{1,0:T(1,128)} %param.31) | copy-start | bytes 6148
  157.3 20.7 %copy-start.14 = (f32[1,512]{1,0:T(1,128)S(1)}, f32[1,512]{1,0:T(1,128)}, u32[]{:S(2)}) copy-start(f32[1,512]{1,0:T(1,128)} %param.30) | copy-start | bytes 6148
  157.3 20.9 %copy-start = (bf16[1536,512]{1,0:T(8,128)(2,1)S(1)}, bf16[1536,512]{1,0:T(8,128)(2,1)}, u32[]{:S(2)}) copy-start(bf16[1536,512]{1,0:T(8,128)(2,1)} %cin_ref.1) | copy-start | bytes 4718596
  178.2 1.0 copy-start.1
  179.2 23.9 %copy-start.2 = (bf16[2,2048,128]{2,1,0:T(8,128)(2,1)S(1)}, bf16[2,2048,128]{2,1,0:T(8,128)(2,1)}, u32[]{:S(2)}) copy-start(bf16[2,2048,128]{2,1,0:T(8,128)(2,1)} %wkv_ref.3) | copy-start | bytes 3145732
  179.2 23.9 %copy-start.15 = (bf16[2048,512]{1,0:T(8,128)(2,1)S(1)}, bf16[2048,512]{1,0:T(8,128)(2,1)}, u32[]{:S(2)}) copy-start(bf16[2048,512]{1,0:T(8,128)(2,1)} %wq_ref.3) | copy-start | bytes 6291460
  203.0 68.7 %copy-start.7 = (bf16[512,2048]{1,0:T(8,128)(2,1)}, bf16[512,2048]{1,0:T(8,128)(2,1)S(1)}, u32[]{:S(2)}) copy-start(bf16[512,2048]{1,0:T(8,128)(2,1)S(1)} %get-tuple-element.52.x_ref.base_ref) | copy-start | bytes 6291460
  203.1 0.7 copy-start.6
  203.8 69.3 %copy-start.16 = (bf16[2048,512]{1,0:T(8,128)(2,1)S(1)}, bf16[2048,512]{1,0:T(8,128)(2,1)}, u32[]{:S(2)}) copy-start(bf16[2048,512]{1,0:T(8,128)(2,1)} %wq_ref.3) | copy-start | bytes 6291460
  425.4 0.7 copy-start.10
  425.7 1.0 copy-start.12

commit v5 on v4

--- a/solution.py
+++ b/solution.py
@@ -24,20 +24,14 @@
     return values_in * lax.rsqrt(jnp.mean(values_in * values_in, axis=-1, keepdims=True) + epsilon)
 
 
-def norm_backward(source, normed, grad_in):
-    factor = lax.rsqrt(jnp.mean(source * source, axis=-1, keepdims=True) + epsilon)
-    return factor * (grad_in - normed * jnp.mean(grad_in * normed, axis=-1, keepdims=True))
-
-
-def policy_backward(hidden, side, w_policy):
+def policy_backward(hidden, action, advantage, old_values, scale, w_policy):
     source = hidden.astype(F32)
     factor = lax.rsqrt(jnp.mean(source * source, axis=-1, keepdims=True) + epsilon)
     normed = source * factor
     logits = jnp.dot(normed.astype(BF), w_policy, preferred_element_type=F32)
     shifted = logits - jnp.max(logits, axis=-1, keepdims=True)
     log_probs = shifted - jnp.log(jnp.sum(jnp.exp(shifted), axis=-1, keepdims=True))
-    action, advantage, old_values, scale = (side[:, k : k + 1] for k in range(4))
-    command = lax.broadcasted_iota(jnp.int32, logits.shape, 1).astype(F32)
+    command = lax.broadcasted_iota(jnp.int32, logits.shape, 1)
     onehot = (action == command).astype(F32)
     chosen = jnp.sum(onehot * log_probs, axis=-1, keepdims=True)
     prob_ratio = jnp.exp(chosen - old_values)
@@ -51,19 +45,33 @@
     return factor * (dnormed - normed * jnp.mean(dnormed * normed, axis=-1, keepdims=True))
 
 
-def value_backward(mixed_out, target, live_mask, live_total, w_value):
-    normed = rms_normed(mixed_out)
-    value_pred = jnp.dot(normed.astype(BF), w_value, preferred_element_type=F32)
-    slope_term = jnp.where(live_mask, value_pred - target, jnp.float32(0.0)) / live_total
-    dnormed = slope_term[:, None] * w_value.astype(F32)[None, :]
-    return (value_pred, norm_backward(mixed_out, normed, dnormed))
+def value_backward(mixed_out, target, scale, w_value):
+    factor = lax.rsqrt(jnp.mean(mixed_out * mixed_out, axis=-1, keepdims=True) + epsilon)
+    normed = mixed_out * factor
+    weight = w_value.astype(F32)
+    value_pred = jnp.sum(normed.astype(BF).astype(F32) * weight, axis=-1, keepdims=True)
+    slope_term = jnp.where(scale > 0.0, (value_pred - target) * scale, 0.0)
+    dnormed = slope_term * weight
+    inner = jnp.mean(dnormed * normed, axis=-1, keepdims=True)
+    return (value_pred, (factor * (dnormed - normed * inner)).astype(BF))
+
+
+def standing(row):
+    return jnp.transpose(jnp.broadcast_to(row, (HEAD, row.shape[1])))
+
+
+def live_scale(count_ref, rows):
+    total = count_ref[lax.axis_index("sec")]
+    both = jnp.full((rows, 1), count_ref[0] + count_ref[1], jnp.int32).astype(F32)
+    index = lax.axis_index("rep") * rows + lax.broadcasted_iota(jnp.int32, (rows, 1), 0)
+    return jnp.where(index < total, 1.0 / both, 0.0)
 
 
 PIECES = 2
 
 
 def attend_kernel(
-    heads, count_ref, x_ref, wq_ref, wkv_ref, w_ref, out_ref, sums_ref, kvout_ref, wfull_ref, *refs
+    heads, count_ref, x_ref, wq_ref, wkv_ref, w_ref, out_ref, wfull_ref, *refs
 ):
     buf, acc, q_ref, kv_ref, send, recv, local, wsend, wrecv, wlocal = refs
     rows = x_ref.shape[0]
@@ -149,25 +157,16 @@
         where = buf.at[block_rows(src[slot], part), pl.ds(0, 2 * HEAD)]
         pltpu.make_async_copy(where, where, recv.at[slot, part]).wait()
 
-    def keep(slot):
-        block = me if slot is None else src[slot]
-        where = pl.ds(pl.multiple_of(block * rows, rows), rows)
-        index = 15 if slot is None else slot
-        source = kv_ref if slot is None else buf.at[where, pl.ds(0, 2 * HEAD)]
-        return pltpu.make_async_copy(source, kvout_ref.at[where], local.at[index])
-
     def pass_on(slot):
         for part in range(PIECES):
             arrived(slot, part)
             for index, (from_slot, _, _) in enumerate(plan):
                 if from_slot == slot:
                     plan_copy(index, part).start()
-        keep(slot).start()
 
     def take(slot):
         for part in range(PIECES):
             arrived(slot, part)
-        keep(slot).start()
 
     for part in range(PIECES):
         for index in range(4):
@@ -175,10 +174,9 @@
     own_copy = pltpu.make_async_copy(
         kv_ref,
         buf.at[pl.ds(pl.multiple_of(me * rows, rows), rows), pl.ds(0, 2 * HEAD)],
-        local.at[16],
+        local.at[0],
     )
     own_copy.start()
-    keep(None).start()
 
     wrows = w_ref.shape[0]
     wpiece = wrows // 4
@@ -309,11 +307,10 @@
     for head in range(heads):
         part = acc[head * rows : (head + 1) * rows, :]
         sums = part[:, HEAD:]
-        out_ref[:, head * HEAD : (head + 1) * HEAD] = (part[:, :HEAD] / sums).astype(BF)
-        low = jnp.min(sums, axis=0, keepdims=True)
-        high = jnp.max(sums, axis=0, keepdims=True)
-        sums_ref[2 * head : 2 * head + 1, :] = low
-        sums_ref[2 * head + 1 : 2 * head + 2, :] = high
+        safe = (sums > sum_low) & (sums < sum_high)
+        out_ref[:, head * HEAD : (head + 1) * HEAD] = jnp.where(
+            safe, part[:, :HEAD] / sums, jnp.nan
+        ).astype(BF)
 
     for slot in range(3, 6):
         for part in range(2):
@@ -328,9 +325,6 @@
     for part in range(PIECES):
         for index in range(len(plan)):
             plan_copy(index, part).wait_send()
-    keep(None).wait()
-    for slot in range(15):
-        keep(slot).wait()
 
 
 def attend_call(counts, source, w_query, w_keyval, w, ident):
@@ -338,17 +332,15 @@
     rows = source.shape[0]
     keys = rows * 16
     vmem = pl.BlockSpec(memory_space=pltpu.VMEM)
-    hbm = pl.BlockSpec(memory_space=pltpu.HBM)
+    anywhere = pl.BlockSpec(memory_space=pl.ANY)
     return pl.pallas_call(
         functools.partial(attend_kernel, heads),
         out_shape=[
             jax.ShapeDtypeStruct((rows, heads * HEAD), BF),
-            jax.ShapeDtypeStruct((2 * heads, HEAD), F32),
-            pltpu.HBM((keys, 2 * HEAD), BF),
-            pltpu.HBM((4,) + w.shape, BF),
+            jax.ShapeDtypeStruct((4,) + w.shape, BF),
         ],
-        in_specs=[pl.BlockSpec(memory_space=pltpu.SMEM), vmem, vmem, vmem, hbm],
-        out_specs=[vmem, vmem, hbm, hbm],
+        in_specs=[pl.BlockSpec(memory_space=pltpu.SMEM), vmem, vmem, vmem, anywhere],
+        out_specs=[vmem, anywhere],
         scratch_shapes=[
             pltpu.VMEM((keys, 3 * HEAD), BF),
             pltpu.VMEM((heads * rows, 2 * HEAD), F32),
@@ -356,7 +348,7 @@
             pltpu.VMEM((rows, 2 * HEAD), BF),
             pltpu.SemaphoreType.DMA((15, PIECES)),
             pltpu.SemaphoreType.DMA((15, PIECES)),
-            pltpu.SemaphoreType.DMA((17,)),
+            pltpu.SemaphoreType.DMA((1,)),
             pltpu.SemaphoreType.DMA((6, 2)),
             pltpu.SemaphoreType.DMA((6, 2)),
             pltpu.SemaphoreType.DMA((1,)),
@@ -369,7 +361,7 @@
             bytes_accessed=keys * 4 * HEAD,
             transcendentals=heads * rows * keys,
         ),
-    )(counts, source, w_query, w_keyval, pltpu.with_memory_space_constraint(w, pltpu.HBM))
+    )(counts, source, w_query, w_keyval, w)
 
 
 def careful_kernel(total_ref, q_ref, kv_ref, out_ref, top, acc, total_sum):
@@ -424,19 +416,6 @@
         scratch_shapes=[pltpu.VMEM((heads * rows, HEAD), F32)] * 3,
         compiler_params=pltpu.CompilerParams(vmem_limit_bytes=20 * 2**20),
     )(total, queries, kv_full)
-
-
-def attend(counts, total, source, w_query, w_keyval, w, ident):
-    plain, sums, kv_full, w_full = attend_call(counts, source, w_query, w_keyval, w, ident)
-    safe = jnp.all((sums > sum_low) & (sums < sum_high))
-    attended = lax.cond(
-        safe,
-        lambda: plain,
-        lambda: careful_call(
-            total, stacked_queries(source, w_query), kv_full, source.shape[0]
-        ),
-    )
-    return (attended, w_full)
 
 
 class YGather:
@@ -778,7 +757,21 @@
 
 
 def policy_kernel(
-    shape, x_ref, cin_ref, wp_ref, side_ref, att_ref, out_ref, sum_a, sum_b, part_ref, d_ref, *refs
+    shape,
+    count_ref,
+    x_ref,
+    cin_ref,
+    wp_ref,
+    action_ref,
+    advantage_ref,
+    old_ref,
+    att_ref,
+    out_ref,
+    sum_a,
+    sum_b,
+    part_ref,
+    d_ref,
+    *refs,
 ):
     scatter, semaphores, (send, recv, local) = refs[:5], refs[5:9], refs[9:]
     work = Reduce(shape, att_ref, d_ref, None, scatter, (sum_a, sum_b), None, semaphores)
@@ -800,7 +793,14 @@
         part_ref, out_ref.at[:, pl.ds(pl.multiple_of(ring.ypos * width, HEAD), width)], local.at[0]
     )
     mine.start()
-    d_ref[...] = policy_backward(x_ref[...], side_ref[...], wp_ref[...]).astype(BF)
+    d_ref[...] = policy_backward(
+        x_ref[...],
+        standing(action_ref[...]),
+        standing(advantage_ref[...])[:, :1],
+        standing(old_ref[...])[:, :1],
+        live_scale(count_ref, rows),
+        wp_ref[...],
+    ).astype(BF)
     ring.pass_on(0)
     ring.pass_on(1)
     work.begin()
@@ -815,7 +815,7 @@
     mine.wait()
 
 
-def policy_call(hidden, c_in, w_policy, side, attended, ident):
+def policy_call(counts, hidden, c_in, w_policy, action, advantage, old_values, attended, ident):
     rows = hidden.shape[0]
     width = c_in.shape[1]
     shape = Geometry(attended.shape[1], hidden.shape[1], False)
@@ -824,7 +824,7 @@
         functools.partial(policy_kernel, shape),
         out_shape=[jax.ShapeDtypeStruct((rows, 4 * width), BF)]
         + [jax.ShapeDtypeStruct(q, BF) for q in shape.quarter_shape],
-        in_specs=[vmem] * 5,
+        in_specs=[pl.BlockSpec(memory_space=pltpu.SMEM)] + [vmem] * 7,
         out_specs=[vmem] * 3,
         scratch_shapes=[pltpu.VMEM((rows, width), BF), pltpu.VMEM(hidden.shape, BF)]
         + shape.scatter_scratch()
@@ -837,17 +837,17 @@
         compiler_params=pltpu.CompilerParams(
             collective_id=ident, has_side_effects=True, vmem_limit_bytes=32 * 2**20
         ),
-    )(hidden, c_in, w_policy, side, attended)
-
-
-def output_kernel(shape, x_ref, w_hbm, base_ref, *refs):
-    *refs, w_ref, loaded = refs
+    )(counts, hidden, c_in, w_policy, action, advantage, old_values, attended)
+
+
+def output_kernel(shape, x_ref, w_ref, base_ref, *refs):
     if shape is None:
         out_ref, acc, blocks, send, recv = refs
         work = None
     else:
-        sum_a, sum_b, out_ref, grad_ref, acc, blocks, send, recv = refs[:8]
-        work = Reduce(shape, None, None, grad_ref, None, (sum_a, sum_b), refs[8:10], refs[10:14])
+        count_ref, return_ref, wv_ref, sum_a, sum_b, value_ref, out_ref, grad_ref = refs[:8]
+        acc, blocks, send, recv = refs[8:12]
+        work = Reduce(shape, None, None, grad_ref, None, (sum_a, sum_b), refs[12:14], refs[14:18])
     rows = x_ref.shape[0]
     half = rows // 2
     ring = YGather(
@@ -856,12 +856,6 @@
         send,
         recv,
     )
-    loads = [
-        pltpu.make_async_copy(w_hbm.at[there], w_ref.at[there], loaded.at[k])
-        for k, there in enumerate((ring.ypos, ring.ym, ring.yp, ring.y2))
-    ]
-    for load in loads:
-        load.start()
     barrier = pltpu.get_barrier_semaphore()
     expected = ring.greet(barrier)
     if work is not None:
@@ -870,8 +864,6 @@
     ring.start()
     if work is not None:
         work.second_scatter()
-    for load in loads:
-        load.wait()
     acc[...] = base_ref[...].astype(F32) + jnp.dot(
         x_ref[...], w_ref[ring.ypos], preferred_element_type=F32
     )
@@ -901,37 +893,47 @@
     add(2, 0)
     ring.arrived(2, 1)
     add(2, 1)
-    out_ref[...] = acc[...].astype(out_ref.dtype)
+    if work is None:
+        out_ref[...] = acc[...].astype(BF)
+    else:
+        value, out_ref[...] = value_backward(
+            acc[...], standing(return_ref[...])[:, :1], live_scale(count_ref, rows), wv_ref[...]
+        )
+        value_ref[...] = jnp.transpose(jnp.broadcast_to(value, (rows, HEAD)))[:8]
     if work is not None:
         work.finish()
     ring.wait_sent()
 
 
-def output_call(x, w_full, base, out_type, shape, sums, ident):
+def output_call(x, w_full, base, value_args, ident):
     rows, width = x.shape
     columns = w_full.shape[2]
     vmem = pl.BlockSpec(memory_space=pltpu.VMEM)
-    args = [x, pltpu.with_memory_space_constraint(w_full, pltpu.HBM), base]
-    out_shape = [jax.ShapeDtypeStruct((rows, columns), out_type)]
+    args = [x, w_full, base]
+    in_specs = [vmem] * 3
+    out_shape = [jax.ShapeDtypeStruct((rows, columns), BF)]
     scratch = [
         pltpu.VMEM((rows, columns), F32),
         pltpu.VMEM((3, rows, width), BF),
         pltpu.SemaphoreType.DMA((4, 2)),
         pltpu.SemaphoreType.DMA((3, 2)),
     ]
-    if shape is not None:
-        args += list(sums)
+    shape = None
+    if value_args is not None:
+        shape, counts, target, w_value, sums = value_args
+        args += [counts, target, w_value] + list(sums)
+        in_specs += [pl.BlockSpec(memory_space=pltpu.SMEM)] + [vmem] * 4
+        out_shape = [jax.ShapeDtypeStruct((8, rows), F32)] + out_shape
         out_shape.append(jax.ShapeDtypeStruct((shape.rows, shape.columns), BF))
         scratch += shape.sub_scratch() + shape.semaphores()
-    scratch += [pltpu.VMEM(w_full.shape, BF), pltpu.SemaphoreType.DMA((4,))]
     return pl.pallas_call(
         functools.partial(output_kernel, shape),
         out_shape=out_shape,
-        in_specs=[vmem, pl.BlockSpec(memory_space=pltpu.HBM)] + [vmem] * (len(args) - 2),
+        in_specs=in_specs,
         out_specs=[vmem] * len(out_shape),
         scratch_shapes=scratch,
         compiler_params=pltpu.CompilerParams(
-            collective_id=ident, has_side_effects=True, vmem_limit_bytes=40 * 2**20
+            collective_id=ident, has_side_effects=True, vmem_limit_bytes=(20 if shape is None else 32) * 2**20
         ),
     )(*args)
 
@@ -944,6 +946,39 @@
     ).astype(BF)
     heads = queries.shape[1] // HEAD
     return jnp.transpose(queries.reshape(rows, heads, HEAD), (1, 0, 2)).reshape(heads * rows, HEAD)
+
+
+def careful_attend(total, source, w_query, w_keyval):
+    normed = rms_normed(source.astype(F32)).astype(BF)
+    keyval = [jnp.dot(normed, w_keyval[part], preferred_element_type=F32) for part in range(2)]
+    joined = jnp.concatenate(keyval, axis=1).astype(BF)
+    everyone = lax.all_gather(joined, "rep", axis=0, tiled=True)
+    return careful_call(total, stacked_queries(source, w_query), everyone, source.shape[0])
+
+
+def summed_grad(attended, grad_in):
+    grad = lax.dot_general(
+        attended, grad_in, (((0,), (0,)), ((), ())), preferred_element_type=F32
+    )
+    return lax.psum(grad.astype(BF), ("rep", "sec")).astype(F32)
+
+
+def careful_path(
+    obs, a_query, a_keyval, a_out, w_policy, c_in, c_query, c_keyval, c_out, w_value, columns, total
+):
+    attended = careful_attend(total, obs, a_query, a_keyval)
+    mixed_sum = lax.psum(jnp.dot(attended, a_out, preferred_element_type=F32), "mdl")
+    hidden = (obs.astype(F32) + mixed_sum).astype(BF)
+    action, advantage, old_values, target, scale = columns
+    dhidden = policy_backward(hidden, action, advantage, old_values, scale, w_policy).astype(BF)
+    embed_part = jnp.dot(hidden, c_in, preferred_element_type=F32).astype(BF)
+    embedded = lax.all_gather(embed_part, "mdl", axis=1, tiled=True)
+    critic_attended = careful_attend(total, embedded, c_query, c_keyval)
+    critic_sum = lax.psum(jnp.dot(critic_attended, c_out, preferred_element_type=F32), "mdl")
+    value, dmixed = value_backward(
+        embedded.astype(F32) + critic_sum, target, scale, w_value[None, :]
+    )
+    return (value[:, 0], summed_grad(attended, dhidden), summed_grad(critic_attended, dmixed))
 
 
 def on_device(
@@ -963,38 +998,54 @@
     returns,
     robot_count,
 ):
-    row_count = obs.shape[1]
-    batch_index = lax.axis_index("sec")
-    robot_total = robot_count[batch_index]
-    total = robot_total.reshape(1)
-    live_total = jnp.sum(robot_count).astype(F32)
-    first_row = lax.axis_index("rep") * row_count
-    live_mask = first_row + lax.iota(jnp.int32, row_count) < robot_total
-    mdl_count = lax.axis_size("mdl")
-    part_rows = row_count // mdl_count
+    rows = obs.shape[1]
+    part_rows = rows // lax.axis_size("mdl")
     row_start = lax.axis_index("mdl") * part_rows
-    side = jnp.stack(
-        [
-            actions[0].astype(F32),
-            advantages[0],
-            old_logp[0],
-            jnp.where(live_mask, 1.0 / live_total, 0.0),
-        ],
-        axis=1,
-    )
-
-    attended, a_out_full = attend(robot_count, total, obs[0], a_query, a_keyval, a_out, 1)
-    (hidden,) = output_call(attended, a_out_full, obs[0], BF, None, None, 3)
-    embedded, *sums = policy_call(hidden, c_in, w_policy, side, attended, 4)
-    critic_attended, c_out_full = attend(
-        robot_count, total, embedded, c_query, c_keyval, c_out, 2
+
+    def careful():
+        total = robot_count[lax.axis_index("sec")]
+        live = lax.axis_index("rep") * rows + lax.iota(jnp.int32, rows) < total
+        scale = jnp.where(live, 1.0 / jnp.sum(robot_count).astype(F32), 0.0)
+        columns = (actions[0], advantages[0], old_logp[0], returns[0], scale)
+        return careful_path(
+            obs[0],
+            a_query,
+            a_keyval,
+            a_out,
+            w_policy,
+            c_in,
+            c_query,
+            c_keyval,
+            c_out,
+            w_value,
+            tuple(column[:, None] for column in columns),
+            total.reshape(1),
+        )
+
+    attended, a_out_full = attend_call(robot_count, obs[0], a_query, a_keyval, a_out, 1)
+    (hidden,) = output_call(attended, a_out_full, obs[0], None, 3)
+    embedded, *sums = policy_call(
+        robot_count, hidden, c_in, w_policy, actions, advantages, old_logp, attended, 4
+    )
+    critic_attended, c_out_full = attend_call(
+        robot_count, embedded, c_query, c_keyval, c_out, 2
     )
     shape = Geometry(attended.shape[1], hidden.shape[1], False)
-    mixed, actor_summed = output_call(critic_attended, c_out_full, embedded, F32, shape, sums, 5)
-    value_pred, dmixed = value_backward(mixed, returns[0], live_mask, live_total, w_value)
-    value_part = lax.dynamic_slice_in_dim(value_pred, row_start, part_rows, 0)
-    critic_summed = reduced_grad(critic_attended, dmixed.astype(BF), 6).astype(F32)
-    return (value_part[None, :], actor_summed.astype(F32), critic_summed)
+    values, dmixed, actor_summed = output_call(
+        critic_attended,
+        c_out_full,
+        embedded,
+        (shape, robot_count, returns, w_value[None, :], sums),
+        5,
+    )
+    critic_summed = reduced_grad(critic_attended, dmixed, 6)
+    mark = critic_summed[0, 0].astype(F32)
+    values, actor_grad, critic_grad = lax.cond(
+        mark == mark,
+        lambda: (values[0], actor_summed.astype(F32), critic_summed.astype(F32)),
+        careful,
+    )
+    return (lax.dynamic_slice_in_dim(values, row_start, part_rows, 0)[None, :], actor_grad, critic_grad)
 
 
 def solution(mesh):

time: 473 us -> 876 us (1.85)
  waiting for transfers between devices: 0 us -> 394 us
  Pallas kernels: 425 us -> 395 us
  matrix products: 4.59 us -> 34.2 us
  between operations: 3.29 us -> 15.8 us
  loops' own time: 13.7 us -> 1.22 us
    psum x0 -> x3, waiting for transfers between devices: none -> 262 us  [the longest x1 110 us: summed_grad(): return lax.psum(grad.astype(BF), ('rep', 'sec')).astype(F32)]
    all_gather x0 -> x3, waiting for transfers between devices: none -> 132 us  [the longest x2 101 us: careful_attend(): everyone = lax.all_gather(joined, 'rep', axis=0, tiled=True)]
    pallas_call x2, Pallas kernels: 112 us -> 83.7 us  [attend_call(): pl.pallas_call(functools.partial(attend_kernel, heads), out_shape=[jax.Sh...]
    dot_general x1 -> x11, matrix products: 0.71 us -> 29.1 us  [the longest x4 6.49 us: careful_attend(): jnp.dot(normed, w_keyval[part], preferred_element_type=F32)]
    another operation x2 -> x0, loops' own time: 13.7 us -> none  [attend(): lax.cond(safe, lambda: plain, lambda: careful_call(total, stacked_queries...]
  transfers between devices with their start and end apart: 0 -> 6, of which waited for: 0 -> 6; matrix products, arithmetic and copies ran while one was open for 0% -> 2% of each run, Pallas kernels for 0% -> 0%
where the time goes in v5:
time: 876 us; the launch traced here: 869 us
  Pallas kernels  395 us (45%)
  waiting for transfers between devices  394 us (45%)
  matrix products  34.2 us (4%)
  other arithmetic  19.4 us (2%)
  between operations  15.8 us (2%)
  local copies, waits for them, and re-layouts  9.02 us (1%)
    pallas_call x2, Pallas kernels, careful_call(): pl.pallas_call(careful_kernel, out_shape=jax.ShapeDtypeStruct((rows, head...  214 us
    psum x1, waiting for transfers between devices, summed_grad(): return lax.psum(grad.astype(BF), ('rep', 'sec')).astype(F32)  110 us
    all_gather x2, waiting for transfers between devices, careful_attend(): everyone = lax.all_gather(joined, 'rep', axis=0, tiled=True)  101 us
    pallas_call x2, Pallas kernels, attend_call(): pl.pallas_call(functools.partial(attend_kernel, heads), out_shape=[jax.Sh...  83.7 us
    psum x1, waiting for transfers between devices, careful_path(): lax.psum(jnp.dot(critic_attended, c_out, preferred_element_type=F32), 'mdl')  78.8 us
    psum x1, waiting for transfers between devices, careful_path(): lax.psum(jnp.dot(attended, a_out, preferred_element_type=F32), 'mdl')  73.2 us
    pallas_call x2, Pallas kernels, output_call(): pl.pallas_call(functools.partial(output_kernel, shape), out_shape=out_sha...  43.8 us
    pallas_call x1, Pallas kernels, reduced_grad(): pl.pallas_call(functools.partial(reduce_kernel, shape), out_shape=jax.Sha...  31 us
  transfers between devices with their start and end apart: 6, of which 6 were waited for; matrix products, arithmetic and copies ran while one was open for 2% of the time, Pallas kernels for 0%

profile of v5, /device:TPU:1, one launch (start us, length us, event | category | flops | bytes accessed | tf_op | source)
XLA Modules:
  0.0 869.1 jit_solution(13033381539855331728)
XLA Ops:
  7.2 40.5 %shard_map.166 = (bf16[512,384]{1,0:T(8,128)(2,1)S(1)}, bf16[4,384,1536]{2,1,0:T(8,128)(2,1)S(1)}) custom-call(s32[2]{0:T(128)} %refs_0_.1, bf16[512,1536]{1,0:T(8,128)(2,1)} %bitcast.68, bf16[1536,384]{1,0:T(8,128)(2,1)} %wq_ref.2, bf16[2,1536,128]{2,1,0:T(8,128)(2,1)} %wkv_ref.2, bf16[384,1536]{1,0:T(8,128)(2,1)} %w_ref.2), custom_call_target="tpu_custom_call" | custom-call | flops 6442450944 | bytes 4194304 | tf_op jit(solution)/shard_map/pallas_call | solution.py:336
  47.7 17.2 %shard_map.167.x_ref = bf16[512,1536]{1,0:T(8,128)(2,1)S(1)} custom-call(bf16[512,384]{1,0:T(8,128)(2,1)S(1)} %get-tuple-element.84.x_ref.att_ref, bf16[4,384,1536]{2,1,0:T(8,128)(2,1)S(1)} %get-tuple-element.85.w_ref, bf16[512,1536]{1,0:T(8,128)(2,1)S(1)} %bitcast.69), custom_call_target="tpu_custom_call" | custom-call | tf_op jit(solution)/shard_map/pallas_call | solution.py:929
  65.0 23.3 %shard_map.168 = (bf16[512,2048]{1,0:T(8,128)(2,1)S(1)}, bf16[96,512]{1,0:T(8,128)(2,1)S(1)}, bf16[96,256]{1,0:T(8,128)(2,1)S(1)}) custom-call(s32[2]{0:T(128)S(1)} %copy-done.18, bf16[512,1536]{1,0:T(8,128)(2,1)S(1)} %shard_map.167.x_ref, bf16[1536,512]{1,0:T(8,128)(2,1)S(1)} %copy-done.7, bf16[1536,128]{1,0:T(8,128)(2,1)S(1)} %copy-done.6, ...), custom_call_target="tpu_custom_call" | custom-call | tf_op jit(solution)/shard_map/pallas_call | solution.py:823
  88.3 43.2 %shard_map.169 = (bf16[512,512]{1,0:T(8,128)(2,1)S(1)}, bf16[4,512,2048]{2,1,0:T(8,128)(2,1)S(1)}) custom-call(s32[2]{0:T(128)S(1)} %copy-done.18, bf16[512,2048]{1,0:T(8,128)(2,1)S(1)} %get-tuple-element.86.x_ref.base_ref, bf16[2048,512]{1,0:T(8,128)(2,1)} %wq_ref.3, bf16[2,2048,128]{2,1,0:T(8,128)(2,1)S(1)} %copy-done.20, bf16[512,2048]{1,0:T(8,128)(2,1)} %w_ref.3), custom_call_target="tpu_custom_call" | custom-call | flops 8589934592 | bytes 4194304 | tf_op jit(solution)/shard_map/pallas_call | solution.py:336
  131.6 26.6 %shard_map.170 = (f32[8,512]{1,0:T(8,128)}, bf16[512,2048]{1,0:T(8,128)(2,1)S(1)}, bf16[384,1536]{1,0:T(8,128)(2,1)}) custom-call(bf16[512,512]{1,0:T(8,128)(2,1)S(1)} %get-tuple-element.87.x_ref.att_ref, bf16[4,512,2048]{2,1,0:T(8,128)(2,1)S(1)} %get-tuple-element.88.w_ref, bf16[512,2048]{1,0:T(8,128)(2,1)S(1)} %get-tuple-element.86.x_ref.base_ref, ...), custom_call_target="tpu_custom_call" | custom-call | tf_op jit(solution)/shard_map/pallas_call | solution.py:929
  158.2 31.0 %shard_map.171 = bf16[512,2048]{1,0:T(8,128)(2,1)S(1)} custom-call(bf16[512,512]{1,0:T(8,128)(2,1)S(1)} %get-tuple-element.87.x_ref.att_ref, bf16[512,2048]{1,0:T(8,128)(2,1)S(1)} %get-tuple-element.91.d_ref), custom_call_target="tpu_custom_call" | custom-call | tf_op jit(solution)/shard_map/pallas_call | solution.py:744
  189.2 0.5 slice.18
  191.0 669.6 %conditional.4 = (f32[512]{0:T(512)S(1)}, f32[384,1536]{1,0:T(8,128)S(1)}, f32[512,2048]{1,0:T(8,128)}) conditional(s32[]{:T(128)} %bitcast.19, (bf16[1,512,1536]{2,1,0:T(8,128)(2,1)S(1)}, s32[2]{0:T(128)}, bf16[1536,384]{1,0:T(8,128)(2,1)}, bf16[2,1536,128]{2,1,0:T(8,128)(2,1)}, bf16[384,1536]{1,0:T(8,128)(2,1)S(1)}, ...), branch_computations={%region_0.16_spmd, %region_16.17_spmd} | conditional | flops 7254061056 | bytes 262703872
  191.1 0.0 all-gather.4.cloned.1.call-start
  191.1 0.4 fusion.16
  191.5 1.6 convolution_convert_fusion.5
  193.2 0.6 convolution_convert_fusion.6
  193.8 0.7 pad_maximum_fusion
  194.5 0.0 all-gather.4.cloned.1.call-update
  194.5 0.0 all-reduce.5.cloned.1.call-start
  194.6 2.2 fusion.39
  196.8 0.2 copy.18
  197.0 1.3 dynamic_slice.4.total_ref
  198.3 48.4 %all-gather.4.cloned.1.call-done.kv_ref = bf16[8192,256]{1,0:T(8,128)(2,1)} async-done(((bf16[512,256]{1,0:T(8,128)(2,1)}), bf16[8192,256]{1,0:T(8,128)(2,1)}) %all-gather.4.cloned.1.call-update) | async-done | bytes 4194320 | tf_op jit(solution)/shard_map/cond/branch_0_fun/all_gather | solution.py:955
  246.7 2.2 copy-done
  248.9 91.3 %branch_0_fun.2 = bf16[512,384]{1,0:T(8,128)(2,1)S(1)} custom-call(s32[1]{0:T(128)} %dynamic_slice.4.total_ref, bf16[1536,128]{1,0:T(8,128)(2,1)S(1)} %bitcast.67, bf16[8192,256]{1,0:T(8,128)(2,1)S(1)} %copy-done), custom_call_target="tpu_custom_call" | custom-call | tf_op jit(solution)/shard_map/cond/branch_0_fun/pallas_call | solution.py:406
  340.2 2.6 fusion.65
  342.9 0.0 all-reduce.5.cloned.1.call-update
  342.9 0.0 all-gather.6.cloned.1.call-start
  342.9 73.2 %all-reduce.5.cloned.1.call-done = f32[512,1536]{1,0:T(8,128)} async-done(((f32[512,1536]{1,0:T(8,128)}), f32[512,1536]{1,0:T(8,128)}) %all-reduce.5.cloned.1.call-update) | async-done | bytes 3145744 | tf_op jit(solution)/shard_map/cond/branch_0_fun/psum | solution.py:970
  416.1 4.1 fusion.15
  420.2 3.7 convolution_convert_fusion.2
  423.8 0.0 all-gather.6.cloned.1.call-update
  423.9 0.0 all-gather.8.cloned.1.call-start
  423.9 30.8 %all-gather.6.cloned.1.call-done = bf16[512,2048]{1,0:T(8,128)(2,1)} async-done(((bf16[512,512]{1,0:T(8,128)(2,1)}), bf16[512,2048]{1,0:T(8,128)(2,1)}) %all-gather.6.cloned.1.call-update) | async-done | bytes 2097168 | tf_op jit(solution)/shard_map/cond/branch_0_fun/all_gather | solution.py:975
  454.7 2.2 fusion.3
  456.9 2.4 convolution_convert_fusion.4
  459.4 1.8 convolution_convert_fusion.3
  461.2 0.7 pad_maximum_fusion.1
  461.9 0.0 all-gather.8.cloned.1.call-update
  461.9 0.0 all-reduce.7.cloned.1.call-start
  462.0 3.0 fusion.35
  465.0 0.3 copy.21
  465.2 52.7 %all-gather.8.cloned.1.call-done.kv_ref = bf16[8192,256]{1,0:T(8,128)(2,1)} async-done(((bf16[512,256]{1,0:T(8,128)(2,1)}), bf16[8192,256]{1,0:T(8,128)(2,1)}) %all-gather.8.cloned.1.call-update) | async-done | bytes 4194320 | tf_op jit(solution)/shard_map/cond/branch_0_fun/all_gather | solution.py:955
  518.0 2.2 copy-done.1
  520.2 122.2 %branch_0_fun.3 = bf16[512,512]{1,0:T(8,128)(2,1)S(1)} custom-call(s32[1]{0:T(128)} %dynamic_slice.4.total_ref, bf16[2048,128]{1,0:T(8,128)(2,1)S(1)} %bitcast.66, bf16[8192,256]{1,0:T(8,128)(2,1)S(1)} %copy-done.1), custom_call_target="tpu_custom_call" | custom-call | tf_op jit(solution)/shard_map/cond/branch_0_fun/pallas_call | solution.py:406
  642.4 4.9 fusion.66
  647.2 0.2 all-reduce.9.cloned.1.call-start
  647.5 0.4 copy-done.19
  647.9 0.7 reduce_sum.65
  649.3 2.2 fusion.64
  651.6 0.1 exponential_reduce_fusion
  651.6 0.1 select_reduce_fusion
  651.7 0.6 fusion.57
  652.3 2.9 fusion.11
  655.3 3.4 convolution_convert_fusion.1
  658.7 78.8 %all-reduce.7.cloned.1.call-done = f32[512,2048]{1,0:T(8,128)} async-done(((f32[512,2048]{1,0:T(8,128)}), f32[512,2048]{1,0:T(8,128)}) %all-reduce.7.cloned.1.call-update) | async-done | bytes 4194320 | tf_op jit(solution)/shard_map/cond/branch_0_fun/psum | solution.py:977
  737.5 3.0 multiply_reduce_fusion.1
  740.5 0.5 copy-done.2
  741.0 0.8 multiply_reduce_fusion
  741.8 0.6 fusion.58
  742.4 0.9 fusion
  743.3 2.8 convolution_convert_fusion
  746.2 0.0 all-reduce.9.cloned.1.call-update
  746.2 109.7 %all-reduce.9.cloned.1.call-done = (bf16[384,1536]{1,0:T(8,128)(2,1)}, bf16[512,2048]{1,0:T(8,128)(2,1)}) async-done(((bf16[384,1536]{1,0:T(8,128)(2,1)}, bf16[512,2048]{1,0:T(8,128)(2,1)}), (bf16[384,1536]{1,0:T(8,128)(2,1)}, bf16[512,2048]{1,0:T(8,128)(2,1)})) %all-reduce.9.cloned.1.call-update) | async-done | bytes 3276816 | tf_op jit(solution)/shard_map/cond/branch_0_fun/psum | solution.py:963
  855.9 4.2 convert_element_type.125
  860.1 0.3 convert_element_type.123
  860.6 0.7 dynamic-slice_bitcast_fusion
  861.3 0.7 copy-done.5
  (47 shorter events, 0.2 us)
Async XLA Ops:
  7.2 40.5 %copy-start.4 = (bf16[1,512,1536]{2,1,0:T(8,128)(2,1)S(1)}, bf16[1,512,1536]{2,1,0:T(8,128)(2,1)}, u32[]{:S(2)}) copy-start(bf16[1,512,1536]{2,1,0:T(8,128)(2,1)} %param.17) | copy-start | bytes 4718596
  47.7 17.3 %copy-start.6 = (bf16[1536,128]{1,0:T(8,128)(2,1)S(1)}, bf16[1536,128]{1,0:T(8,128)(2,1)}, u32[]{:S(2)}) copy-start(bf16[1536,128]{1,0:T(8,128)(2,1)} %wp_ref.1) | copy-start | bytes 1179652
  47.7 17.3 %copy-start.7 = (bf16[1536,512]{1,0:T(8,128)(2,1)S(1)}, bf16[1536,512]{1,0:T(8,128)(2,1)}, u32[]{:S(2)}) copy-start(bf16[1536,512]{1,0:T(8,128)(2,1)} %cin_ref.1) | copy-start | bytes 4718596
  47.7 17.2 %copy-start.11 = (s32[1,512]{1,0:T(1,128)S(1)}, s32[1,512]{1,0:T(1,128)}, u32[]{:S(2)}) copy-start(s32[1,512]{1,0:T(1,128)} %action_ref.1) | copy-start | bytes 6148
  47.7 17.2 %copy-start.13 = (f32[1,512]{1,0:T(1,128)S(1)}, f32[1,512]{1,0:T(1,128)}, u32[]{:S(2)}) copy-start(f32[1,512]{1,0:T(1,128)} %advantage_ref.1) | copy-start | bytes 6148
  47.7 17.2 %copy-start.14 = (f32[1,512]{1,0:T(1,128)S(1)}, f32[1,512]{1,0:T(1,128)}, u32[]{:S(2)}) copy-start(f32[1,512]{1,0:T(1,128)} %old_ref.1) | copy-start | bytes 6148
  47.7 17.2 %copy-start.18 = (s32[2]{0:T(128)S(1)}, s32[2]{0:T(128)}, u32[]{:S(2)}) copy-start(s32[2]{0:T(128)} %refs_0_.1) | copy-start | bytes 28
  65.0 23.3 %copy-start.20 = (bf16[2,2048,128]{2,1,0:T(8,128)(2,1)S(1)}, bf16[2,2048,128]{2,1,0:T(8,128)(2,1)}, u32[]{:S(2)}) copy-start(bf16[2,2048,128]{2,1,0:T(8,128)(2,1)} %wkv_ref.3) | copy-start | bytes 3145732
  88.3 43.3 %copy-start.12 = (bf16[2048]{0:T(1024)(128)(2,1)S(1)}, bf16[2048]{0:T(1024)(128)(2,1)}, u32[]{:S(2)}) copy-start(bf16[2048]{0:T(1024)(128)(2,1)} %param.26) | copy-start | bytes 12292
  88.3 43.3 %copy-start.16 = (f32[1,512]{1,0:T(1,128)S(1)}, f32[1,512]{1,0:T(1,128)}, u32[]{:S(2)}) copy-start(f32[1,512]{1,0:T(1,128)} %refs_1_.1) | copy-start | bytes 6148
  158.2 32.9 %copy-start.8 = (bf16[384,1536]{1,0:T(8,128)(2,1)S(1)}, bf16[384,1536]{1,0:T(8,128)(2,1)}, u32[]{:S(2)}) copy-start(bf16[384,1536]{1,0:T(8,128)(2,1)} %w_ref.2) | copy-start | bytes 3538948
  191.1 55.6 %all-gather.4.cloned.1.call-start = ((), (), s32[]{:S(2)}) async-start(), calls=%async_computation | async-start | bytes 4456448 | tf_op jit(solution)/shard_map/cond/branch_0_fun/all_gather | solution.py:955
  191.1 2.0 copy-start.21
  194.5 221.6 %all-reduce.5.cloned.1.call-start = ((), (), s32[]{:S(2)}) async-start(), calls=%async_computation.1 | async-start | bytes 6291456 | tf_op jit(solution)/shard_map/cond/branch_0_fun/psum | solution.py:970
  246.7 2.2 copy-start
  342.9 111.8 %all-gather.6.cloned.1.call-start = ((), (), s32[]{:S(2)}) async-start(), calls=%async_computation.2 | async-start | bytes 2621440 | tf_op jit(solution)/shard_map/cond/branch_0_fun/all_gather | solution.py:975
  423.9 94.1 %all-gather.8.cloned.1.call-start = ((), (), s32[]{:S(2)}) async-start(), calls=%async_computation.3 | async-start | bytes 4456448 | tf_op jit(solution)/shard_map/cond/branch_0_fun/all_gather | solution.py:955
  454.7 4.7 copy-start.3
  461.9 275.6 %all-reduce.7.cloned.1.call-start = ((), (), s32[]{:S(2)}) async-start(), calls=%async_computation.4 | async-start | bytes 8388608 | tf_op jit(solution)/shard_map/cond/branch_0_fun/psum | solution.py:977
  518.0 2.2 copy-start.1
  647.2 0.7 copy-start.19
  647.2 2.1 copy-start.15
  647.2 208.6 %all-reduce.9.cloned.1.call-start = ((), (), s32[]{:S(2)}) async-start(), calls=%async_computation.5 | async-start | bytes 6553600 | tf_op jit(solution)/shard_map/cond/branch_0_fun/psum | solution.py:963
  737.5 3.4 copy-start.2
  741.0 0.8 copy-start.17
  855.9 4.2 copy-start.10
  860.6 1.4 copy-start.5
Sparse Core Ops, SparseCore 0:
  194.9 51.6 all-gather.3
  343.0 73.0 all-reduce.4
  424.0 30.6 all-gather.5
  462.1 55.8 all-gather.7
  647.4 90.1 all-reduce.6
  746.3 109.5 all-reduce.8

commit v6 on v5

--- a/solution.py
+++ b/solution.py
@@ -655,6 +655,9 @@
 
     def swap_and_scatter(self):
         self.swap().start()
+        self.scatter_own()
+
+    def scatter_own(self):
         own = self.grad(self.core)
         self.swap().wait_recv()
         self.mine[...] = (own + self.got[...].astype(F32)).astype(BF)
@@ -721,35 +724,63 @@
 
 
 def reduce_kernel(shape, att_ref, d_ref, out_ref, *scratch):
-    work = Reduce(
-        shape, att_ref, d_ref, out_ref, scratch[:5], scratch[5:7], scratch[7:9], scratch[9:13]
-    )
+    each = len(scratch) // 2
+    works = []
+    for index in range(2):
+        part = scratch[index * each : (index + 1) * each]
+        span = pl.ds(index * shape.columns, shape.columns)
+        works.append(
+            Reduce(
+                shape,
+                att_ref,
+                d_ref.at[:, span],
+                out_ref.at[:, span],
+                part[:5],
+                part[5:7],
+                part[7:9],
+                part[9:13],
+            )
+        )
+    early, late = works
     barrier = pltpu.get_barrier_semaphore()
-    expected = work.greet(barrier)
-    work.begin()
+    expected = early.greet(barrier)
+    early.begin()
     pl.semaphore_wait(barrier, expected)
-    work.swap_and_scatter()
-    work.first_sums()
-    work.second_scatter()
-    work.first_gather()
-    work.second_gather()
-    work.last_shares()
-    work.finish_scatter()
-    work.finish()
+    early.swap().start()
+    late.begin()
+    late.swap().start()
+    early.scatter_own()
+    late.scatter_own()
+    early.first_sums()
+    early.second_scatter()
+    late.first_sums()
+    late.second_scatter()
+    early.first_gather()
+    late.first_gather()
+    early.second_gather()
+    late.second_gather()
+    early.last_shares()
+    late.last_shares()
+    for work in works:
+        work.finish_scatter()
+        work.finish()
 
 
 def reduced_grad(attended, grad_in, ident):
-    shape = Geometry(attended.shape[1], grad_in.shape[1], True)
+    shape = Geometry(attended.shape[1], grad_in.shape[1] // 2, True)
     vmem = pl.BlockSpec(memory_space=pltpu.VMEM)
     return pl.pallas_call(
         functools.partial(reduce_kernel, shape),
-        out_shape=jax.ShapeDtypeStruct((shape.rows, shape.columns), BF),
+        out_shape=jax.ShapeDtypeStruct((attended.shape[1], grad_in.shape[1]), BF),
         in_specs=[vmem, vmem],
         out_specs=vmem,
-        scratch_shapes=shape.scatter_scratch()
-        + [pltpu.VMEM(q, BF) for q in shape.quarter_shape]
-        + shape.sub_scratch()
-        + shape.semaphores(),
+        scratch_shapes=2
+        * (
+            shape.scatter_scratch()
+            + [pltpu.VMEM(q, BF) for q in shape.quarter_shape]
+            + shape.sub_scratch()
+            + shape.semaphores()
+        ),
         compiler_params=pltpu.CompilerParams(
             collective_id=ident, has_side_effects=True, vmem_limit_bytes=24 * 2**20
         ),
@@ -846,8 +877,8 @@
         work = None
     else:
         count_ref, return_ref, wv_ref, sum_a, sum_b, value_ref, out_ref, grad_ref = refs[:8]
-        acc, blocks, send, recv = refs[8:12]
-        work = Reduce(shape, None, None, grad_ref, None, (sum_a, sum_b), refs[12:14], refs[14:18])
+        acc, blocks, send, recv, lanes = refs[8:13]
+        work = Reduce(shape, None, None, grad_ref, None, (sum_a, sum_b), refs[13:15], refs[15:19])
     rows = x_ref.shape[0]
     half = rows // 2
     ring = YGather(
@@ -899,7 +930,9 @@
         value, out_ref[...] = value_backward(
             acc[...], standing(return_ref[...])[:, :1], live_scale(count_ref, rows), wv_ref[...]
         )
-        value_ref[...] = jnp.transpose(jnp.broadcast_to(value, (rows, HEAD)))[:8]
+        lanes[...] = jnp.broadcast_to(value, lanes.shape)
+        mine = lanes[pl.ds(pl.multiple_of(ring.ypos * value_ref.shape[1], 8), value_ref.shape[1]), :]
+        value_ref[...] = jnp.transpose(mine)[:1]
     if work is not None:
         work.finish()
     ring.wait_sent()
@@ -923,7 +956,8 @@
         shape, counts, target, w_value, sums = value_args
         args += [counts, target, w_value] + list(sums)
         in_specs += [pl.BlockSpec(memory_space=pltpu.SMEM)] + [vmem] * 4
-        out_shape = [jax.ShapeDtypeStruct((8, rows), F32)] + out_shape
+        out_shape = [jax.ShapeDtypeStruct((1, rows // 4), F32)] + out_shape
+        scratch.append(pltpu.VMEM((rows, HEAD), F32))
         out_shape.append(jax.ShapeDtypeStruct((shape.rows, shape.columns), BF))
         scratch += shape.sub_scratch() + shape.semaphores()
     return pl.pallas_call(
@@ -948,11 +982,29 @@
     return jnp.transpose(queries.reshape(rows, heads, HEAD), (1, 0, 2)).reshape(heads * rows, HEAD)
 
 
+def ring_gather(block, axis):
+    count = lax.axis_size(axis)
+    me = lax.axis_index(axis)
+    onward = [(k, (k + 1) % count) for k in range(count)]
+    blocks = jnp.zeros((count,) + block.shape, block.dtype)
+
+    def turn(k, carried):
+        blocks, moving = carried
+        blocks = lax.dynamic_update_index_in_dim(blocks, moving, lax.rem(me + count - k, count), 0)
+        return (blocks, lax.ppermute(moving, axis, onward))
+
+    return lax.fori_loop(0, count, turn, (blocks, block))[0]
+
+
+def ring_sum(block, axis):
+    return jnp.sum(ring_gather(block, axis).astype(F32), axis=0)
+
+
 def careful_attend(total, source, w_query, w_keyval):
     normed = rms_normed(source.astype(F32)).astype(BF)
     keyval = [jnp.dot(normed, w_keyval[part], preferred_element_type=F32) for part in range(2)]
     joined = jnp.concatenate(keyval, axis=1).astype(BF)
-    everyone = lax.all_gather(joined, "rep", axis=0, tiled=True)
+    everyone = ring_gather(joined, "rep").reshape(-1, 2 * HEAD)
     return careful_call(total, stacked_queries(source, w_query), everyone, source.shape[0])
 
 
@@ -960,25 +1012,29 @@
     grad = lax.dot_general(
         attended, grad_in, (((0,), (0,)), ((), ())), preferred_element_type=F32
     )
-    return lax.psum(grad.astype(BF), ("rep", "sec")).astype(F32)
+    return ring_sum(ring_sum(grad.astype(BF), "rep").astype(BF), "sec")
 
 
 def careful_path(
     obs, a_query, a_keyval, a_out, w_policy, c_in, c_query, c_keyval, c_out, w_value, columns, total
 ):
     attended = careful_attend(total, obs, a_query, a_keyval)
-    mixed_sum = lax.psum(jnp.dot(attended, a_out, preferred_element_type=F32), "mdl")
+    mixed_sum = ring_sum(jnp.dot(attended, a_out, preferred_element_type=F32), "mdl")
     hidden = (obs.astype(F32) + mixed_sum).astype(BF)
     action, advantage, old_values, target, scale = columns
     dhidden = policy_backward(hidden, action, advantage, old_values, scale, w_policy).astype(BF)
     embed_part = jnp.dot(hidden, c_in, preferred_element_type=F32).astype(BF)
-    embedded = lax.all_gather(embed_part, "mdl", axis=1, tiled=True)
+    embedded = jnp.concatenate(list(ring_gather(embed_part, "mdl")), axis=1)
     critic_attended = careful_attend(total, embedded, c_query, c_keyval)
-    critic_sum = lax.psum(jnp.dot(critic_attended, c_out, preferred_element_type=F32), "mdl")
+    critic_sum = ring_sum(
+        jnp.dot(critic_attended, c_out, preferred_element_type=F32), "mdl"
+    )
     value, dmixed = value_backward(
         embedded.astype(F32) + critic_sum, target, scale, w_value[None, :]
     )
-    return (value[:, 0], summed_grad(attended, dhidden), summed_grad(critic_attended, dmixed))
+    part_rows = value.shape[0] // 4
+    value = lax.dynamic_slice_in_dim(value[:, 0], lax.axis_index("mdl") * part_rows, part_rows, 0)
+    return (value[None, :], summed_grad(attended, dhidden), summed_grad(critic_attended, dmixed))
 
 
 def on_device(
@@ -999,8 +1055,6 @@
     robot_count,
 ):
     rows = obs.shape[1]
-    part_rows = rows // lax.axis_size("mdl")
-    row_start = lax.axis_index("mdl") * part_rows
 
     def careful():
         total = robot_count[lax.axis_index("sec")]
@@ -1042,10 +1096,10 @@
     mark = critic_summed[0, 0].astype(F32)
     values, actor_grad, critic_grad = lax.cond(
         mark == mark,
-        lambda: (values[0], actor_summed.astype(F32), critic_summed.astype(F32)),
+        lambda: (values, actor_summed.astype(F32), critic_summed.astype(F32)),
         careful,
     )
-    return (lax.dynamic_slice_in_dim(values, row_start, part_rows, 0)[None, :], actor_grad, critic_grad)
+    return (values, actor_grad, critic_grad)
 
 
 def solution(mesh):

time: 876 us -> 2460 us (2.81)
  waiting for transfers between devices: 394 us -> 1710 us
  local copies, waits for them, and re-layouts: 9.02 us -> 204 us
  other arithmetic: 19.4 us -> 62.6 us
  starting transfers between devices: 0.42 us -> 40.7 us
    ppermute x0 -> x80, waiting for transfers between devices: none -> 1710 us  [turn(): return (blocks, lax.ppermute(moving, axis, onward))]
    psum x3 -> x0, waiting for transfers between devices: 262 us -> none  [the longest x1 110 us: summed_grad(): return lax.psum(grad.astype(BF), ('rep', 'sec')).astype(F32)]
    all_gather x3 -> x0, waiting for transfers between devices: 132 us -> none  [the longest x2 101 us: careful_attend(): everyone = lax.all_gather(joined, 'rep', axis=0, tiled=True)]
    another operation x0 -> x90, local copies, waits for them, and re-layouts: none -> 99.5 us
    dynamic_update_slice x0 -> x80, local copies, waits for them, and re-layouts: none -> 96.1 us  [turn(): lax.dynamic_update_index_in_dim(blocks, moving, lax.rem(me + count - k, c...]
    reduce_sum x0 -> x6, other arithmetic: none -> 49.7 us  [ring_sum(): return jnp.sum(ring_gather(block, axis).astype(F32), axis=0)]
    ppermute x0 -> x80, starting transfers between devices: none -> 40.7 us  [turn(): return (blocks, lax.ppermute(moving, axis, onward))]
  transfers between devices with their start and end apart: 6 -> 80, of which waited for: 6 -> 80; matrix products, arithmetic and copies ran while one was open for 2% -> 4% of each run, Pallas kernels for 0% -> 0%
where the time goes in v6:
time: 2460 us; the launch traced here: 2440 us
  waiting for transfers between devices  1710 us (70%)
  Pallas kernels  393 us (16%)
  local copies, waits for them, and re-layouts  204 us (8%)
  other arithmetic  62.6 us (3%)
  starting transfers between devices  40.7 us (2%)
    ppermute x80, waiting for transfers between devices, turn(): return (blocks, lax.ppermute(moving, axis, onward))  1710 us
    pallas_call x2, Pallas kernels, careful_call(): pl.pallas_call(careful_kernel, out_shape=jax.ShapeDtypeStruct((rows, head...  216 us
    another operation x89, local copies, waits for them, and re-layouts  97.8 us
    dynamic_update_slice x80, local copies, waits for them, and re-layouts, turn(): lax.dynamic_update_index_in_dim(blocks, moving, lax.rem(me + count - k, c...  96.1 us
    pallas_call x2, Pallas kernels, attend_call(): pl.pallas_call(functools.partial(attend_kernel, heads), out_shape=[jax.Sh...  82.5 us
    reduce_sum x6, other arithmetic, ring_sum(): return jnp.sum(ring_gather(block, axis).astype(F32), axis=0)  49.7 us
  transfers between devices with their start and end apart: 80, of which 80 were waited for; matrix products, arithmetic and copies ran while one was open for 4% of the time, Pallas kernels for 0%

profile of v6, /device:TPU:1, one launch (start us, length us, event | category | flops | bytes accessed | tf_op | source)
XLA Modules:
  0.0 2435.4 jit_solution(15103574704010061314)
XLA Ops:
  0.6 40.5 %shard_map.172 = (bf16[512,384]{1,0:T(8,128)(2,1)S(1)}, bf16[4,384,1536]{2,1,0:T(8,128)(2,1)S(1)}) custom-call(s32[2]{0:T(128)} %refs_0_.1, bf16[512,1536]{1,0:T(8,128)(2,1)} %bitcast.115, bf16[1536,384]{1,0:T(8,128)(2,1)} %wq_ref.2, bf16[2,1536,128]{2,1,0:T(8,128)(2,1)} %wkv_ref.2, bf16[384,1536]{1,0:T(8,128)(2,1)} %w_ref.2), custom_call_target="tpu_custom_call" | custom-call | flops 6442450944 | bytes 4194304 | tf_op jit(solution)/shard_map/pallas_call | solution.py:336
  41.2 17.2 shard_map.173.x_ref
  58.5 23.3 shard_map.174
  81.8 42.0 %shard_map.175 = (bf16[512,512]{1,0:T(8,128)(2,1)S(1)}, bf16[4,512,2048]{2,1,0:T(8,128)(2,1)S(1)}) custom-call(s32[2]{0:T(128)S(1)} %copy-done.35, bf16[512,2048]{1,0:T(8,128)(2,1)S(1)} %get-tuple-element.1032.x_ref.base_ref, bf16[2048,512]{1,0:T(8,128)(2,1)S(1)} %copy-done.38, bf16[2,2048,128]{2,1,0:T(8,128)(2,1)S(1)} %copy-done.40, ...), custom_call_target="tpu_custom_call" | custom-call | flops 8589934592 | bytes 4194304 | tf_op jit(solution)/shard_map/pallas_call | solution.py:336
  123.9 26.7 %shard_map.176 = (f32[1,128]{1,0:T(1,128)}, bf16[512,2048]{1,0:T(8,128)(2,1)S(1)}, bf16[384,1536]{1,0:T(8,128)(2,1)}) custom-call(bf16[512,512]{1,0:T(8,128)(2,1)S(1)} %get-tuple-element.1033.x_ref.att_ref, bf16[4,512,2048]{2,1,0:T(8,128)(2,1)S(1)} %get-tuple-element.1034.w_ref, bf16[512,2048]{1,0:T(8,128)(2,1)S(1)} %get-tuple-element.1032.x_ref.base_ref, ...), custom_call_target="tpu_custom_call" | custom-call | tf_op jit(solution)/shard_map/pallas_call | solution.py:963
  150.5 27.8 %shard_map.177 = bf16[512,2048]{1,0:T(8,128)(2,1)S(1)} custom-call(bf16[512,512]{1,0:T(8,128)(2,1)S(1)} %get-tuple-element.1033.x_ref.att_ref, bf16[512,2048]{1,0:T(8,128)(2,1)S(1)} %get-tuple-element.1037.d_ref), custom_call_target="tpu_custom_call" | custom-call | tf_op jit(solution)/shard_map/pallas_call | solution.py:772
  180.2 2253.3 %conditional.1 = (f32[1,128]{1,0:T(1,128)}, f32[384,1536]{1,0:T(8,128)S(1)}, f32[512,2048]{1,0:T(8,128)}) conditional(s32[]{:T(128)} %bitcast.34, (bf16[1,512,1536]{2,1,0:T(8,128)(2,1)S(1)}, s32[2]{0:T(128)S(1)}, bf16[1536,384]{1,0:T(8,128)(2,1)}, bf16[2,1536,128]{2,1,0:T(8,128)(2,1)S(1)}, bf16[384,1536]{1,0:T(8,128)(2,1)S(1)}, ...), branch_computations={%region_0.36_spmd, %region_36.37_spmd} | conditional | flops 7342663680 | bytes 525171424 | solution.py:1097
  185.4 143.9 %while.144 = (s32[]{:T(128)}, bf16[16,512,256]{2,1,0:T(8,128)(2,1)}, bf16[512,256]{1,0:T(8,128)(2,1)S(1)}, s32[]{:T(128)}, s32[]{:T(128)}, /*index=5*/s32[]{:T(128)}, s32[]{:T(128)}, s32[]{:T(128)}) while((s32[]{:T(128)}, bf16[16,512,256]{2,1,0:T(8,128)(2,1)}, bf16[512,256]{1,0:T(8,128)(2,1)S(1)}, s32[]{:T(128)}, s32[]{:T(128)}, ...), condition=%wide.region_3.3_spmd, body=%wide.region_2.2_spmd.sunk | while | flops 12 | bytes 2097390 | solution.py:996
  332.4 92.2 %branch_0_fun.2 = bf16[512,384]{1,0:T(8,128)(2,1)S(1)} custom-call(s32[1]{0:T(128)} %dynamic_slice.4.total_ref, bf16[1536,128]{1,0:T(8,128)(2,1)S(1)} %bitcast.112, bf16[8192,256]{1,0:T(8,128)(2,1)} %bitcast.113), custom_call_target="tpu_custom_call" | custom-call | tf_op jit(solution)/shard_map/cond/branch_0_fun/pallas_call | solution.py:406
  433.3 264.1 %while.145 = (s32[]{:T(128)}, f32[4,512,1536]{2,1,0:T(8,128)}, f32[512,1536]{1,0:T(8,128)}, s32[]{:T(128)}, s32[]{:T(128)}, /*index=5*/s32[]{:T(128)}, s32[]{:T(128)}, s32[]{:T(128)}) while((s32[]{:T(128)}, f32[4,512,1536]{2,1,0:T(8,128)}, f32[512,1536]{1,0:T(8,128)}, s32[]{:T(128)}, s32[]{:T(128)}, /*index=5*/s32[]{:T(128)}, s32[]{:T(128)}, ...), condition=%wide.region_5.5_spmd, body=%wide.region_4.4_spmd.sunk | while | flops 12 | bytes 25166060 | solution.py:996
  437.2 60.5 %collective-permute-done.1 = f32[512,1536]{1,0:T(8,128)} collective-permute-done((f32[512,1536]{1,0:T(8,128)S(1)}, f32[512,1536]{1,0:T(8,128)}, u32[]{:S(2)}, u32[]{:S(2)}) %collective-permute-start.1) | collective-permute-done | bytes 3145760 | tf_op jit(solution)/shard_map/cond/branch_0_fun/while/body/eval_jaxpr/ppermute | solution.py:994
  501.5 62.8 %collective-permute-done.1 = f32[512,1536]{1,0:T(8,128)} collective-permute-done((f32[512,1536]{1,0:T(8,128)S(1)}, f32[512,1536]{1,0:T(8,128)}, u32[]{:S(2)}, u32[]{:S(2)}) %collective-permute-start.1) | collective-permute-done | bytes 3145760 | tf_op jit(solution)/shard_map/cond/branch_0_fun/while/body/eval_jaxpr/ppermute | solution.py:994
  568.1 62.7 %collective-permute-done.1 = f32[512,1536]{1,0:T(8,128)} collective-permute-done((f32[512,1536]{1,0:T(8,128)S(1)}, f32[512,1536]{1,0:T(8,128)}, u32[]{:S(2)}, u32[]{:S(2)}) %collective-permute-start.1) | collective-permute-done | bytes 3145760 | tf_op jit(solution)/shard_map/cond/branch_0_fun/while/body/eval_jaxpr/ppermute | solution.py:994
  634.6 62.8 %collective-permute-done.1 = f32[512,1536]{1,0:T(8,128)} collective-permute-done((f32[512,1536]{1,0:T(8,128)S(1)}, f32[512,1536]{1,0:T(8,128)}, u32[]{:S(2)}, u32[]{:S(2)}) %collective-permute-start.1) | collective-permute-done | bytes 3145760 | tf_op jit(solution)/shard_map/cond/branch_0_fun/while/body/eval_jaxpr/ppermute | solution.py:994
  711.0 43.4 %while.146 = (s32[]{:T(128)}, bf16[4,512,512]{2,1,0:T(8,128)(2,1)S(1)}, bf16[512,512]{1,0:T(8,128)(2,1)S(1)}, s32[]{:T(128)}, s32[]{:T(128)}, /*index=5*/s32[]{:T(128)}, s32[]{:T(128)}, s32[]{:T(128)}) while((s32[]{:T(128)}, bf16[4,512,512]{2,1,0:T(8,128)(2,1)S(1)}, bf16[512,512]{1,0:T(8,128)(2,1)S(1)}, s32[]{:T(128)}, s32[]{:T(128)}, ...), condition=%wide.region_8.8_spmd, body=%wide.region_7.7_spmd.sunk | while | flops 12 | bytes 4194542 | solution.py:996
  720.5 12.0 collective-permute-done.2
  762.4 162.0 %while.147 = (s32[]{:T(128)}, bf16[16,512,256]{2,1,0:T(8,128)(2,1)}, bf16[512,256]{1,0:T(8,128)(2,1)S(1)}, s32[]{:T(128)}, s32[]{:T(128)}, /*index=5*/s32[]{:T(128)}, s32[]{:T(128)}, s32[]{:T(128)}) while((s32[]{:T(128)}, bf16[16,512,256]{2,1,0:T(8,128)(2,1)}, bf16[512,256]{1,0:T(8,128)(2,1)S(1)}, s32[]{:T(128)}, s32[]{:T(128)}, ...), condition=%wide.region_11.11_spmd, body=%wide.region_10.10_spmd.sunk | while | flops 12 | bytes 2097390 | solution.py:996
  928.5 123.6 %branch_0_fun.3 = bf16[512,512]{1,0:T(8,128)(2,1)S(1)} custom-call(s32[1]{0:T(128)} %dynamic_slice.4.total_ref, bf16[2048,128]{1,0:T(8,128)(2,1)S(1)} %bitcast.111, bf16[8192,256]{1,0:T(8,128)(2,1)} %bitcast.114), custom_call_target="tpu_custom_call" | custom-call | tf_op jit(solution)/shard_map/cond/branch_0_fun/pallas_call | solution.py:406
  1063.2 357.2 %while.148 = (s32[]{:T(128)}, f32[4,512,2048]{2,1,0:T(8,128)}, f32[512,2048]{1,0:T(8,128)}, s32[]{:T(128)}, s32[]{:T(128)}, /*index=5*/s32[]{:T(128)}, s32[]{:T(128)}, s32[]{:T(128)}) while((s32[]{:T(128)}, f32[4,512,2048]{2,1,0:T(8,128)}, f32[512,2048]{1,0:T(8,128)}, s32[]{:T(128)}, s32[]{:T(128)}, /*index=5*/s32[]{:T(128)}, s32[]{:T(128)}, ...), condition=%wide.region_13.13_spmd, body=%wide.region_12.12_spmd.sunk | while | flops 12 | bytes 33554668 | solution.py:996
  1072.5 80.5 %collective-permute-done.4 = f32[512,2048]{1,0:T(8,128)} collective-permute-done((f32[512,2048]{1,0:T(8,128)}, f32[512,2048]{1,0:T(8,128)}, u32[]{:S(2)}, u32[]{:S(2)}) %collective-permute-start.4) | collective-permute-done | bytes 4194336 | tf_op jit(solution)/shard_map/cond/branch_0_fun/while/body/eval_jaxpr/ppermute | solution.py:994
  1162.4 79.6 %collective-permute-done.4 = f32[512,2048]{1,0:T(8,128)} collective-permute-done((f32[512,2048]{1,0:T(8,128)}, f32[512,2048]{1,0:T(8,128)}, u32[]{:S(2)}, u32[]{:S(2)}) %collective-permute-start.4) | collective-permute-done | bytes 4194336 | tf_op jit(solution)/shard_map/cond/branch_0_fun/while/body/eval_jaxpr/ppermute | solution.py:994
  1251.5 79.6 %collective-permute-done.4 = f32[512,2048]{1,0:T(8,128)} collective-permute-done((f32[512,2048]{1,0:T(8,128)}, f32[512,2048]{1,0:T(8,128)}, u32[]{:S(2)}, u32[]{:S(2)}) %collective-permute-start.4) | collective-permute-done | bytes 4194336 | tf_op jit(solution)/shard_map/cond/branch_0_fun/while/body/eval_jaxpr/ppermute | solution.py:994
  1340.5 79.6 %collective-permute-done.4 = f32[512,2048]{1,0:T(8,128)} collective-permute-done((f32[512,2048]{1,0:T(8,128)}, f32[512,2048]{1,0:T(8,128)}, u32[]{:S(2)}, u32[]{:S(2)}) %collective-permute-start.4) | collective-permute-done | bytes 4194336 | tf_op jit(solution)/shard_map/cond/branch_0_fun/while/body/eval_jaxpr/ppermute | solution.py:994
  1455.1 483.7 %while.151 = (s32[]{:T(128)}, bf16[16,512,2048]{2,1,0:T(8,128)(2,1)}, bf16[512,2048]{1,0:T(8,128)(2,1)}, s32[]{:T(128)}, s32[]{:T(128)}, /*index=5*/s32[]{:T(128)}, s32[]{:T(128)}, s32[]{:T(128)}) while((s32[]{:T(128)}, bf16[16,512,2048]{2,1,0:T(8,128)(2,1)}, bf16[512,2048]{1,0:T(8,128)(2,1)}, s32[]{:T(128)}, s32[]{:T(128)}, ...), condition=%wide.region_31.31_spmd, body=%wide.region_30.30_spmd.sunk | while | flops 12 | bytes 16777452 | solution.py:996
  1459.6 21.5 collective-permute-done.7
  1488.3 21.5 collective-permute-done.7
  1516.9 21.9 collective-permute-done.7
  1545.6 24.0 collective-permute-done.7
  1574.3 26.1 %collective-permute-done.7 = bf16[512,2048]{1,0:T(8,128)(2,1)} collective-permute-done((bf16[512,2048]{1,0:T(8,128)(2,1)S(1)}, bf16[512,2048]{1,0:T(8,128)(2,1)}, u32[]{:S(2)}, u32[]{:S(2)}) %collective-permute-start.7) | collective-permute-done | bytes 2097184 | tf_op jit(solution)/shard_map/cond/branch_0_fun/while/body/eval_jaxpr/ppermute | solution.py:994
  1603.5 27.7 %collective-permute-done.7 = bf16[512,2048]{1,0:T(8,128)(2,1)} collective-permute-done((bf16[512,2048]{1,0:T(8,128)(2,1)S(1)}, bf16[512,2048]{1,0:T(8,128)(2,1)}, u32[]{:S(2)}, u32[]{:S(2)}) %collective-permute-start.7) | collective-permute-done | bytes 2097184 | tf_op jit(solution)/shard_map/cond/branch_0_fun/while/body/eval_jaxpr/ppermute | solution.py:994
  1634.2 27.7 %collective-permute-done.7 = bf16[512,2048]{1,0:T(8,128)(2,1)} collective-permute-done((bf16[512,2048]{1,0:T(8,128)(2,1)S(1)}, bf16[512,2048]{1,0:T(8,128)(2,1)}, u32[]{:S(2)}, u32[]{:S(2)}) %collective-permute-start.7) | collective-permute-done | bytes 2097184 | tf_op jit(solution)/shard_map/cond/branch_0_fun/while/body/eval_jaxpr/ppermute | solution.py:994
  1665.0 27.7 %collective-permute-done.7 = bf16[512,2048]{1,0:T(8,128)(2,1)} collective-permute-done((bf16[512,2048]{1,0:T(8,128)(2,1)S(1)}, bf16[512,2048]{1,0:T(8,128)(2,1)}, u32[]{:S(2)}, u32[]{:S(2)}) %collective-permute-start.7) | collective-permute-done | bytes 2097184 | tf_op jit(solution)/shard_map/cond/branch_0_fun/while/body/eval_jaxpr/ppermute | solution.py:994
  1695.7 27.7 %collective-permute-done.7 = bf16[512,2048]{1,0:T(8,128)(2,1)} collective-permute-done((bf16[512,2048]{1,0:T(8,128)(2,1)S(1)}, bf16[512,2048]{1,0:T(8,128)(2,1)}, u32[]{:S(2)}, u32[]{:S(2)}) %collective-permute-start.7) | collective-permute-done | bytes 2097184 | tf_op jit(solution)/shard_map/cond/branch_0_fun/while/body/eval_jaxpr/ppermute | solution.py:994
  1726.5 27.7 %collective-permute-done.7 = bf16[512,2048]{1,0:T(8,128)(2,1)} collective-permute-done((bf16[512,2048]{1,0:T(8,128)(2,1)S(1)}, bf16[512,2048]{1,0:T(8,128)(2,1)}, u32[]{:S(2)}, u32[]{:S(2)}) %collective-permute-start.7) | collective-permute-done | bytes 2097184 | tf_op jit(solution)/shard_map/cond/branch_0_fun/while/body/eval_jaxpr/ppermute | solution.py:994
  1757.3 27.7 %collective-permute-done.7 = bf16[512,2048]{1,0:T(8,128)(2,1)} collective-permute-done((bf16[512,2048]{1,0:T(8,128)(2,1)S(1)}, bf16[512,2048]{1,0:T(8,128)(2,1)}, u32[]{:S(2)}, u32[]{:S(2)}) %collective-permute-start.7) | collective-permute-done | bytes 2097184 | tf_op jit(solution)/shard_map/cond/branch_0_fun/while/body/eval_jaxpr/ppermute | solution.py:994
  1788.1 27.7 %collective-permute-done.7 = bf16[512,2048]{1,0:T(8,128)(2,1)} collective-permute-done((bf16[512,2048]{1,0:T(8,128)(2,1)S(1)}, bf16[512,2048]{1,0:T(8,128)(2,1)}, u32[]{:S(2)}, u32[]{:S(2)}) %collective-permute-start.7) | collective-permute-done | bytes 2097184 | tf_op jit(solution)/shard_map/cond/branch_0_fun/while/body/eval_jaxpr/ppermute | solution.py:994
  1818.8 27.7 %collective-permute-done.7 = bf16[512,2048]{1,0:T(8,128)(2,1)} collective-permute-done((bf16[512,2048]{1,0:T(8,128)(2,1)S(1)}, bf16[512,2048]{1,0:T(8,128)(2,1)}, u32[]{:S(2)}, u32[]{:S(2)}) %collective-permute-start.7) | collective-permute-done | bytes 2097184 | tf_op jit(solution)/shard_map/cond/branch_0_fun/while/body/eval_jaxpr/ppermute | solution.py:994
  1849.7 27.6 %collective-permute-done.7 = bf16[512,2048]{1,0:T(8,128)(2,1)} collective-permute-done((bf16[512,2048]{1,0:T(8,128)(2,1)S(1)}, bf16[512,2048]{1,0:T(8,128)(2,1)}, u32[]{:S(2)}, u32[]{:S(2)}) %collective-permute-start.7) | collective-permute-done | bytes 2097184 | tf_op jit(solution)/shard_map/cond/branch_0_fun/while/body/eval_jaxpr/ppermute | solution.py:994
  1880.4 27.7 %collective-permute-done.7 = bf16[512,2048]{1,0:T(8,128)(2,1)} collective-permute-done((bf16[512,2048]{1,0:T(8,128)(2,1)S(1)}, bf16[512,2048]{1,0:T(8,128)(2,1)}, u32[]{:S(2)}, u32[]{:S(2)}) %collective-permute-start.7) | collective-permute-done | bytes 2097184 | tf_op jit(solution)/shard_map/cond/branch_0_fun/while/body/eval_jaxpr/ppermute | solution.py:994
  1911.2 27.7 %collective-permute-done.7 = bf16[512,2048]{1,0:T(8,128)(2,1)} collective-permute-done((bf16[512,2048]{1,0:T(8,128)(2,1)S(1)}, bf16[512,2048]{1,0:T(8,128)(2,1)}, u32[]{:S(2)}, u32[]{:S(2)}) %collective-permute-start.7) | collective-permute-done | bytes 2097184 | tf_op jit(solution)/shard_map/cond/branch_0_fun/while/body/eval_jaxpr/ppermute | solution.py:994
  1938.9 13.0 reduce_sum.156
  1954.4 70.9 %while.152 = (s32[]{:T(128)}, bf16[2,512,2048]{2,1,0:T(8,128)(2,1)}, bf16[512,2048]{1,0:T(8,128)(2,1)}, s32[]{:T(128)}, s32[]{:T(128)}, /*index=5*/s32[]{:T(128)}, s32[]{:T(128)}) while((s32[]{:T(128)}, bf16[2,512,2048]{2,1,0:T(8,128)(2,1)}, bf16[512,2048]{1,0:T(8,128)(2,1)}, s32[]{:T(128)}, s32[]{:T(128)}, /*index=5*/s32[]{:T(128)}, ...), condition=%wide.region_34.34_spmd, body=%wide.region_33.33_spmd.sunk | while | flops 12 | bytes 16777444 | solution.py:996
  1957.8 23.2 collective-permute-done.8
  1984.3 41.0 %collective-permute-done.8 = bf16[512,2048]{1,0:T(8,128)(2,1)} collective-permute-done((bf16[512,2048]{1,0:T(8,128)(2,1)S(1)}, bf16[512,2048]{1,0:T(8,128)(2,1)}, u32[]{:S(2)}, u32[]{:S(2)}) %collective-permute-start.8) | collective-permute-done | bytes 2097184 | tf_op jit(solution)/shard_map/cond/branch_0_fun/while/body/eval_jaxpr/ppermute | solution.py:994
  2039.6 339.2 %while.149 = (s32[]{:T(128)}, bf16[16,384,1536]{2,1,0:T(8,128)(2,1)}, bf16[384,1536]{1,0:T(8,128)(2,1)S(1)}, s32[]{:T(128)}, s32[]{:T(128)}, /*index=5*/s32[]{:T(128)}, s32[]{:T(128)}, s32[]{:T(128)}) while((s32[]{:T(128)}, bf16[16,384,1536]{2,1,0:T(8,128)(2,1)}, bf16[384,1536]{1,0:T(8,128)(2,1)S(1)}, s32[]{:T(128)}, s32[]{:T(128)}, ...), condition=%wide.region_24.24_spmd, body=%wide.region_23.23_spmd.sunk | while | flops 12 | bytes 9437422 | solution.py:996
  2041.3 46.5 %collective-permute-done.5 = bf16[384,1536]{1,0:T(8,128)(2,1)S(1)} collective-permute-done((bf16[384,1536]{1,0:T(8,128)(2,1)S(1)}, bf16[384,1536]{1,0:T(8,128)(2,1)S(1)}, u32[]{:S(2)}, u32[]{:S(2)}) %collective-permute-start.5) | collective-permute-done | bytes 1179680 | tf_op jit(solution)/shard_map/cond/branch_0_fun/while/body/eval_jaxpr/ppermute | solution.py:994
  2089.1 18.1 collective-permute-done.5
  2108.5 18.1 collective-permute-done.5
  2127.9 18.1 collective-permute-done.5
  2147.3 18.1 collective-permute-done.5
  2166.7 18.1 collective-permute-done.5
  2186.1 18.1 collective-permute-done.5
  2205.5 18.0 collective-permute-done.5
  2224.9 18.1 collective-permute-done.5
  2244.3 18.1 collective-permute-done.5
  2263.7 18.0 collective-permute-done.5
  2283.1 18.1 collective-permute-done.5
  2302.4 18.1 collective-permute-done.5
  2321.8 18.1 collective-permute-done.5
  2341.2 18.1 collective-permute-done.5
  2360.6 18.1 collective-permute-done.5
  2390.6 38.9 %while.150 = (s32[]{:T(128)}, bf16[2,384,1536]{2,1,0:T(8,128)(2,1)}, bf16[384,1536]{1,0:T(8,128)(2,1)S(1)}, s32[]{:T(128)}, s32[]{:T(128)}, /*index=5*/s32[]{:T(128)}, s32[]{:T(128)}) while((s32[]{:T(128)}, bf16[2,384,1536]{2,1,0:T(8,128)(2,1)}, bf16[384,1536]{1,0:T(8,128)(2,1)S(1)}, s32[]{:T(128)}, s32[]{:T(128)}, /*index=5*/s32[]{:T(128)}, ...), condition=%wide.region_27.27_spmd, body=%wide.region_26.26_spmd.sunk | while | flops 12 | bytes 9437414 | solution.py:996
  2392.2 13.6 collective-permute-done.6
  2407.4 22.1 collective-permute-done.6
  (416 shorter events, 605.3 us)
Async XLA Ops:
  205.8 9.5 collective-permute-start
  215.3 9.5 collective-permute-start
  224.8 9.5 collective-permute-start
  234.3 9.5 collective-permute-start
  243.8 9.5 collective-permute-start
  253.3 9.5 collective-permute-start
  262.8 9.5 collective-permute-start
  272.4 9.5 collective-permute-start
  281.9 9.5 collective-permute-start
  291.4 9.5 collective-permute-start
  300.9 9.5 collective-permute-start
  310.4 9.5 collective-permute-start
  319.9 9.5 collective-permute-start
  435.2 62.5 %collective-permute-start.1 = (f32[512,1536]{1,0:T(8,128)S(1)}, f32[512,1536]{1,0:T(8,128)}, u32[]{:S(2)}, u32[]{:S(2)}) collective-permute-start(f32[512,1536]{1,0:T(8,128)S(1)} %copy.51), channel_id=1, source_target_pairs={{0,1},{1,2},{2,3},{3,0},{4,5},{5,6},{6,7},{7,4},{8,9},{9,10},{10,1... | collective-permute-start | bytes 9437192 | tf_op jit(solution)/shard_map/cond/branch_0_fun/while/body/eval_jaxpr/ppermute | solution.py:994
  499.6 64.7 %collective-permute-start.1 = (f32[512,1536]{1,0:T(8,128)S(1)}, f32[512,1536]{1,0:T(8,128)}, u32[]{:S(2)}, u32[]{:S(2)}) collective-permute-start(f32[512,1536]{1,0:T(8,128)S(1)} %copy.51), channel_id=1, source_target_pairs={{0,1},{1,2},{2,3},{3,0},{4,5},{5,6},{6,7},{7,4},{8,9},{9,10},{10,1... | collective-permute-start | bytes 9437192 | tf_op jit(solution)/shard_map/cond/branch_0_fun/while/body/eval_jaxpr/ppermute | solution.py:994
  566.1 64.7 %collective-permute-start.1 = (f32[512,1536]{1,0:T(8,128)S(1)}, f32[512,1536]{1,0:T(8,128)}, u32[]{:S(2)}, u32[]{:S(2)}) collective-permute-start(f32[512,1536]{1,0:T(8,128)S(1)} %copy.51), channel_id=1, source_target_pairs={{0,1},{1,2},{2,3},{3,0},{4,5},{5,6},{6,7},{7,4},{8,9},{9,10},{10,1... | collective-permute-start | bytes 9437192 | tf_op jit(solution)/shard_map/cond/branch_0_fun/while/body/eval_jaxpr/ppermute | solution.py:994
  632.7 64.7 %collective-permute-start.1 = (f32[512,1536]{1,0:T(8,128)S(1)}, f32[512,1536]{1,0:T(8,128)}, u32[]{:S(2)}, u32[]{:S(2)}) collective-permute-start(f32[512,1536]{1,0:T(8,128)S(1)} %copy.51), channel_id=1, source_target_pairs={{0,1},{1,2},{2,3},{3,0},{4,5},{5,6},{6,7},{7,4},{8,9},{9,10},{10,1... | collective-permute-start | bytes 9437192 | tf_op jit(solution)/shard_map/cond/branch_0_fun/while/body/eval_jaxpr/ppermute | solution.py:994
  720.4 12.2 collective-permute-start.2
  732.6 11.2 collective-permute-start.2
  743.9 10.3 collective-permute-start.2
  762.4 16.9 collective-permute-start.3
  779.3 12.1 collective-permute-start.3
  791.4 9.5 collective-permute-start.3
  800.9 9.5 collective-permute-start.3
  1067.9 85.2 %collective-permute-start.4 = (f32[512,2048]{1,0:T(8,128)}, f32[512,2048]{1,0:T(8,128)}, u32[]{:S(2)}, u32[]{:S(2)}) collective-permute-start(f32[512,2048]{1,0:T(8,128)} %copy.78), channel_id=1, source_target_pairs={{0,1},{1,2},{2,3},{3,0},{4,5},{5,6},{6,7},{7,4},{8,9},{9,10},{10,1... | collective-permute-start | bytes 12582920 | tf_op jit(solution)/shard_map/cond/branch_0_fun/while/body/eval_jaxpr/ppermute | solution.py:994
  1157.8 84.3 %collective-permute-start.4 = (f32[512,2048]{1,0:T(8,128)}, f32[512,2048]{1,0:T(8,128)}, u32[]{:S(2)}, u32[]{:S(2)}) collective-permute-start(f32[512,2048]{1,0:T(8,128)} %copy.78), channel_id=1, source_target_pairs={{0,1},{1,2},{2,3},{3,0},{4,5},{5,6},{6,7},{7,4},{8,9},{9,10},{10,1... | collective-permute-start | bytes 12582920 | tf_op jit(solution)/shard_map/cond/branch_0_fun/while/body/eval_jaxpr/ppermute | solution.py:994
  1246.8 84.3 %collective-permute-start.4 = (f32[512,2048]{1,0:T(8,128)}, f32[512,2048]{1,0:T(8,128)}, u32[]{:S(2)}, u32[]{:S(2)}) collective-permute-start(f32[512,2048]{1,0:T(8,128)} %copy.78), channel_id=1, source_target_pairs={{0,1},{1,2},{2,3},{3,0},{4,5},{5,6},{6,7},{7,4},{8,9},{9,10},{10,1... | collective-permute-start | bytes 12582920 | tf_op jit(solution)/shard_map/cond/branch_0_fun/while/body/eval_jaxpr/ppermute | solution.py:994
  1335.8 84.3 %collective-permute-start.4 = (f32[512,2048]{1,0:T(8,128)}, f32[512,2048]{1,0:T(8,128)}, u32[]{:S(2)}, u32[]{:S(2)}) collective-permute-start(f32[512,2048]{1,0:T(8,128)} %copy.78), channel_id=1, source_target_pairs={{0,1},{1,2},{2,3},{3,0},{4,5},{5,6},{6,7},{7,4},{8,9},{9,10},{10,1... | collective-permute-start | bytes 12582920 | tf_op jit(solution)/shard_map/cond/branch_0_fun/while/body/eval_jaxpr/ppermute | solution.py:994
  1456.7 24.4 %collective-permute-start.7 = (bf16[512,2048]{1,0:T(8,128)(2,1)S(1)}, bf16[512,2048]{1,0:T(8,128)(2,1)}, u32[]{:S(2)}, u32[]{:S(2)}) collective-permute-start(bf16[512,2048]{1,0:T(8,128)(2,1)S(1)} %copy.105), channel_id=1, source_target_pairs={{0,8},{8,16},{16,24},{24,32},{32,40},{40,48},{48,56},{56,64},{64,7... | collective-permute-start | bytes 6291464 | tf_op jit(solution)/shard_map/cond/branch_0_fun/while/body/eval_jaxpr/ppermute | solution.py:994
  1482.7 27.1 %collective-permute-start.7 = (bf16[512,2048]{1,0:T(8,128)(2,1)S(1)}, bf16[512,2048]{1,0:T(8,128)(2,1)}, u32[]{:S(2)}, u32[]{:S(2)}) collective-permute-start(bf16[512,2048]{1,0:T(8,128)(2,1)S(1)} %copy.105), channel_id=1, source_target_pairs={{0,8},{8,16},{16,24},{24,32},{32,40},{40,48},{48,56},{56,64},{64,7... | collective-permute-start | bytes 6291464 | tf_op jit(solution)/shard_map/cond/branch_0_fun/while/body/eval_jaxpr/ppermute | solution.py:994
  1511.4 27.4 %collective-permute-start.7 = (bf16[512,2048]{1,0:T(8,128)(2,1)S(1)}, bf16[512,2048]{1,0:T(8,128)(2,1)}, u32[]{:S(2)}, u32[]{:S(2)}) collective-permute-start(bf16[512,2048]{1,0:T(8,128)(2,1)S(1)} %copy.105), channel_id=1, source_target_pairs={{0,8},{8,16},{16,24},{24,32},{32,40},{40,48},{48,56},{56,64},{64,7... | collective-permute-start | bytes 6291464 | tf_op jit(solution)/shard_map/cond/branch_0_fun/while/body/eval_jaxpr/ppermute | solution.py:994
  1540.4 29.2 %collective-permute-start.7 = (bf16[512,2048]{1,0:T(8,128)(2,1)S(1)}, bf16[512,2048]{1,0:T(8,128)(2,1)}, u32[]{:S(2)}, u32[]{:S(2)}) collective-permute-start(bf16[512,2048]{1,0:T(8,128)(2,1)S(1)} %copy.105), channel_id=1, source_target_pairs={{0,8},{8,16},{16,24},{24,32},{32,40},{40,48},{48,56},{56,64},{64,7... | collective-permute-start | bytes 6291464 | tf_op jit(solution)/shard_map/cond/branch_0_fun/while/body/eval_jaxpr/ppermute | solution.py:994
  1571.2 29.2 %collective-permute-start.7 = (bf16[512,2048]{1,0:T(8,128)(2,1)S(1)}, bf16[512,2048]{1,0:T(8,128)(2,1)}, u32[]{:S(2)}, u32[]{:S(2)}) collective-permute-start(bf16[512,2048]{1,0:T(8,128)(2,1)S(1)} %copy.105), channel_id=1, source_target_pairs={{0,8},{8,16},{16,24},{24,32},{32,40},{40,48},{48,56},{56,64},{64,7... | collective-permute-start | bytes 6291464 | tf_op jit(solution)/shard_map/cond/branch_0_fun/while/body/eval_jaxpr/ppermute | solution.py:994
  1602.0 29.2 %collective-permute-start.7 = (bf16[512,2048]{1,0:T(8,128)(2,1)S(1)}, bf16[512,2048]{1,0:T(8,128)(2,1)}, u32[]{:S(2)}, u32[]{:S(2)}) collective-permute-start(bf16[512,2048]{1,0:T(8,128)(2,1)S(1)} %copy.105), channel_id=1, source_target_pairs={{0,8},{8,16},{16,24},{24,32},{32,40},{40,48},{48,56},{56,64},{64,7... | collective-permute-start | bytes 6291464 | tf_op jit(solution)/shard_map/cond/branch_0_fun/while/body/eval_jaxpr/ppermute | solution.py:994
  1632.7 29.2 %collective-permute-start.7 = (bf16[512,2048]{1,0:T(8,128)(2,1)S(1)}, bf16[512,2048]{1,0:T(8,128)(2,1)}, u32[]{:S(2)}, u32[]{:S(2)}) collective-permute-start(bf16[512,2048]{1,0:T(8,128)(2,1)S(1)} %copy.105), channel_id=1, source_target_pairs={{0,8},{8,16},{16,24},{24,32},{32,40},{40,48},{48,56},{56,64},{64,7... | collective-permute-start | bytes 6291464 | tf_op jit(solution)/shard_map/cond/branch_0_fun/while/body/eval_jaxpr/ppermute | solution.py:994
  1663.5 29.2 %collective-permute-start.7 = (bf16[512,2048]{1,0:T(8,128)(2,1)S(1)}, bf16[512,2048]{1,0:T(8,128)(2,1)}, u32[]{:S(2)}, u32[]{:S(2)}) collective-permute-start(bf16[512,2048]{1,0:T(8,128)(2,1)S(1)} %copy.105), channel_id=1, source_target_pairs={{0,8},{8,16},{16,24},{24,32},{32,40},{40,48},{48,56},{56,64},{64,7... | collective-permute-start | bytes 6291464 | tf_op jit(solution)/shard_map/cond/branch_0_fun/while/body/eval_jaxpr/ppermute | solution.py:994
  1694.3 29.2 %collective-permute-start.7 = (bf16[512,2048]{1,0:T(8,128)(2,1)S(1)}, bf16[512,2048]{1,0:T(8,128)(2,1)}, u32[]{:S(2)}, u32[]{:S(2)}) collective-permute-start(bf16[512,2048]{1,0:T(8,128)(2,1)S(1)} %copy.105), channel_id=1, source_target_pairs={{0,8},{8,16},{16,24},{24,32},{32,40},{40,48},{48,56},{56,64},{64,7... | collective-permute-start | bytes 6291464 | tf_op jit(solution)/shard_map/cond/branch_0_fun/while/body/eval_jaxpr/ppermute | solution.py:994
  1725.0 29.2 %collective-permute-start.7 = (bf16[512,2048]{1,0:T(8,128)(2,1)S(1)}, bf16[512,2048]{1,0:T(8,128)(2,1)}, u32[]{:S(2)}, u32[]{:S(2)}) collective-permute-start(bf16[512,2048]{1,0:T(8,128)(2,1)S(1)} %copy.105), channel_id=1, source_target_pairs={{0,8},{8,16},{16,24},{24,32},{32,40},{40,48},{48,56},{56,64},{64,7... | collective-permute-start | bytes 6291464 | tf_op jit(solution)/shard_map/cond/branch_0_fun/while/body/eval_jaxpr/ppermute | solution.py:994
  1755.8 29.2 %collective-permute-start.7 = (bf16[512,2048]{1,0:T(8,128)(2,1)S(1)}, bf16[512,2048]{1,0:T(8,128)(2,1)}, u32[]{:S(2)}, u32[]{:S(2)}) collective-permute-start(bf16[512,2048]{1,0:T(8,128)(2,1)S(1)} %copy.105), channel_id=1, source_target_pairs={{0,8},{8,16},{16,24},{24,32},{32,40},{40,48},{48,56},{56,64},{64,7... | collective-permute-start | bytes 6291464 | tf_op jit(solution)/shard_map/cond/branch_0_fun/while/body/eval_jaxpr/ppermute | solution.py:994
  1786.6 29.2 %collective-permute-start.7 = (bf16[512,2048]{1,0:T(8,128)(2,1)S(1)}, bf16[512,2048]{1,0:T(8,128)(2,1)}, u32[]{:S(2)}, u32[]{:S(2)}) collective-permute-start(bf16[512,2048]{1,0:T(8,128)(2,1)S(1)} %copy.105), channel_id=1, source_target_pairs={{0,8},{8,16},{16,24},{24,32},{32,40},{40,48},{48,56},{56,64},{64,7... | collective-permute-start | bytes 6291464 | tf_op jit(solution)/shard_map/cond/branch_0_fun/while/body/eval_jaxpr/ppermute | solution.py:994
  1817.4 29.2 %collective-permute-start.7 = (bf16[512,2048]{1,0:T(8,128)(2,1)S(1)}, bf16[512,2048]{1,0:T(8,128)(2,1)}, u32[]{:S(2)}, u32[]{:S(2)}) collective-permute-start(bf16[512,2048]{1,0:T(8,128)(2,1)S(1)} %copy.105), channel_id=1, source_target_pairs={{0,8},{8,16},{16,24},{24,32},{32,40},{40,48},{48,56},{56,64},{64,7... | collective-permute-start | bytes 6291464 | tf_op jit(solution)/shard_map/cond/branch_0_fun/while/body/eval_jaxpr/ppermute | solution.py:994
  1848.1 29.2 %collective-permute-start.7 = (bf16[512,2048]{1,0:T(8,128)(2,1)S(1)}, bf16[512,2048]{1,0:T(8,128)(2,1)}, u32[]{:S(2)}, u32[]{:S(2)}) collective-permute-start(bf16[512,2048]{1,0:T(8,128)(2,1)S(1)} %copy.105), channel_id=1, source_target_pairs={{0,8},{8,16},{16,24},{24,32},{32,40},{40,48},{48,56},{56,64},{64,7... | collective-permute-start | bytes 6291464 | tf_op jit(solution)/shard_map/cond/branch_0_fun/while/body/eval_jaxpr/ppermute | solution.py:994
  1878.9 29.2 %collective-permute-start.7 = (bf16[512,2048]{1,0:T(8,128)(2,1)S(1)}, bf16[512,2048]{1,0:T(8,128)(2,1)}, u32[]{:S(2)}, u32[]{:S(2)}) collective-permute-start(bf16[512,2048]{1,0:T(8,128)(2,1)S(1)} %copy.105), channel_id=1, source_target_pairs={{0,8},{8,16},{16,24},{24,32},{32,40},{40,48},{48,56},{56,64},{64,7... | collective-permute-start | bytes 6291464 | tf_op jit(solution)/shard_map/cond/branch_0_fun/while/body/eval_jaxpr/ppermute | solution.py:994
  1909.7 29.2 %collective-permute-start.7 = (bf16[512,2048]{1,0:T(8,128)(2,1)S(1)}, bf16[512,2048]{1,0:T(8,128)(2,1)}, u32[]{:S(2)}, u32[]{:S(2)}) collective-permute-start(bf16[512,2048]{1,0:T(8,128)(2,1)S(1)} %copy.105), channel_id=1, source_target_pairs={{0,8},{8,16},{16,24},{24,32},{32,40},{40,48},{48,56},{56,64},{64,7... | collective-permute-start | bytes 6291464 | tf_op jit(solution)/shard_map/cond/branch_0_fun/while/body/eval_jaxpr/ppermute | solution.py:994
  1955.9 25.0 %collective-permute-start.8 = (bf16[512,2048]{1,0:T(8,128)(2,1)S(1)}, bf16[512,2048]{1,0:T(8,128)(2,1)}, u32[]{:S(2)}, u32[]{:S(2)}) collective-permute-start(bf16[512,2048]{1,0:T(8,128)(2,1)S(1)} %copy.114), channel_id=1, source_target_pairs={{0,4},{4,0},{1,5},{5,1},{2,6},{6,2},{3,7},{7,3},{8,12},{12,8},{9,1... | collective-permute-start | bytes 6291464 | tf_op jit(solution)/shard_map/cond/branch_0_fun/while/body/eval_jaxpr/ppermute | solution.py:994
  1982.5 42.7 %collective-permute-start.8 = (bf16[512,2048]{1,0:T(8,128)(2,1)S(1)}, bf16[512,2048]{1,0:T(8,128)(2,1)}, u32[]{:S(2)}, u32[]{:S(2)}) collective-permute-start(bf16[512,2048]{1,0:T(8,128)(2,1)S(1)} %copy.114), channel_id=1, source_target_pairs={{0,4},{4,0},{1,5},{5,1},{2,6},{6,2},{3,7},{7,3},{8,12},{12,8},{9,1... | collective-permute-start | bytes 6291464 | tf_op jit(solution)/shard_map/cond/branch_0_fun/while/body/eval_jaxpr/ppermute | solution.py:994
  2039.6 48.2 %collective-permute-start.5 = (bf16[384,1536]{1,0:T(8,128)(2,1)S(1)}, bf16[384,1536]{1,0:T(8,128)(2,1)S(1)}, u32[]{:S(2)}, u32[]{:S(2)}) collective-permute-start(bf16[384,1536]{1,0:T(8,128)(2,1)S(1)} %copy.87), channel_id=1, source_target_pairs={{0,8},{8,16},{16,24},{24,32},{32,40},{40,48},{48,56},{56,64},{64,7... | collective-permute-start | bytes 3538952 | tf_op jit(solution)/shard_map/cond/branch_0_fun/while/body/eval_jaxpr/ppermute | solution.py:994
  2087.9 19.3 collective-permute-start.5
  2107.3 19.3 collective-permute-start.5
  2126.7 19.3 collective-permute-start.5
  2146.1 19.3 collective-permute-start.5
  2165.5 19.3 collective-permute-start.5
  2184.9 19.3 collective-permute-start.5
  2204.3 19.3 collective-permute-start.5
  2223.7 19.3 collective-permute-start.5
  2243.1 19.3 collective-permute-start.5
  2262.4 19.3 collective-permute-start.5
  2281.8 19.3 collective-permute-start.5
  2301.2 19.3 collective-permute-start.5
  2320.6 19.3 collective-permute-start.5
  2340.0 19.3 collective-permute-start.5
  2359.4 19.3 collective-permute-start.5
  2390.7 15.1 collective-permute-start.6
  2405.9 23.7 collective-permute-start.6
  (58 other events, 1019.5 us)

commit v7 on v6

--- a/solution.py
+++ b/solution.py
@@ -70,10 +70,102 @@
 PIECES = 2
 
 
+class WeightGather:
+    def __init__(self, columns, own_ref, full_ref, semaphores):
+        self.own, self.full = own_ref, full_ref
+        self.send, self.recv, self.local = semaphores
+        self.columns = pl.ds(*columns)
+        self.piece = own_ref.shape[0] // 4
+        me = lax.axis_index("rep")
+        self.core = lax.rem(me, 2)
+        self.other = me + 1 - 2 * self.core
+        self.ypos = lax.axis_index("mdl")
+        self.yp = lax.rem(self.ypos + 1, 4)
+        self.ym = lax.rem(self.ypos + 3, 4)
+        self.src = [self.ym, self.yp, lax.rem(self.ypos + 2, 4)]
+
+    def span(self, which, part):
+        return pl.ds(pl.multiple_of((2 * which + part) * self.piece, 16), self.piece)
+
+    def copy(self, source_y, part, slot, target, lane, own=False):
+        span = self.span(self.core, part)
+        where = self.full.at[source_y, span]
+        return pltpu.make_async_remote_copy(
+            src_ref=self.own.at[span, self.columns] if own else where,
+            dst_ref=where,
+            send_sem=self.send.at[lane, part],
+            recv_sem=self.recv.at[slot, part],
+            device_id=target,
+            device_id_type=MESH,
+        )
+
+    def first(self):
+        up, down = {"mdl": self.yp}, {"mdl": self.ym}
+        return [
+            self.copy(self.ypos, 0, 0, up, 0, own=True),
+            self.copy(self.ypos, 1, 1, down, 1, own=True),
+            self.copy(self.ypos, 1, 0, up, 0, own=True),
+            self.copy(self.ypos, 0, 1, down, 1, own=True),
+        ]
+
+    def kept(self):
+        return pltpu.make_async_copy(
+            self.own.at[:, self.columns], self.full.at[self.ypos], self.local.at[0]
+        )
+
+    def start(self):
+        for item in self.first():
+            item.start()
+        self.kept().start()
+
+    def relay(self, part):
+        if part == 0:
+            return self.copy(self.ym, 0, 2, {"mdl": self.yp}, 2)
+        return self.copy(self.yp, 1, 2, {"mdl": self.ym}, 2)
+
+    def share(self, slot, part):
+        return self.copy(self.src[slot], part, 3 + slot, {"rep": self.other}, 3 + slot)
+
+    def arrived(self, slot, part):
+        which = self.core if slot < 3 else 1 - self.core
+        where = self.full.at[self.src[slot % 3], self.span(which, part)]
+        pltpu.make_async_copy(where, where, self.recv.at[slot, part]).wait()
+
+    def pass_on(self):
+        for part in range(2):
+            self.arrived(part, part)
+            self.relay(part).start()
+            self.share(part, part).start()
+
+    def take_rest(self):
+        for part in range(2):
+            self.arrived(1 - part, part)
+            self.share(1 - part, part).start()
+
+    def take_last(self):
+        for part in range(2):
+            self.arrived(2, part)
+            self.share(2, part).start()
+
+    def finish(self):
+        for slot in range(3, 6):
+            for part in range(2):
+                self.arrived(slot, part)
+        for item in self.first():
+            item.wait_send()
+        for part in range(2):
+            self.relay(part).wait_send()
+            for slot in range(3):
+                self.share(slot, part).wait_send()
+        self.kept().wait()
+
+
 def attend_kernel(
-    heads, count_ref, x_ref, wq_ref, wkv_ref, w_ref, out_ref, wfull_ref, *refs
+    heads, spans, count_ref, x_ref, wq_ref, wkv_ref, *refs
 ):
-    buf, acc, q_ref, kv_ref, send, recv, local, wsend, wrecv, wlocal = refs
+    each = len(spans)
+    w_refs, out_ref, full_refs = refs[:each], refs[each], refs[each + 1 : 2 * each + 1]
+    buf, acc, q_ref, kv_ref, send, recv, local, *w_semaphores = refs[2 * each + 1 :]
     rows = x_ref.shape[0]
     piece = rows // PIECES
     all_keys = buf.shape[0]
@@ -99,13 +191,20 @@
     ypos = lax.axis_index("mdl")
     yp = lax.rem(ypos + 1, 4)
     ym = lax.rem(ypos + 3, 4)
-    y2 = lax.rem(ypos + 2, 4)
 
     barrier = pltpu.get_barrier_semaphore()
     peers = [{"rep": zp}, {"rep": zm}, {"rep": xpeer}, {"rep": other}]
     peers += [{"mdl": yp}, {"mdl": ym}]
     for peer in peers:
         pl.semaphore_signal(barrier, inc=1, device_id=peer, device_id_type=MESH)
+
+    rings = [
+        WeightGather(columns, w_refs[k], full_refs[k], w_semaphores[3 * k : 3 * k + 3])
+        for k, columns in enumerate(spans)
+    ]
+    pl.semaphore_wait(barrier, len(peers))
+    for ring in rings:
+        ring.start()
 
     total = count_ref[lax.axis_index("sec")]
     normed = rms_normed(x_ref[...].astype(F32)).astype(BF)
@@ -113,7 +212,6 @@
     for part in range(2):
         made = jnp.dot(normed, wkv_ref[part], preferred_element_type=F32)
         kv_ref[:, part * HEAD : (part + 1) * HEAD] = jnp.where(live, made, 0.0).astype(BF)
-    pl.semaphore_wait(barrier, len(peers))
 
     def block_rows(block, part):
         return pl.ds(pl.multiple_of(block * rows + part * piece, piece), piece)
@@ -178,49 +276,6 @@
     )
     own_copy.start()
 
-    wrows = w_ref.shape[0]
-    wpiece = wrows // 4
-    wown = pltpu.make_async_copy(w_ref, wfull_ref.at[ypos], wlocal.at[0])
-    wown.start()
-
-    wsrc = [ym, yp, y2]
-
-    def wcopy(source_y, which, part, slot, target, lane, own=False):
-        span = pl.ds((2 * which + part) * wpiece, wpiece)
-        where = wfull_ref.at[source_y, span]
-        return pltpu.make_async_remote_copy(
-            src_ref=w_ref.at[span] if own else where,
-            dst_ref=where,
-            send_sem=wsend.at[lane, part],
-            recv_sem=wrecv.at[slot, part],
-            device_id=target,
-            device_id_type=MESH,
-        )
-
-    def wfirst(part):
-        return [
-            wcopy(ypos, core, part, 0, {"mdl": yp}, 0, own=True),
-            wcopy(ypos, core, part, 1, {"mdl": ym}, 1, own=True),
-        ]
-
-    def wrelay(part):
-        if part == 0:
-            return wcopy(ym, core, 0, 2, {"mdl": yp}, 2)
-        return wcopy(yp, core, 1, 2, {"mdl": ym}, 2)
-
-    def wshare(slot, part):
-        return wcopy(wsrc[slot], core, part, 3 + slot, {"rep": other}, 3 + slot)
-
-    def warrived(slot, part):
-        which = core if slot < 3 else 1 - core
-        span = pl.ds((2 * which + part) * wpiece, wpiece)
-        where = wfull_ref.at[wsrc[slot % 3], span]
-        pltpu.make_async_copy(where, where, wrecv.at[slot, part]).wait()
-
-    for part in range(2):
-        for copy in wfirst(part):
-            copy.start()
-
     queries = jnp.dot(normed, wq_ref[...], preferred_element_type=F32) * (HEAD ** (-0.5) * LOG2E)
     for head in range(heads):
         q_ref[head * rows : (head + 1) * rows, :] = queries[
@@ -260,14 +315,9 @@
             pass_on(5)
             take(11)
 
-        @pl.when(i == 5)
-        def _():
-            for part in range(2):
-                warrived(0, part)
-                warrived(1, part)
-                wrelay(part).start()
-                wshare(0, part).start()
-                wshare(1, part).start()
+        for k, ring in enumerate(rings):
+            pl.when(i == 3 + 2 * k)(ring.pass_on)
+            pl.when(i == (5, 7)[k] if each > 1 else i == 7)(ring.take_rest)
 
         @pl.when(i == 5)
         def _():
@@ -300,9 +350,8 @@
 
     lax.fori_loop(0, 8, step, 0)
 
-    for part in range(2):
-        warrived(2, part)
-        wshare(2, part).start()
+    for ring in rings:
+        ring.take_last()
 
     for head in range(heads):
         part = acc[head * rows : (head + 1) * rows, :]
@@ -312,35 +361,30 @@
             safe, part[:, :HEAD] / sums, jnp.nan
         ).astype(BF)
 
-    for slot in range(3, 6):
-        for part in range(2):
-            warrived(slot, part)
-    for part in range(2):
-        for copy in wfirst(part):
-            copy.wait_send()
-        wrelay(part).wait_send()
-        for slot in range(3):
-            wshare(slot, part).wait_send()
-    wown.wait()
+    for ring in rings:
+        ring.finish()
     for part in range(PIECES):
         for index in range(len(plan)):
             plan_copy(index, part).wait_send()
 
 
-def attend_call(counts, source, w_query, w_keyval, w, ident):
+def attend_call(counts, source, w_query, w_keyval, weights, ident):
     heads = w_query.shape[1] // HEAD
     rows = source.shape[0]
     keys = rows * 16
     vmem = pl.BlockSpec(memory_space=pltpu.VMEM)
     anywhere = pl.BlockSpec(memory_space=pl.ANY)
     return pl.pallas_call(
-        functools.partial(attend_kernel, heads),
+        functools.partial(attend_kernel, heads, tuple(columns for _, columns in weights)),
         out_shape=[
             jax.ShapeDtypeStruct((rows, heads * HEAD), BF),
-            jax.ShapeDtypeStruct((4,) + w.shape, BF),
+        ]
+        + [
+            jax.ShapeDtypeStruct((4, w.shape[0], columns[1]), BF) for w, columns in weights
         ],
-        in_specs=[pl.BlockSpec(memory_space=pltpu.SMEM), vmem, vmem, vmem, anywhere],
-        out_specs=[vmem, anywhere],
+        in_specs=[pl.BlockSpec(memory_space=pltpu.SMEM), vmem, vmem, vmem]
+        + [anywhere] * len(weights),
+        out_specs=[vmem] + [anywhere] * len(weights),
         scratch_shapes=[
             pltpu.VMEM((keys, 3 * HEAD), BF),
             pltpu.VMEM((heads * rows, 2 * HEAD), F32),
@@ -349,10 +393,13 @@
             pltpu.SemaphoreType.DMA((15, PIECES)),
             pltpu.SemaphoreType.DMA((15, PIECES)),
             pltpu.SemaphoreType.DMA((1,)),
+        ]
+        + [
             pltpu.SemaphoreType.DMA((6, 2)),
             pltpu.SemaphoreType.DMA((6, 2)),
             pltpu.SemaphoreType.DMA((1,)),
-        ],
+        ]
+        * len(weights),
         compiler_params=pltpu.CompilerParams(
             collective_id=ident, has_side_effects=True, vmem_limit_bytes=40 * 2**20
         ),
@@ -361,7 +408,7 @@
             bytes_accessed=keys * 4 * HEAD,
             transcendentals=heads * rows * keys,
         ),
-    )(counts, source, w_query, w_keyval, w)
+    )(counts, source, w_query, w_keyval, *(w for w, _ in weights))
 
 
 def careful_kernel(total_ref, q_ref, kv_ref, out_ref, top, acc, total_sum):
@@ -871,7 +918,8 @@
     )(counts, hidden, c_in, w_policy, action, advantage, old_values, attended)
 
 
-def output_kernel(shape, x_ref, w_ref, base_ref, *refs):
+def output_kernel(shape, starts, x_ref, base_ref, *refs):
+    w_refs, refs = refs[: len(starts)], refs[len(starts) :]
     if shape is None:
         out_ref, acc, blocks, send, recv = refs
         work = None
@@ -895,16 +943,20 @@
     ring.start()
     if work is not None:
         work.second_scatter()
-    acc[...] = base_ref[...].astype(F32) + jnp.dot(
-        x_ref[...], w_ref[ring.ypos], preferred_element_type=F32
-    )
+    for start, w_ref in zip(starts, w_refs):
+        columns = slice(start, start + w_ref.shape[2])
+        acc[:, columns] = base_ref[:, columns].astype(F32) + jnp.dot(
+            x_ref[...], w_ref[ring.ypos], preferred_element_type=F32
+        )
 
     def add(slot, part):
         source_y = (ring.ym, ring.yp, ring.y2)[slot]
         span = pl.ds(part * half, half)
-        acc[span, :] += jnp.dot(
-            blocks[slot, span, :], w_ref[source_y], preferred_element_type=F32
-        )
+        for start, w_ref in zip(starts, w_refs):
+            columns = slice(start, start + w_ref.shape[2])
+            acc[span, columns] += jnp.dot(
+                blocks[slot, span, :], w_ref[source_y], preferred_element_type=F32
+            )
 
     if work is not None:
         work.first_gather()
@@ -938,12 +990,15 @@
     ring.wait_sent()
 
 
-def output_call(x, w_full, base, value_args, ident):
+def output_call(x, weights, base, value_args, ident):
     rows, width = x.shape
-    columns = w_full.shape[2]
+    columns = base.shape[1]
+    starts = []
+    for w_full in weights:
+        starts.append(sum(other.shape[2] for other in weights[: len(starts)]))
     vmem = pl.BlockSpec(memory_space=pltpu.VMEM)
-    args = [x, w_full, base]
-    in_specs = [vmem] * 3
+    args = [x, base] + list(weights)
+    in_specs = [vmem] * len(args)
     out_shape = [jax.ShapeDtypeStruct((rows, columns), BF)]
     scratch = [
         pltpu.VMEM((rows, columns), F32),
@@ -961,7 +1016,7 @@
         out_shape.append(jax.ShapeDtypeStruct((shape.rows, shape.columns), BF))
         scratch += shape.sub_scratch() + shape.semaphores()
     return pl.pallas_call(
-        functools.partial(output_kernel, shape),
+        functools.partial(output_kernel, shape, tuple(starts)),
         out_shape=out_shape,
         in_specs=in_specs,
         out_specs=[vmem] * len(out_shape),
@@ -1076,18 +1131,26 @@
             total.reshape(1),
         )
 
-    attended, a_out_full = attend_call(robot_count, obs[0], a_query, a_keyval, a_out, 1)
-    (hidden,) = output_call(attended, a_out_full, obs[0], None, 3)
+    early = c_out.shape[1] // 4
+    attended, a_out_full, c_out_early = attend_call(
+        robot_count,
+        obs[0],
+        a_query,
+        a_keyval,
+        [(a_out, (0, a_out.shape[1])), (c_out, (0, early))],
+        1,
+    )
+    (hidden,) = output_call(attended, [a_out_full], obs[0], None, 3)
     embedded, *sums = policy_call(
         robot_count, hidden, c_in, w_policy, actions, advantages, old_logp, attended, 4
     )
-    critic_attended, c_out_full = attend_call(
-        robot_count, embedded, c_query, c_keyval, c_out, 2
+    critic_attended, c_out_late = attend_call(
+        robot_count, embedded, c_query, c_keyval, [(c_out, (early, 3 * early))], 2
     )
     shape = Geometry(attended.shape[1], hidden.shape[1], False)
     values, dmixed, actor_summed = output_call(
         critic_attended,
-        c_out_full,
+        [c_out_early, c_out_late],
         embedded,
         (shape, robot_count, returns, w_value[None, :], sums),
         5,

time: 2460 us -> 2460 us (level)
  no operation moved by 1% of the time
where the time goes in v7:
time: 2460 us; the launch traced here: 2430 us
  waiting for transfers between devices  1710 us (70%)
  Pallas kernels  392 us (16%)
  local copies, waits for them, and re-layouts  204 us (8%)
  other arithmetic  62.6 us (3%)
  starting transfers between devices  39.7 us (2%)
    ppermute x80, waiting for transfers between devices, turn(): return (blocks, lax.ppermute(moving, axis, onward))  1710 us
    pallas_call x2, Pallas kernels, careful_call(): pl.pallas_call(careful_kernel, out_shape=jax.ShapeDtypeStruct((rows, head...  216 us
    another operation x89, local copies, waits for them, and re-layouts  97.8 us
    dynamic_update_slice x80, local copies, waits for them, and re-layouts, turn(): lax.dynamic_update_index_in_dim(blocks, moving, lax.rem(me + count - k, c...  96.1 us
    pallas_call x2, Pallas kernels, attend_call(): pl.pallas_call(functools.partial(attend_kernel, heads, tuple((columns for...  79 us
    reduce_sum x6, other arithmetic, ring_sum(): return jnp.sum(ring_gather(block, axis).astype(F32), axis=0)  49.7 us
  transfers between devices with their start and end apart: 80, of which 80 were waited for; matrix products, arithmetic and copies ran while one was open for 4% of the time, Pallas kernels for 0%

profile of v7, /device:TPU:1, one launch (start us, length us, event | category | flops | bytes accessed | tf_op | source)
XLA Modules:
  0.0 2433.9 jit_solution(6395496710102510450)
XLA Ops:
  0.6 41.7 %shard_map.172 = (bf16[512,384]{1,0:T(8,128)(2,1)S(1)}, bf16[4,384,1536]{2,1,0:T(8,128)(2,1)S(1)}, bf16[4,512,512]{2,1,0:T(8,128)(2,1)S(1)}) custom-call(s32[2]{0:T(128)} %refs_2_.1, bf16[512,1536]{1,0:T(8,128)(2,1)} %bitcast.115, bf16[1536,384]{1,0:T(8,128)(2,1)} %wq_ref.2, bf16[2,1536,128]{2,1,0:T(8,128)(2,1)} %wkv_ref.2, bf16[384,1536]{1,0:T(8,128)(2,1)} %refs_0_.2, ...), custom_call_target="tpu_custom_call" | custom-call | flops 6442450944 | bytes 4194304 | tf_op jit(solution)/shard_map/pallas_call | solution.py:377
  42.4 17.7 shard_map.173.x_ref
  60.2 23.6 shard_map.174
  83.8 37.3 %shard_map.175 = (bf16[512,512]{1,0:T(8,128)(2,1)S(1)}, bf16[4,512,1536]{2,1,0:T(8,128)(2,1)S(1)}) custom-call(s32[2]{0:T(128)S(1)} %copy-done.35, bf16[512,2048]{1,0:T(8,128)(2,1)S(1)} %get-tuple-element.1033.x_ref.base_ref, bf16[2048,512]{1,0:T(8,128)(2,1)S(1)} %copy-done.38, bf16[2,2048,128]{2,1,0:T(8,128)(2,1)S(1)} %copy-done.40, ...), custom_call_target="tpu_custom_call" | custom-call | flops 8589934592 | bytes 4194304 | tf_op jit(solution)/shard_map/pallas_call | solution.py:377
  121.1 27.5 %shard_map.176 = (f32[1,128]{1,0:T(1,128)}, bf16[512,2048]{1,0:T(8,128)(2,1)S(1)}, bf16[384,1536]{1,0:T(8,128)(2,1)}) custom-call(bf16[512,512]{1,0:T(8,128)(2,1)S(1)} %get-tuple-element.1034.x_ref.att_ref, bf16[512,2048]{1,0:T(8,128)(2,1)S(1)} %get-tuple-element.1033.x_ref.base_ref, bf16[4,512,512]{2,1,0:T(8,128)(2,1)S(1)} %get-tuple-element.1035.refs_0_, ...), custom_call_target="tpu_custom_call" | custom-call | tf_op jit(solution)/shard_map/pallas_call | solution.py:1018
  148.6 28.3 %shard_map.177 = bf16[512,2048]{1,0:T(8,128)(2,1)S(1)} custom-call(bf16[512,512]{1,0:T(8,128)(2,1)S(1)} %get-tuple-element.1034.x_ref.att_ref, bf16[512,2048]{1,0:T(8,128)(2,1)S(1)} %get-tuple-element.1039.d_ref), custom_call_target="tpu_custom_call" | custom-call | tf_op jit(solution)/shard_map/pallas_call | solution.py:819
  178.7 2253.2 %conditional.1 = (f32[1,128]{1,0:T(1,128)}, f32[384,1536]{1,0:T(8,128)S(1)}, f32[512,2048]{1,0:T(8,128)}) conditional(s32[]{:T(128)} %bitcast.34, (bf16[1,512,1536]{2,1,0:T(8,128)(2,1)S(1)}, s32[2]{0:T(128)S(1)}, bf16[1536,384]{1,0:T(8,128)(2,1)}, bf16[2,1536,128]{2,1,0:T(8,128)(2,1)S(1)}, bf16[384,1536]{1,0:T(8,128)(2,1)S(1)}, ...), branch_computations={%region_0.36_spmd, %region_36.37_spmd} | conditional | flops 7342663680 | bytes 525171424 | solution.py:1160
  183.9 143.9 %while.144 = (s32[]{:T(128)}, bf16[16,512,256]{2,1,0:T(8,128)(2,1)}, bf16[512,256]{1,0:T(8,128)(2,1)S(1)}, s32[]{:T(128)}, s32[]{:T(128)}, /*index=5*/s32[]{:T(128)}, s32[]{:T(128)}, s32[]{:T(128)}) while((s32[]{:T(128)}, bf16[16,512,256]{2,1,0:T(8,128)(2,1)}, bf16[512,256]{1,0:T(8,128)(2,1)S(1)}, s32[]{:T(128)}, s32[]{:T(128)}, ...), condition=%wide.region_3.3_spmd, body=%wide.region_2.2_spmd.sunk | while | flops 12 | bytes 2097390 | solution.py:1051
  330.9 92.2 %branch_0_fun.2 = bf16[512,384]{1,0:T(8,128)(2,1)S(1)} custom-call(s32[1]{0:T(128)} %dynamic_slice.4.total_ref, bf16[1536,128]{1,0:T(8,128)(2,1)S(1)} %bitcast.112, bf16[8192,256]{1,0:T(8,128)(2,1)} %bitcast.113), custom_call_target="tpu_custom_call" | custom-call | tf_op jit(solution)/shard_map/cond/branch_0_fun/pallas_call | solution.py:453
  431.8 264.1 %while.145 = (s32[]{:T(128)}, f32[4,512,1536]{2,1,0:T(8,128)}, f32[512,1536]{1,0:T(8,128)}, s32[]{:T(128)}, s32[]{:T(128)}, /*index=5*/s32[]{:T(128)}, s32[]{:T(128)}, s32[]{:T(128)}) while((s32[]{:T(128)}, f32[4,512,1536]{2,1,0:T(8,128)}, f32[512,1536]{1,0:T(8,128)}, s32[]{:T(128)}, s32[]{:T(128)}, /*index=5*/s32[]{:T(128)}, s32[]{:T(128)}, ...), condition=%wide.region_5.5_spmd, body=%wide.region_4.4_spmd.sunk | while | flops 12 | bytes 25166060 | solution.py:1051
  435.8 60.4 %collective-permute-done.1 = f32[512,1536]{1,0:T(8,128)} collective-permute-done((f32[512,1536]{1,0:T(8,128)S(1)}, f32[512,1536]{1,0:T(8,128)}, u32[]{:S(2)}, u32[]{:S(2)}) %collective-permute-start.1) | collective-permute-done | bytes 3145760 | tf_op jit(solution)/shard_map/cond/branch_0_fun/while/body/eval_jaxpr/ppermute | solution.py:1049
  500.0 62.8 %collective-permute-done.1 = f32[512,1536]{1,0:T(8,128)} collective-permute-done((f32[512,1536]{1,0:T(8,128)S(1)}, f32[512,1536]{1,0:T(8,128)}, u32[]{:S(2)}, u32[]{:S(2)}) %collective-permute-start.1) | collective-permute-done | bytes 3145760 | tf_op jit(solution)/shard_map/cond/branch_0_fun/while/body/eval_jaxpr/ppermute | solution.py:1049
  566.6 62.7 %collective-permute-done.1 = f32[512,1536]{1,0:T(8,128)} collective-permute-done((f32[512,1536]{1,0:T(8,128)S(1)}, f32[512,1536]{1,0:T(8,128)}, u32[]{:S(2)}, u32[]{:S(2)}) %collective-permute-start.1) | collective-permute-done | bytes 3145760 | tf_op jit(solution)/shard_map/cond/branch_0_fun/while/body/eval_jaxpr/ppermute | solution.py:1049
  633.1 62.8 %collective-permute-done.1 = f32[512,1536]{1,0:T(8,128)} collective-permute-done((f32[512,1536]{1,0:T(8,128)S(1)}, f32[512,1536]{1,0:T(8,128)}, u32[]{:S(2)}, u32[]{:S(2)}) %collective-permute-start.1) | collective-permute-done | bytes 3145760 | tf_op jit(solution)/shard_map/cond/branch_0_fun/while/body/eval_jaxpr/ppermute | solution.py:1049
  709.5 43.4 %while.146 = (s32[]{:T(128)}, bf16[4,512,512]{2,1,0:T(8,128)(2,1)S(1)}, bf16[512,512]{1,0:T(8,128)(2,1)S(1)}, s32[]{:T(128)}, s32[]{:T(128)}, /*index=5*/s32[]{:T(128)}, s32[]{:T(128)}, s32[]{:T(128)}) while((s32[]{:T(128)}, bf16[4,512,512]{2,1,0:T(8,128)(2,1)S(1)}, bf16[512,512]{1,0:T(8,128)(2,1)S(1)}, s32[]{:T(128)}, s32[]{:T(128)}, ...), condition=%wide.region_8.8_spmd, body=%wide.region_7.7_spmd.sunk | while | flops 12 | bytes 4194542 | solution.py:1051
  719.0 12.0 collective-permute-done.2
  761.0 162.0 %while.147 = (s32[]{:T(128)}, bf16[16,512,256]{2,1,0:T(8,128)(2,1)}, bf16[512,256]{1,0:T(8,128)(2,1)S(1)}, s32[]{:T(128)}, s32[]{:T(128)}, /*index=5*/s32[]{:T(128)}, s32[]{:T(128)}, s32[]{:T(128)}) while((s32[]{:T(128)}, bf16[16,512,256]{2,1,0:T(8,128)(2,1)}, bf16[512,256]{1,0:T(8,128)(2,1)S(1)}, s32[]{:T(128)}, s32[]{:T(128)}, ...), condition=%wide.region_11.11_spmd, body=%wide.region_10.10_spmd.sunk | while | flops 12 | bytes 2097390 | solution.py:1051
  927.0 123.6 %branch_0_fun.3 = bf16[512,512]{1,0:T(8,128)(2,1)S(1)} custom-call(s32[1]{0:T(128)} %dynamic_slice.4.total_ref, bf16[2048,128]{1,0:T(8,128)(2,1)S(1)} %bitcast.111, bf16[8192,256]{1,0:T(8,128)(2,1)} %bitcast.114), custom_call_target="tpu_custom_call" | custom-call | tf_op jit(solution)/shard_map/cond/branch_0_fun/pallas_call | solution.py:453
  1061.7 357.2 %while.148 = (s32[]{:T(128)}, f32[4,512,2048]{2,1,0:T(8,128)}, f32[512,2048]{1,0:T(8,128)}, s32[]{:T(128)}, s32[]{:T(128)}, /*index=5*/s32[]{:T(128)}, s32[]{:T(128)}, s32[]{:T(128)}) while((s32[]{:T(128)}, f32[4,512,2048]{2,1,0:T(8,128)}, f32[512,2048]{1,0:T(8,128)}, s32[]{:T(128)}, s32[]{:T(128)}, /*index=5*/s32[]{:T(128)}, s32[]{:T(128)}, ...), condition=%wide.region_13.13_spmd, body=%wide.region_12.12_spmd.sunk | while | flops 12 | bytes 33554668 | solution.py:1051
  1071.0 80.5 %collective-permute-done.4 = f32[512,2048]{1,0:T(8,128)} collective-permute-done((f32[512,2048]{1,0:T(8,128)}, f32[512,2048]{1,0:T(8,128)}, u32[]{:S(2)}, u32[]{:S(2)}) %collective-permute-start.4) | collective-permute-done | bytes 4194336 | tf_op jit(solution)/shard_map/cond/branch_0_fun/while/body/eval_jaxpr/ppermute | solution.py:1049
  1160.9 79.6 %collective-permute-done.4 = f32[512,2048]{1,0:T(8,128)} collective-permute-done((f32[512,2048]{1,0:T(8,128)}, f32[512,2048]{1,0:T(8,128)}, u32[]{:S(2)}, u32[]{:S(2)}) %collective-permute-start.4) | collective-permute-done | bytes 4194336 | tf_op jit(solution)/shard_map/cond/branch_0_fun/while/body/eval_jaxpr/ppermute | solution.py:1049
  1250.0 79.6 %collective-permute-done.4 = f32[512,2048]{1,0:T(8,128)} collective-permute-done((f32[512,2048]{1,0:T(8,128)}, f32[512,2048]{1,0:T(8,128)}, u32[]{:S(2)}, u32[]{:S(2)}) %collective-permute-start.4) | collective-permute-done | bytes 4194336 | tf_op jit(solution)/shard_map/cond/branch_0_fun/while/body/eval_jaxpr/ppermute | solution.py:1049
  1339.0 79.6 %collective-permute-done.4 = f32[512,2048]{1,0:T(8,128)} collective-permute-done((f32[512,2048]{1,0:T(8,128)}, f32[512,2048]{1,0:T(8,128)}, u32[]{:S(2)}, u32[]{:S(2)}) %collective-permute-start.4) | collective-permute-done | bytes 4194336 | tf_op jit(solution)/shard_map/cond/branch_0_fun/while/body/eval_jaxpr/ppermute | solution.py:1049
  1453.6 483.7 %while.151 = (s32[]{:T(128)}, bf16[16,512,2048]{2,1,0:T(8,128)(2,1)}, bf16[512,2048]{1,0:T(8,128)(2,1)}, s32[]{:T(128)}, s32[]{:T(128)}, /*index=5*/s32[]{:T(128)}, s32[]{:T(128)}, s32[]{:T(128)}) while((s32[]{:T(128)}, bf16[16,512,2048]{2,1,0:T(8,128)(2,1)}, bf16[512,2048]{1,0:T(8,128)(2,1)}, s32[]{:T(128)}, s32[]{:T(128)}, ...), condition=%wide.region_31.31_spmd, body=%wide.region_30.30_spmd.sunk | while | flops 12 | bytes 16777452 | solution.py:1051
  1458.1 21.5 collective-permute-done.7
  1486.8 21.5 collective-permute-done.7
  1515.4 21.9 collective-permute-done.7
  1544.1 24.0 collective-permute-done.7
  1572.8 26.1 %collective-permute-done.7 = bf16[512,2048]{1,0:T(8,128)(2,1)} collective-permute-done((bf16[512,2048]{1,0:T(8,128)(2,1)S(1)}, bf16[512,2048]{1,0:T(8,128)(2,1)}, u32[]{:S(2)}, u32[]{:S(2)}) %collective-permute-start.7) | collective-permute-done | bytes 2097184 | tf_op jit(solution)/shard_map/cond/branch_0_fun/while/body/eval_jaxpr/ppermute | solution.py:1049
  1602.0 27.7 %collective-permute-done.7 = bf16[512,2048]{1,0:T(8,128)(2,1)} collective-permute-done((bf16[512,2048]{1,0:T(8,128)(2,1)S(1)}, bf16[512,2048]{1,0:T(8,128)(2,1)}, u32[]{:S(2)}, u32[]{:S(2)}) %collective-permute-start.7) | collective-permute-done | bytes 2097184 | tf_op jit(solution)/shard_map/cond/branch_0_fun/while/body/eval_jaxpr/ppermute | solution.py:1049
  1632.7 27.7 %collective-permute-done.7 = bf16[512,2048]{1,0:T(8,128)(2,1)} collective-permute-done((bf16[512,2048]{1,0:T(8,128)(2,1)S(1)}, bf16[512,2048]{1,0:T(8,128)(2,1)}, u32[]{:S(2)}, u32[]{:S(2)}) %collective-permute-start.7) | collective-permute-done | bytes 2097184 | tf_op jit(solution)/shard_map/cond/branch_0_fun/while/body/eval_jaxpr/ppermute | solution.py:1049
  1663.5 27.7 %collective-permute-done.7 = bf16[512,2048]{1,0:T(8,128)(2,1)} collective-permute-done((bf16[512,2048]{1,0:T(8,128)(2,1)S(1)}, bf16[512,2048]{1,0:T(8,128)(2,1)}, u32[]{:S(2)}, u32[]{:S(2)}) %collective-permute-start.7) | collective-permute-done | bytes 2097184 | tf_op jit(solution)/shard_map/cond/branch_0_fun/while/body/eval_jaxpr/ppermute | solution.py:1049
  1694.2 27.7 %collective-permute-done.7 = bf16[512,2048]{1,0:T(8,128)(2,1)} collective-permute-done((bf16[512,2048]{1,0:T(8,128)(2,1)S(1)}, bf16[512,2048]{1,0:T(8,128)(2,1)}, u32[]{:S(2)}, u32[]{:S(2)}) %collective-permute-start.7) | collective-permute-done | bytes 2097184 | tf_op jit(solution)/shard_map/cond/branch_0_fun/while/body/eval_jaxpr/ppermute | solution.py:1049
  1725.0 27.7 %collective-permute-done.7 = bf16[512,2048]{1,0:T(8,128)(2,1)} collective-permute-done((bf16[512,2048]{1,0:T(8,128)(2,1)S(1)}, bf16[512,2048]{1,0:T(8,128)(2,1)}, u32[]{:S(2)}, u32[]{:S(2)}) %collective-permute-start.7) | collective-permute-done | bytes 2097184 | tf_op jit(solution)/shard_map/cond/branch_0_fun/while/body/eval_jaxpr/ppermute | solution.py:1049
  1755.8 27.7 %collective-permute-done.7 = bf16[512,2048]{1,0:T(8,128)(2,1)} collective-permute-done((bf16[512,2048]{1,0:T(8,128)(2,1)S(1)}, bf16[512,2048]{1,0:T(8,128)(2,1)}, u32[]{:S(2)}, u32[]{:S(2)}) %collective-permute-start.7) | collective-permute-done | bytes 2097184 | tf_op jit(solution)/shard_map/cond/branch_0_fun/while/body/eval_jaxpr/ppermute | solution.py:1049
  1786.6 27.7 %collective-permute-done.7 = bf16[512,2048]{1,0:T(8,128)(2,1)} collective-permute-done((bf16[512,2048]{1,0:T(8,128)(2,1)S(1)}, bf16[512,2048]{1,0:T(8,128)(2,1)}, u32[]{:S(2)}, u32[]{:S(2)}) %collective-permute-start.7) | collective-permute-done | bytes 2097184 | tf_op jit(solution)/shard_map/cond/branch_0_fun/while/body/eval_jaxpr/ppermute | solution.py:1049
  1817.3 27.7 %collective-permute-done.7 = bf16[512,2048]{1,0:T(8,128)(2,1)} collective-permute-done((bf16[512,2048]{1,0:T(8,128)(2,1)S(1)}, bf16[512,2048]{1,0:T(8,128)(2,1)}, u32[]{:S(2)}, u32[]{:S(2)}) %collective-permute-start.7) | collective-permute-done | bytes 2097184 | tf_op jit(solution)/shard_map/cond/branch_0_fun/while/body/eval_jaxpr/ppermute | solution.py:1049
  1848.2 27.6 %collective-permute-done.7 = bf16[512,2048]{1,0:T(8,128)(2,1)} collective-permute-done((bf16[512,2048]{1,0:T(8,128)(2,1)S(1)}, bf16[512,2048]{1,0:T(8,128)(2,1)}, u32[]{:S(2)}, u32[]{:S(2)}) %collective-permute-start.7) | collective-permute-done | bytes 2097184 | tf_op jit(solution)/shard_map/cond/branch_0_fun/while/body/eval_jaxpr/ppermute | solution.py:1049
  1878.9 27.7 %collective-permute-done.7 = bf16[512,2048]{1,0:T(8,128)(2,1)} collective-permute-done((bf16[512,2048]{1,0:T(8,128)(2,1)S(1)}, bf16[512,2048]{1,0:T(8,128)(2,1)}, u32[]{:S(2)}, u32[]{:S(2)}) %collective-permute-start.7) | collective-permute-done | bytes 2097184 | tf_op jit(solution)/shard_map/cond/branch_0_fun/while/body/eval_jaxpr/ppermute | solution.py:1049
  1909.7 27.7 %collective-permute-done.7 = bf16[512,2048]{1,0:T(8,128)(2,1)} collective-permute-done((bf16[512,2048]{1,0:T(8,128)(2,1)S(1)}, bf16[512,2048]{1,0:T(8,128)(2,1)}, u32[]{:S(2)}, u32[]{:S(2)}) %collective-permute-start.7) | collective-permute-done | bytes 2097184 | tf_op jit(solution)/shard_map/cond/branch_0_fun/while/body/eval_jaxpr/ppermute | solution.py:1049
  1937.4 13.0 reduce_sum.156
  1952.9 70.9 %while.152 = (s32[]{:T(128)}, bf16[2,512,2048]{2,1,0:T(8,128)(2,1)}, bf16[512,2048]{1,0:T(8,128)(2,1)}, s32[]{:T(128)}, s32[]{:T(128)}, /*index=5*/s32[]{:T(128)}, s32[]{:T(128)}) while((s32[]{:T(128)}, bf16[2,512,2048]{2,1,0:T(8,128)(2,1)}, bf16[512,2048]{1,0:T(8,128)(2,1)}, s32[]{:T(128)}, s32[]{:T(128)}, /*index=5*/s32[]{:T(128)}, ...), condition=%wide.region_34.34_spmd, body=%wide.region_33.33_spmd.sunk | while | flops 12 | bytes 16777444 | solution.py:1051
  1956.2 23.2 collective-permute-done.8
  1982.8 41.0 %collective-permute-done.8 = bf16[512,2048]{1,0:T(8,128)(2,1)} collective-permute-done((bf16[512,2048]{1,0:T(8,128)(2,1)S(1)}, bf16[512,2048]{1,0:T(8,128)(2,1)}, u32[]{:S(2)}, u32[]{:S(2)}) %collective-permute-start.8) | collective-permute-done | bytes 2097184 | tf_op jit(solution)/shard_map/cond/branch_0_fun/while/body/eval_jaxpr/ppermute | solution.py:1049
  2038.0 339.2 %while.149 = (s32[]{:T(128)}, bf16[16,384,1536]{2,1,0:T(8,128)(2,1)}, bf16[384,1536]{1,0:T(8,128)(2,1)S(1)}, s32[]{:T(128)}, s32[]{:T(128)}, /*index=5*/s32[]{:T(128)}, s32[]{:T(128)}, s32[]{:T(128)}) while((s32[]{:T(128)}, bf16[16,384,1536]{2,1,0:T(8,128)(2,1)}, bf16[384,1536]{1,0:T(8,128)(2,1)S(1)}, s32[]{:T(128)}, s32[]{:T(128)}, ...), condition=%wide.region_24.24_spmd, body=%wide.region_23.23_spmd.sunk | while | flops 12 | bytes 9437422 | solution.py:1051
  2039.8 46.5 %collective-permute-done.5 = bf16[384,1536]{1,0:T(8,128)(2,1)S(1)} collective-permute-done((bf16[384,1536]{1,0:T(8,128)(2,1)S(1)}, bf16[384,1536]{1,0:T(8,128)(2,1)S(1)}, u32[]{:S(2)}, u32[]{:S(2)}) %collective-permute-start.5) | collective-permute-done | bytes 1179680 | tf_op jit(solution)/shard_map/cond/branch_0_fun/while/body/eval_jaxpr/ppermute | solution.py:1049
  2087.6 18.1 collective-permute-done.5
  2107.0 18.1 collective-permute-done.5
  2126.4 18.1 collective-permute-done.5
  2145.8 18.1 collective-permute-done.5
  2165.2 18.1 collective-permute-done.5
  2184.6 18.1 collective-permute-done.5
  2204.0 18.0 collective-permute-done.5
  2223.4 18.1 collective-permute-done.5
  2242.8 18.1 collective-permute-done.5
  2262.2 18.0 collective-permute-done.5
  2281.6 18.1 collective-permute-done.5
  2301.0 18.1 collective-permute-done.5
  2320.4 18.1 collective-permute-done.5
  2339.7 18.1 collective-permute-done.5
  2359.1 18.1 collective-permute-done.5
  2389.1 38.9 %while.150 = (s32[]{:T(128)}, bf16[2,384,1536]{2,1,0:T(8,128)(2,1)}, bf16[384,1536]{1,0:T(8,128)(2,1)S(1)}, s32[]{:T(128)}, s32[]{:T(128)}, /*index=5*/s32[]{:T(128)}, s32[]{:T(128)}) while((s32[]{:T(128)}, bf16[2,384,1536]{2,1,0:T(8,128)(2,1)}, bf16[384,1536]{1,0:T(8,128)(2,1)S(1)}, s32[]{:T(128)}, s32[]{:T(128)}, /*index=5*/s32[]{:T(128)}, ...), condition=%wide.region_27.27_spmd, body=%wide.region_26.26_spmd.sunk | while | flops 12 | bytes 9437414 | solution.py:1051
  2390.7 13.6 collective-permute-done.6
  2405.9 22.1 collective-permute-done.6
  (416 shorter events, 605.4 us)
Async XLA Ops:
  204.3 9.5 collective-permute-start
  213.8 9.5 collective-permute-start
  223.3 9.5 collective-permute-start
  232.8 9.5 collective-permute-start
  242.3 9.5 collective-permute-start
  251.9 9.5 collective-permute-start
  261.4 9.5 collective-permute-start
  270.9 9.5 collective-permute-start
  280.4 9.5 collective-permute-start
  289.9 9.5 collective-permute-start
  299.4 9.5 collective-permute-start
  308.9 9.5 collective-permute-start
  318.4 9.5 collective-permute-start
  433.7 62.5 %collective-permute-start.1 = (f32[512,1536]{1,0:T(8,128)S(1)}, f32[512,1536]{1,0:T(8,128)}, u32[]{:S(2)}, u32[]{:S(2)}) collective-permute-start(f32[512,1536]{1,0:T(8,128)S(1)} %copy.51), channel_id=1, source_target_pairs={{0,1},{1,2},{2,3},{3,0},{4,5},{5,6},{6,7},{7,4},{8,9},{9,10},{10,1... | collective-permute-start | bytes 9437192 | tf_op jit(solution)/shard_map/cond/branch_0_fun/while/body/eval_jaxpr/ppermute | solution.py:1049
  498.1 64.7 %collective-permute-start.1 = (f32[512,1536]{1,0:T(8,128)S(1)}, f32[512,1536]{1,0:T(8,128)}, u32[]{:S(2)}, u32[]{:S(2)}) collective-permute-start(f32[512,1536]{1,0:T(8,128)S(1)} %copy.51), channel_id=1, source_target_pairs={{0,1},{1,2},{2,3},{3,0},{4,5},{5,6},{6,7},{7,4},{8,9},{9,10},{10,1... | collective-permute-start | bytes 9437192 | tf_op jit(solution)/shard_map/cond/branch_0_fun/while/body/eval_jaxpr/ppermute | solution.py:1049
  564.7 64.7 %collective-permute-start.1 = (f32[512,1536]{1,0:T(8,128)S(1)}, f32[512,1536]{1,0:T(8,128)}, u32[]{:S(2)}, u32[]{:S(2)}) collective-permute-start(f32[512,1536]{1,0:T(8,128)S(1)} %copy.51), channel_id=1, source_target_pairs={{0,1},{1,2},{2,3},{3,0},{4,5},{5,6},{6,7},{7,4},{8,9},{9,10},{10,1... | collective-permute-start | bytes 9437192 | tf_op jit(solution)/shard_map/cond/branch_0_fun/while/body/eval_jaxpr/ppermute | solution.py:1049
  631.2 64.7 %collective-permute-start.1 = (f32[512,1536]{1,0:T(8,128)S(1)}, f32[512,1536]{1,0:T(8,128)}, u32[]{:S(2)}, u32[]{:S(2)}) collective-permute-start(f32[512,1536]{1,0:T(8,128)S(1)} %copy.51), channel_id=1, source_target_pairs={{0,1},{1,2},{2,3},{3,0},{4,5},{5,6},{6,7},{7,4},{8,9},{9,10},{10,1... | collective-permute-start | bytes 9437192 | tf_op jit(solution)/shard_map/cond/branch_0_fun/while/body/eval_jaxpr/ppermute | solution.py:1049
  718.9 12.2 collective-permute-start.2
  731.1 11.3 collective-permute-start.2
  742.4 10.3 collective-permute-start.2
  761.0 16.9 collective-permute-start.3
  777.9 12.0 collective-permute-start.3
  789.9 9.5 collective-permute-start.3
  799.4 9.5 collective-permute-start.3
  1066.4 85.2 %collective-permute-start.4 = (f32[512,2048]{1,0:T(8,128)}, f32[512,2048]{1,0:T(8,128)}, u32[]{:S(2)}, u32[]{:S(2)}) collective-permute-start(f32[512,2048]{1,0:T(8,128)} %copy.78), channel_id=1, source_target_pairs={{0,1},{1,2},{2,3},{3,0},{4,5},{5,6},{6,7},{7,4},{8,9},{9,10},{10,1... | collective-permute-start | bytes 12582920 | tf_op jit(solution)/shard_map/cond/branch_0_fun/while/body/eval_jaxpr/ppermute | solution.py:1049
  1156.3 84.3 %collective-permute-start.4 = (f32[512,2048]{1,0:T(8,128)}, f32[512,2048]{1,0:T(8,128)}, u32[]{:S(2)}, u32[]{:S(2)}) collective-permute-start(f32[512,2048]{1,0:T(8,128)} %copy.78), channel_id=1, source_target_pairs={{0,1},{1,2},{2,3},{3,0},{4,5},{5,6},{6,7},{7,4},{8,9},{9,10},{10,1... | collective-permute-start | bytes 12582920 | tf_op jit(solution)/shard_map/cond/branch_0_fun/while/body/eval_jaxpr/ppermute | solution.py:1049
  1245.3 84.3 %collective-permute-start.4 = (f32[512,2048]{1,0:T(8,128)}, f32[512,2048]{1,0:T(8,128)}, u32[]{:S(2)}, u32[]{:S(2)}) collective-permute-start(f32[512,2048]{1,0:T(8,128)} %copy.78), channel_id=1, source_target_pairs={{0,1},{1,2},{2,3},{3,0},{4,5},{5,6},{6,7},{7,4},{8,9},{9,10},{10,1... | collective-permute-start | bytes 12582920 | tf_op jit(solution)/shard_map/cond/branch_0_fun/while/body/eval_jaxpr/ppermute | solution.py:1049
  1334.3 84.3 %collective-permute-start.4 = (f32[512,2048]{1,0:T(8,128)}, f32[512,2048]{1,0:T(8,128)}, u32[]{:S(2)}, u32[]{:S(2)}) collective-permute-start(f32[512,2048]{1,0:T(8,128)} %copy.78), channel_id=1, source_target_pairs={{0,1},{1,2},{2,3},{3,0},{4,5},{5,6},{6,7},{7,4},{8,9},{9,10},{10,1... | collective-permute-start | bytes 12582920 | tf_op jit(solution)/shard_map/cond/branch_0_fun/while/body/eval_jaxpr/ppermute | solution.py:1049
  1455.2 24.4 %collective-permute-start.7 = (bf16[512,2048]{1,0:T(8,128)(2,1)S(1)}, bf16[512,2048]{1,0:T(8,128)(2,1)}, u32[]{:S(2)}, u32[]{:S(2)}) collective-permute-start(bf16[512,2048]{1,0:T(8,128)(2,1)S(1)} %copy.105), channel_id=1, source_target_pairs={{0,8},{8,16},{16,24},{24,32},{32,40},{40,48},{48,56},{56,64},{64,7... | collective-permute-start | bytes 6291464 | tf_op jit(solution)/shard_map/cond/branch_0_fun/while/body/eval_jaxpr/ppermute | solution.py:1049
  1481.2 27.1 %collective-permute-start.7 = (bf16[512,2048]{1,0:T(8,128)(2,1)S(1)}, bf16[512,2048]{1,0:T(8,128)(2,1)}, u32[]{:S(2)}, u32[]{:S(2)}) collective-permute-start(bf16[512,2048]{1,0:T(8,128)(2,1)S(1)} %copy.105), channel_id=1, source_target_pairs={{0,8},{8,16},{16,24},{24,32},{32,40},{40,48},{48,56},{56,64},{64,7... | collective-permute-start | bytes 6291464 | tf_op jit(solution)/shard_map/cond/branch_0_fun/while/body/eval_jaxpr/ppermute | solution.py:1049
  1509.9 27.4 %collective-permute-start.7 = (bf16[512,2048]{1,0:T(8,128)(2,1)S(1)}, bf16[512,2048]{1,0:T(8,128)(2,1)}, u32[]{:S(2)}, u32[]{:S(2)}) collective-permute-start(bf16[512,2048]{1,0:T(8,128)(2,1)S(1)} %copy.105), channel_id=1, source_target_pairs={{0,8},{8,16},{16,24},{24,32},{32,40},{40,48},{48,56},{56,64},{64,7... | collective-permute-start | bytes 6291464 | tf_op jit(solution)/shard_map/cond/branch_0_fun/while/body/eval_jaxpr/ppermute | solution.py:1049
  1538.9 29.2 %collective-permute-start.7 = (bf16[512,2048]{1,0:T(8,128)(2,1)S(1)}, bf16[512,2048]{1,0:T(8,128)(2,1)}, u32[]{:S(2)}, u32[]{:S(2)}) collective-permute-start(bf16[512,2048]{1,0:T(8,128)(2,1)S(1)} %copy.105), channel_id=1, source_target_pairs={{0,8},{8,16},{16,24},{24,32},{32,40},{40,48},{48,56},{56,64},{64,7... | collective-permute-start | bytes 6291464 | tf_op jit(solution)/shard_map/cond/branch_0_fun/while/body/eval_jaxpr/ppermute | solution.py:1049
  1569.7 29.2 %collective-permute-start.7 = (bf16[512,2048]{1,0:T(8,128)(2,1)S(1)}, bf16[512,2048]{1,0:T(8,128)(2,1)}, u32[]{:S(2)}, u32[]{:S(2)}) collective-permute-start(bf16[512,2048]{1,0:T(8,128)(2,1)S(1)} %copy.105), channel_id=1, source_target_pairs={{0,8},{8,16},{16,24},{24,32},{32,40},{40,48},{48,56},{56,64},{64,7... | collective-permute-start | bytes 6291464 | tf_op jit(solution)/shard_map/cond/branch_0_fun/while/body/eval_jaxpr/ppermute | solution.py:1049
  1600.5 29.2 %collective-permute-start.7 = (bf16[512,2048]{1,0:T(8,128)(2,1)S(1)}, bf16[512,2048]{1,0:T(8,128)(2,1)}, u32[]{:S(2)}, u32[]{:S(2)}) collective-permute-start(bf16[512,2048]{1,0:T(8,128)(2,1)S(1)} %copy.105), channel_id=1, source_target_pairs={{0,8},{8,16},{16,24},{24,32},{32,40},{40,48},{48,56},{56,64},{64,7... | collective-permute-start | bytes 6291464 | tf_op jit(solution)/shard_map/cond/branch_0_fun/while/body/eval_jaxpr/ppermute | solution.py:1049
  1631.2 29.2 %collective-permute-start.7 = (bf16[512,2048]{1,0:T(8,128)(2,1)S(1)}, bf16[512,2048]{1,0:T(8,128)(2,1)}, u32[]{:S(2)}, u32[]{:S(2)}) collective-permute-start(bf16[512,2048]{1,0:T(8,128)(2,1)S(1)} %copy.105), channel_id=1, source_target_pairs={{0,8},{8,16},{16,24},{24,32},{32,40},{40,48},{48,56},{56,64},{64,7... | collective-permute-start | bytes 6291464 | tf_op jit(solution)/shard_map/cond/branch_0_fun/while/body/eval_jaxpr/ppermute | solution.py:1049
  1662.0 29.2 %collective-permute-start.7 = (bf16[512,2048]{1,0:T(8,128)(2,1)S(1)}, bf16[512,2048]{1,0:T(8,128)(2,1)}, u32[]{:S(2)}, u32[]{:S(2)}) collective-permute-start(bf16[512,2048]{1,0:T(8,128)(2,1)S(1)} %copy.105), channel_id=1, source_target_pairs={{0,8},{8,16},{16,24},{24,32},{32,40},{40,48},{48,56},{56,64},{64,7... | collective-permute-start | bytes 6291464 | tf_op jit(solution)/shard_map/cond/branch_0_fun/while/body/eval_jaxpr/ppermute | solution.py:1049
  1692.8 29.2 %collective-permute-start.7 = (bf16[512,2048]{1,0:T(8,128)(2,1)S(1)}, bf16[512,2048]{1,0:T(8,128)(2,1)}, u32[]{:S(2)}, u32[]{:S(2)}) collective-permute-start(bf16[512,2048]{1,0:T(8,128)(2,1)S(1)} %copy.105), channel_id=1, source_target_pairs={{0,8},{8,16},{16,24},{24,32},{32,40},{40,48},{48,56},{56,64},{64,7... | collective-permute-start | bytes 6291464 | tf_op jit(solution)/shard_map/cond/branch_0_fun/while/body/eval_jaxpr/ppermute | solution.py:1049
  1723.6 29.2 %collective-permute-start.7 = (bf16[512,2048]{1,0:T(8,128)(2,1)S(1)}, bf16[512,2048]{1,0:T(8,128)(2,1)}, u32[]{:S(2)}, u32[]{:S(2)}) collective-permute-start(bf16[512,2048]{1,0:T(8,128)(2,1)S(1)} %copy.105), channel_id=1, source_target_pairs={{0,8},{8,16},{16,24},{24,32},{32,40},{40,48},{48,56},{56,64},{64,7... | collective-permute-start | bytes 6291464 | tf_op jit(solution)/shard_map/cond/branch_0_fun/while/body/eval_jaxpr/ppermute | solution.py:1049
  1754.3 29.2 %collective-permute-start.7 = (bf16[512,2048]{1,0:T(8,128)(2,1)S(1)}, bf16[512,2048]{1,0:T(8,128)(2,1)}, u32[]{:S(2)}, u32[]{:S(2)}) collective-permute-start(bf16[512,2048]{1,0:T(8,128)(2,1)S(1)} %copy.105), channel_id=1, source_target_pairs={{0,8},{8,16},{16,24},{24,32},{32,40},{40,48},{48,56},{56,64},{64,7... | collective-permute-start | bytes 6291464 | tf_op jit(solution)/shard_map/cond/branch_0_fun/while/body/eval_jaxpr/ppermute | solution.py:1049
  1785.1 29.2 %collective-permute-start.7 = (bf16[512,2048]{1,0:T(8,128)(2,1)S(1)}, bf16[512,2048]{1,0:T(8,128)(2,1)}, u32[]{:S(2)}, u32[]{:S(2)}) collective-permute-start(bf16[512,2048]{1,0:T(8,128)(2,1)S(1)} %copy.105), channel_id=1, source_target_pairs={{0,8},{8,16},{16,24},{24,32},{32,40},{40,48},{48,56},{56,64},{64,7... | collective-permute-start | bytes 6291464 | tf_op jit(solution)/shard_map/cond/branch_0_fun/while/body/eval_jaxpr/ppermute | solution.py:1049
  1815.9 29.2 %collective-permute-start.7 = (bf16[512,2048]{1,0:T(8,128)(2,1)S(1)}, bf16[512,2048]{1,0:T(8,128)(2,1)}, u32[]{:S(2)}, u32[]{:S(2)}) collective-permute-start(bf16[512,2048]{1,0:T(8,128)(2,1)S(1)} %copy.105), channel_id=1, source_target_pairs={{0,8},{8,16},{16,24},{24,32},{32,40},{40,48},{48,56},{56,64},{64,7... | collective-permute-start | bytes 6291464 | tf_op jit(solution)/shard_map/cond/branch_0_fun/while/body/eval_jaxpr/ppermute | solution.py:1049
  1846.6 29.2 %collective-permute-start.7 = (bf16[512,2048]{1,0:T(8,128)(2,1)S(1)}, bf16[512,2048]{1,0:T(8,128)(2,1)}, u32[]{:S(2)}, u32[]{:S(2)}) collective-permute-start(bf16[512,2048]{1,0:T(8,128)(2,1)S(1)} %copy.105), channel_id=1, source_target_pairs={{0,8},{8,16},{16,24},{24,32},{32,40},{40,48},{48,56},{56,64},{64,7... | collective-permute-start | bytes 6291464 | tf_op jit(solution)/shard_map/cond/branch_0_fun/while/body/eval_jaxpr/ppermute | solution.py:1049
  1877.4 29.2 %collective-permute-start.7 = (bf16[512,2048]{1,0:T(8,128)(2,1)S(1)}, bf16[512,2048]{1,0:T(8,128)(2,1)}, u32[]{:S(2)}, u32[]{:S(2)}) collective-permute-start(bf16[512,2048]{1,0:T(8,128)(2,1)S(1)} %copy.105), channel_id=1, source_target_pairs={{0,8},{8,16},{16,24},{24,32},{32,40},{40,48},{48,56},{56,64},{64,7... | collective-permute-start | bytes 6291464 | tf_op jit(solution)/shard_map/cond/branch_0_fun/while/body/eval_jaxpr/ppermute | solution.py:1049
  1908.2 29.2 %collective-permute-start.7 = (bf16[512,2048]{1,0:T(8,128)(2,1)S(1)}, bf16[512,2048]{1,0:T(8,128)(2,1)}, u32[]{:S(2)}, u32[]{:S(2)}) collective-permute-start(bf16[512,2048]{1,0:T(8,128)(2,1)S(1)} %copy.105), channel_id=1, source_target_pairs={{0,8},{8,16},{16,24},{24,32},{32,40},{40,48},{48,56},{56,64},{64,7... | collective-permute-start | bytes 6291464 | tf_op jit(solution)/shard_map/cond/branch_0_fun/while/body/eval_jaxpr/ppermute | solution.py:1049
  1954.5 25.0 %collective-permute-start.8 = (bf16[512,2048]{1,0:T(8,128)(2,1)S(1)}, bf16[512,2048]{1,0:T(8,128)(2,1)}, u32[]{:S(2)}, u32[]{:S(2)}) collective-permute-start(bf16[512,2048]{1,0:T(8,128)(2,1)S(1)} %copy.114), channel_id=1, source_target_pairs={{0,4},{4,0},{1,5},{5,1},{2,6},{6,2},{3,7},{7,3},{8,12},{12,8},{9,1... | collective-permute-start | bytes 6291464 | tf_op jit(solution)/shard_map/cond/branch_0_fun/while/body/eval_jaxpr/ppermute | solution.py:1049
  1981.0 42.7 %collective-permute-start.8 = (bf16[512,2048]{1,0:T(8,128)(2,1)S(1)}, bf16[512,2048]{1,0:T(8,128)(2,1)}, u32[]{:S(2)}, u32[]{:S(2)}) collective-permute-start(bf16[512,2048]{1,0:T(8,128)(2,1)S(1)} %copy.114), channel_id=1, source_target_pairs={{0,4},{4,0},{1,5},{5,1},{2,6},{6,2},{3,7},{7,3},{8,12},{12,8},{9,1... | collective-permute-start | bytes 6291464 | tf_op jit(solution)/shard_map/cond/branch_0_fun/while/body/eval_jaxpr/ppermute | solution.py:1049
  2038.1 48.2 %collective-permute-start.5 = (bf16[384,1536]{1,0:T(8,128)(2,1)S(1)}, bf16[384,1536]{1,0:T(8,128)(2,1)S(1)}, u32[]{:S(2)}, u32[]{:S(2)}) collective-permute-start(bf16[384,1536]{1,0:T(8,128)(2,1)S(1)} %copy.87), channel_id=1, source_target_pairs={{0,8},{8,16},{16,24},{24,32},{32,40},{40,48},{48,56},{56,64},{64,7... | collective-permute-start | bytes 3538952 | tf_op jit(solution)/shard_map/cond/branch_0_fun/while/body/eval_jaxpr/ppermute | solution.py:1049
  2086.4 19.3 collective-permute-start.5
  2105.8 19.3 collective-permute-start.5
  2125.2 19.3 collective-permute-start.5
  2144.6 19.3 collective-permute-start.5
  2164.0 19.3 collective-permute-start.5
  2183.4 19.3 collective-permute-start.5
  2202.8 19.3 collective-permute-start.5
  2222.2 19.3 collective-permute-start.5
  2241.6 19.3 collective-permute-start.5
  2261.0 19.3 collective-permute-start.5
  2280.3 19.3 collective-permute-start.5
  2299.7 19.3 collective-permute-start.5
  2319.1 19.3 collective-permute-start.5
  2338.5 19.3 collective-permute-start.5
  2357.9 19.3 collective-permute-start.5
  2389.2 15.1 collective-permute-start.6
  2404.4 23.6 collective-permute-start.6
  (58 other events, 1016.6 us)

commit v8 on v7

--- a/solution.py
+++ b/solution.py
@@ -240,7 +240,7 @@
         (3, 4, zp),
         (3, 11, other),
         (2, 10, other),
-        (5, 6, zm),
+        (2, 6, xpeer),
         (5, 13, other),
         (4, 12, other),
         (6, 14, other),
@@ -296,8 +296,8 @@
 
         @pl.when(i == 1)
         def _():
+            pass_on(0)
             pass_on(1)
-            pass_on(0)
             take(9)
 
         @pl.when(i == 2)

time: 2460 us -> 2460 us (level)
  no operation moved by 1% of the time
where the time goes in v8:
time: 2460 us; the launch traced here: 2430 us
  waiting for transfers between devices  1710 us (70%)
  Pallas kernels  388 us (16%)
  local copies, waits for them, and re-layouts  204 us (8%)
  other arithmetic  62.6 us (3%)
  starting transfers between devices  39.4 us (2%)
    ppermute x80, waiting for transfers between devices, turn(): return (blocks, lax.ppermute(moving, axis, onward))  1710 us
    pallas_call x2, Pallas kernels, careful_call(): pl.pallas_call(careful_kernel, out_shape=jax.ShapeDtypeStruct((rows, head...  216 us
    another operation x89, local copies, waits for them, and re-layouts  97.8 us
    dynamic_update_slice x80, local copies, waits for them, and re-layouts, turn(): lax.dynamic_update_index_in_dim(blocks, moving, lax.rem(me + count - k, c...  96.1 us
    pallas_call x2, Pallas kernels, attend_call(): pl.pallas_call(functools.partial(attend_kernel, heads, tuple((columns for...  78.3 us
    reduce_sum x6, other arithmetic, ring_sum(): return jnp.sum(ring_gather(block, axis).astype(F32), axis=0)  49.7 us
  transfers between devices with their start and end apart: 80, of which 80 were waited for; matrix products, arithmetic and copies ran while one was open for 4% of the time, Pallas kernels for 0%

profile of v8, /device:TPU:1, one launch (start us, length us, event | category | flops | bytes accessed | tf_op | source)
XLA Modules:
  0.0 2430.7 jit_solution(13598118779991537949)
XLA Ops:
  0.6 40.8 %shard_map.172 = (bf16[512,384]{1,0:T(8,128)(2,1)S(1)}, bf16[4,384,1536]{2,1,0:T(8,128)(2,1)S(1)}, bf16[4,512,512]{2,1,0:T(8,128)(2,1)S(1)}) custom-call(s32[2]{0:T(128)} %refs_2_.1, bf16[512,1536]{1,0:T(8,128)(2,1)} %bitcast.115, bf16[1536,384]{1,0:T(8,128)(2,1)} %wq_ref.2, bf16[2,1536,128]{2,1,0:T(8,128)(2,1)} %wkv_ref.2, bf16[384,1536]{1,0:T(8,128)(2,1)} %refs_0_.2, ...), custom_call_target="tpu_custom_call" | custom-call | flops 6442450944 | bytes 4194304 | tf_op jit(solution)/shard_map/pallas_call | solution.py:377
  41.6 17.4 shard_map.173.x_ref
  59.1 22.3 shard_map.174
  81.5 37.5 %shard_map.175 = (bf16[512,512]{1,0:T(8,128)(2,1)S(1)}, bf16[4,512,1536]{2,1,0:T(8,128)(2,1)S(1)}) custom-call(s32[2]{0:T(128)S(1)} %copy-done.35, bf16[512,2048]{1,0:T(8,128)(2,1)S(1)} %get-tuple-element.1033.x_ref.base_ref, bf16[2048,512]{1,0:T(8,128)(2,1)S(1)} %copy-done.38, bf16[2,2048,128]{2,1,0:T(8,128)(2,1)S(1)} %copy-done.40, ...), custom_call_target="tpu_custom_call" | custom-call | flops 8589934592 | bytes 4194304 | tf_op jit(solution)/shard_map/pallas_call | solution.py:377
  119.0 26.4 %shard_map.176 = (f32[1,128]{1,0:T(1,128)}, bf16[512,2048]{1,0:T(8,128)(2,1)S(1)}, bf16[384,1536]{1,0:T(8,128)(2,1)}) custom-call(bf16[512,512]{1,0:T(8,128)(2,1)S(1)} %get-tuple-element.1034.x_ref.att_ref, bf16[512,2048]{1,0:T(8,128)(2,1)S(1)} %get-tuple-element.1033.x_ref.base_ref, bf16[4,512,512]{2,1,0:T(8,128)(2,1)S(1)} %get-tuple-element.1035.refs_0_, ...), custom_call_target="tpu_custom_call" | custom-call | tf_op jit(solution)/shard_map/pallas_call | solution.py:1018
  145.5 28.2 %shard_map.177 = bf16[512,2048]{1,0:T(8,128)(2,1)S(1)} custom-call(bf16[512,512]{1,0:T(8,128)(2,1)S(1)} %get-tuple-element.1034.x_ref.att_ref, bf16[512,2048]{1,0:T(8,128)(2,1)S(1)} %get-tuple-element.1039.d_ref), custom_call_target="tpu_custom_call" | custom-call | tf_op jit(solution)/shard_map/pallas_call | solution.py:819
  175.5 2253.2 %conditional.1 = (f32[1,128]{1,0:T(1,128)}, f32[384,1536]{1,0:T(8,128)S(1)}, f32[512,2048]{1,0:T(8,128)}) conditional(s32[]{:T(128)} %bitcast.34, (bf16[1,512,1536]{2,1,0:T(8,128)(2,1)S(1)}, s32[2]{0:T(128)S(1)}, bf16[1536,384]{1,0:T(8,128)(2,1)}, bf16[2,1536,128]{2,1,0:T(8,128)(2,1)S(1)}, bf16[384,1536]{1,0:T(8,128)(2,1)S(1)}, ...), branch_computations={%region_0.36_spmd, %region_36.37_spmd} | conditional | flops 7342663680 | bytes 525171424 | solution.py:1160
  180.7 143.9 %while.144 = (s32[]{:T(128)}, bf16[16,512,256]{2,1,0:T(8,128)(2,1)}, bf16[512,256]{1,0:T(8,128)(2,1)S(1)}, s32[]{:T(128)}, s32[]{:T(128)}, /*index=5*/s32[]{:T(128)}, s32[]{:T(128)}, s32[]{:T(128)}) while((s32[]{:T(128)}, bf16[16,512,256]{2,1,0:T(8,128)(2,1)}, bf16[512,256]{1,0:T(8,128)(2,1)S(1)}, s32[]{:T(128)}, s32[]{:T(128)}, ...), condition=%wide.region_3.3_spmd, body=%wide.region_2.2_spmd.sunk | while | flops 12 | bytes 2097390 | solution.py:1051
  327.7 92.2 %branch_0_fun.2 = bf16[512,384]{1,0:T(8,128)(2,1)S(1)} custom-call(s32[1]{0:T(128)} %dynamic_slice.4.total_ref, bf16[1536,128]{1,0:T(8,128)(2,1)S(1)} %bitcast.112, bf16[8192,256]{1,0:T(8,128)(2,1)} %bitcast.113), custom_call_target="tpu_custom_call" | custom-call | tf_op jit(solution)/shard_map/cond/branch_0_fun/pallas_call | solution.py:453
  428.6 264.1 %while.145 = (s32[]{:T(128)}, f32[4,512,1536]{2,1,0:T(8,128)}, f32[512,1536]{1,0:T(8,128)}, s32[]{:T(128)}, s32[]{:T(128)}, /*index=5*/s32[]{:T(128)}, s32[]{:T(128)}, s32[]{:T(128)}) while((s32[]{:T(128)}, f32[4,512,1536]{2,1,0:T(8,128)}, f32[512,1536]{1,0:T(8,128)}, s32[]{:T(128)}, s32[]{:T(128)}, /*index=5*/s32[]{:T(128)}, s32[]{:T(128)}, ...), condition=%wide.region_5.5_spmd, body=%wide.region_4.4_spmd.sunk | while | flops 12 | bytes 25166060 | solution.py:1051
  432.3 60.7 %collective-permute-done.1 = f32[512,1536]{1,0:T(8,128)} collective-permute-done((f32[512,1536]{1,0:T(8,128)S(1)}, f32[512,1536]{1,0:T(8,128)}, u32[]{:S(2)}, u32[]{:S(2)}) %collective-permute-start.1) | collective-permute-done | bytes 3145760 | tf_op jit(solution)/shard_map/cond/branch_0_fun/while/body/eval_jaxpr/ppermute | solution.py:1049
  496.7 62.8 %collective-permute-done.1 = f32[512,1536]{1,0:T(8,128)} collective-permute-done((f32[512,1536]{1,0:T(8,128)S(1)}, f32[512,1536]{1,0:T(8,128)}, u32[]{:S(2)}, u32[]{:S(2)}) %collective-permute-start.1) | collective-permute-done | bytes 3145760 | tf_op jit(solution)/shard_map/cond/branch_0_fun/while/body/eval_jaxpr/ppermute | solution.py:1049
  563.3 62.7 %collective-permute-done.1 = f32[512,1536]{1,0:T(8,128)} collective-permute-done((f32[512,1536]{1,0:T(8,128)S(1)}, f32[512,1536]{1,0:T(8,128)}, u32[]{:S(2)}, u32[]{:S(2)}) %collective-permute-start.1) | collective-permute-done | bytes 3145760 | tf_op jit(solution)/shard_map/cond/branch_0_fun/while/body/eval_jaxpr/ppermute | solution.py:1049
  629.9 62.8 %collective-permute-done.1 = f32[512,1536]{1,0:T(8,128)} collective-permute-done((f32[512,1536]{1,0:T(8,128)S(1)}, f32[512,1536]{1,0:T(8,128)}, u32[]{:S(2)}, u32[]{:S(2)}) %collective-permute-start.1) | collective-permute-done | bytes 3145760 | tf_op jit(solution)/shard_map/cond/branch_0_fun/while/body/eval_jaxpr/ppermute | solution.py:1049
  706.3 43.4 %while.146 = (s32[]{:T(128)}, bf16[4,512,512]{2,1,0:T(8,128)(2,1)S(1)}, bf16[512,512]{1,0:T(8,128)(2,1)S(1)}, s32[]{:T(128)}, s32[]{:T(128)}, /*index=5*/s32[]{:T(128)}, s32[]{:T(128)}, s32[]{:T(128)}) while((s32[]{:T(128)}, bf16[4,512,512]{2,1,0:T(8,128)(2,1)S(1)}, bf16[512,512]{1,0:T(8,128)(2,1)S(1)}, s32[]{:T(128)}, s32[]{:T(128)}, ...), condition=%wide.region_8.8_spmd, body=%wide.region_7.7_spmd.sunk | while | flops 12 | bytes 4194542 | solution.py:1051
  715.8 12.0 collective-permute-done.2
  757.7 162.0 %while.147 = (s32[]{:T(128)}, bf16[16,512,256]{2,1,0:T(8,128)(2,1)}, bf16[512,256]{1,0:T(8,128)(2,1)S(1)}, s32[]{:T(128)}, s32[]{:T(128)}, /*index=5*/s32[]{:T(128)}, s32[]{:T(128)}, s32[]{:T(128)}) while((s32[]{:T(128)}, bf16[16,512,256]{2,1,0:T(8,128)(2,1)}, bf16[512,256]{1,0:T(8,128)(2,1)S(1)}, s32[]{:T(128)}, s32[]{:T(128)}, ...), condition=%wide.region_11.11_spmd, body=%wide.region_10.10_spmd.sunk | while | flops 12 | bytes 2097390 | solution.py:1051
  923.8 123.6 %branch_0_fun.3 = bf16[512,512]{1,0:T(8,128)(2,1)S(1)} custom-call(s32[1]{0:T(128)} %dynamic_slice.4.total_ref, bf16[2048,128]{1,0:T(8,128)(2,1)S(1)} %bitcast.111, bf16[8192,256]{1,0:T(8,128)(2,1)} %bitcast.114), custom_call_target="tpu_custom_call" | custom-call | tf_op jit(solution)/shard_map/cond/branch_0_fun/pallas_call | solution.py:453
  1058.4 357.2 %while.148 = (s32[]{:T(128)}, f32[4,512,2048]{2,1,0:T(8,128)}, f32[512,2048]{1,0:T(8,128)}, s32[]{:T(128)}, s32[]{:T(128)}, /*index=5*/s32[]{:T(128)}, s32[]{:T(128)}, s32[]{:T(128)}) while((s32[]{:T(128)}, f32[4,512,2048]{2,1,0:T(8,128)}, f32[512,2048]{1,0:T(8,128)}, s32[]{:T(128)}, s32[]{:T(128)}, /*index=5*/s32[]{:T(128)}, s32[]{:T(128)}, ...), condition=%wide.region_13.13_spmd, body=%wide.region_12.12_spmd.sunk | while | flops 12 | bytes 33554668 | solution.py:1051
  1067.8 80.5 %collective-permute-done.4 = f32[512,2048]{1,0:T(8,128)} collective-permute-done((f32[512,2048]{1,0:T(8,128)}, f32[512,2048]{1,0:T(8,128)}, u32[]{:S(2)}, u32[]{:S(2)}) %collective-permute-start.4) | collective-permute-done | bytes 4194336 | tf_op jit(solution)/shard_map/cond/branch_0_fun/while/body/eval_jaxpr/ppermute | solution.py:1049
  1157.7 79.6 %collective-permute-done.4 = f32[512,2048]{1,0:T(8,128)} collective-permute-done((f32[512,2048]{1,0:T(8,128)}, f32[512,2048]{1,0:T(8,128)}, u32[]{:S(2)}, u32[]{:S(2)}) %collective-permute-start.4) | collective-permute-done | bytes 4194336 | tf_op jit(solution)/shard_map/cond/branch_0_fun/while/body/eval_jaxpr/ppermute | solution.py:1049
  1246.7 79.6 %collective-permute-done.4 = f32[512,2048]{1,0:T(8,128)} collective-permute-done((f32[512,2048]{1,0:T(8,128)}, f32[512,2048]{1,0:T(8,128)}, u32[]{:S(2)}, u32[]{:S(2)}) %collective-permute-start.4) | collective-permute-done | bytes 4194336 | tf_op jit(solution)/shard_map/cond/branch_0_fun/while/body/eval_jaxpr/ppermute | solution.py:1049
  1335.8 79.6 %collective-permute-done.4 = f32[512,2048]{1,0:T(8,128)} collective-permute-done((f32[512,2048]{1,0:T(8,128)}, f32[512,2048]{1,0:T(8,128)}, u32[]{:S(2)}, u32[]{:S(2)}) %collective-permute-start.4) | collective-permute-done | bytes 4194336 | tf_op jit(solution)/shard_map/cond/branch_0_fun/while/body/eval_jaxpr/ppermute | solution.py:1049
  1450.4 483.7 %while.151 = (s32[]{:T(128)}, bf16[16,512,2048]{2,1,0:T(8,128)(2,1)}, bf16[512,2048]{1,0:T(8,128)(2,1)}, s32[]{:T(128)}, s32[]{:T(128)}, /*index=5*/s32[]{:T(128)}, s32[]{:T(128)}, s32[]{:T(128)}) while((s32[]{:T(128)}, bf16[16,512,2048]{2,1,0:T(8,128)(2,1)}, bf16[512,2048]{1,0:T(8,128)(2,1)}, s32[]{:T(128)}, s32[]{:T(128)}, ...), condition=%wide.region_31.31_spmd, body=%wide.region_30.30_spmd.sunk | while | flops 12 | bytes 16777452 | solution.py:1051
  1454.9 21.5 collective-permute-done.7
  1483.6 21.5 collective-permute-done.7
  1512.2 21.9 collective-permute-done.7
  1540.9 24.0 collective-permute-done.7
  1569.6 26.1 %collective-permute-done.7 = bf16[512,2048]{1,0:T(8,128)(2,1)} collective-permute-done((bf16[512,2048]{1,0:T(8,128)(2,1)S(1)}, bf16[512,2048]{1,0:T(8,128)(2,1)}, u32[]{:S(2)}, u32[]{:S(2)}) %collective-permute-start.7) | collective-permute-done | bytes 2097184 | tf_op jit(solution)/shard_map/cond/branch_0_fun/while/body/eval_jaxpr/ppermute | solution.py:1049
  1598.8 27.7 %collective-permute-done.7 = bf16[512,2048]{1,0:T(8,128)(2,1)} collective-permute-done((bf16[512,2048]{1,0:T(8,128)(2,1)S(1)}, bf16[512,2048]{1,0:T(8,128)(2,1)}, u32[]{:S(2)}, u32[]{:S(2)}) %collective-permute-start.7) | collective-permute-done | bytes 2097184 | tf_op jit(solution)/shard_map/cond/branch_0_fun/while/body/eval_jaxpr/ppermute | solution.py:1049
  1629.5 27.7 %collective-permute-done.7 = bf16[512,2048]{1,0:T(8,128)(2,1)} collective-permute-done((bf16[512,2048]{1,0:T(8,128)(2,1)S(1)}, bf16[512,2048]{1,0:T(8,128)(2,1)}, u32[]{:S(2)}, u32[]{:S(2)}) %collective-permute-start.7) | collective-permute-done | bytes 2097184 | tf_op jit(solution)/shard_map/cond/branch_0_fun/while/body/eval_jaxpr/ppermute | solution.py:1049
  1660.3 27.7 %collective-permute-done.7 = bf16[512,2048]{1,0:T(8,128)(2,1)} collective-permute-done((bf16[512,2048]{1,0:T(8,128)(2,1)S(1)}, bf16[512,2048]{1,0:T(8,128)(2,1)}, u32[]{:S(2)}, u32[]{:S(2)}) %collective-permute-start.7) | collective-permute-done | bytes 2097184 | tf_op jit(solution)/shard_map/cond/branch_0_fun/while/body/eval_jaxpr/ppermute | solution.py:1049
  1691.0 27.7 %collective-permute-done.7 = bf16[512,2048]{1,0:T(8,128)(2,1)} collective-permute-done((bf16[512,2048]{1,0:T(8,128)(2,1)S(1)}, bf16[512,2048]{1,0:T(8,128)(2,1)}, u32[]{:S(2)}, u32[]{:S(2)}) %collective-permute-start.7) | collective-permute-done | bytes 2097184 | tf_op jit(solution)/shard_map/cond/branch_0_fun/while/body/eval_jaxpr/ppermute | solution.py:1049
  1721.8 27.7 %collective-permute-done.7 = bf16[512,2048]{1,0:T(8,128)(2,1)} collective-permute-done((bf16[512,2048]{1,0:T(8,128)(2,1)S(1)}, bf16[512,2048]{1,0:T(8,128)(2,1)}, u32[]{:S(2)}, u32[]{:S(2)}) %collective-permute-start.7) | collective-permute-done | bytes 2097184 | tf_op jit(solution)/shard_map/cond/branch_0_fun/while/body/eval_jaxpr/ppermute | solution.py:1049
  1752.6 27.7 %collective-permute-done.7 = bf16[512,2048]{1,0:T(8,128)(2,1)} collective-permute-done((bf16[512,2048]{1,0:T(8,128)(2,1)S(1)}, bf16[512,2048]{1,0:T(8,128)(2,1)}, u32[]{:S(2)}, u32[]{:S(2)}) %collective-permute-start.7) | collective-permute-done | bytes 2097184 | tf_op jit(solution)/shard_map/cond/branch_0_fun/while/body/eval_jaxpr/ppermute | solution.py:1049
  1783.3 27.7 %collective-permute-done.7 = bf16[512,2048]{1,0:T(8,128)(2,1)} collective-permute-done((bf16[512,2048]{1,0:T(8,128)(2,1)S(1)}, bf16[512,2048]{1,0:T(8,128)(2,1)}, u32[]{:S(2)}, u32[]{:S(2)}) %collective-permute-start.7) | collective-permute-done | bytes 2097184 | tf_op jit(solution)/shard_map/cond/branch_0_fun/while/body/eval_jaxpr/ppermute | solution.py:1049
  1814.1 27.7 %collective-permute-done.7 = bf16[512,2048]{1,0:T(8,128)(2,1)} collective-permute-done((bf16[512,2048]{1,0:T(8,128)(2,1)S(1)}, bf16[512,2048]{1,0:T(8,128)(2,1)}, u32[]{:S(2)}, u32[]{:S(2)}) %collective-permute-start.7) | collective-permute-done | bytes 2097184 | tf_op jit(solution)/shard_map/cond/branch_0_fun/while/body/eval_jaxpr/ppermute | solution.py:1049
  1845.0 27.6 %collective-permute-done.7 = bf16[512,2048]{1,0:T(8,128)(2,1)} collective-permute-done((bf16[512,2048]{1,0:T(8,128)(2,1)S(1)}, bf16[512,2048]{1,0:T(8,128)(2,1)}, u32[]{:S(2)}, u32[]{:S(2)}) %collective-permute-start.7) | collective-permute-done | bytes 2097184 | tf_op jit(solution)/shard_map/cond/branch_0_fun/while/body/eval_jaxpr/ppermute | solution.py:1049
  1875.7 27.7 %collective-permute-done.7 = bf16[512,2048]{1,0:T(8,128)(2,1)} collective-permute-done((bf16[512,2048]{1,0:T(8,128)(2,1)S(1)}, bf16[512,2048]{1,0:T(8,128)(2,1)}, u32[]{:S(2)}, u32[]{:S(2)}) %collective-permute-start.7) | collective-permute-done | bytes 2097184 | tf_op jit(solution)/shard_map/cond/branch_0_fun/while/body/eval_jaxpr/ppermute | solution.py:1049
  1906.4 27.7 %collective-permute-done.7 = bf16[512,2048]{1,0:T(8,128)(2,1)} collective-permute-done((bf16[512,2048]{1,0:T(8,128)(2,1)S(1)}, bf16[512,2048]{1,0:T(8,128)(2,1)}, u32[]{:S(2)}, u32[]{:S(2)}) %collective-permute-start.7) | collective-permute-done | bytes 2097184 | tf_op jit(solution)/shard_map/cond/branch_0_fun/while/body/eval_jaxpr/ppermute | solution.py:1049
  1934.1 13.0 reduce_sum.156
  1949.6 70.9 %while.152 = (s32[]{:T(128)}, bf16[2,512,2048]{2,1,0:T(8,128)(2,1)}, bf16[512,2048]{1,0:T(8,128)(2,1)}, s32[]{:T(128)}, s32[]{:T(128)}, /*index=5*/s32[]{:T(128)}, s32[]{:T(128)}) while((s32[]{:T(128)}, bf16[2,512,2048]{2,1,0:T(8,128)(2,1)}, bf16[512,2048]{1,0:T(8,128)(2,1)}, s32[]{:T(128)}, s32[]{:T(128)}, /*index=5*/s32[]{:T(128)}, ...), condition=%wide.region_34.34_spmd, body=%wide.region_33.33_spmd.sunk | while | flops 12 | bytes 16777444 | solution.py:1051
  1953.0 23.2 collective-permute-done.8
  1979.5 41.0 %collective-permute-done.8 = bf16[512,2048]{1,0:T(8,128)(2,1)} collective-permute-done((bf16[512,2048]{1,0:T(8,128)(2,1)S(1)}, bf16[512,2048]{1,0:T(8,128)(2,1)}, u32[]{:S(2)}, u32[]{:S(2)}) %collective-permute-start.8) | collective-permute-done | bytes 2097184 | tf_op jit(solution)/shard_map/cond/branch_0_fun/while/body/eval_jaxpr/ppermute | solution.py:1049
  2034.8 339.2 %while.149 = (s32[]{:T(128)}, bf16[16,384,1536]{2,1,0:T(8,128)(2,1)}, bf16[384,1536]{1,0:T(8,128)(2,1)S(1)}, s32[]{:T(128)}, s32[]{:T(128)}, /*index=5*/s32[]{:T(128)}, s32[]{:T(128)}, s32[]{:T(128)}) while((s32[]{:T(128)}, bf16[16,384,1536]{2,1,0:T(8,128)(2,1)}, bf16[384,1536]{1,0:T(8,128)(2,1)S(1)}, s32[]{:T(128)}, s32[]{:T(128)}, ...), condition=%wide.region_24.24_spmd, body=%wide.region_23.23_spmd.sunk | while | flops 12 | bytes 9437422 | solution.py:1051
  2036.6 46.5 %collective-permute-done.5 = bf16[384,1536]{1,0:T(8,128)(2,1)S(1)} collective-permute-done((bf16[384,1536]{1,0:T(8,128)(2,1)S(1)}, bf16[384,1536]{1,0:T(8,128)(2,1)S(1)}, u32[]{:S(2)}, u32[]{:S(2)}) %collective-permute-start.5) | collective-permute-done | bytes 1179680 | tf_op jit(solution)/shard_map/cond/branch_0_fun/while/body/eval_jaxpr/ppermute | solution.py:1049
  2084.4 18.1 collective-permute-done.5
  2103.8 18.1 collective-permute-done.5
  2123.2 18.1 collective-permute-done.5
  2142.6 18.1 collective-permute-done.5
  2162.0 18.1 collective-permute-done.5
  2181.4 18.1 collective-permute-done.5
  2200.8 18.0 collective-permute-done.5
  2220.1 18.1 collective-permute-done.5
  2239.6 18.1 collective-permute-done.5
  2259.0 18.0 collective-permute-done.5
  2278.4 18.1 collective-permute-done.5
  2297.7 18.1 collective-permute-done.5
  2317.1 18.1 collective-permute-done.5
  2336.5 18.1 collective-permute-done.5
  2355.9 18.1 collective-permute-done.5
  2385.9 38.9 %while.150 = (s32[]{:T(128)}, bf16[2,384,1536]{2,1,0:T(8,128)(2,1)}, bf16[384,1536]{1,0:T(8,128)(2,1)S(1)}, s32[]{:T(128)}, s32[]{:T(128)}, /*index=5*/s32[]{:T(128)}, s32[]{:T(128)}) while((s32[]{:T(128)}, bf16[2,384,1536]{2,1,0:T(8,128)(2,1)}, bf16[384,1536]{1,0:T(8,128)(2,1)S(1)}, s32[]{:T(128)}, s32[]{:T(128)}, /*index=5*/s32[]{:T(128)}, ...), condition=%wide.region_27.27_spmd, body=%wide.region_26.26_spmd.sunk | while | flops 12 | bytes 9437414 | solution.py:1051
  2387.5 13.7 collective-permute-done.6
  2402.7 22.1 collective-permute-done.6
  (416 shorter events, 605.1 us)
Async XLA Ops:
  201.1 9.5 collective-permute-start
  210.6 9.5 collective-permute-start
  220.1 9.5 collective-permute-start
  229.6 9.5 collective-permute-start
  239.1 9.5 collective-permute-start
  248.6 9.5 collective-permute-start
  258.1 9.5 collective-permute-start
  267.6 9.5 collective-permute-start
  277.1 9.5 collective-permute-start
  286.6 9.5 collective-permute-start
  296.1 9.5 collective-permute-start
  305.6 9.5 collective-permute-start
  315.1 9.5 collective-permute-start
  430.5 62.5 %collective-permute-start.1 = (f32[512,1536]{1,0:T(8,128)S(1)}, f32[512,1536]{1,0:T(8,128)}, u32[]{:S(2)}, u32[]{:S(2)}) collective-permute-start(f32[512,1536]{1,0:T(8,128)S(1)} %copy.51), channel_id=1, source_target_pairs={{0,1},{1,2},{2,3},{3,0},{4,5},{5,6},{6,7},{7,4},{8,9},{9,10},{10,1... | collective-permute-start | bytes 9437192 | tf_op jit(solution)/shard_map/cond/branch_0_fun/while/body/eval_jaxpr/ppermute | solution.py:1049
  494.9 64.7 %collective-permute-start.1 = (f32[512,1536]{1,0:T(8,128)S(1)}, f32[512,1536]{1,0:T(8,128)}, u32[]{:S(2)}, u32[]{:S(2)}) collective-permute-start(f32[512,1536]{1,0:T(8,128)S(1)} %copy.51), channel_id=1, source_target_pairs={{0,1},{1,2},{2,3},{3,0},{4,5},{5,6},{6,7},{7,4},{8,9},{9,10},{10,1... | collective-permute-start | bytes 9437192 | tf_op jit(solution)/shard_map/cond/branch_0_fun/while/body/eval_jaxpr/ppermute | solution.py:1049
  561.4 64.7 %collective-permute-start.1 = (f32[512,1536]{1,0:T(8,128)S(1)}, f32[512,1536]{1,0:T(8,128)}, u32[]{:S(2)}, u32[]{:S(2)}) collective-permute-start(f32[512,1536]{1,0:T(8,128)S(1)} %copy.51), channel_id=1, source_target_pairs={{0,1},{1,2},{2,3},{3,0},{4,5},{5,6},{6,7},{7,4},{8,9},{9,10},{10,1... | collective-permute-start | bytes 9437192 | tf_op jit(solution)/shard_map/cond/branch_0_fun/while/body/eval_jaxpr/ppermute | solution.py:1049
  628.0 64.7 %collective-permute-start.1 = (f32[512,1536]{1,0:T(8,128)S(1)}, f32[512,1536]{1,0:T(8,128)}, u32[]{:S(2)}, u32[]{:S(2)}) collective-permute-start(f32[512,1536]{1,0:T(8,128)S(1)} %copy.51), channel_id=1, source_target_pairs={{0,1},{1,2},{2,3},{3,0},{4,5},{5,6},{6,7},{7,4},{8,9},{9,10},{10,1... | collective-permute-start | bytes 9437192 | tf_op jit(solution)/shard_map/cond/branch_0_fun/while/body/eval_jaxpr/ppermute | solution.py:1049
  715.7 12.2 collective-permute-start.2
  727.9 11.3 collective-permute-start.2
  739.2 10.3 collective-permute-start.2
  757.7 16.9 collective-permute-start.3
  774.6 12.1 collective-permute-start.3
  786.7 9.5 collective-permute-start.3
  796.2 9.5 collective-permute-start.3
  1063.1 85.2 %collective-permute-start.4 = (f32[512,2048]{1,0:T(8,128)}, f32[512,2048]{1,0:T(8,128)}, u32[]{:S(2)}, u32[]{:S(2)}) collective-permute-start(f32[512,2048]{1,0:T(8,128)} %copy.78), channel_id=1, source_target_pairs={{0,1},{1,2},{2,3},{3,0},{4,5},{5,6},{6,7},{7,4},{8,9},{9,10},{10,1... | collective-permute-start | bytes 12582920 | tf_op jit(solution)/shard_map/cond/branch_0_fun/while/body/eval_jaxpr/ppermute | solution.py:1049
  1153.1 84.3 %collective-permute-start.4 = (f32[512,2048]{1,0:T(8,128)}, f32[512,2048]{1,0:T(8,128)}, u32[]{:S(2)}, u32[]{:S(2)}) collective-permute-start(f32[512,2048]{1,0:T(8,128)} %copy.78), channel_id=1, source_target_pairs={{0,1},{1,2},{2,3},{3,0},{4,5},{5,6},{6,7},{7,4},{8,9},{9,10},{10,1... | collective-permute-start | bytes 12582920 | tf_op jit(solution)/shard_map/cond/branch_0_fun/while/body/eval_jaxpr/ppermute | solution.py:1049
  1242.0 84.3 %collective-permute-start.4 = (f32[512,2048]{1,0:T(8,128)}, f32[512,2048]{1,0:T(8,128)}, u32[]{:S(2)}, u32[]{:S(2)}) collective-permute-start(f32[512,2048]{1,0:T(8,128)} %copy.78), channel_id=1, source_target_pairs={{0,1},{1,2},{2,3},{3,0},{4,5},{5,6},{6,7},{7,4},{8,9},{9,10},{10,1... | collective-permute-start | bytes 12582920 | tf_op jit(solution)/shard_map/cond/branch_0_fun/while/body/eval_jaxpr/ppermute | solution.py:1049
  1331.1 84.3 %collective-permute-start.4 = (f32[512,2048]{1,0:T(8,128)}, f32[512,2048]{1,0:T(8,128)}, u32[]{:S(2)}, u32[]{:S(2)}) collective-permute-start(f32[512,2048]{1,0:T(8,128)} %copy.78), channel_id=1, source_target_pairs={{0,1},{1,2},{2,3},{3,0},{4,5},{5,6},{6,7},{7,4},{8,9},{9,10},{10,1... | collective-permute-start | bytes 12582920 | tf_op jit(solution)/shard_map/cond/branch_0_fun/while/body/eval_jaxpr/ppermute | solution.py:1049
  1452.0 24.4 %collective-permute-start.7 = (bf16[512,2048]{1,0:T(8,128)(2,1)S(1)}, bf16[512,2048]{1,0:T(8,128)(2,1)}, u32[]{:S(2)}, u32[]{:S(2)}) collective-permute-start(bf16[512,2048]{1,0:T(8,128)(2,1)S(1)} %copy.105), channel_id=1, source_target_pairs={{0,8},{8,16},{16,24},{24,32},{32,40},{40,48},{48,56},{56,64},{64,7... | collective-permute-start | bytes 6291464 | tf_op jit(solution)/shard_map/cond/branch_0_fun/while/body/eval_jaxpr/ppermute | solution.py:1049
  1478.0 27.1 %collective-permute-start.7 = (bf16[512,2048]{1,0:T(8,128)(2,1)S(1)}, bf16[512,2048]{1,0:T(8,128)(2,1)}, u32[]{:S(2)}, u32[]{:S(2)}) collective-permute-start(bf16[512,2048]{1,0:T(8,128)(2,1)S(1)} %copy.105), channel_id=1, source_target_pairs={{0,8},{8,16},{16,24},{24,32},{32,40},{40,48},{48,56},{56,64},{64,7... | collective-permute-start | bytes 6291464 | tf_op jit(solution)/shard_map/cond/branch_0_fun/while/body/eval_jaxpr/ppermute | solution.py:1049
  1506.7 27.4 %collective-permute-start.7 = (bf16[512,2048]{1,0:T(8,128)(2,1)S(1)}, bf16[512,2048]{1,0:T(8,128)(2,1)}, u32[]{:S(2)}, u32[]{:S(2)}) collective-permute-start(bf16[512,2048]{1,0:T(8,128)(2,1)S(1)} %copy.105), channel_id=1, source_target_pairs={{0,8},{8,16},{16,24},{24,32},{32,40},{40,48},{48,56},{56,64},{64,7... | collective-permute-start | bytes 6291464 | tf_op jit(solution)/shard_map/cond/branch_0_fun/while/body/eval_jaxpr/ppermute | solution.py:1049
  1535.7 29.2 %collective-permute-start.7 = (bf16[512,2048]{1,0:T(8,128)(2,1)S(1)}, bf16[512,2048]{1,0:T(8,128)(2,1)}, u32[]{:S(2)}, u32[]{:S(2)}) collective-permute-start(bf16[512,2048]{1,0:T(8,128)(2,1)S(1)} %copy.105), channel_id=1, source_target_pairs={{0,8},{8,16},{16,24},{24,32},{32,40},{40,48},{48,56},{56,64},{64,7... | collective-permute-start | bytes 6291464 | tf_op jit(solution)/shard_map/cond/branch_0_fun/while/body/eval_jaxpr/ppermute | solution.py:1049
  1566.5 29.2 %collective-permute-start.7 = (bf16[512,2048]{1,0:T(8,128)(2,1)S(1)}, bf16[512,2048]{1,0:T(8,128)(2,1)}, u32[]{:S(2)}, u32[]{:S(2)}) collective-permute-start(bf16[512,2048]{1,0:T(8,128)(2,1)S(1)} %copy.105), channel_id=1, source_target_pairs={{0,8},{8,16},{16,24},{24,32},{32,40},{40,48},{48,56},{56,64},{64,7... | collective-permute-start | bytes 6291464 | tf_op jit(solution)/shard_map/cond/branch_0_fun/while/body/eval_jaxpr/ppermute | solution.py:1049
  1597.2 29.2 %collective-permute-start.7 = (bf16[512,2048]{1,0:T(8,128)(2,1)S(1)}, bf16[512,2048]{1,0:T(8,128)(2,1)}, u32[]{:S(2)}, u32[]{:S(2)}) collective-permute-start(bf16[512,2048]{1,0:T(8,128)(2,1)S(1)} %copy.105), channel_id=1, source_target_pairs={{0,8},{8,16},{16,24},{24,32},{32,40},{40,48},{48,56},{56,64},{64,7... | collective-permute-start | bytes 6291464 | tf_op jit(solution)/shard_map/cond/branch_0_fun/while/body/eval_jaxpr/ppermute | solution.py:1049
  1628.0 29.2 %collective-permute-start.7 = (bf16[512,2048]{1,0:T(8,128)(2,1)S(1)}, bf16[512,2048]{1,0:T(8,128)(2,1)}, u32[]{:S(2)}, u32[]{:S(2)}) collective-permute-start(bf16[512,2048]{1,0:T(8,128)(2,1)S(1)} %copy.105), channel_id=1, source_target_pairs={{0,8},{8,16},{16,24},{24,32},{32,40},{40,48},{48,56},{56,64},{64,7... | collective-permute-start | bytes 6291464 | tf_op jit(solution)/shard_map/cond/branch_0_fun/while/body/eval_jaxpr/ppermute | solution.py:1049
  1658.8 29.2 %collective-permute-start.7 = (bf16[512,2048]{1,0:T(8,128)(2,1)S(1)}, bf16[512,2048]{1,0:T(8,128)(2,1)}, u32[]{:S(2)}, u32[]{:S(2)}) collective-permute-start(bf16[512,2048]{1,0:T(8,128)(2,1)S(1)} %copy.105), channel_id=1, source_target_pairs={{0,8},{8,16},{16,24},{24,32},{32,40},{40,48},{48,56},{56,64},{64,7... | collective-permute-start | bytes 6291464 | tf_op jit(solution)/shard_map/cond/branch_0_fun/while/body/eval_jaxpr/ppermute | solution.py:1049
  1689.6 29.2 %collective-permute-start.7 = (bf16[512,2048]{1,0:T(8,128)(2,1)S(1)}, bf16[512,2048]{1,0:T(8,128)(2,1)}, u32[]{:S(2)}, u32[]{:S(2)}) collective-permute-start(bf16[512,2048]{1,0:T(8,128)(2,1)S(1)} %copy.105), channel_id=1, source_target_pairs={{0,8},{8,16},{16,24},{24,32},{32,40},{40,48},{48,56},{56,64},{64,7... | collective-permute-start | bytes 6291464 | tf_op jit(solution)/shard_map/cond/branch_0_fun/while/body/eval_jaxpr/ppermute | solution.py:1049
  1720.3 29.2 %collective-permute-start.7 = (bf16[512,2048]{1,0:T(8,128)(2,1)S(1)}, bf16[512,2048]{1,0:T(8,128)(2,1)}, u32[]{:S(2)}, u32[]{:S(2)}) collective-permute-start(bf16[512,2048]{1,0:T(8,128)(2,1)S(1)} %copy.105), channel_id=1, source_target_pairs={{0,8},{8,16},{16,24},{24,32},{32,40},{40,48},{48,56},{56,64},{64,7... | collective-permute-start | bytes 6291464 | tf_op jit(solution)/shard_map/cond/branch_0_fun/while/body/eval_jaxpr/ppermute | solution.py:1049
  1751.1 29.2 %collective-permute-start.7 = (bf16[512,2048]{1,0:T(8,128)(2,1)S(1)}, bf16[512,2048]{1,0:T(8,128)(2,1)}, u32[]{:S(2)}, u32[]{:S(2)}) collective-permute-start(bf16[512,2048]{1,0:T(8,128)(2,1)S(1)} %copy.105), channel_id=1, source_target_pairs={{0,8},{8,16},{16,24},{24,32},{32,40},{40,48},{48,56},{56,64},{64,7... | collective-permute-start | bytes 6291464 | tf_op jit(solution)/shard_map/cond/branch_0_fun/while/body/eval_jaxpr/ppermute | solution.py:1049
  1781.9 29.2 %collective-permute-start.7 = (bf16[512,2048]{1,0:T(8,128)(2,1)S(1)}, bf16[512,2048]{1,0:T(8,128)(2,1)}, u32[]{:S(2)}, u32[]{:S(2)}) collective-permute-start(bf16[512,2048]{1,0:T(8,128)(2,1)S(1)} %copy.105), channel_id=1, source_target_pairs={{0,8},{8,16},{16,24},{24,32},{32,40},{40,48},{48,56},{56,64},{64,7... | collective-permute-start | bytes 6291464 | tf_op jit(solution)/shard_map/cond/branch_0_fun/while/body/eval_jaxpr/ppermute | solution.py:1049
  1812.6 29.2 %collective-permute-start.7 = (bf16[512,2048]{1,0:T(8,128)(2,1)S(1)}, bf16[512,2048]{1,0:T(8,128)(2,1)}, u32[]{:S(2)}, u32[]{:S(2)}) collective-permute-start(bf16[512,2048]{1,0:T(8,128)(2,1)S(1)} %copy.105), channel_id=1, source_target_pairs={{0,8},{8,16},{16,24},{24,32},{32,40},{40,48},{48,56},{56,64},{64,7... | collective-permute-start | bytes 6291464 | tf_op jit(solution)/shard_map/cond/branch_0_fun/while/body/eval_jaxpr/ppermute | solution.py:1049
  1843.4 29.2 %collective-permute-start.7 = (bf16[512,2048]{1,0:T(8,128)(2,1)S(1)}, bf16[512,2048]{1,0:T(8,128)(2,1)}, u32[]{:S(2)}, u32[]{:S(2)}) collective-permute-start(bf16[512,2048]{1,0:T(8,128)(2,1)S(1)} %copy.105), channel_id=1, source_target_pairs={{0,8},{8,16},{16,24},{24,32},{32,40},{40,48},{48,56},{56,64},{64,7... | collective-permute-start | bytes 6291464 | tf_op jit(solution)/shard_map/cond/branch_0_fun/while/body/eval_jaxpr/ppermute | solution.py:1049
  1874.2 29.2 %collective-permute-start.7 = (bf16[512,2048]{1,0:T(8,128)(2,1)S(1)}, bf16[512,2048]{1,0:T(8,128)(2,1)}, u32[]{:S(2)}, u32[]{:S(2)}) collective-permute-start(bf16[512,2048]{1,0:T(8,128)(2,1)S(1)} %copy.105), channel_id=1, source_target_pairs={{0,8},{8,16},{16,24},{24,32},{32,40},{40,48},{48,56},{56,64},{64,7... | collective-permute-start | bytes 6291464 | tf_op jit(solution)/shard_map/cond/branch_0_fun/while/body/eval_jaxpr/ppermute | solution.py:1049
  1905.0 29.2 %collective-permute-start.7 = (bf16[512,2048]{1,0:T(8,128)(2,1)S(1)}, bf16[512,2048]{1,0:T(8,128)(2,1)}, u32[]{:S(2)}, u32[]{:S(2)}) collective-permute-start(bf16[512,2048]{1,0:T(8,128)(2,1)S(1)} %copy.105), channel_id=1, source_target_pairs={{0,8},{8,16},{16,24},{24,32},{32,40},{40,48},{48,56},{56,64},{64,7... | collective-permute-start | bytes 6291464 | tf_op jit(solution)/shard_map/cond/branch_0_fun/while/body/eval_jaxpr/ppermute | solution.py:1049
  1951.2 25.0 %collective-permute-start.8 = (bf16[512,2048]{1,0:T(8,128)(2,1)S(1)}, bf16[512,2048]{1,0:T(8,128)(2,1)}, u32[]{:S(2)}, u32[]{:S(2)}) collective-permute-start(bf16[512,2048]{1,0:T(8,128)(2,1)S(1)} %copy.114), channel_id=1, source_target_pairs={{0,4},{4,0},{1,5},{5,1},{2,6},{6,2},{3,7},{7,3},{8,12},{12,8},{9,1... | collective-permute-start | bytes 6291464 | tf_op jit(solution)/shard_map/cond/branch_0_fun/while/body/eval_jaxpr/ppermute | solution.py:1049
  1977.8 42.7 %collective-permute-start.8 = (bf16[512,2048]{1,0:T(8,128)(2,1)S(1)}, bf16[512,2048]{1,0:T(8,128)(2,1)}, u32[]{:S(2)}, u32[]{:S(2)}) collective-permute-start(bf16[512,2048]{1,0:T(8,128)(2,1)S(1)} %copy.114), channel_id=1, source_target_pairs={{0,4},{4,0},{1,5},{5,1},{2,6},{6,2},{3,7},{7,3},{8,12},{12,8},{9,1... | collective-permute-start | bytes 6291464 | tf_op jit(solution)/shard_map/cond/branch_0_fun/while/body/eval_jaxpr/ppermute | solution.py:1049
  2034.9 48.2 %collective-permute-start.5 = (bf16[384,1536]{1,0:T(8,128)(2,1)S(1)}, bf16[384,1536]{1,0:T(8,128)(2,1)S(1)}, u32[]{:S(2)}, u32[]{:S(2)}) collective-permute-start(bf16[384,1536]{1,0:T(8,128)(2,1)S(1)} %copy.87), channel_id=1, source_target_pairs={{0,8},{8,16},{16,24},{24,32},{32,40},{40,48},{48,56},{56,64},{64,7... | collective-permute-start | bytes 3538952 | tf_op jit(solution)/shard_map/cond/branch_0_fun/while/body/eval_jaxpr/ppermute | solution.py:1049
  2083.2 19.3 collective-permute-start.5
  2102.6 19.3 collective-permute-start.5
  2122.0 19.3 collective-permute-start.5
  2141.4 19.3 collective-permute-start.5
  2160.8 19.3 collective-permute-start.5
  2180.2 19.3 collective-permute-start.5
  2199.6 19.3 collective-permute-start.5
  2218.9 19.3 collective-permute-start.5
  2238.3 19.3 collective-permute-start.5
  2257.7 19.3 collective-permute-start.5
  2277.1 19.3 collective-permute-start.5
  2296.5 19.3 collective-permute-start.5
  2315.9 19.3 collective-permute-start.5
  2335.3 19.3 collective-permute-start.5
  2354.7 19.3 collective-permute-start.5
  2386.0 15.1 collective-permute-start.6
  2401.2 23.6 collective-permute-start.6
  (58 other events, 1010.6 us)

commit v9 on v8

--- a/solution.py
+++ b/solution.py
@@ -235,6 +235,7 @@
         (None, 7, other),
         (1, 9, other),
         (0, 2, zp),
+        (1, 2, zm),
         (0, 8, other),
         (3, 5, zm),
         (3, 4, zp),
@@ -246,6 +247,9 @@
         (6, 14, other),
     ]
 
+    def parts_of(index):
+        return {5: (0,), 6: (1,)}.get(index, range(PIECES))
+
     def plan_copy(index, part):
         from_slot, to_slot, target = plan[index]
         block = me if from_slot is None else src[from_slot]
@@ -259,7 +263,7 @@
         for part in range(PIECES):
             arrived(slot, part)
             for index, (from_slot, _, _) in enumerate(plan):
-                if from_slot == slot:
+                if from_slot == slot and part in parts_of(index):
                     plan_copy(index, part).start()
 
     def take(slot):
@@ -363,8 +367,8 @@
 
     for ring in rings:
         ring.finish()
-    for part in range(PIECES):
-        for index in range(len(plan)):
+    for index in range(len(plan)):
+        for part in parts_of(index):
             plan_copy(index, part).wait_send()
 
 
@@ -390,7 +394,7 @@
             pltpu.VMEM((heads * rows, 2 * HEAD), F32),
             pltpu.VMEM((heads * rows, HEAD), BF),
             pltpu.VMEM((rows, 2 * HEAD), BF),
-            pltpu.SemaphoreType.DMA((15, PIECES)),
+            pltpu.SemaphoreType.DMA((16, PIECES)),
             pltpu.SemaphoreType.DMA((15, PIECES)),
             pltpu.SemaphoreType.DMA((1,)),
         ]

time: 2460 us -> 2460 us (level)
  no operation moved by 1% of the time
where the time goes in v9:
time: 2460 us; the launch traced here: 2430 us
  waiting for transfers between devices  1710 us (70%)
  Pallas kernels  388 us (16%)
  local copies, waits for them, and re-layouts  204 us (8%)
  other arithmetic  62.6 us (3%)
  starting transfers between devices  39.4 us (2%)
    ppermute x80, waiting for transfers between devices, turn(): return (blocks, lax.ppermute(moving, axis, onward))  1710 us
    pallas_call x2, Pallas kernels, careful_call(): pl.pallas_call(careful_kernel, out_shape=jax.ShapeDtypeStruct((rows, head...  216 us
    another operation x89, local copies, waits for them, and re-layouts  97.8 us
    dynamic_update_slice x80, local copies, waits for them, and re-layouts, turn(): lax.dynamic_update_index_in_dim(blocks, moving, lax.rem(me + count - k, c...  96.1 us
    pallas_call x2, Pallas kernels, attend_call(): pl.pallas_call(functools.partial(attend_kernel, heads, tuple((columns for...  78.3 us
    reduce_sum x6, other arithmetic, ring_sum(): return jnp.sum(ring_gather(block, axis).astype(F32), axis=0)  49.7 us
  transfers between devices with their start and end apart: 80, of which 80 were waited for; matrix products, arithmetic and copies ran while one was open for 4% of the time, Pallas kernels for 0%

profile of v9, /device:TPU:1, one launch (start us, length us, event | category | flops | bytes accessed | tf_op | source)
XLA Modules:
  0.0 2430.7 jit_solution(3075359510220257567)
XLA Ops:
  0.6 40.8 %shard_map.172 = (bf16[512,384]{1,0:T(8,128)(2,1)S(1)}, bf16[4,384,1536]{2,1,0:T(8,128)(2,1)S(1)}, bf16[4,512,512]{2,1,0:T(8,128)(2,1)S(1)}) custom-call(s32[2]{0:T(128)} %refs_2_.1, bf16[512,1536]{1,0:T(8,128)(2,1)} %bitcast.115, bf16[1536,384]{1,0:T(8,128)(2,1)} %wq_ref.2, bf16[2,1536,128]{2,1,0:T(8,128)(2,1)} %wkv_ref.2, bf16[384,1536]{1,0:T(8,128)(2,1)} %refs_0_.2, ...), custom_call_target="tpu_custom_call" | custom-call | flops 6442450944 | bytes 4194304 | tf_op jit(solution)/shard_map/pallas_call | solution.py:381
  41.6 17.4 shard_map.173.x_ref
  59.1 22.3 shard_map.174
  81.5 37.5 %shard_map.175 = (bf16[512,512]{1,0:T(8,128)(2,1)S(1)}, bf16[4,512,1536]{2,1,0:T(8,128)(2,1)S(1)}) custom-call(s32[2]{0:T(128)S(1)} %copy-done.35, bf16[512,2048]{1,0:T(8,128)(2,1)S(1)} %get-tuple-element.1033.x_ref.base_ref, bf16[2048,512]{1,0:T(8,128)(2,1)S(1)} %copy-done.38, bf16[2,2048,128]{2,1,0:T(8,128)(2,1)S(1)} %copy-done.40, ...), custom_call_target="tpu_custom_call" | custom-call | flops 8589934592 | bytes 4194304 | tf_op jit(solution)/shard_map/pallas_call | solution.py:381
  119.0 26.4 %shard_map.176 = (f32[1,128]{1,0:T(1,128)}, bf16[512,2048]{1,0:T(8,128)(2,1)S(1)}, bf16[384,1536]{1,0:T(8,128)(2,1)}) custom-call(bf16[512,512]{1,0:T(8,128)(2,1)S(1)} %get-tuple-element.1034.x_ref.att_ref, bf16[512,2048]{1,0:T(8,128)(2,1)S(1)} %get-tuple-element.1033.x_ref.base_ref, bf16[4,512,512]{2,1,0:T(8,128)(2,1)S(1)} %get-tuple-element.1035.refs_0_, ...), custom_call_target="tpu_custom_call" | custom-call | tf_op jit(solution)/shard_map/pallas_call | solution.py:1022
  145.5 28.2 %shard_map.177 = bf16[512,2048]{1,0:T(8,128)(2,1)S(1)} custom-call(bf16[512,512]{1,0:T(8,128)(2,1)S(1)} %get-tuple-element.1034.x_ref.att_ref, bf16[512,2048]{1,0:T(8,128)(2,1)S(1)} %get-tuple-element.1039.d_ref), custom_call_target="tpu_custom_call" | custom-call | tf_op jit(solution)/shard_map/pallas_call | solution.py:823
  175.5 2253.2 %conditional.1 = (f32[1,128]{1,0:T(1,128)}, f32[384,1536]{1,0:T(8,128)S(1)}, f32[512,2048]{1,0:T(8,128)}) conditional(s32[]{:T(128)} %bitcast.34, (bf16[1,512,1536]{2,1,0:T(8,128)(2,1)S(1)}, s32[2]{0:T(128)S(1)}, bf16[1536,384]{1,0:T(8,128)(2,1)}, bf16[2,1536,128]{2,1,0:T(8,128)(2,1)S(1)}, bf16[384,1536]{1,0:T(8,128)(2,1)S(1)}, ...), branch_computations={%region_0.36_spmd, %region_36.37_spmd} | conditional | flops 7342663680 | bytes 525171424 | solution.py:1164
  180.7 143.9 %while.144 = (s32[]{:T(128)}, bf16[16,512,256]{2,1,0:T(8,128)(2,1)}, bf16[512,256]{1,0:T(8,128)(2,1)S(1)}, s32[]{:T(128)}, s32[]{:T(128)}, /*index=5*/s32[]{:T(128)}, s32[]{:T(128)}, s32[]{:T(128)}) while((s32[]{:T(128)}, bf16[16,512,256]{2,1,0:T(8,128)(2,1)}, bf16[512,256]{1,0:T(8,128)(2,1)S(1)}, s32[]{:T(128)}, s32[]{:T(128)}, ...), condition=%wide.region_3.3_spmd, body=%wide.region_2.2_spmd.sunk | while | flops 12 | bytes 2097390 | solution.py:1055
  327.7 92.2 %branch_0_fun.2 = bf16[512,384]{1,0:T(8,128)(2,1)S(1)} custom-call(s32[1]{0:T(128)} %dynamic_slice.4.total_ref, bf16[1536,128]{1,0:T(8,128)(2,1)S(1)} %bitcast.112, bf16[8192,256]{1,0:T(8,128)(2,1)} %bitcast.113), custom_call_target="tpu_custom_call" | custom-call | tf_op jit(solution)/shard_map/cond/branch_0_fun/pallas_call | solution.py:457
  428.6 264.1 %while.145 = (s32[]{:T(128)}, f32[4,512,1536]{2,1,0:T(8,128)}, f32[512,1536]{1,0:T(8,128)}, s32[]{:T(128)}, s32[]{:T(128)}, /*index=5*/s32[]{:T(128)}, s32[]{:T(128)}, s32[]{:T(128)}) while((s32[]{:T(128)}, f32[4,512,1536]{2,1,0:T(8,128)}, f32[512,1536]{1,0:T(8,128)}, s32[]{:T(128)}, s32[]{:T(128)}, /*index=5*/s32[]{:T(128)}, s32[]{:T(128)}, ...), condition=%wide.region_5.5_spmd, body=%wide.region_4.4_spmd.sunk | while | flops 12 | bytes 25166060 | solution.py:1055
  432.3 60.7 %collective-permute-done.1 = f32[512,1536]{1,0:T(8,128)} collective-permute-done((f32[512,1536]{1,0:T(8,128)S(1)}, f32[512,1536]{1,0:T(8,128)}, u32[]{:S(2)}, u32[]{:S(2)}) %collective-permute-start.1) | collective-permute-done | bytes 3145760 | tf_op jit(solution)/shard_map/cond/branch_0_fun/while/body/eval_jaxpr/ppermute | solution.py:1053
  496.8 62.8 %collective-permute-done.1 = f32[512,1536]{1,0:T(8,128)} collective-permute-done((f32[512,1536]{1,0:T(8,128)S(1)}, f32[512,1536]{1,0:T(8,128)}, u32[]{:S(2)}, u32[]{:S(2)}) %collective-permute-start.1) | collective-permute-done | bytes 3145760 | tf_op jit(solution)/shard_map/cond/branch_0_fun/while/body/eval_jaxpr/ppermute | solution.py:1053
  563.4 62.7 %collective-permute-done.1 = f32[512,1536]{1,0:T(8,128)} collective-permute-done((f32[512,1536]{1,0:T(8,128)S(1)}, f32[512,1536]{1,0:T(8,128)}, u32[]{:S(2)}, u32[]{:S(2)}) %collective-permute-start.1) | collective-permute-done | bytes 3145760 | tf_op jit(solution)/shard_map/cond/branch_0_fun/while/body/eval_jaxpr/ppermute | solution.py:1053
  629.9 62.8 %collective-permute-done.1 = f32[512,1536]{1,0:T(8,128)} collective-permute-done((f32[512,1536]{1,0:T(8,128)S(1)}, f32[512,1536]{1,0:T(8,128)}, u32[]{:S(2)}, u32[]{:S(2)}) %collective-permute-start.1) | collective-permute-done | bytes 3145760 | tf_op jit(solution)/shard_map/cond/branch_0_fun/while/body/eval_jaxpr/ppermute | solution.py:1053
  706.3 43.4 %while.146 = (s32[]{:T(128)}, bf16[4,512,512]{2,1,0:T(8,128)(2,1)S(1)}, bf16[512,512]{1,0:T(8,128)(2,1)S(1)}, s32[]{:T(128)}, s32[]{:T(128)}, /*index=5*/s32[]{:T(128)}, s32[]{:T(128)}, s32[]{:T(128)}) while((s32[]{:T(128)}, bf16[4,512,512]{2,1,0:T(8,128)(2,1)S(1)}, bf16[512,512]{1,0:T(8,128)(2,1)S(1)}, s32[]{:T(128)}, s32[]{:T(128)}, ...), condition=%wide.region_8.8_spmd, body=%wide.region_7.7_spmd.sunk | while | flops 12 | bytes 4194542 | solution.py:1055
  715.8 12.0 collective-permute-done.2
  757.7 162.0 %while.147 = (s32[]{:T(128)}, bf16[16,512,256]{2,1,0:T(8,128)(2,1)}, bf16[512,256]{1,0:T(8,128)(2,1)S(1)}, s32[]{:T(128)}, s32[]{:T(128)}, /*index=5*/s32[]{:T(128)}, s32[]{:T(128)}, s32[]{:T(128)}) while((s32[]{:T(128)}, bf16[16,512,256]{2,1,0:T(8,128)(2,1)}, bf16[512,256]{1,0:T(8,128)(2,1)S(1)}, s32[]{:T(128)}, s32[]{:T(128)}, ...), condition=%wide.region_11.11_spmd, body=%wide.region_10.10_spmd.sunk | while | flops 12 | bytes 2097390 | solution.py:1055
  923.8 123.6 %branch_0_fun.3 = bf16[512,512]{1,0:T(8,128)(2,1)S(1)} custom-call(s32[1]{0:T(128)} %dynamic_slice.4.total_ref, bf16[2048,128]{1,0:T(8,128)(2,1)S(1)} %bitcast.111, bf16[8192,256]{1,0:T(8,128)(2,1)} %bitcast.114), custom_call_target="tpu_custom_call" | custom-call | tf_op jit(solution)/shard_map/cond/branch_0_fun/pallas_call | solution.py:457
  1058.5 357.2 %while.148 = (s32[]{:T(128)}, f32[4,512,2048]{2,1,0:T(8,128)}, f32[512,2048]{1,0:T(8,128)}, s32[]{:T(128)}, s32[]{:T(128)}, /*index=5*/s32[]{:T(128)}, s32[]{:T(128)}, s32[]{:T(128)}) while((s32[]{:T(128)}, f32[4,512,2048]{2,1,0:T(8,128)}, f32[512,2048]{1,0:T(8,128)}, s32[]{:T(128)}, s32[]{:T(128)}, /*index=5*/s32[]{:T(128)}, s32[]{:T(128)}, ...), condition=%wide.region_13.13_spmd, body=%wide.region_12.12_spmd.sunk | while | flops 12 | bytes 33554668 | solution.py:1055
  1067.8 80.5 %collective-permute-done.4 = f32[512,2048]{1,0:T(8,128)} collective-permute-done((f32[512,2048]{1,0:T(8,128)}, f32[512,2048]{1,0:T(8,128)}, u32[]{:S(2)}, u32[]{:S(2)}) %collective-permute-start.4) | collective-permute-done | bytes 4194336 | tf_op jit(solution)/shard_map/cond/branch_0_fun/while/body/eval_jaxpr/ppermute | solution.py:1053
  1157.7 79.6 %collective-permute-done.4 = f32[512,2048]{1,0:T(8,128)} collective-permute-done((f32[512,2048]{1,0:T(8,128)}, f32[512,2048]{1,0:T(8,128)}, u32[]{:S(2)}, u32[]{:S(2)}) %collective-permute-start.4) | collective-permute-done | bytes 4194336 | tf_op jit(solution)/shard_map/cond/branch_0_fun/while/body/eval_jaxpr/ppermute | solution.py:1053
  1246.8 79.6 %collective-permute-done.4 = f32[512,2048]{1,0:T(8,128)} collective-permute-done((f32[512,2048]{1,0:T(8,128)}, f32[512,2048]{1,0:T(8,128)}, u32[]{:S(2)}, u32[]{:S(2)}) %collective-permute-start.4) | collective-permute-done | bytes 4194336 | tf_op jit(solution)/shard_map/cond/branch_0_fun/while/body/eval_jaxpr/ppermute | solution.py:1053
  1335.8 79.6 %collective-permute-done.4 = f32[512,2048]{1,0:T(8,128)} collective-permute-done((f32[512,2048]{1,0:T(8,128)}, f32[512,2048]{1,0:T(8,128)}, u32[]{:S(2)}, u32[]{:S(2)}) %collective-permute-start.4) | collective-permute-done | bytes 4194336 | tf_op jit(solution)/shard_map/cond/branch_0_fun/while/body/eval_jaxpr/ppermute | solution.py:1053
  1450.4 483.7 %while.151 = (s32[]{:T(128)}, bf16[16,512,2048]{2,1,0:T(8,128)(2,1)}, bf16[512,2048]{1,0:T(8,128)(2,1)}, s32[]{:T(128)}, s32[]{:T(128)}, /*index=5*/s32[]{:T(128)}, s32[]{:T(128)}, s32[]{:T(128)}) while((s32[]{:T(128)}, bf16[16,512,2048]{2,1,0:T(8,128)(2,1)}, bf16[512,2048]{1,0:T(8,128)(2,1)}, s32[]{:T(128)}, s32[]{:T(128)}, ...), condition=%wide.region_31.31_spmd, body=%wide.region_30.30_spmd.sunk | while | flops 12 | bytes 16777452 | solution.py:1055
  1454.9 21.5 collective-permute-done.7
  1483.6 21.5 collective-permute-done.7
  1512.2 21.9 collective-permute-done.7
  1540.9 24.0 collective-permute-done.7
  1569.6 26.1 %collective-permute-done.7 = bf16[512,2048]{1,0:T(8,128)(2,1)} collective-permute-done((bf16[512,2048]{1,0:T(8,128)(2,1)S(1)}, bf16[512,2048]{1,0:T(8,128)(2,1)}, u32[]{:S(2)}, u32[]{:S(2)}) %collective-permute-start.7) | collective-permute-done | bytes 2097184 | tf_op jit(solution)/shard_map/cond/branch_0_fun/while/body/eval_jaxpr/ppermute | solution.py:1053
  1598.8 27.7 %collective-permute-done.7 = bf16[512,2048]{1,0:T(8,128)(2,1)} collective-permute-done((bf16[512,2048]{1,0:T(8,128)(2,1)S(1)}, bf16[512,2048]{1,0:T(8,128)(2,1)}, u32[]{:S(2)}, u32[]{:S(2)}) %collective-permute-start.7) | collective-permute-done | bytes 2097184 | tf_op jit(solution)/shard_map/cond/branch_0_fun/while/body/eval_jaxpr/ppermute | solution.py:1053
  1629.5 27.7 %collective-permute-done.7 = bf16[512,2048]{1,0:T(8,128)(2,1)} collective-permute-done((bf16[512,2048]{1,0:T(8,128)(2,1)S(1)}, bf16[512,2048]{1,0:T(8,128)(2,1)}, u32[]{:S(2)}, u32[]{:S(2)}) %collective-permute-start.7) | collective-permute-done | bytes 2097184 | tf_op jit(solution)/shard_map/cond/branch_0_fun/while/body/eval_jaxpr/ppermute | solution.py:1053
  1660.3 27.7 %collective-permute-done.7 = bf16[512,2048]{1,0:T(8,128)(2,1)} collective-permute-done((bf16[512,2048]{1,0:T(8,128)(2,1)S(1)}, bf16[512,2048]{1,0:T(8,128)(2,1)}, u32[]{:S(2)}, u32[]{:S(2)}) %collective-permute-start.7) | collective-permute-done | bytes 2097184 | tf_op jit(solution)/shard_map/cond/branch_0_fun/while/body/eval_jaxpr/ppermute | solution.py:1053
  1691.0 27.7 %collective-permute-done.7 = bf16[512,2048]{1,0:T(8,128)(2,1)} collective-permute-done((bf16[512,2048]{1,0:T(8,128)(2,1)S(1)}, bf16[512,2048]{1,0:T(8,128)(2,1)}, u32[]{:S(2)}, u32[]{:S(2)}) %collective-permute-start.7) | collective-permute-done | bytes 2097184 | tf_op jit(solution)/shard_map/cond/branch_0_fun/while/body/eval_jaxpr/ppermute | solution.py:1053
  1721.8 27.7 %collective-permute-done.7 = bf16[512,2048]{1,0:T(8,128)(2,1)} collective-permute-done((bf16[512,2048]{1,0:T(8,128)(2,1)S(1)}, bf16[512,2048]{1,0:T(8,128)(2,1)}, u32[]{:S(2)}, u32[]{:S(2)}) %collective-permute-start.7) | collective-permute-done | bytes 2097184 | tf_op jit(solution)/shard_map/cond/branch_0_fun/while/body/eval_jaxpr/ppermute | solution.py:1053
  1752.6 27.7 %collective-permute-done.7 = bf16[512,2048]{1,0:T(8,128)(2,1)} collective-permute-done((bf16[512,2048]{1,0:T(8,128)(2,1)S(1)}, bf16[512,2048]{1,0:T(8,128)(2,1)}, u32[]{:S(2)}, u32[]{:S(2)}) %collective-permute-start.7) | collective-permute-done | bytes 2097184 | tf_op jit(solution)/shard_map/cond/branch_0_fun/while/body/eval_jaxpr/ppermute | solution.py:1053
  1783.4 27.7 %collective-permute-done.7 = bf16[512,2048]{1,0:T(8,128)(2,1)} collective-permute-done((bf16[512,2048]{1,0:T(8,128)(2,1)S(1)}, bf16[512,2048]{1,0:T(8,128)(2,1)}, u32[]{:S(2)}, u32[]{:S(2)}) %collective-permute-start.7) | collective-permute-done | bytes 2097184 | tf_op jit(solution)/shard_map/cond/branch_0_fun/while/body/eval_jaxpr/ppermute | solution.py:1053
  1814.1 27.7 %collective-permute-done.7 = bf16[512,2048]{1,0:T(8,128)(2,1)} collective-permute-done((bf16[512,2048]{1,0:T(8,128)(2,1)S(1)}, bf16[512,2048]{1,0:T(8,128)(2,1)}, u32[]{:S(2)}, u32[]{:S(2)}) %collective-permute-start.7) | collective-permute-done | bytes 2097184 | tf_op jit(solution)/shard_map/cond/branch_0_fun/while/body/eval_jaxpr/ppermute | solution.py:1053
  1845.0 27.6 %collective-permute-done.7 = bf16[512,2048]{1,0:T(8,128)(2,1)} collective-permute-done((bf16[512,2048]{1,0:T(8,128)(2,1)S(1)}, bf16[512,2048]{1,0:T(8,128)(2,1)}, u32[]{:S(2)}, u32[]{:S(2)}) %collective-permute-start.7) | collective-permute-done | bytes 2097184 | tf_op jit(solution)/shard_map/cond/branch_0_fun/while/body/eval_jaxpr/ppermute | solution.py:1053
  1875.7 27.7 %collective-permute-done.7 = bf16[512,2048]{1,0:T(8,128)(2,1)} collective-permute-done((bf16[512,2048]{1,0:T(8,128)(2,1)S(1)}, bf16[512,2048]{1,0:T(8,128)(2,1)}, u32[]{:S(2)}, u32[]{:S(2)}) %collective-permute-start.7) | collective-permute-done | bytes 2097184 | tf_op jit(solution)/shard_map/cond/branch_0_fun/while/body/eval_jaxpr/ppermute | solution.py:1053
  1906.5 27.7 %collective-permute-done.7 = bf16[512,2048]{1,0:T(8,128)(2,1)} collective-permute-done((bf16[512,2048]{1,0:T(8,128)(2,1)S(1)}, bf16[512,2048]{1,0:T(8,128)(2,1)}, u32[]{:S(2)}, u32[]{:S(2)}) %collective-permute-start.7) | collective-permute-done | bytes 2097184 | tf_op jit(solution)/shard_map/cond/branch_0_fun/while/body/eval_jaxpr/ppermute | solution.py:1053
  1934.2 13.0 reduce_sum.156
  1949.7 70.9 %while.152 = (s32[]{:T(128)}, bf16[2,512,2048]{2,1,0:T(8,128)(2,1)}, bf16[512,2048]{1,0:T(8,128)(2,1)}, s32[]{:T(128)}, s32[]{:T(128)}, /*index=5*/s32[]{:T(128)}, s32[]{:T(128)}) while((s32[]{:T(128)}, bf16[2,512,2048]{2,1,0:T(8,128)(2,1)}, bf16[512,2048]{1,0:T(8,128)(2,1)}, s32[]{:T(128)}, s32[]{:T(128)}, /*index=5*/s32[]{:T(128)}, ...), condition=%wide.region_34.34_spmd, body=%wide.region_33.33_spmd.sunk | while | flops 12 | bytes 16777444 | solution.py:1055
  1953.0 23.2 collective-permute-done.8
  1979.6 41.0 %collective-permute-done.8 = bf16[512,2048]{1,0:T(8,128)(2,1)} collective-permute-done((bf16[512,2048]{1,0:T(8,128)(2,1)S(1)}, bf16[512,2048]{1,0:T(8,128)(2,1)}, u32[]{:S(2)}, u32[]{:S(2)}) %collective-permute-start.8) | collective-permute-done | bytes 2097184 | tf_op jit(solution)/shard_map/cond/branch_0_fun/while/body/eval_jaxpr/ppermute | solution.py:1053
  2034.8 339.2 %while.149 = (s32[]{:T(128)}, bf16[16,384,1536]{2,1,0:T(8,128)(2,1)}, bf16[384,1536]{1,0:T(8,128)(2,1)S(1)}, s32[]{:T(128)}, s32[]{:T(128)}, /*index=5*/s32[]{:T(128)}, s32[]{:T(128)}, s32[]{:T(128)}) while((s32[]{:T(128)}, bf16[16,384,1536]{2,1,0:T(8,128)(2,1)}, bf16[384,1536]{1,0:T(8,128)(2,1)S(1)}, s32[]{:T(128)}, s32[]{:T(128)}, ...), condition=%wide.region_24.24_spmd, body=%wide.region_23.23_spmd.sunk | while | flops 12 | bytes 9437422 | solution.py:1055
  2036.6 46.5 %collective-permute-done.5 = bf16[384,1536]{1,0:T(8,128)(2,1)S(1)} collective-permute-done((bf16[384,1536]{1,0:T(8,128)(2,1)S(1)}, bf16[384,1536]{1,0:T(8,128)(2,1)S(1)}, u32[]{:S(2)}, u32[]{:S(2)}) %collective-permute-start.5) | collective-permute-done | bytes 1179680 | tf_op jit(solution)/shard_map/cond/branch_0_fun/while/body/eval_jaxpr/ppermute | solution.py:1053
  2084.4 18.1 collective-permute-done.5
  2103.8 18.1 collective-permute-done.5
  2123.2 18.1 collective-permute-done.5
  2142.6 18.1 collective-permute-done.5
  2162.0 18.1 collective-permute-done.5
  2181.4 18.1 collective-permute-done.5
  2200.8 18.0 collective-permute-done.5
  2220.2 18.1 collective-permute-done.5
  2239.6 18.1 collective-permute-done.5
  2259.0 18.0 collective-permute-done.5
  2278.4 18.1 collective-permute-done.5
  2297.7 18.1 collective-permute-done.5
  2317.1 18.1 collective-permute-done.5
  2336.5 18.1 collective-permute-done.5
  2355.9 18.1 collective-permute-done.5
  2385.9 38.9 %while.150 = (s32[]{:T(128)}, bf16[2,384,1536]{2,1,0:T(8,128)(2,1)}, bf16[384,1536]{1,0:T(8,128)(2,1)S(1)}, s32[]{:T(128)}, s32[]{:T(128)}, /*index=5*/s32[]{:T(128)}, s32[]{:T(128)}) while((s32[]{:T(128)}, bf16[2,384,1536]{2,1,0:T(8,128)(2,1)}, bf16[384,1536]{1,0:T(8,128)(2,1)S(1)}, s32[]{:T(128)}, s32[]{:T(128)}, /*index=5*/s32[]{:T(128)}, ...), condition=%wide.region_27.27_spmd, body=%wide.region_26.26_spmd.sunk | while | flops 12 | bytes 9437414 | solution.py:1055
  2387.5 13.6 collective-permute-done.6
  2402.7 22.1 collective-permute-done.6
  (416 shorter events, 605.1 us)
Async XLA Ops:
  201.1 9.5 collective-permute-start
  210.6 9.5 collective-permute-start
  220.1 9.5 collective-permute-start
  229.6 9.5 collective-permute-start
  239.1 9.5 collective-permute-start
  248.6 9.5 collective-permute-start
  258.1 9.5 collective-permute-start
  267.6 9.5 collective-permute-start
  277.2 9.5 collective-permute-start
  286.7 9.5 collective-permute-start
  296.2 9.5 collective-permute-start
  305.7 9.5 collective-permute-start
  315.2 9.5 collective-permute-start
  430.5 62.5 %collective-permute-start.1 = (f32[512,1536]{1,0:T(8,128)S(1)}, f32[512,1536]{1,0:T(8,128)}, u32[]{:S(2)}, u32[]{:S(2)}) collective-permute-start(f32[512,1536]{1,0:T(8,128)S(1)} %copy.51), channel_id=1, source_target_pairs={{0,1},{1,2},{2,3},{3,0},{4,5},{5,6},{6,7},{7,4},{8,9},{9,10},{10,1... | collective-permute-start | bytes 9437192 | tf_op jit(solution)/shard_map/cond/branch_0_fun/while/body/eval_jaxpr/ppermute | solution.py:1053
  494.9 64.7 %collective-permute-start.1 = (f32[512,1536]{1,0:T(8,128)S(1)}, f32[512,1536]{1,0:T(8,128)}, u32[]{:S(2)}, u32[]{:S(2)}) collective-permute-start(f32[512,1536]{1,0:T(8,128)S(1)} %copy.51), channel_id=1, source_target_pairs={{0,1},{1,2},{2,3},{3,0},{4,5},{5,6},{6,7},{7,4},{8,9},{9,10},{10,1... | collective-permute-start | bytes 9437192 | tf_op jit(solution)/shard_map/cond/branch_0_fun/while/body/eval_jaxpr/ppermute | solution.py:1053
  561.5 64.7 %collective-permute-start.1 = (f32[512,1536]{1,0:T(8,128)S(1)}, f32[512,1536]{1,0:T(8,128)}, u32[]{:S(2)}, u32[]{:S(2)}) collective-permute-start(f32[512,1536]{1,0:T(8,128)S(1)} %copy.51), channel_id=1, source_target_pairs={{0,1},{1,2},{2,3},{3,0},{4,5},{5,6},{6,7},{7,4},{8,9},{9,10},{10,1... | collective-permute-start | bytes 9437192 | tf_op jit(solution)/shard_map/cond/branch_0_fun/while/body/eval_jaxpr/ppermute | solution.py:1053
  628.0 64.7 %collective-permute-start.1 = (f32[512,1536]{1,0:T(8,128)S(1)}, f32[512,1536]{1,0:T(8,128)}, u32[]{:S(2)}, u32[]{:S(2)}) collective-permute-start(f32[512,1536]{1,0:T(8,128)S(1)} %copy.51), channel_id=1, source_target_pairs={{0,1},{1,2},{2,3},{3,0},{4,5},{5,6},{6,7},{7,4},{8,9},{9,10},{10,1... | collective-permute-start | bytes 9437192 | tf_op jit(solution)/shard_map/cond/branch_0_fun/while/body/eval_jaxpr/ppermute | solution.py:1053
  715.7 12.2 collective-permute-start.2
  727.9 11.2 collective-permute-start.2
  739.2 10.3 collective-permute-start.2
  757.7 16.9 collective-permute-start.3
  774.6 12.1 collective-permute-start.3
  786.7 9.5 collective-permute-start.3
  796.2 9.5 collective-permute-start.3
  1063.2 85.2 %collective-permute-start.4 = (f32[512,2048]{1,0:T(8,128)}, f32[512,2048]{1,0:T(8,128)}, u32[]{:S(2)}, u32[]{:S(2)}) collective-permute-start(f32[512,2048]{1,0:T(8,128)} %copy.78), channel_id=1, source_target_pairs={{0,1},{1,2},{2,3},{3,0},{4,5},{5,6},{6,7},{7,4},{8,9},{9,10},{10,1... | collective-permute-start | bytes 12582920 | tf_op jit(solution)/shard_map/cond/branch_0_fun/while/body/eval_jaxpr/ppermute | solution.py:1053
  1153.1 84.3 %collective-permute-start.4 = (f32[512,2048]{1,0:T(8,128)}, f32[512,2048]{1,0:T(8,128)}, u32[]{:S(2)}, u32[]{:S(2)}) collective-permute-start(f32[512,2048]{1,0:T(8,128)} %copy.78), channel_id=1, source_target_pairs={{0,1},{1,2},{2,3},{3,0},{4,5},{5,6},{6,7},{7,4},{8,9},{9,10},{10,1... | collective-permute-start | bytes 12582920 | tf_op jit(solution)/shard_map/cond/branch_0_fun/while/body/eval_jaxpr/ppermute | solution.py:1053
  1242.1 84.3 %collective-permute-start.4 = (f32[512,2048]{1,0:T(8,128)}, f32[512,2048]{1,0:T(8,128)}, u32[]{:S(2)}, u32[]{:S(2)}) collective-permute-start(f32[512,2048]{1,0:T(8,128)} %copy.78), channel_id=1, source_target_pairs={{0,1},{1,2},{2,3},{3,0},{4,5},{5,6},{6,7},{7,4},{8,9},{9,10},{10,1... | collective-permute-start | bytes 12582920 | tf_op jit(solution)/shard_map/cond/branch_0_fun/while/body/eval_jaxpr/ppermute | solution.py:1053
  1331.1 84.3 %collective-permute-start.4 = (f32[512,2048]{1,0:T(8,128)}, f32[512,2048]{1,0:T(8,128)}, u32[]{:S(2)}, u32[]{:S(2)}) collective-permute-start(f32[512,2048]{1,0:T(8,128)} %copy.78), channel_id=1, source_target_pairs={{0,1},{1,2},{2,3},{3,0},{4,5},{5,6},{6,7},{7,4},{8,9},{9,10},{10,1... | collective-permute-start | bytes 12582920 | tf_op jit(solution)/shard_map/cond/branch_0_fun/while/body/eval_jaxpr/ppermute | solution.py:1053
  1452.0 24.4 %collective-permute-start.7 = (bf16[512,2048]{1,0:T(8,128)(2,1)S(1)}, bf16[512,2048]{1,0:T(8,128)(2,1)}, u32[]{:S(2)}, u32[]{:S(2)}) collective-permute-start(bf16[512,2048]{1,0:T(8,128)(2,1)S(1)} %copy.105), channel_id=1, source_target_pairs={{0,8},{8,16},{16,24},{24,32},{32,40},{40,48},{48,56},{56,64},{64,7... | collective-permute-start | bytes 6291464 | tf_op jit(solution)/shard_map/cond/branch_0_fun/while/body/eval_jaxpr/ppermute | solution.py:1053
  1478.0 27.1 %collective-permute-start.7 = (bf16[512,2048]{1,0:T(8,128)(2,1)S(1)}, bf16[512,2048]{1,0:T(8,128)(2,1)}, u32[]{:S(2)}, u32[]{:S(2)}) collective-permute-start(bf16[512,2048]{1,0:T(8,128)(2,1)S(1)} %copy.105), channel_id=1, source_target_pairs={{0,8},{8,16},{16,24},{24,32},{32,40},{40,48},{48,56},{56,64},{64,7... | collective-permute-start | bytes 6291464 | tf_op jit(solution)/shard_map/cond/branch_0_fun/while/body/eval_jaxpr/ppermute | solution.py:1053
  1506.7 27.4 %collective-permute-start.7 = (bf16[512,2048]{1,0:T(8,128)(2,1)S(1)}, bf16[512,2048]{1,0:T(8,128)(2,1)}, u32[]{:S(2)}, u32[]{:S(2)}) collective-permute-start(bf16[512,2048]{1,0:T(8,128)(2,1)S(1)} %copy.105), channel_id=1, source_target_pairs={{0,8},{8,16},{16,24},{24,32},{32,40},{40,48},{48,56},{56,64},{64,7... | collective-permute-start | bytes 6291464 | tf_op jit(solution)/shard_map/cond/branch_0_fun/while/body/eval_jaxpr/ppermute | solution.py:1053
  1535.7 29.2 %collective-permute-start.7 = (bf16[512,2048]{1,0:T(8,128)(2,1)S(1)}, bf16[512,2048]{1,0:T(8,128)(2,1)}, u32[]{:S(2)}, u32[]{:S(2)}) collective-permute-start(bf16[512,2048]{1,0:T(8,128)(2,1)S(1)} %copy.105), channel_id=1, source_target_pairs={{0,8},{8,16},{16,24},{24,32},{32,40},{40,48},{48,56},{56,64},{64,7... | collective-permute-start | bytes 6291464 | tf_op jit(solution)/shard_map/cond/branch_0_fun/while/body/eval_jaxpr/ppermute | solution.py:1053
  1566.5 29.2 %collective-permute-start.7 = (bf16[512,2048]{1,0:T(8,128)(2,1)S(1)}, bf16[512,2048]{1,0:T(8,128)(2,1)}, u32[]{:S(2)}, u32[]{:S(2)}) collective-permute-start(bf16[512,2048]{1,0:T(8,128)(2,1)S(1)} %copy.105), channel_id=1, source_target_pairs={{0,8},{8,16},{16,24},{24,32},{32,40},{40,48},{48,56},{56,64},{64,7... | collective-permute-start | bytes 6291464 | tf_op jit(solution)/shard_map/cond/branch_0_fun/while/body/eval_jaxpr/ppermute | solution.py:1053
  1597.3 29.2 %collective-permute-start.7 = (bf16[512,2048]{1,0:T(8,128)(2,1)S(1)}, bf16[512,2048]{1,0:T(8,128)(2,1)}, u32[]{:S(2)}, u32[]{:S(2)}) collective-permute-start(bf16[512,2048]{1,0:T(8,128)(2,1)S(1)} %copy.105), channel_id=1, source_target_pairs={{0,8},{8,16},{16,24},{24,32},{32,40},{40,48},{48,56},{56,64},{64,7... | collective-permute-start | bytes 6291464 | tf_op jit(solution)/shard_map/cond/branch_0_fun/while/body/eval_jaxpr/ppermute | solution.py:1053
  1628.0 29.2 %collective-permute-start.7 = (bf16[512,2048]{1,0:T(8,128)(2,1)S(1)}, bf16[512,2048]{1,0:T(8,128)(2,1)}, u32[]{:S(2)}, u32[]{:S(2)}) collective-permute-start(bf16[512,2048]{1,0:T(8,128)(2,1)S(1)} %copy.105), channel_id=1, source_target_pairs={{0,8},{8,16},{16,24},{24,32},{32,40},{40,48},{48,56},{56,64},{64,7... | collective-permute-start | bytes 6291464 | tf_op jit(solution)/shard_map/cond/branch_0_fun/while/body/eval_jaxpr/ppermute | solution.py:1053
  1658.8 29.2 %collective-permute-start.7 = (bf16[512,2048]{1,0:T(8,128)(2,1)S(1)}, bf16[512,2048]{1,0:T(8,128)(2,1)}, u32[]{:S(2)}, u32[]{:S(2)}) collective-permute-start(bf16[512,2048]{1,0:T(8,128)(2,1)S(1)} %copy.105), channel_id=1, source_target_pairs={{0,8},{8,16},{16,24},{24,32},{32,40},{40,48},{48,56},{56,64},{64,7... | collective-permute-start | bytes 6291464 | tf_op jit(solution)/shard_map/cond/branch_0_fun/while/body/eval_jaxpr/ppermute | solution.py:1053
  1689.6 29.2 %collective-permute-start.7 = (bf16[512,2048]{1,0:T(8,128)(2,1)S(1)}, bf16[512,2048]{1,0:T(8,128)(2,1)}, u32[]{:S(2)}, u32[]{:S(2)}) collective-permute-start(bf16[512,2048]{1,0:T(8,128)(2,1)S(1)} %copy.105), channel_id=1, source_target_pairs={{0,8},{8,16},{16,24},{24,32},{32,40},{40,48},{48,56},{56,64},{64,7... | collective-permute-start | bytes 6291464 | tf_op jit(solution)/shard_map/cond/branch_0_fun/while/body/eval_jaxpr/ppermute | solution.py:1053
  1720.4 29.2 %collective-permute-start.7 = (bf16[512,2048]{1,0:T(8,128)(2,1)S(1)}, bf16[512,2048]{1,0:T(8,128)(2,1)}, u32[]{:S(2)}, u32[]{:S(2)}) collective-permute-start(bf16[512,2048]{1,0:T(8,128)(2,1)S(1)} %copy.105), channel_id=1, source_target_pairs={{0,8},{8,16},{16,24},{24,32},{32,40},{40,48},{48,56},{56,64},{64,7... | collective-permute-start | bytes 6291464 | tf_op jit(solution)/shard_map/cond/branch_0_fun/while/body/eval_jaxpr/ppermute | solution.py:1053
  1751.1 29.2 %collective-permute-start.7 = (bf16[512,2048]{1,0:T(8,128)(2,1)S(1)}, bf16[512,2048]{1,0:T(8,128)(2,1)}, u32[]{:S(2)}, u32[]{:S(2)}) collective-permute-start(bf16[512,2048]{1,0:T(8,128)(2,1)S(1)} %copy.105), channel_id=1, source_target_pairs={{0,8},{8,16},{16,24},{24,32},{32,40},{40,48},{48,56},{56,64},{64,7... | collective-permute-start | bytes 6291464 | tf_op jit(solution)/shard_map/cond/branch_0_fun/while/body/eval_jaxpr/ppermute | solution.py:1053
  1781.9 29.2 %collective-permute-start.7 = (bf16[512,2048]{1,0:T(8,128)(2,1)S(1)}, bf16[512,2048]{1,0:T(8,128)(2,1)}, u32[]{:S(2)}, u32[]{:S(2)}) collective-permute-start(bf16[512,2048]{1,0:T(8,128)(2,1)S(1)} %copy.105), channel_id=1, source_target_pairs={{0,8},{8,16},{16,24},{24,32},{32,40},{40,48},{48,56},{56,64},{64,7... | collective-permute-start | bytes 6291464 | tf_op jit(solution)/shard_map/cond/branch_0_fun/while/body/eval_jaxpr/ppermute | solution.py:1053
  1812.7 29.2 %collective-permute-start.7 = (bf16[512,2048]{1,0:T(8,128)(2,1)S(1)}, bf16[512,2048]{1,0:T(8,128)(2,1)}, u32[]{:S(2)}, u32[]{:S(2)}) collective-permute-start(bf16[512,2048]{1,0:T(8,128)(2,1)S(1)} %copy.105), channel_id=1, source_target_pairs={{0,8},{8,16},{16,24},{24,32},{32,40},{40,48},{48,56},{56,64},{64,7... | collective-permute-start | bytes 6291464 | tf_op jit(solution)/shard_map/cond/branch_0_fun/while/body/eval_jaxpr/ppermute | solution.py:1053
  1843.4 29.2 %collective-permute-start.7 = (bf16[512,2048]{1,0:T(8,128)(2,1)S(1)}, bf16[512,2048]{1,0:T(8,128)(2,1)}, u32[]{:S(2)}, u32[]{:S(2)}) collective-permute-start(bf16[512,2048]{1,0:T(8,128)(2,1)S(1)} %copy.105), channel_id=1, source_target_pairs={{0,8},{8,16},{16,24},{24,32},{32,40},{40,48},{48,56},{56,64},{64,7... | collective-permute-start | bytes 6291464 | tf_op jit(solution)/shard_map/cond/branch_0_fun/while/body/eval_jaxpr/ppermute | solution.py:1053
  1874.2 29.2 %collective-permute-start.7 = (bf16[512,2048]{1,0:T(8,128)(2,1)S(1)}, bf16[512,2048]{1,0:T(8,128)(2,1)}, u32[]{:S(2)}, u32[]{:S(2)}) collective-permute-start(bf16[512,2048]{1,0:T(8,128)(2,1)S(1)} %copy.105), channel_id=1, source_target_pairs={{0,8},{8,16},{16,24},{24,32},{32,40},{40,48},{48,56},{56,64},{64,7... | collective-permute-start | bytes 6291464 | tf_op jit(solution)/shard_map/cond/branch_0_fun/while/body/eval_jaxpr/ppermute | solution.py:1053
  1905.0 29.2 %collective-permute-start.7 = (bf16[512,2048]{1,0:T(8,128)(2,1)S(1)}, bf16[512,2048]{1,0:T(8,128)(2,1)}, u32[]{:S(2)}, u32[]{:S(2)}) collective-permute-start(bf16[512,2048]{1,0:T(8,128)(2,1)S(1)} %copy.105), channel_id=1, source_target_pairs={{0,8},{8,16},{16,24},{24,32},{32,40},{40,48},{48,56},{56,64},{64,7... | collective-permute-start | bytes 6291464 | tf_op jit(solution)/shard_map/cond/branch_0_fun/while/body/eval_jaxpr/ppermute | solution.py:1053
  1951.2 25.0 %collective-permute-start.8 = (bf16[512,2048]{1,0:T(8,128)(2,1)S(1)}, bf16[512,2048]{1,0:T(8,128)(2,1)}, u32[]{:S(2)}, u32[]{:S(2)}) collective-permute-start(bf16[512,2048]{1,0:T(8,128)(2,1)S(1)} %copy.114), channel_id=1, source_target_pairs={{0,4},{4,0},{1,5},{5,1},{2,6},{6,2},{3,7},{7,3},{8,12},{12,8},{9,1... | collective-permute-start | bytes 6291464 | tf_op jit(solution)/shard_map/cond/branch_0_fun/while/body/eval_jaxpr/ppermute | solution.py:1053
  1977.8 42.7 %collective-permute-start.8 = (bf16[512,2048]{1,0:T(8,128)(2,1)S(1)}, bf16[512,2048]{1,0:T(8,128)(2,1)}, u32[]{:S(2)}, u32[]{:S(2)}) collective-permute-start(bf16[512,2048]{1,0:T(8,128)(2,1)S(1)} %copy.114), channel_id=1, source_target_pairs={{0,4},{4,0},{1,5},{5,1},{2,6},{6,2},{3,7},{7,3},{8,12},{12,8},{9,1... | collective-permute-start | bytes 6291464 | tf_op jit(solution)/shard_map/cond/branch_0_fun/while/body/eval_jaxpr/ppermute | solution.py:1053
  2034.9 48.2 %collective-permute-start.5 = (bf16[384,1536]{1,0:T(8,128)(2,1)S(1)}, bf16[384,1536]{1,0:T(8,128)(2,1)S(1)}, u32[]{:S(2)}, u32[]{:S(2)}) collective-permute-start(bf16[384,1536]{1,0:T(8,128)(2,1)S(1)} %copy.87), channel_id=1, source_target_pairs={{0,8},{8,16},{16,24},{24,32},{32,40},{40,48},{48,56},{56,64},{64,7... | collective-permute-start | bytes 3538952 | tf_op jit(solution)/shard_map/cond/branch_0_fun/while/body/eval_jaxpr/ppermute | solution.py:1053
  2083.2 19.3 collective-permute-start.5
  2102.6 19.3 collective-permute-start.5
  2122.0 19.3 collective-permute-start.5
  2141.4 19.3 collective-permute-start.5
  2160.8 19.3 collective-permute-start.5
  2180.2 19.3 collective-permute-start.5
  2199.6 19.3 collective-permute-start.5
  2219.0 19.3 collective-permute-start.5
  2238.4 19.3 collective-permute-start.5
  2257.7 19.3 collective-permute-start.5
  2277.1 19.3 collective-permute-start.5
  2296.5 19.3 collective-permute-start.5
  2315.9 19.3 collective-permute-start.5
  2335.3 19.3 collective-permute-start.5
  2354.7 19.3 collective-permute-start.5
  2386.0 15.1 collective-permute-start.6
  2401.2 23.6 collective-permute-start.6
  (58 other events, 1010.6 us)
